TPU v7x, 32 devices: a whole 2x2x4 slice. The times are simulated.
32 devices in a mesh: dp: 4 (over y, core), fsdp: 8 (over z, x).
Axes of the slice: x: 2, y: 2, z: 4, core: 2. Of those that a mesh axis runs over, the one named last changes fastest.
Arguments:
- gate_act: bfloat16 [1536, 14336], P('dp', 'fsdp'), may hold values from -6 to 6
- up_act: bfloat16 [1536, 14336], P('dp', 'fsdp'), may hold values from -6 to 6
- out_grad: bfloat16 [1536, 5120], P('dp', 'fsdp'), may hold values from -6 to 6
- down_weight: bfloat16 [14336, 5120], P('fsdp'), may hold values from -0.046875 to 0.046875
- val_hidden: bfloat16 [1024, 14336], P('dp', 'fsdp'), may hold values from -4 to 4
- val_grad: bfloat16 [1024, 5120], P('dp', 'fsdp'), may hold values from -6 to 6
- assign: int32 [12], P('dp'), may hold values from 0 to 3
Outputs:
- grad_gate: bfloat16 [1536, 14336], P('dp', 'fsdp')
- grad_up: bfloat16 [1536, 14336], P('dp', 'fsdp')
- weight_grad: bfloat16 [14336, 5120], P('fsdp', 'dp')
- row_scores: float32 [12, 4], P('dp')
- group_values: float32 [4], replicated
All inputs are finite; a program needn't handle non-finite values.
Results may differ from a plain program's by a relative error of at most 0.012.
The roundings to bfloat16 on the way count: a program that leaves them out, or rounds other values in their place, can miss the bound.
Values may be sent and summed in bfloat16 or wider, within the bound.
No kernel may reach another device: no remote copies, remote signals or barrier semaphores. Data moves between devices by JAX's collectives and lax.ppermute only.
A program may use at most 128 MiB of HBM per device.

v0:
```python
import jax
import jax.numpy as jnp
from jax import lax
from jax.sharding import PartitionSpec as P

D = 5120
FFW = 14336
L = 128
VAL = 256


def per_device(gate_act, up_act, out_grad, down_weight, val_hidden, val_grad, assign):
    gate = gate_act.astype(jnp.float32)
    up = up_act.astype(jnp.float32)
    sig = jax.nn.sigmoid(gate)
    act = gate * sig
    hidden = (act * up).astype(jnp.bfloat16)
    tok_count = gate_act.shape[0]
    dp_count = lax.axis_size("dp")
    rows_here = assign.shape[0]
    piece = lax.all_gather(out_grad, "fsdp", axis=1, tiled=True)
    grad_hidden = lax.dot_general(
        piece, down_weight, (((1,), (1,)), ((), ())), preferred_element_type=jnp.float32
    )
    block = lax.dot_general(
        hidden, piece, (((0,), (0,)), ((), ())), preferred_element_type=jnp.float32
    )
    grad_hidden, folded = (grad_hidden, block)
    rounded = lax.optimization_barrier(folded.astype(jnp.bfloat16))
    weight_grad = lax.psum_scatter(
        rounded.astype(jnp.float32).astype(jnp.bfloat16), "dp", scatter_dimension=1, tiled=True
    )
    grad_gate = (grad_hidden * up * sig * (1.0 + gate * (1.0 - sig))).astype(jnp.bfloat16)
    grad_up = (grad_hidden * act).astype(jnp.bfloat16)
    val_h = lax.all_gather(val_hidden, "dp", axis=0, tiled=True)
    val_g = lax.all_gather(val_grad, "dp", axis=0, tiled=True)
    part_h = lax.dot_general(
        hidden, val_h, (((1,), (1,)), ((), ())), preferred_element_type=jnp.float32
    )
    part_g = lax.dot_general(
        out_grad, val_g, (((1,), (1,)), ((), ())), preferred_element_type=jnp.float32
    )
    hidden_gram = part_h
    grad_gram = part_g
    hidden_gram, grad_gram = (hidden_gram, grad_gram)
    whole_grad = lax.psum(grad_gram, "fsdp")
    product = hidden_gram * whole_grad
    columns = product.shape[1]
    per_row = jnp.sum(product.reshape(rows_here, tok_count // rows_here, columns), axis=1)
    col_group = jnp.arange(columns, dtype=jnp.int32) // VAL
    col_onehot = (col_group[:, None] == jnp.arange(dp_count, dtype=jnp.int32)[None, :]).astype(
        jnp.float32
    )
    scale = 1.0 / jnp.sqrt(jnp.float32(L) * VAL * FFW * D)
    partial_scores = (
        jnp.dot(
            per_row, col_onehot, precision=lax.Precision.HIGHEST, preferred_element_type=jnp.float32
        )
        * scale
    )
    row_onehot = (assign[:, None] == jnp.arange(dp_count, dtype=jnp.int32)[None, :]).astype(
        jnp.float32
    )
    row_scores = lax.psum(partial_scores, "fsdp")
    group_values = lax.psum(jnp.sum(row_onehot * row_scores, axis=0), "dp")
    return (grad_gate, grad_up, weight_grad, row_scores, group_values)


def solution(mesh):
    in_specs = (
        P("dp", "fsdp"),
        P("dp", "fsdp"),
        P("dp", "fsdp"),
        P("fsdp", None),
        P("dp", "fsdp"),
        P("dp", "fsdp"),
        P("dp"),
    )
    out_specs = (P("dp", "fsdp"), P("dp", "fsdp"), P("fsdp", "dp"), P("dp", None), P())
    return jax.shard_map(
        per_device, mesh=mesh, in_specs=in_specs, out_specs=out_specs, check_vma=False
    )
```

profile of v0, /device:TPU:0, one launch (start us, length us, event | category | flops | bytes accessed | tf_op | source)
XLA Modules:
  0.0 371.8 jit_solution(7830866197153155463)
XLA Ops:
  7.2 0.0 all-gather.8.cloned.1.call-start
  7.2 0.7 all-gather.8.cloned.1.call-update
  7.9 0.0 all-gather.4.cloned.1.call-start
  7.9 0.7 all-gather.4.cloned.1.call-update
  8.7 0.0 all-reduce.2.cloned.1.call-start
  8.7 21.8 %all-gather.8.cloned.1.call-done = bf16[1024,640]{1,0:T(8,128)(2,1)} async-done(((bf16[256,640]{1,0:T(8,128)(2,1)}), bf16[1024,640]{1,0:T(8,128)(2,1)}) %all-gather.8.cloned.1.call-update) | async-done | bytes 1310736 | tf_op jit(solution)/shard_map/all_gather | solution.py:36
  30.5 3.4 fusion.14
  33.9 0.0 all-reduce.2.cloned.1.call-update
  33.9 0.0 all-gather.6.cloned.1.call-start
  34.0 0.5 all-gather.6.cloned.1.call-update
  34.5 0.0 reduce-scatter.2.cloned.1.call-start
  34.6 68.0 %all-gather.4.cloned.1.call-done = bf16[384,5120]{1,0:T(8,128)(2,1)} async-done(((bf16[384,640]{1,0:T(8,128)(2,1)}), bf16[384,5120]{1,0:T(8,128)(2,1)}) %all-gather.4.cloned.1.call-update) | async-done | bytes 3932176 | tf_op jit(solution)/shard_map/all_gather | solution.py:21
  102.5 15.9 %convolution_convert_fusion = bf16[1792,5120]{1,0:T(8,128)(2,1)} fusion(bf16[384,5120]{1,0:T(8,128)(2,1)} %all-gather.4.cloned.1.call-done, bf16[384,1792]{1,0:T(8,128)(2,1)S(1)} %copy-done.3, bf16[384,1792]{1,0:T(8,128)(2,1)S(1)} %copy-done.2), kind=kOutput, calls=%fused_computation | convolution fusion | flops 7061110784 | bytes 25034752 | tf_op jit(solution)/shard_map/dot_general | solution.py:25
  118.4 0.0 reduce-scatter.2.cloned.1.call-update
  118.5 75.3 %all-reduce.2.cloned.1.call-done = f32[384,1024]{1,0:T(8,128)} async-done(((f32[384,1024]{1,0:T(8,128)}), f32[384,1024]{1,0:T(8,128)}) %all-reduce.2.cloned.1.call-update) | async-done | bytes 1572880 | tf_op jit(solution)/shard_map/psum | solution.py:46
  193.8 32.3 %all-gather.6.cloned.1.call-done = bf16[1024,1792]{1,0:T(8,128)(2,1)} async-done(((bf16[256,1792]{1,0:T(8,128)(2,1)}), bf16[1024,1792]{1,0:T(8,128)(2,1)}) %all-gather.6.cloned.1.call-update) | async-done | bytes 3670032 | tf_op jit(solution)/shard_map/all_gather | solution.py:35
  226.1 4.7 %convolution_multiply_fusion = f32[384,1024]{1,0:T(8,128)S(1)} fusion(f32[384,1024]{1,0:T(8,128)} %all-reduce.2.cloned.1.call-done, bf16[1024,1792]{1,0:T(8,128)(2,1)} %all-gather.6.cloned.1.call-done, bf16[384,1792]{1,0:T(8,128)(2,1)} %param.8, bf16[384,1792]{1,0:T(8,128)(2,1)S(1)} %copy-done.2), kind=kOutput, calls=%fused_computation.15 | convolution fusion | flops 1415184384 | bytes 9568256 | tf_op jit(solution)/shard_map/dot_general | solution.py:37
  230.9 0.1 reduce_sum.18
  231.0 0.4 convolution_multiply_fusion.1
  231.4 21.3 %psum.22 = f32[3,4]{1,0:T(4,128)S(1)} all-reduce(f32[3,4]{1,0:T(4,128)S(1)} %convolution_multiply_fusion.1), channel_id=1, replica_groups=mesh['dp'=4,'fsdp'=8] {'fsdp'}, use_global_device_ids=true, to_apply=%region_3.4 | all-reduce | flops 12 | bytes 96 | tf_op jit(solution)/shard_map/psum | solution.py:64
  252.7 0.1 select_reduce_fusion
  252.8 6.6 %psum.23 = f32[4]{0:T(128)} all-reduce(f32[4]{0:T(128)S(1)} %select_reduce_fusion), channel_id=1, replica_groups=mesh['dp'=4,'fsdp'=8] {'dp'}, use_global_device_ids=true, to_apply=%region_5.6 | all-reduce | flops 4 | bytes 32 | tf_op jit(solution)/shard_map/psum | solution.py:65
  259.4 16.0 %multiply_convert_fusion = (bf16[384,1792]{1,0:T(8,128)(2,1)}, bf16[384,1792]{1,0:T(8,128)(2,1)}) fusion(bf16[384,1792]{1,0:T(8,128)(2,1)S(1)} %copy-done.2, bf16[384,1792]{1,0:T(8,128)(2,1)} %param.8, bf16[384,5120]{1,0:T(8,128)(2,1)} %all-gather.4.cloned.1.call-done, bf16[1792,5120]{1,0:T(8,128)(2,1)} %param.10), kind=kOutput, calls=%fused_computation.14 | convolution fusion | flops 7056752640 | bytes 27787264 | tf_op jit(solution)/shard_map/dot_general | solution.py:22
  275.4 89.9 %reduce-scatter.2.cloned.1.call-done = bf16[1792,1280]{1,0:T(8,128)(2,1)} async-done(((bf16[1792,5120]{1,0:T(8,128)(2,1)}), bf16[1792,1280]{1,0:T(8,128)(2,1)}) %reduce-scatter.2.cloned.1.call-update) | async-done | bytes 4587536 | tf_op jit(solution)/shard_map/reduce_scatter | solution.py:30
  (9 shorter events, 0.0 us)
Async XLA Ops:
  7.2 23.3 %all-gather.8.cloned.1.call-start = ((), (), s32[]{:S(2)}) async-start(), calls=%async_computation.4 | async-start | bytes 1638400 | tf_op jit(solution)/shard_map/all_gather | solution.py:36
  7.9 94.6 %all-gather.4.cloned.1.call-start = ((), (), s32[]{:S(2)}) async-start(), calls=%async_computation.1 | async-start | bytes 4423680 | tf_op jit(solution)/shard_map/all_gather | solution.py:21
  8.7 93.9 %copy-start.2 = (bf16[384,1792]{1,0:T(8,128)(2,1)S(1)}, bf16[384,1792]{1,0:T(8,128)(2,1)}, u32[]{:S(2)}) copy-start(bf16[384,1792]{1,0:T(8,128)(2,1)} %param.7) | copy-start | bytes 4128772
  8.7 93.9 %copy-start.3 = (bf16[384,1792]{1,0:T(8,128)(2,1)S(1)}, bf16[384,1792]{1,0:T(8,128)(2,1)}, u32[]{:S(2)}) copy-start(bf16[384,1792]{1,0:T(8,128)(2,1)} %param.8) | copy-start | bytes 4128772
  8.7 185.1 %all-reduce.2.cloned.1.call-start = ((), (), s32[]{:S(2)}) async-start(), calls=%async_computation.5 | async-start | bytes 3145728 | tf_op jit(solution)/shard_map/psum | solution.py:46
  33.9 192.2 %all-gather.6.cloned.1.call-start = ((), (), s32[]{:S(2)}) async-start(), calls=%async_computation.3 | async-start | bytes 4587520 | tf_op jit(solution)/shard_map/all_gather | solution.py:35
  34.5 330.8 %reduce-scatter.2.cloned.1.call-start = ((), (), s32[]{:S(2)}) async-start(), calls=%async_computation.2 | async-start | bytes 22937600 | tf_op jit(solution)/shard_map/reduce_scatter | solution.py:30
  118.5 134.3 %copy-start.1 = (s32[3]{0:T(128)S(1)}, s32[3]{0:T(128)}, u32[]{:S(2)}) copy-start(s32[3]{0:T(128)} %param.13) | copy-start | bytes 40
  252.7 22.7 %copy-start = (f32[3,4]{1,0:T(4,128)}, f32[3,4]{1,0:T(4,128)S(1)}, u32[]{:S(2)}) copy-start(f32[3,4]{1,0:T(4,128)S(1)} %psum.22) | copy-start | bytes 148
Sparse Core Ops, SparseCore 0:
  9.6 20.8 all-gather.7
  32.7 69.7 all-gather.3
  106.1 87.6 all-reduce.1
  195.2 30.8 all-gather.5
  229.2 136.0 reduce-scatter.1
where the time goes:
time: 372 us
  waiting for transfers between devices  289 us (78%)
  matrix products  40.4 us (11%)
  blocking collectives  28 us (8%)
  between operations  13.8 us (4%)
    reduce_scatter x1, waiting for transfers between devices, per_device(): lax.psum_scatter(rounded.astype(jnp.float32).astype(jnp.bfloat16), 'dp',...  89.9 us
    psum x1, waiting for transfers between devices, per_device(): whole_grad = lax.psum(grad_gram, 'fsdp')  75.3 us
    all_gather x1, waiting for transfers between devices, per_device(): piece = lax.all_gather(out_grad, 'fsdp', axis=1, tiled=True)  68 us
    all_gather x1, waiting for transfers between devices, per_device(): val_h = lax.all_gather(val_hidden, 'dp', axis=0, tiled=True)  32.3 us
    all_gather x1, waiting for transfers between devices, per_device(): val_g = lax.all_gather(val_grad, 'dp', axis=0, tiled=True)  21.8 us
    psum x1, blocking collectives, per_device(): row_scores = lax.psum(partial_scores, 'fsdp')  21.3 us
    dot_general x1, matrix products, per_device(): lax.dot_general(piece, down_weight, (((1,), (1,)), ((), ())), preferred_e...  16 us
    dot_general x1, matrix products, per_device(): lax.dot_general(hidden, piece, (((0,), (0,)), ((), ())), preferred_elemen...  15.9 us
  transfers between devices with their start and end apart: 5, of which 5 were waited for; matrix products, arithmetic and copies ran while one was open for 11% of the time, Pallas kernels for 0%

commit v1 on v0

v1 whole, which is shorter than its diff:
```python
import jax
import jax.numpy as jnp
from jax import lax
from jax.sharding import PartitionSpec as P

D = 5120
FFW = 14336
L = 128
VAL = 256

F32 = jnp.float32
BF16 = jnp.bfloat16


def dot_nt(a, b):
    return lax.dot_general(a, b, (((1,), (1,)), ((), ())), preferred_element_type=F32)


def dot_tn(a, b):
    return lax.dot_general(a, b, (((0,), (0,)), ((), ())), preferred_element_type=F32)


def per_device(gate_act, up_act, out_grad, down_weight, val_hidden, val_grad, assign):
    dp_count = lax.axis_size("dp")
    me = lax.axis_index("dp")
    rows_here = assign.shape[0]
    tok_count = gate_act.shape[0]
    gate = gate_act.astype(F32)
    up = up_act.astype(F32)
    sig = jax.nn.sigmoid(gate)
    act = gate * sig
    hidden = (act * up).astype(BF16)

    hidden, gate_act, up_act = lax.optimization_barrier((hidden, gate_act, up_act))
    gate = gate_act.astype(F32)
    up = up_act.astype(F32)
    sig = jax.nn.sigmoid(gate)
    act = gate * sig

    grad_feat = lax.all_gather(out_grad, "dp", axis=0, tiled=True)
    piece = lax.all_gather(out_grad, "fsdp", axis=1, tiled=True)
    hidden_all = lax.all_gather(hidden, "dp", axis=0, tiled=True)

    grad_gram = lax.psum(dot_nt(grad_feat, val_grad), "fsdp")

    grad_cols = lax.all_to_all(piece, "dp", split_axis=1, concat_axis=0, tiled=True)

    grad_hidden = dot_nt(piece, down_weight)
    grad_gate = (grad_hidden * up * sig * (1.0 + gate * (1.0 - sig))).astype(BF16)
    grad_up = (grad_hidden * act).astype(BF16)

    hidden_gram = dot_nt(hidden_all, val_hidden)
    product = hidden_gram * grad_gram
    part = jnp.sum(product.reshape(dp_count * rows_here, tok_count // rows_here * VAL), axis=1)

    weight_grad = dot_tn(hidden_all, grad_cols).astype(BF16)

    scale = 1.0 / jnp.sqrt(F32(L) * VAL * FFW * D)
    mine = jnp.concatenate([part, assign.astype(F32)])
    every = lax.all_gather(mine, ("dp", "fsdp"), axis=0, tiled=False)
    every = every.reshape(dp_count, -1, mine.shape[0])
    rows = dp_count * rows_here
    scores = jnp.sum(every[:, :, :rows], axis=1) * scale
    groups = every[:, 0, rows:].reshape(rows)
    onehot = (groups[None, :] == jnp.arange(dp_count, dtype=F32)[:, None]).astype(F32)
    group_values = jnp.sum(onehot * scores, axis=1)
    row_scores = lax.dynamic_slice_in_dim(scores, me * rows_here, rows_here, axis=1).T
    return (grad_gate, grad_up, weight_grad, row_scores, group_values)


def solution(mesh):
    in_specs = (
        P("dp", "fsdp"),
        P("dp", "fsdp"),
        P("dp", "fsdp"),
        P("fsdp", None),
        P("dp", "fsdp"),
        P("dp", "fsdp"),
        P("dp"),
    )
    out_specs = (P("dp", "fsdp"), P("dp", "fsdp"), P("fsdp", "dp"), P("dp", None), P())
    return jax.shard_map(
        per_device, mesh=mesh, in_specs=in_specs, out_specs=out_specs, check_vma=False
    )
```

time: 372 us -> 313 us (0.84)
  waiting for transfers between devices: 289 us -> 205 us
  blocking collectives: 28 us -> 39.5 us
  local copies, waits for them, and re-layouts: 0.02 us -> 9.37 us
  starting transfers between devices: 0.19 us -> 4.95 us
  matrix products: 40.4 us -> 35.8 us
  other arithmetic: 0.2 us -> 4.22 us
    reduce_scatter x1 -> x0, waiting for transfers between devices: 89.9 us -> none  [per_device(): lax.psum_scatter(rounded.astype(jnp.float32).astype(jnp.bfloat16), 'dp',...]
    unnamed x0 -> x1, blocking collectives: none -> 39.5 us
    psum x2 -> x0, blocking collectives: 28 us -> none  [the longest x1 21.3 us: per_device(): row_scores = lax.psum(partial_scores, 'fsdp')]
    all_gather x2, waiting for transfers between devices: 54.1 us -> 66.9 us  [the longest x1 42.8 us: per_device(): hidden_all = lax.all_gather(hidden, 'dp', axis=0, tiled=True)]
    all_to_all x0 -> x1, local copies, waits for them, and re-layouts: none -> 6.32 us  [per_device(): lax.all_to_all(piece, 'dp', split_axis=1, concat_axis=0, tiled=True)]
    all_to_all x0 -> x1, starting transfers between devices: none -> 4.79 us  [per_device(): lax.all_to_all(piece, 'dp', split_axis=1, concat_axis=0, tiled=True)]
    dot_general x5 -> x4, matrix products: 40.4 us -> 35.8 us  [the longest x3 23.8 us: dot_nt(): lax.dot_general(a, b, (((1,), (1,)), ((), ())), preferred_element_type=F32)]
    psum x1, waiting for transfers between devices: 75.3 us -> 71 us  [per_device(): grad_gram = lax.psum(dot_nt(grad_feat, val_grad), 'fsdp')]
  transfers between devices with their start and end apart: 5 -> 5, of which waited for: 5 -> 4; matrix products, arithmetic and copies ran while one was open for 11% -> 10% of each run, Pallas kernels for 0% -> 0%
where the time goes in v1:
time: 313 us; the launch traced here: 312 us
  waiting for transfers between devices  205 us (65%)
  blocking collectives  39.5 us (13%)
  matrix products  35.8 us (11%)
  between operations  13.9 us (4%)
  local copies, waits for them, and re-layouts  9.37 us (3%)
  starting transfers between devices  4.95 us (2%)
  other arithmetic  4.22 us (1%)
    psum x1, waiting for transfers between devices, per_device(): grad_gram = lax.psum(dot_nt(grad_feat, val_grad), 'fsdp')  71 us
    all_gather x1, waiting for transfers between devices, per_device(): piece = lax.all_gather(out_grad, 'fsdp', axis=1, tiled=True)  65.9 us
    all_gather x1, waiting for transfers between devices, per_device(): hidden_all = lax.all_gather(hidden, 'dp', axis=0, tiled=True)  42.8 us
    unnamed x1, blocking collectives  39.5 us
    all_gather x1, waiting for transfers between devices, per_device(): grad_feat = lax.all_gather(out_grad, 'dp', axis=0, tiled=True)  24.1 us
    dot_general x3, matrix products, dot_nt(): lax.dot_general(a, b, (((1,), (1,)), ((), ())), preferred_element_type=F32)  23.8 us
    dot_general x1, matrix products, dot_tn(): lax.dot_general(a, b, (((0,), (0,)), ((), ())), preferred_element_type=F32)  12 us
    all_to_all x1, local copies, waits for them, and re-layouts, per_device(): lax.all_to_all(piece, 'dp', split_axis=1, concat_axis=0, tiled=True)  6.32 us
  transfers between devices with their start and end apart: 5, of which 4 were waited for; matrix products, arithmetic and copies ran while one was open for 10% of the time, Pallas kernels for 0%

profile of v1, /device:TPU:0, one launch (start us, length us, event | category | flops | bytes accessed | tf_op | source)
XLA Modules:
  0.0 312.2 jit_solution(11510825101543453134)
XLA Ops:
  7.2 0.7 all-gather.9.cloned.1.call-update
  8.0 2.0 copy.21
  10.0 0.0 all-reduce.3.cloned.1.call-start
  10.1 24.1 %all-gather.9.cloned.1.call-done = bf16[1536,640]{1,0:T(8,128)(2,1)} async-done(((bf16[384,640]{1,0:T(8,128)(2,1)}), bf16[1536,640]{1,0:T(8,128)(2,1)}) %all-gather.9.cloned.1.call-update) | async-done | bytes 1966096 | tf_op jit(solution)/shard_map/all_gather | solution.py:40
  34.2 3.5 %fusion.14 = f32[1536,256]{0,1:T(8,128)} fusion(bf16[1536,640]{1,0:T(8,128)(2,1)} %all-gather.9.cloned.1.call-done, bf16[256,640]{1,0:T(8,128)(2,1)} %param.12), kind=kOutput, calls=%fused_computation.29 | convolution fusion | flops 503316480 | bytes 3866624 | tf_op jit(solution)/shard_map/dot_general | solution.py:16
  37.7 0.0 all-gather.7.cloned.1.call-start
  37.8 3.3 %fusion.12 = bf16[384,1792]{1,0:T(8,128)(2,1)} fusion(bf16[384,1792]{1,0:T(8,128)(2,1)} %param.8, bf16[384,1792]{1,0:T(8,128)(2,1)S(1)} %copy-done.1), kind=kLoop, calls=%fused_computation.19 | loop fusion | flops 5505024 | bytes 4128768 | tf_op jit(solution)/shard_map/convert_element_type | solution.py:32
  41.1 65.9 %all-gather.5.cloned.1.call-done = bf16[384,5120]{0,1:T(8,128)(2,1)} async-done(((bf16[384,640]{0,1:T(8,128)(2,1)}), bf16[384,5120]{0,1:T(8,128)(2,1)}) %all-gather.5.cloned.1.call-update) | async-done | bytes 3932176 | tf_op jit(solution)/shard_map/all_gather | solution.py:41
  107.1 4.8 %all-to-all-start = ((bf16[384,4,1280]{0,2,1:T(8,128)(2,1)}), bf16[384,4,1280]{0,2,1:T(8,128)(2,1)}, u32[]{:S(2)}, u32[]{:S(2)}) async-start(bf16[384,4,1280]{0,2,1:T(8,128)(2,1)} %bitcast.15), calls=%async_computation | async-start | bytes 7864320 | tf_op jit(solution)/shard_map/all_to_all | solution.py:46
  111.9 15.6 %fusion.11 = (bf16[384,1792]{1,0:T(8,128)(2,1)}, bf16[384,1792]{1,0:T(8,128)(2,1)}) fusion(bf16[384,1792]{1,0:T(8,128)(2,1)S(1)} %copy-done.1, bf16[384,1792]{1,0:T(8,128)(2,1)} %param.8, bf16[384,5120]{0,1:T(8,128)(2,1)} %all-gather.5.cloned.1.call-done, bf16[1792,5120]{1,0:T(8,128)(2,1)} %param.10), kind=kOutput, calls=%fused_computation.18 | convolution fusion | flops 7056752640 | bytes 27787264 | tf_op jit(solution)/shard_map/dot_general | solution.py:16
  127.5 71.0 %all-reduce.3.cloned.1.call-done = f32[1536,256]{0,1:T(8,128)} async-done(((f32[1536,256]{0,1:T(8,128)}), f32[1536,256]{0,1:T(8,128)}) %all-reduce.3.cloned.1.call-update) | async-done | bytes 1572880 | tf_op jit(solution)/shard_map/psum | solution.py:44
  198.5 42.8 %all-gather.7.cloned.1.call-done = bf16[1536,1792]{1,0:T(8,128)(2,1)} async-done(((bf16[384,1792]{1,0:T(8,128)(2,1)}), bf16[1536,1792]{1,0:T(8,128)(2,1)}) %all-gather.7.cloned.1.call-update) | async-done | bytes 5505040 | tf_op jit(solution)/shard_map/all_gather | solution.py:42
  241.3 4.7 %fusion.13 = f32[1536]{0:T(1024)S(1)} fusion(f32[1536,256]{0,1:T(8,128)} %all-reduce.3.cloned.1.call-done, bf16[1536,1792]{1,0:T(8,128)(2,1)} %all-gather.7.cloned.1.call-done, bf16[256,1792]{1,0:T(8,128)(2,1)S(1)} %copy-done), kind=kOutput, calls=%fused_computation.20 | convolution fusion | flops 1410071040 | bytes 8001536 | tf_op jit(solution)/shard_map/dot_general | solution.py:16
  246.0 0.1 bitcast_reduce_fusion
  246.1 0.2 maximum_dynamic-update-slice_fusion
  246.2 39.5 %all-reduce = f32[480]{0:T(512)S(1)} all-reduce(f32[480]{0:T(512)S(1)} %maximum_dynamic-update-slice_fusion), channel_id=2, replica_groups=mesh['dp'=4,'fsdp'=8] {'dp','fsdp'}, use_global_device_ids=true, to_apply=%add | all-reduce | flops 480 | bytes 3840
  285.7 0.1 reshape.19
  285.8 0.1 slice_reduce_fusion.1
  285.9 0.1 eq.15
  286.0 0.6 select_reduce_fusion
  286.7 0.1 dynamic-slice_bitcast_fusion
  286.7 0.7 copy.24
  287.4 6.3 %copy.22 = bf16[4,384,1280]{2,1,0:T(8,128)(2,1)} copy(bf16[4,384,1280]{1,2,0:T(8,128)(2,1)} %bitcast.1) | data formatting | bytes 7864320 | tf_op jit(solution)/shard_map/all_to_all | solution.py:46
  293.7 12.0 %convolution_convert_fusion = bf16[1792,1280]{1,0:T(8,128)(2,1)} fusion(bf16[1536,1792]{1,0:T(8,128)(2,1)} %all-gather.7.cloned.1.call-done, bf16[1536,1280]{1,0:T(8,128)(2,1)} %bitcast.16), kind=kOutput, calls=%fused_computation | convolution fusion | flops 7048724480 | bytes 14024704 | tf_op jit(solution)/shard_map/dot_general | solution.py:20
  (15 shorter events, 0.2 us)
Async XLA Ops:
  7.2 234.1 %copy-start = (bf16[256,1792]{1,0:T(8,128)(2,1)S(1)}, bf16[256,1792]{1,0:T(8,128)(2,1)}, u32[]{:S(2)}) copy-start(bf16[256,1792]{1,0:T(8,128)(2,1)} %param.11) | copy-start | bytes 2752516
  7.2 27.0 %all-gather.9.cloned.1.call-start = ((), (), s32[]{:S(2)}) async-start(), calls=%async_computation.3 | async-start | bytes 2457600 | tf_op jit(solution)/shard_map/all_gather | solution.py:40
  7.9 99.1 %all-gather.5.cloned.1.call-start = ((), (), s32[]{:S(2)}) async-start(), calls=%async_computation.1 | async-start | bytes 4423680 | tf_op jit(solution)/shard_map/all_gather | solution.py:41
  10.0 27.8 %copy-start.1 = (bf16[384,1792]{1,0:T(8,128)(2,1)S(1)}, bf16[384,1792]{1,0:T(8,128)(2,1)}, u32[]{:S(2)}) copy-start(bf16[384,1792]{1,0:T(8,128)(2,1)} %param.7) | copy-start | bytes 4128772
  10.0 188.5 %all-reduce.3.cloned.1.call-start = ((), (), s32[]{:S(2)}) async-start(), calls=%async_computation.4 | async-start | bytes 3145728 | tf_op jit(solution)/shard_map/psum | solution.py:44
  37.7 3.4 %copy-start.2 = (s32[3]{0:T(128)S(1)}, s32[3]{0:T(128)}, u32[]{:S(2)}) copy-start(s32[3]{0:T(128)} %param.13) | copy-start | bytes 40
  37.7 203.6 %all-gather.7.cloned.1.call-start = ((), (), s32[]{:S(2)}) async-start(), calls=%async_computation.2 | async-start | bytes 6881280 | tf_op jit(solution)/shard_map/all_gather | solution.py:42
  107.1 180.4 %all-to-all-start = ((bf16[384,4,1280]{0,2,1:T(8,128)(2,1)}), bf16[384,4,1280]{0,2,1:T(8,128)(2,1)}, u32[]{:S(2)}, u32[]{:S(2)}) async-start(bf16[384,4,1280]{0,2,1:T(8,128)(2,1)} %bitcast.15), calls=%async_computation | async-start | bytes 7864320 | tf_op jit(solution)/shard_map/all_to_all | solution.py:46
Sparse Core Ops, SparseCore 0:
  9.6 24.5 all-gather.8
  36.9 70.0 all-gather.4
  111.2 87.3 all-reduce.2
  199.9 41.2 all-gather.6

commit v2 on v1

v2 whole, which is shorter than its diff:
```python
import functools

import jax
import jax.numpy as jnp
from jax import lax
from jax.experimental import pallas as pl
from jax.experimental.pallas import tpu as pltpu
from jax.sharding import PartitionSpec as P

D = 5120
FFW = 14336
L = 128
VAL = 256

F32 = jnp.float32
BF16 = jnp.bfloat16
VMEM_LIMIT = 48 * 1024 * 1024


def dot_nt(a, b):
    return lax.dot_general(a, b, (((1,), (1,)), ((), ())), preferred_element_type=F32)


def dot_tn(a, b):
    return lax.dot_general(a, b, (((0,), (0,)), ((), ())), preferred_element_type=F32)


def swap(x, axis, k):
    n = lax.axis_size(axis)
    return lax.ppermute(x, axis, [(s, s ^ k) for s in range(n)])


def shift(x, axis, k):
    n = lax.axis_size(axis)
    return lax.ppermute(x, axis, [(s, (s + k) % n) for s in range(n)])


def whole(shape):
    return pl.BlockSpec(shape, lambda *_: (0,) * len(shape))


def grads_body(n, width, offs_ref, *refs):
    blocks, (w_ref, gate_ref, up_ref, gg_ref, gu_ref) = refs[:n], refs[n:]
    total = None
    for j in range(n):
        cols = pl.ds(pl.multiple_of(offs_ref[j], 128), width)
        term = dot_nt(blocks[j][...], w_ref[:, cols])
        total = term if total is None else total + term
    gate = gate_ref[...].astype(F32)
    up = up_ref[...].astype(F32)
    sig = jax.nn.sigmoid(gate)
    gg_ref[...] = (total * up * sig * (1.0 + gate * (1.0 - sig))).astype(BF16)
    gu_ref[...] = (total * (gate * sig)).astype(BF16)


def grads(offs, blocks, weight, gate, up):
    n = len(blocks)
    toks, width = blocks[0].shape
    units, feats = weight.shape
    tile = 256
    cols = pl.BlockSpec((toks, tile), lambda i, _: (0, i))
    out = jax.ShapeDtypeStruct((toks, units), BF16)
    return pl.pallas_call(
        functools.partial(grads_body, n, width),
        grid_spec=pltpu.PrefetchScalarGridSpec(
            num_scalar_prefetch=1,
            grid=(units // tile,),
            in_specs=[whole((toks, width))] * n
            + [pl.BlockSpec((tile, feats), lambda i, _: (i, 0)), cols, cols],
            out_specs=[cols, cols],
        ),
        out_shape=(out, out),
        compiler_params=pltpu.CompilerParams(vmem_limit_bytes=VMEM_LIMIT),
        cost_estimate=pl.CostEstimate(
            flops=2 * toks * units * feats,
            bytes_accessed=2 * (units * feats + toks * feats + 4 * toks * units),
            transcendentals=toks * units,
        ),
        name="grads",
    )(offs, *blocks, weight, gate, up)


def wgrad_body(n, width, offs_ref, *refs):
    hid, cols, out_ref = refs[:n], refs[n : 2 * n], refs[2 * n]
    for half in range(2):
        total = None
        for k in range(n):
            term = dot_tn(hid[k][...], cols[k][half])
            total = term if total is None else total + term
        place = pl.ds(pl.multiple_of(offs_ref[half], 128), width)
        out_ref[:, place] = total.astype(BF16)


def wgrad(offs, hid, cols):
    n = len(hid)
    toks, units = hid[0].shape
    width = cols[0].shape[2]
    tile = 256
    return pl.pallas_call(
        functools.partial(wgrad_body, n, width),
        grid_spec=pltpu.PrefetchScalarGridSpec(
            num_scalar_prefetch=1,
            grid=(units // tile,),
            in_specs=[pl.BlockSpec((toks, tile), lambda i, _: (0, i))] * n
            + [whole((2, toks, width))] * n,
            out_specs=pl.BlockSpec((tile, 2 * width), lambda i, _: (i, 0)),
        ),
        out_shape=jax.ShapeDtypeStruct((units, 2 * width), BF16),
        compiler_params=pltpu.CompilerParams(vmem_limit_bytes=VMEM_LIMIT),
        cost_estimate=pl.CostEstimate(
            flops=4 * n * toks * units * width,
            bytes_accessed=2 * (n * toks * (units + 2 * width) + 2 * units * width),
            transcendentals=0,
        ),
        name="wgrad",
    )(offs, *hid, *cols)


def gram_body(n, parts, *refs):
    toks_refs, (val_ref, out_ref) = refs[:n], refs[n:]
    for k in range(n):
        toks = toks_refs[k].shape[0]
        size = toks // parts
        part = dot_nt(toks_refs[k][...], val_ref[...])
        for p in range(parts):
            out_ref[p % 2, p // 2, k * size : (k + 1) * size] = part[p * size : (p + 1) * size]


def gram(toks_dp, vals, parts, name):
    n = len(toks_dp)
    toks, feats = toks_dp[0].shape
    count = vals.shape[0]
    return pl.pallas_call(
        functools.partial(gram_body, n, parts),
        out_shape=jax.ShapeDtypeStruct((2, parts // 2, n * toks // parts, count), F32),
        compiler_params=pltpu.CompilerParams(vmem_limit_bytes=VMEM_LIMIT),
        cost_estimate=pl.CostEstimate(
            flops=2 * n * toks * count * feats,
            bytes_accessed=2 * (n * toks + count) * feats + 4 * n * toks * count,
            transcendentals=0,
        ),
        name=name,
    )(*toks_dp, vals)


def gram_sum(part):
    n_fs = lax.axis_size("fsdp")
    inner = lax.axis_index("fsdp") % 2
    away = lax.dynamic_index_in_dim(part, 1 - inner, axis=0, keepdims=False)
    kept = lax.dynamic_index_in_dim(part, inner, axis=0, keepdims=False)
    pair = kept + swap(away, "fsdp", 1)
    groups = [list(range(x, n_fs, 2)) for x in range(2)]
    pair = lax.all_to_all(
        pair, "fsdp", split_axis=0, concat_axis=0, axis_index_groups=groups, tiled=True
    )
    return jnp.sum(pair, axis=0)


def per_device(gate_act, up_act, out_grad, down_weight, val_hidden, val_grad, assign):
    n_dp = lax.axis_size("dp")
    n_fs = lax.axis_size("fsdp")
    d = lax.axis_index("dp")
    f = lax.axis_index("fsdp")
    rows_here = assign.shape[0]
    toks, width = out_grad.shape
    n_out = n_fs // 2
    outer, inner = f // 2, f % 2

    gate = gate_act.astype(F32)
    up = up_act.astype(F32)
    hidden = (gate * jax.nn.sigmoid(gate) * up).astype(BF16)

    ring = [out_grad]
    for _ in range(n_out - 1):
        ring.append(shift(ring[-1], "fsdp", 2))
    pairs = [(own, swap(own, "fsdp", 1)) for own in ring]

    def over_dp(x):
        far = swap(x, "dp", 2)
        return [x, swap(x, "dp", 1), far, swap(far, "dp", 1)]

    grad_dp = over_dp(out_grad)
    hid_dp = over_dp(hidden)

    def columns_of(q):
        at = (outer - q) % n_out
        return jnp.stack([lax.select_n(at, *[p[i] for p in pairs]) for i in range(2)])

    cols_dp = [columns_of(d)] + [swap(columns_of(d ^ k), "dp", k) for k in range(1, n_dp)]

    grad_gram = gram_sum(gram(grad_dp, val_grad, n_fs, "grad_gram"))
    hidden_gram = gram_sum(gram(hid_dp, val_hidden, n_fs, "hidden_gram"))
    by_tok = jnp.sum(hidden_gram * grad_gram, axis=1).reshape(n_dp, toks // n_fs)

    place = jnp.arange(n_out, dtype=jnp.int32)
    place = ((outer - place) % n_out)[:, None] * 2 + jnp.stack([inner, 1 - inner])[None, :]
    offs = (place * width).reshape(-1).astype(jnp.int32)
    blocks = [b for p in pairs for b in p]
    grad_gate, grad_up = grads(offs, blocks, down_weight, gate_act, up_act)

    half_offs = (jnp.stack([inner, 1 - inner]) * width).astype(jnp.int32)
    weight_grad = wgrad(half_offs, hid_dp, cols_dp)

    row_of = (f * (toks // n_fs) + jnp.arange(toks // n_fs)) // (toks // rows_here)
    in_row = (row_of[:, None] == jnp.arange(rows_here)[None, :]).astype(F32)
    by_row = jnp.sum(by_tok[:, :, None] * in_row[None], axis=1)
    mine = jnp.concatenate([by_row.reshape(-1), assign.astype(F32)])
    mine = jnp.pad(mine, (0, 128 - mine.shape[0]))
    every = lax.all_to_all(
        jnp.broadcast_to(mine[None], (n_dp * n_fs, 128)),
        ("dp", "fsdp"), split_axis=0, concat_axis=0, tiled=True,
    ).reshape(n_dp, n_fs, 128)
    rows = n_dp * rows_here
    scale = 1.0 / jnp.sqrt(F32(L) * VAL * FFW * D)
    sums = jnp.sum(every[:, :, :rows], axis=1).reshape(n_dp, n_dp, rows_here)
    groups = every[:, 0, rows : rows + rows_here]
    scores = jnp.stack(
        [jnp.stack([sums[g, t ^ g] for g in range(n_dp)], axis=-1) for t in range(n_dp)]
    ) * scale
    onehot = (groups[:, :, None] == jnp.arange(n_dp, dtype=F32)).astype(F32)
    group_values = jnp.sum(onehot * scores, axis=(0, 1))
    row_scores = lax.dynamic_index_in_dim(scores, d, axis=0, keepdims=False)
    return (grad_gate, grad_up, weight_grad, row_scores, group_values)


def per_device_any(gate_act, up_act, out_grad, down_weight, val_hidden, val_grad, assign):
    n_dp = lax.axis_size("dp")
    me = lax.axis_index("dp")
    rows_here = assign.shape[0]
    toks = gate_act.shape[0]
    gate = gate_act.astype(F32)
    up = up_act.astype(F32)
    sig = jax.nn.sigmoid(gate)
    act = gate * sig
    hidden = (act * up).astype(BF16)
    grad_feat = lax.all_gather(out_grad, "dp", axis=0, tiled=True)
    piece = lax.all_gather(out_grad, "fsdp", axis=1, tiled=True)
    hidden_all = lax.all_gather(hidden, "dp", axis=0, tiled=True)
    grad_gram = lax.psum(dot_nt(grad_feat, val_grad), "fsdp")
    grad_cols = lax.all_to_all(piece, "dp", split_axis=1, concat_axis=0, tiled=True)
    grad_hidden = dot_nt(piece, down_weight)
    grad_gate = (grad_hidden * up * sig * (1.0 + gate * (1.0 - sig))).astype(BF16)
    grad_up = (grad_hidden * act).astype(BF16)
    product = dot_nt(hidden_all, val_hidden) * grad_gram
    part = jnp.sum(product.reshape(n_dp * rows_here, toks // rows_here * VAL), axis=1)
    weight_grad = dot_tn(hidden_all, grad_cols).astype(BF16)
    scale = 1.0 / jnp.sqrt(F32(L) * VAL * FFW * D)
    scores = lax.all_gather(lax.psum(part, "fsdp"), "dp") * scale
    groups = lax.all_gather(assign, "dp", tiled=True)
    onehot = (groups[None, :] == jnp.arange(n_dp, dtype=jnp.int32)[:, None]).astype(F32)
    group_values = jnp.sum(onehot * scores, axis=1)
    row_scores = lax.dynamic_slice_in_dim(scores, me * rows_here, rows_here, axis=1).T
    return (grad_gate, grad_up, weight_grad, row_scores, group_values)


def solution(mesh):
    in_specs = (
        P("dp", "fsdp"),
        P("dp", "fsdp"),
        P("dp", "fsdp"),
        P("fsdp", None),
        P("dp", "fsdp"),
        P("dp", "fsdp"),
        P("dp"),
    )
    out_specs = (P("dp", "fsdp"), P("dp", "fsdp"), P("fsdp", "dp"), P("dp", None), P())
    n_dp, n_fs = mesh.shape["dp"], mesh.shape["fsdp"]
    fits = n_dp == 4 and n_fs == 2 * n_dp
    return jax.shard_map(
        per_device if fits else per_device_any,
        mesh=mesh, in_specs=in_specs, out_specs=out_specs, check_vma=False,
    )
```

time: 313 us -> 210 us (0.67)
  waiting for transfers between devices: 205 us -> 108 us
  blocking collectives: 39.5 us -> 0 us
  Pallas kernels: 0 us -> 36.8 us
  matrix products: 35.8 us -> 0 us
  starting transfers between devices: 4.95 us -> 29.8 us
  other arithmetic: 4.22 us -> 20.4 us
  between operations: 13.9 us -> 0.83 us
  local copies, waits for them, and re-layouts: 9.37 us -> 12.9 us
    all_gather x3 -> x0, waiting for transfers between devices: 133 us -> none  [the longest x1 65.9 us: per_device(): piece = lax.all_gather(out_grad, 'fsdp', axis=1, tiled=True)]
    ppermute x0 -> x18, waiting for transfers between devices: none -> 108 us  [the longest x15 104 us: swap(): return lax.ppermute(x, axis, [(s, s ^ k) for s in range(n)])]
    psum x1 -> x0, waiting for transfers between devices: 71 us -> none  [per_device(): grad_gram = lax.psum(dot_nt(grad_feat, val_grad), 'fsdp')]
    unnamed x1 -> x0, blocking collectives: 39.5 us -> none
    pallas_call x0 -> x4, Pallas kernels: none -> 36.8 us  [the longest x1 15.6 us: wgrad(): pl.pallas_call(functools.partial(wgrad_body, n, width), grid_spec=pltpu.P...]
    dot_general x4 -> x0, matrix products: 35.8 us -> none  [the longest x3 23.8 us: dot_nt(): lax.dot_general(a, b, (((1,), (1,)), ((), ())), preferred_element_type=F32)]
    ppermute x0 -> x18, starting transfers between devices: none -> 15.5 us  [the longest x15 11.6 us: swap(): return lax.ppermute(x, axis, [(s, s ^ k) for s in range(n)])]
    another operation x0 -> x8, other arithmetic: none -> 10 us  [the longest x6 10 us: columns_of(): jnp.stack([lax.select_n(at, *[p[i] for p in pairs]) for i in range(2)])]
  transfers between devices with their start and end apart: 5 -> 21, of which waited for: 4 -> 7; matrix products, arithmetic and copies ran while one was open for 10% -> 10% of each run, Pallas kernels for 0% -> 18%
where the time goes in v2:
time: 210 us; the launch traced here: 209 us
  waiting for transfers between devices  108 us (51%)
  Pallas kernels  36.8 us (18%)
  starting transfers between devices  29.8 us (14%)
  other arithmetic  20.4 us (10%)
  local copies, waits for them, and re-layouts  12.9 us (6%)
    ppermute x15, waiting for transfers between devices, swap(): return lax.ppermute(x, axis, [(s, s ^ k) for s in range(n)])  104 us
    pallas_call x1, Pallas kernels, wgrad(): pl.pallas_call(functools.partial(wgrad_body, n, width), grid_spec=pltpu.P...  15.6 us
    pallas_call x1, Pallas kernels, grads(): pl.pallas_call(functools.partial(grads_body, n, width), grid_spec=pltpu.P...  15.5 us
    ppermute x15, starting transfers between devices, swap(): return lax.ppermute(x, axis, [(s, s ^ k) for s in range(n)])  11.6 us
    another operation x6, other arithmetic, columns_of(): jnp.stack([lax.select_n(at, *[p[i] for p in pairs]) for i in range(2)])  10 us
    all_to_all x2, starting transfers between devices, gram_sum(): lax.all_to_all(pair, 'fsdp', split_axis=0, concat_axis=0, axis_index_grou...  8.51 us
    unnamed x38, local copies, waits for them, and re-layouts  7.83 us
    all_to_all x1, starting transfers between devices, per_device(): lax.all_to_all(jnp.broadcast_to(mine[None], (n_dp * n_fs, 128)), ('dp', '...  5.84 us
  transfers between devices with their start and end apart: 21, of which 7 were waited for; matrix products, arithmetic and copies ran while one was open for 10% of the time, Pallas kernels for 18%

profile of v2, /device:TPU:0, one launch (start us, length us, event | category | flops | bytes accessed | tf_op | source)
XLA Modules:
  0.0 209.1 jit_solution(16417486690466798463)
XLA Ops:
  0.6 2.6 %fusion.4.refs_0_ = bf16[384,1792]{1,0:T(8,128)(2,1)S(1)} fusion(bf16[384,1792]{1,0:T(8,128)(2,1)} %refs_10_.1, bf16[384,1792]{1,0:T(8,128)(2,1)} %refs_9_.1), kind=kLoop, calls=%fused_computation.6 | loop fusion | flops 5505024 | bytes 4128768 | tf_op jit(solution)/shard_map/convert_element_type | solution.py:171
  3.3 3.0 %collective-permute-start.8 = (bf16[384,1792]{1,0:T(8,128)(2,1)S(1)}, bf16[384,1792]{1,0:T(8,128)(2,1)}, u32[]{:S(2)}, u32[]{:S(2)}) collective-permute-start(bf16[384,1792]{1,0:T(8,128)(2,1)S(1)} %fusion.4.refs_0_), channel_id=1, source_target_pairs={{0,16},{8,24},{16,0},{24,8},{1,17},{9,25},{17,1},{25,9},{2,18},{10... | collective-permute-start | bytes 4128776 | tf_op jit(solution)/shard_map/ppermute | solution.py:30
  6.4 2.0 collective-permute-start.1
  8.4 38.6 %collective-permute-done.15.refs_2_ = bf16[384,640]{1,0:T(8,128)(2,1)S(1)} collective-permute-done((bf16[384,640]{1,0:T(8,128)(2,1)S(1)}, bf16[384,640]{1,0:T(8,128)(2,1)S(1)}, u32[]{:S(2)}, u32[]{:S(2)}) %collective-permute-start.15) | collective-permute-done | bytes 491552 | tf_op jit(solution)/shard_map/ppermute | solution.py:30
  48.3 1.8 collective-permute-start.3
  59.7 4.7 %collective-permute-done.3.refs_4_ = bf16[384,640]{1,0:T(8,128)(2,1)} collective-permute-done((bf16[384,640]{1,0:T(8,128)(2,1)}, bf16[384,640]{1,0:T(8,128)(2,1)}, u32[]{:S(2)}, u32[]{:S(2)}) %collective-permute-start.3) | collective-permute-done | bytes 491552 | tf_op jit(solution)/shard_map/ppermute | solution.py:35
  64.5 13.8 %collective-permute-done.17 = f32[4,192,256]{2,1,0:T(8,128)} collective-permute-done((f32[4,192,256]{2,1,0:T(8,128)}, f32[4,192,256]{2,1,0:T(8,128)}, u32[]{:S(2)}, u32[]{:S(2)}) %collective-permute-start.17) | collective-permute-done | bytes 786464 | tf_op jit(solution)/shard_map/ppermute | solution.py:30
  79.8 2.1 %bitcast_add_fusion = f32[4,192,256]{2,1,0:T(8,128)} fusion(f32[4,192,256]{2,1,0:T(8,128)} %collective-permute-done.17, f32[2,4,192,256]{3,2,1,0:T(8,128)S(1)} %grad_gram.1, s32[]{:T(128)S(6)} %select_n.286), kind=kLoop, calls=%fused_computation.11 | loop fusion | flops 196608 | bytes 2359300 | tf_op jit(solution)/shard_map/add | solution.py:151
  81.9 4.2 %all-to-all-start.1 = ((f32[4,192,256]{2,1,0:T(8,128)}), f32[4,192,256]{2,1,0:T(8,128)}, u32[]{:S(2)}, u32[]{:S(2)}) async-start(f32[4,192,256]{2,1,0:T(8,128)} %bitcast_add_fusion), calls=%async_computation.1 | async-start | bytes 1572864 | tf_op jit(solution)/shard_map/all_to_all | solution.py:153
  89.4 4.9 %hidden_gram.1 = f32[2,4,192,256]{3,2,1,0:T(8,128)} custom-call(bf16[384,1792]{1,0:T(8,128)(2,1)S(1)} %fusion.4.refs_0_, bf16[384,1792]{1,0:T(8,128)(2,1)} %collective-permute-done.7.refs_1_, bf16[384,1792]{1,0:T(8,128)(2,1)} %collective-permute-done.8.refs_2_, bf16[384,1792]{1,0:T(8,128)(2,1)} %collective-permute-done.9.refs_3_, bf16[256,1792]{1,0:T(8,128)(2,1)S(1)} %copy-done.2), custom_call_target="tpu_custom_call" | custom-call | flops 1409286144 | bytes 7995392 | tf_op jit(solution)/shard_map/hidden_gram/pallas_call | solution.py:133
  94.3 2.1 dynamic-slice_bitcast_fusion.1
  97.0 2.6 %select_bitcast_fusion.1 = (bf16[1,384,640]{2,1,0:T(8,128)(2,1)S(1)}, bf16[1,384,640]{2,1,0:T(8,128)(2,1)}, bf16[1,384,640]{2,1,0:T(8,128)(2,1)}, bf16[1,384,640]{2,1,0:T(8,128)(2,1)}) fusion(bf16[384,640]{1,0:T(8,128)(2,1)} %collective-permute-done.3.refs_4_, bf16[384,640]{1,0:T(8,128)(2,1)} %collective-permute-done.5.refs_6_, ...), kind=kLoop, calls=%fused_computation.16 | loop fusion | flops 2949120 | bytes 3932172 | tf_op jit(solution)/shard_map/stack | solution.py:187
  99.6 10.2 %collective-permute-done.4.refs_5_ = bf16[384,640]{1,0:T(8,128)(2,1)S(1)} collective-permute-done((bf16[384,640]{1,0:T(8,128)(2,1)}, bf16[384,640]{1,0:T(8,128)(2,1)S(1)}, u32[]{:S(2)}, u32[]{:S(2)}) %collective-permute-start.4) | collective-permute-done | bytes 491552 | tf_op jit(solution)/shard_map/ppermute | solution.py:30
  109.8 10.5 %collective-permute-done.6.refs_7_ = bf16[384,640]{1,0:T(8,128)(2,1)S(1)} collective-permute-done((bf16[384,640]{1,0:T(8,128)(2,1)}, bf16[384,640]{1,0:T(8,128)(2,1)S(1)}, u32[]{:S(2)}, u32[]{:S(2)}) %collective-permute-start.6) | collective-permute-done | bytes 491552 | tf_op jit(solution)/shard_map/ppermute | solution.py:30
  120.3 2.8 %select_bitcast_fusion = (bf16[1,384,640]{2,1,0:T(8,128)(2,1)}, bf16[1,384,640]{2,1,0:T(8,128)(2,1)}, bf16[1,384,640]{2,1,0:T(8,128)(2,1)}, bf16[1,384,640]{2,1,0:T(8,128)(2,1)}) fusion(bf16[384,640]{1,0:T(8,128)(2,1)S(1)} %collective-permute-done.4.refs_5_, bf16[384,640]{1,0:T(8,128)(2,1)S(1)} %collective-permute-done.6.refs_7_, ...), kind=kLoop, calls=%fused_computation.15 | loop fusion | flops 2949120 | bytes 3932172 | tf_op jit(solution)/shard_map/stack | solution.py:187
  123.1 13.4 %collective-permute-done.13 = f32[4,192,256]{2,1,0:T(8,128)} collective-permute-done((f32[4,192,256]{2,1,0:T(8,128)}, f32[4,192,256]{2,1,0:T(8,128)}, u32[]{:S(2)}, u32[]{:S(2)}) %collective-permute-start.13) | collective-permute-done | bytes 786464 | tf_op jit(solution)/shard_map/ppermute | solution.py:30
  136.5 2.1 %bitcast_add_fusion.1 = f32[4,192,256]{2,1,0:T(8,128)} fusion(f32[4,192,256]{2,1,0:T(8,128)} %collective-permute-done.13, f32[2,4,192,256]{3,2,1,0:T(8,128)S(1)} %copy-done.12, s32[]{:T(128)S(6)} %select_n.286), kind=kLoop, calls=%fused_computation.12 | loop fusion | flops 196608 | bytes 2359300 | tf_op jit(solution)/shard_map/add | solution.py:151
  138.6 4.3 %all-to-all-start = ((f32[4,192,256]{2,1,0:T(8,128)}), f32[4,192,256]{2,1,0:T(8,128)}, u32[]{:S(2)}, u32[]{:S(2)}) async-start(f32[4,192,256]{2,1,0:T(8,128)} %bitcast_add_fusion.1), calls=%async_computation | async-start | bytes 1572864 | tf_op jit(solution)/shard_map/all_to_all | solution.py:153
  143.0 2.3 %pad_maximum_fusion.1 = bf16[2,384,640]{2,1,0:T(8,128)(2,1)} fusion(bf16[1,384,640]{2,1,0:T(8,128)(2,1)} %get-tuple-element.19, bf16[1,384,640]{2,1,0:T(8,128)(2,1)} %get-tuple-element.15), kind=kLoop, calls=%fused_computation.8 | loop fusion | flops 491520 | bytes 1966080 | tf_op jit(solution)/shard_map/stack | solution.py:187
  146.4 1.5 collective-permute-start.11
  149.7 15.5 %grads.1 = (bf16[384,1792]{1,0:T(8,128)(2,1)}, bf16[384,1792]{1,0:T(8,128)(2,1)}) custom-call(s32[8]{0:T(128)S(1)} %mul.56.offs_ref, bf16[384,640]{1,0:T(8,128)(2,1)S(1)} %copy-done, bf16[384,640]{1,0:T(8,128)(2,1)} %collective-permute-done.refs_1_, bf16[384,640]{1,0:T(8,128)(2,1)} %collective-permute-done.1.refs_2_, ...), custom_call_target="tpu_custom_call" | custom-call | flops 7046430720 | bytes 27787264 | tf_op jit(solution)/shard_map/grads/pallas_call | solution.py:63
  168.8 5.8 %all-to-all-start.2 = ((f32[32,1,128]{2,1,0:T(1,128)}), f32[32,1,128]{2,1,0:T(1,128)S(1)}, u32[]{:S(2)}, u32[]{:S(2)}) async-start(f32[32,1,128]{2,1,0:T(1,128)} %broadcast_in_dim.2), calls=%async_computation.2 | async-start | bytes 32768 | tf_op jit(solution)/shard_map/all_to_all | solution.py:209
  174.7 17.0 %collective-permute-done.12.refs_7_ = bf16[2,384,640]{2,1,0:T(8,128)(2,1)} collective-permute-done((bf16[2,384,640]{2,1,0:T(8,128)(2,1)}, bf16[2,384,640]{2,1,0:T(8,128)(2,1)}, u32[]{:S(2)}, u32[]{:S(2)}) %collective-permute-start.12) | collective-permute-done | bytes 983072 | tf_op jit(solution)/shard_map/ppermute | solution.py:30
  191.7 15.6 %wgrad.1 = bf16[1792,1280]{1,0:T(8,128)(2,1)} custom-call(s32[2]{0:T(128)S(1)} %get-tuple-element.11.offs_ref, bf16[384,1792]{1,0:T(8,128)(2,1)S(1)} %fusion.4.refs_0_, bf16[384,1792]{1,0:T(8,128)(2,1)} %collective-permute-done.7.refs_1_, bf16[384,1792]{1,0:T(8,128)(2,1)} %collective-permute-done.8.refs_2_, ...), custom_call_target="tpu_custom_call" | custom-call | flops 7046430720 | bytes 14024704 | tf_op jit(solution)/shard_map/wgrad/pallas_call | solution.py:99
  (99 shorter events, 24.6 us)
Async XLA Ops:
  0.6 5.7 %copy-start = (bf16[384,640]{1,0:T(8,128)(2,1)S(1)}, bf16[384,640]{1,0:T(8,128)(2,1)}, u32[]{:S(2)}) copy-start(bf16[384,640]{1,0:T(8,128)(2,1)} %refs_0_.3) | copy-start | bytes 1474564
  3.3 45.0 %collective-permute-start.8 = (bf16[384,1792]{1,0:T(8,128)(2,1)S(1)}, bf16[384,1792]{1,0:T(8,128)(2,1)}, u32[]{:S(2)}, u32[]{:S(2)}) collective-permute-start(bf16[384,1792]{1,0:T(8,128)(2,1)S(1)} %fusion.4.refs_0_), channel_id=1, source_target_pairs={{0,16},{8,24},{16,0},{24,8},{1,17},{9,25},{17,1},{25,9},{2,18},{10... | collective-permute-start | bytes 4128776 | tf_op jit(solution)/shard_map/ppermute | solution.py:30
  6.3 40.7 %collective-permute-start.15 = (bf16[384,640]{1,0:T(8,128)(2,1)S(1)}, bf16[384,640]{1,0:T(8,128)(2,1)S(1)}, u32[]{:S(2)}, u32[]{:S(2)}) collective-permute-start(bf16[384,640]{1,0:T(8,128)(2,1)S(1)} %copy-done), channel_id=1, source_target_pairs={{0,16},{8,24},{16,0},{24,8},{1,17},{9,25},{17,1},{25,9},{2,18},{10... | collective-permute-start | bytes 1474568 | tf_op jit(solution)/shard_map/ppermute | solution.py:30
  6.4 41.9 %collective-permute-start.1 = (bf16[384,640]{1,0:T(8,128)(2,1)S(1)}, bf16[384,640]{1,0:T(8,128)(2,1)}, u32[]{:S(2)}, u32[]{:S(2)}) collective-permute-start(bf16[384,640]{1,0:T(8,128)(2,1)S(1)} %copy-done), channel_id=1, source_target_pairs={{0,2},{1,3},{2,4},{3,5},{4,6},{5,7},{6,0},{7,1},{8,10},{9,11},{10,... | collective-permute-start | bytes 1474568 | tf_op jit(solution)/shard_map/ppermute | solution.py:35
  8.4 41.8 %collective-permute-start.14 = (bf16[384,640]{1,0:T(8,128)(2,1)S(1)}, bf16[384,640]{1,0:T(8,128)(2,1)S(1)}, u32[]{:S(2)}, u32[]{:S(2)}) collective-permute-start(bf16[384,640]{1,0:T(8,128)(2,1)S(1)} %copy-done), channel_id=1, source_target_pairs={{0,8},{8,0},{16,24},{24,16},{1,9},{9,1},{17,25},{25,17},{2,10},{10... | collective-permute-start | bytes 1474568 | tf_op jit(solution)/shard_map/ppermute | solution.py:30
  47.0 3.9 %collective-permute-start.16 = (bf16[384,640]{1,0:T(8,128)(2,1)S(1)}, bf16[384,640]{1,0:T(8,128)(2,1)S(1)}, u32[]{:S(2)}, u32[]{:S(2)}) collective-permute-start(bf16[384,640]{1,0:T(8,128)(2,1)S(1)} %collective-permute-done.15.refs_2_), channel_id=1, source_target_pairs={{0,8},{8,0},{16,24},{24,16},{1,9},{9,1},{17,25},{25,17},{2,10},{10... | collective-permute-start | bytes 1474568 | tf_op jit(solution)/shard_map/ppermute | solution.py:30
  47.8 38.2 %collective-permute-start.7 = (bf16[384,1792]{1,0:T(8,128)(2,1)S(1)}, bf16[384,1792]{1,0:T(8,128)(2,1)}, u32[]{:S(2)}, u32[]{:S(2)}) collective-permute-start(bf16[384,1792]{1,0:T(8,128)(2,1)S(1)} %fusion.4.refs_0_), channel_id=1, source_target_pairs={{0,8},{8,0},{16,24},{24,16},{1,9},{9,1},{17,25},{25,17},{2,10},{10... | collective-permute-start | bytes 4128776 | tf_op jit(solution)/shard_map/ppermute | solution.py:30
  48.3 39.8 %collective-permute-start.9 = (bf16[384,1792]{1,0:T(8,128)(2,1)}, bf16[384,1792]{1,0:T(8,128)(2,1)}, u32[]{:S(2)}, u32[]{:S(2)}) collective-permute-start(bf16[384,1792]{1,0:T(8,128)(2,1)} %collective-permute-done.8.refs_2_), channel_id=1, source_target_pairs={{0,8},{8,0},{16,24},{24,16},{1,9},{9,1},{17,25},{25,17},{2,10},{10... | collective-permute-start | bytes 4128776 | tf_op jit(solution)/shard_map/ppermute | solution.py:30
  48.3 16.0 %collective-permute-start.3 = (bf16[384,640]{1,0:T(8,128)(2,1)}, bf16[384,640]{1,0:T(8,128)(2,1)}, u32[]{:S(2)}, u32[]{:S(2)}) collective-permute-start(bf16[384,640]{1,0:T(8,128)(2,1)} %collective-permute-done.1.refs_2_), channel_id=1, source_target_pairs={{0,2},{1,3},{2,4},{3,5},{4,6},{5,7},{6,0},{7,1},{8,10},{9,11},{10,... | collective-permute-start | bytes 1474568 | tf_op jit(solution)/shard_map/ppermute | solution.py:35
  57.6 20.7 %collective-permute-start.17 = (f32[4,192,256]{2,1,0:T(8,128)}, f32[4,192,256]{2,1,0:T(8,128)}, u32[]{:S(2)}, u32[]{:S(2)}) collective-permute-start(f32[4,192,256]{2,1,0:T(8,128)} %dynamic-slice_bitcast_fusion), channel_id=1, source_target_pairs={{0,1},{1,0},{2,3},{3,2},{4,5},{5,4},{6,7},{7,6},{8,9},{9,8},{10,11... | collective-permute-start | bytes 2359304 | tf_op jit(solution)/shard_map/ppermute | solution.py:30
  59.1 40.5 %collective-permute-start = (bf16[384,640]{1,0:T(8,128)(2,1)S(1)}, bf16[384,640]{1,0:T(8,128)(2,1)}, u32[]{:S(2)}, u32[]{:S(2)}) collective-permute-start(bf16[384,640]{1,0:T(8,128)(2,1)S(1)} %copy-done), channel_id=1, source_target_pairs={{0,1},{1,0},{2,3},{3,2},{4,5},{5,4},{6,7},{7,6},{8,9},{9,8},{10,11... | collective-permute-start | bytes 1474568 | tf_op jit(solution)/shard_map/ppermute | solution.py:30
  64.4 22.3 %collective-permute-start.5 = (bf16[384,640]{1,0:T(8,128)(2,1)}, bf16[384,640]{1,0:T(8,128)(2,1)}, u32[]{:S(2)}, u32[]{:S(2)}) collective-permute-start(bf16[384,640]{1,0:T(8,128)(2,1)} %collective-permute-done.3.refs_4_), channel_id=1, source_target_pairs={{0,2},{1,3},{2,4},{3,5},{4,6},{5,7},{6,0},{7,1},{8,10},{9,11},{10,... | collective-permute-start | bytes 1474568 | tf_op jit(solution)/shard_map/ppermute | solution.py:35
  78.3 21.3 %collective-permute-start.2 = (bf16[384,640]{1,0:T(8,128)(2,1)}, bf16[384,640]{1,0:T(8,128)(2,1)}, u32[]{:S(2)}, u32[]{:S(2)}) collective-permute-start(bf16[384,640]{1,0:T(8,128)(2,1)} %collective-permute-done.1.refs_2_), channel_id=1, source_target_pairs={{0,1},{1,0},{2,3},{3,2},{4,5},{5,4},{6,7},{7,6},{8,9},{9,8},{10,11... | collective-permute-start | bytes 1474568 | tf_op jit(solution)/shard_map/ppermute | solution.py:30
  81.9 56.8 %all-to-all-start.1 = ((f32[4,192,256]{2,1,0:T(8,128)}), f32[4,192,256]{2,1,0:T(8,128)}, u32[]{:S(2)}, u32[]{:S(2)}) async-start(f32[4,192,256]{2,1,0:T(8,128)} %bitcast_add_fusion), calls=%async_computation.1 | async-start | bytes 1572864 | tf_op jit(solution)/shard_map/all_to_all | solution.py:153
  86.1 23.7 %collective-permute-start.4 = (bf16[384,640]{1,0:T(8,128)(2,1)}, bf16[384,640]{1,0:T(8,128)(2,1)S(1)}, u32[]{:S(2)}, u32[]{:S(2)}) collective-permute-start(bf16[384,640]{1,0:T(8,128)(2,1)} %collective-permute-done.3.refs_4_), channel_id=1, source_target_pairs={{0,1},{1,0},{2,3},{3,2},{4,5},{5,4},{6,7},{7,6},{8,9},{9,8},{10,11... | collective-permute-start | bytes 1474568 | tf_op jit(solution)/shard_map/ppermute | solution.py:30
  86.7 33.6 %collective-permute-start.6 = (bf16[384,640]{1,0:T(8,128)(2,1)}, bf16[384,640]{1,0:T(8,128)(2,1)S(1)}, u32[]{:S(2)}, u32[]{:S(2)}) collective-permute-start(bf16[384,640]{1,0:T(8,128)(2,1)} %collective-permute-done.5.refs_6_), channel_id=1, source_target_pairs={{0,1},{1,0},{2,3},{3,2},{4,5},{5,4},{6,7},{7,6},{8,9},{9,8},{10,11... | collective-permute-start | bytes 1474568 | tf_op jit(solution)/shard_map/ppermute | solution.py:30
  96.4 40.1 %collective-permute-start.13 = (f32[4,192,256]{2,1,0:T(8,128)}, f32[4,192,256]{2,1,0:T(8,128)}, u32[]{:S(2)}, u32[]{:S(2)}) collective-permute-start(f32[4,192,256]{2,1,0:T(8,128)} %dynamic-slice_bitcast_fusion.1), channel_id=1, source_target_pairs={{0,1},{1,0},{2,3},{3,2},{4,5},{5,4},{6,7},{7,6},{8,9},{9,8},{10,11... | collective-permute-start | bytes 2359304 | tf_op jit(solution)/shard_map/ppermute | solution.py:30
  99.6 36.9 %copy-start.12 = (f32[2,4,192,256]{3,2,1,0:T(8,128)S(1)}, f32[2,4,192,256]{3,2,1,0:T(8,128)}, u32[]{:S(2)}) copy-start(f32[2,4,192,256]{3,2,1,0:T(8,128)} %hidden_gram.1) | copy-start | bytes 4718596
  138.6 6.7 %copy-start.14 = (bf16[1,384,640]{2,1,0:T(8,128)(2,1)S(1)}, bf16[1,384,640]{2,1,0:T(8,128)(2,1)}, u32[]{:S(2)}) copy-start(bf16[1,384,640]{2,1,0:T(8,128)(2,1)} %get-tuple-element.14) | copy-start | bytes 1474564
  138.6 27.8 %all-to-all-start = ((f32[4,192,256]{2,1,0:T(8,128)}), f32[4,192,256]{2,1,0:T(8,128)}, u32[]{:S(2)}, u32[]{:S(2)}) async-start(f32[4,192,256]{2,1,0:T(8,128)} %bitcast_add_fusion.1), calls=%async_computation | async-start | bytes 1572864 | tf_op jit(solution)/shard_map/all_to_all | solution.py:153
  145.3 29.4 %collective-permute-start.10 = (bf16[2,384,640]{2,1,0:T(8,128)(2,1)}, bf16[2,384,640]{2,1,0:T(8,128)(2,1)}, u32[]{:S(2)}, u32[]{:S(2)}) collective-permute-start(bf16[2,384,640]{2,1,0:T(8,128)(2,1)} %pad_maximum_fusion.1), channel_id=1, source_target_pairs={{0,8},{8,0},{16,24},{24,16},{1,9},{9,1},{17,25},{25,17},{2,10},{10... | collective-permute-start | bytes 2949128 | tf_op jit(solution)/shard_map/ppermute | solution.py:30
  146.4 28.2 %collective-permute-start.11 = (bf16[2,384,640]{2,1,0:T(8,128)(2,1)}, bf16[2,384,640]{2,1,0:T(8,128)(2,1)}, u32[]{:S(2)}, u32[]{:S(2)}) collective-permute-start(bf16[2,384,640]{2,1,0:T(8,128)(2,1)} %pad_maximum_fusion.2), channel_id=1, source_target_pairs={{0,16},{8,24},{16,0},{24,8},{1,17},{9,25},{17,1},{25,9},{2,18},{10... | collective-permute-start | bytes 2949128 | tf_op jit(solution)/shard_map/ppermute | solution.py:30
  149.1 42.6 %collective-permute-start.12 = (bf16[2,384,640]{2,1,0:T(8,128)(2,1)}, bf16[2,384,640]{2,1,0:T(8,128)(2,1)}, u32[]{:S(2)}, u32[]{:S(2)}) collective-permute-start(bf16[2,384,640]{2,1,0:T(8,128)(2,1)} %pad_maximum_fusion.3), channel_id=1, source_target_pairs={{0,24},{8,16},{16,8},{24,0},{1,25},{9,17},{17,9},{25,1},{2,26},{10... | collective-permute-start | bytes 2949128 | tf_op jit(solution)/shard_map/ppermute | solution.py:30
  168.8 38.5 %all-to-all-start.2 = ((f32[32,1,128]{2,1,0:T(1,128)}), f32[32,1,128]{2,1,0:T(1,128)S(1)}, u32[]{:S(2)}, u32[]{:S(2)}) async-start(f32[32,1,128]{2,1,0:T(1,128)} %broadcast_in_dim.2), calls=%async_computation.2 | async-start | bytes 32768 | tf_op jit(solution)/shard_map/all_to_all | solution.py:209
  (16 other events, 32.1 us)

commit v3 on v2

v3 whole, which is shorter than its diff:
```python
import functools

import jax
import jax.numpy as jnp
from jax import lax
from jax.experimental import pallas as pl
from jax.experimental.pallas import tpu as pltpu
from jax.sharding import PartitionSpec as P

D = 5120
FFW = 14336
L = 128
VAL = 256

F32 = jnp.float32
BF16 = jnp.bfloat16
VMEM_LIMIT = 48 * 1024 * 1024


def dot_nt(a, b):
    return lax.dot_general(a, b, (((1,), (1,)), ((), ())), preferred_element_type=F32)


def dot_tn(a, b):
    return lax.dot_general(a, b, (((0,), (0,)), ((), ())), preferred_element_type=F32)


def swap(x, axis, k):
    n = lax.axis_size(axis)
    return lax.ppermute(x, axis, [(s, s ^ k) for s in range(n)])


def shift(x, axis, k):
    n = lax.axis_size(axis)
    return lax.ppermute(x, axis, [(s, (s + k) % n) for s in range(n)])


def whole(shape):
    return pl.BlockSpec(shape, lambda *_: (0,) * len(shape))


ANY = pl.BlockSpec(memory_space=pl.ANY)


def params():
    return pltpu.CompilerParams(vmem_limit_bytes=VMEM_LIMIT)


def hidden_body(gate_ref, up_ref, order_ref, out_ref):
    gate = gate_ref[...].astype(F32)
    up = up_ref[...].astype(F32)
    out_ref[...] = (gate * jax.nn.sigmoid(gate) * up).astype(BF16).T


def hidden_units(gate, up, order):
    toks, units = gate.shape
    tile = 256
    cols = pl.BlockSpec((toks, tile), lambda i: (0, i))
    return pl.pallas_call(
        hidden_body,
        grid=(units // tile,),
        in_specs=[cols, cols, ANY],
        out_specs=pl.BlockSpec((tile, toks), lambda i: (i, 0)),
        out_shape=jax.ShapeDtypeStruct((units, toks), BF16),
        compiler_params=params(),
        cost_estimate=pl.CostEstimate(
            flops=4 * toks * units, bytes_accessed=6 * toks * units, transcendentals=toks * units
        ),
        name="hidden",
    )(gate, up, order)


def arrange_body(n, at_ref, *refs):
    blocks, (order_ref, out_ref) = refs[:n], refs[n:]
    for j in range(n):
        out_ref[at_ref[j]] = blocks[j][...]


def arrange(at, blocks, order, name):
    n = len(blocks)
    vmem = pl.BlockSpec(memory_space=pltpu.VMEM)
    return pl.pallas_call(
        functools.partial(arrange_body, n),
        in_specs=[pl.BlockSpec(memory_space=pltpu.SMEM)] + [vmem] * n + [ANY],
        out_specs=vmem,
        out_shape=jax.ShapeDtypeStruct((n,) + blocks[0].shape, BF16),
        compiler_params=params(),
        cost_estimate=pl.CostEstimate(
            flops=0, bytes_accessed=4 * n * blocks[0].size, transcendentals=0
        ),
        name=name,
    )(at, *blocks, order)


def grads_body(offs_ref, own_ref, other_ref, w_ref, gate_ref, up_ref, gg_ref, gu_ref, piece):
    n, toks, width = own_ref.shape

    @pl.when(pl.program_id(0) == 0)
    def _():
        for half, ref in enumerate((own_ref, other_ref)):
            for j in range(n):
                place = pl.multiple_of(offs_ref[half] + 2 * j * width, 128)
                piece[:, pl.ds(place, width)] = ref[j]

    total = dot_nt(piece[...], w_ref[...])
    gate = gate_ref[...].astype(F32)
    up = up_ref[...].astype(F32)
    sig = jax.nn.sigmoid(gate)
    gg_ref[...] = (total * up * sig * (1.0 + gate * (1.0 - sig))).astype(BF16)
    gu_ref[...] = (total * (gate * sig)).astype(BF16)


def grads(offs, own, other, weight, gate, up):
    n, toks, width = own.shape
    units, feats = weight.shape
    tile = 256
    cols = pl.BlockSpec((toks, tile), lambda i, _: (0, i))
    out = jax.ShapeDtypeStruct((toks, units), BF16)
    return pl.pallas_call(
        grads_body,
        grid_spec=pltpu.PrefetchScalarGridSpec(
            num_scalar_prefetch=1,
            grid=(units // tile,),
            in_specs=[whole(own.shape)] * 2
            + [pl.BlockSpec((tile, feats), lambda i, _: (i, 0)), cols, cols],
            out_specs=[cols, cols],
            scratch_shapes=[pltpu.VMEM((toks, feats), BF16)],
        ),
        out_shape=(out, out),
        compiler_params=params(),
        cost_estimate=pl.CostEstimate(
            flops=2 * toks * units * feats,
            bytes_accessed=2 * (units * feats + toks * feats + 4 * toks * units),
            transcendentals=toks * units,
        ),
        name="grads",
    )(offs, own, other, weight, gate, up)


def wgrad_body(offs_ref, hid_ref, own_ref, other_ref, order_ref, out_ref, cols):
    n, toks, width = own_ref.shape

    @pl.when(pl.program_id(0) == 0)
    def _():
        for half, ref in enumerate((own_ref, other_ref)):
            place = pl.ds(pl.multiple_of(offs_ref[half], 128), width)
            for k in range(n):
                cols[k * toks : (k + 1) * toks, place] = ref[k]

    out_ref[...] = lax.dot_general(
        hid_ref[...], cols[...], (((1,), (0,)), ((), ())), preferred_element_type=F32
    ).astype(BF16)


def wgrad(offs, hid, own, other, order):
    units, total = hid.shape
    width = own.shape[2]
    tile = units // 4
    return pl.pallas_call(
        wgrad_body,
        grid_spec=pltpu.PrefetchScalarGridSpec(
            num_scalar_prefetch=1,
            grid=(units // tile,),
            in_specs=[pl.BlockSpec((tile, total), lambda i, _: (i, 0))]
            + [whole(own.shape)] * 2
            + [ANY],
            out_specs=pl.BlockSpec((tile, 2 * width), lambda i, _: (i, 0)),
            scratch_shapes=[pltpu.VMEM((total, 2 * width), BF16)],
        ),
        out_shape=jax.ShapeDtypeStruct((units, 2 * width), BF16),
        compiler_params=params(),
        cost_estimate=pl.CostEstimate(
            flops=4 * total * units * width,
            bytes_accessed=2 * (total * (units + 2 * width) + 2 * units * width),
            transcendentals=0,
        ),
        name="wgrad",
    )(offs, hid, own, other, order)


def put_slices(part, out_ref):
    inner, outer, size, _ = out_ref.shape
    for p in range(inner * outer):
        out_ref[p % inner, p // inner] = part[p * size : (p + 1) * size]


def gram_shape(count, total, parts):
    return jax.ShapeDtypeStruct((2, parts // 2, count // parts, total), F32)


def grad_gram_body(offs_ref, *refs):
    toks_refs, (val_ref, order_ref, out_ref, wide) = refs[:-4], refs[-4:]
    for k, ref in enumerate(toks_refs):
        toks = ref.shape[0]
        wide[:, pl.ds(pl.multiple_of(offs_ref[k], 128), toks)] = dot_nt(val_ref[...], ref[...])
    put_slices(wide[...], out_ref)


def hidden_gram_body(offs_ref, *refs):
    hid, (val_ref, order_ref, out_ref, all_ref) = refs[:-4], refs[-4:]
    for k, ref in enumerate(hid):
        toks = ref.shape[1]
        all_ref[:, pl.ds(pl.multiple_of(offs_ref[k], 128), toks)] = ref[...]
    part = lax.dot_general(
        val_ref[...], all_ref[...], (((1,), (0,)), ((), ())), preferred_element_type=F32
    )
    put_slices(part, out_ref)


def gram_call(body, offs, operands, order, shapes, scratch, flops, name):
    vmem = pl.BlockSpec(memory_space=pltpu.VMEM)
    return pl.pallas_call(
        body,
        in_specs=[pl.BlockSpec(memory_space=pltpu.SMEM)] + [vmem] * len(operands) + [ANY],
        out_specs=[vmem] * len(shapes),
        out_shape=shapes,
        scratch_shapes=scratch,
        compiler_params=params(),
        cost_estimate=pl.CostEstimate(
            flops=flops,
            bytes_accessed=sum(x.size * x.dtype.itemsize for x in [*operands, *shapes]),
            transcendentals=0,
        ),
        name=name,
    )(offs, *operands, order)


def gram_sum(part):
    n_fs = lax.axis_size("fsdp")
    inner = lax.axis_index("fsdp") % 2
    away = lax.dynamic_index_in_dim(part, 1 - inner, axis=0, keepdims=False)
    kept = lax.dynamic_index_in_dim(part, inner, axis=0, keepdims=False)
    pair = kept + swap(away, "fsdp", 1)
    groups = [list(range(x, n_fs, 2)) for x in range(2)]
    every = lax.all_to_all(
        pair, "fsdp", split_axis=0, concat_axis=0, axis_index_groups=groups, tiled=True
    )
    return jnp.sum(every, axis=0), pair


def per_device(gate_act, up_act, out_grad, down_weight, val_hidden, val_grad, assign):
    n_dp = lax.axis_size("dp")
    n_fs = lax.axis_size("fsdp")
    d = lax.axis_index("dp")
    f = lax.axis_index("fsdp")
    rows_here = assign.shape[0]
    toks, width = out_grad.shape
    units = gate_act.shape[1]
    total = n_dp * toks
    n_out = n_fs // 2
    outer, inner = f // 2, f % 2

    def over_dp(x):
        far = swap(x, "dp", 2)
        near = swap(jnp.stack([x, far]), "dp", 1)
        return [x, near[0], far, near[1]]

    ring = [out_grad]
    for _ in range(n_out - 1):
        ring.append(shift(ring[-1], "fsdp", 2))
    others = [swap(own, "fsdp", 1) for own in ring]

    far = swap(out_grad, "dp", 2)
    grad_dp = [out_grad, swap(out_grad, "dp", 1), far, swap(far, "dp", 1)]
    hid_dp = over_dp(hidden_units(gate_act, up_act, grad_dp[1]))

    at = (outer - jnp.arange(n_out, dtype=jnp.int32)) % n_out
    own = arrange(at, ring, others[0], "own_features")
    own_cols = lax.all_to_all(own, "dp", split_axis=0, concat_axis=0, tiled=True)
    other = arrange(at, others, own, "other_features")
    other_cols = lax.all_to_all(other, "dp", split_axis=0, concat_axis=0, tiled=True)

    tok_offs = (d ^ jnp.arange(n_dp, dtype=jnp.int32)) * toks
    vals = val_grad.shape[0]
    shape = gram_shape(vals, total, n_fs)
    (part,) = gram_call(
        grad_gram_body, tok_offs, [*grad_dp, val_grad], own, [shape],
        [pltpu.VMEM((vals, total), F32)], 2 * vals * total * width, "grad_gram",
    )
    grad_gram, _ = gram_sum(part)
    part, hid_all = gram_call(
        hidden_gram_body, tok_offs, [*hid_dp, val_hidden], other,
        [shape, jax.ShapeDtypeStruct((units, total), BF16)], [],
        2 * vals * total * units, "hidden_gram",
    )
    hidden_gram, order = gram_sum(part)
    by_row = jnp.sum(hidden_gram * grad_gram, axis=0)
    by_row = jnp.sum(by_row.reshape(n_dp * rows_here, toks // rows_here), axis=1)

    offs = (jnp.stack([inner, 1 - inner]) * width).astype(jnp.int32)
    grad_gate, grad_up = grads(offs, own, other, down_weight, gate_act, up_act)
    weight_grad = wgrad(offs, hid_all, own_cols, other_cols, order)

    mine = jnp.concatenate([by_row, assign.astype(F32)])
    mine = jnp.pad(mine, (0, 128 - mine.shape[0]))
    every = lax.all_to_all(
        jnp.broadcast_to(mine[None], (n_dp * n_fs, 128)),
        ("dp", "fsdp"), split_axis=0, concat_axis=0, tiled=True,
    ).reshape(n_dp, n_fs, 128)
    rows = n_dp * rows_here
    scale = 1.0 / jnp.sqrt(F32(L) * VAL * FFW * D)
    scores = jnp.sum(every[:, :, :rows], axis=1) * scale
    groups = every[:, 0, rows : rows + rows_here].reshape(rows)
    onehot = (groups[None, :] == jnp.arange(n_dp, dtype=F32)[:, None]).astype(F32)
    group_values = jnp.sum(onehot * scores, axis=1)
    row_scores = lax.dynamic_slice_in_dim(scores, d * rows_here, rows_here, axis=1).T
    return (grad_gate, grad_up, weight_grad, row_scores, group_values)


def per_device_any(gate_act, up_act, out_grad, down_weight, val_hidden, val_grad, assign):
    n_dp = lax.axis_size("dp")
    me = lax.axis_index("dp")
    rows_here = assign.shape[0]
    toks = gate_act.shape[0]
    gate = gate_act.astype(F32)
    up = up_act.astype(F32)
    sig = jax.nn.sigmoid(gate)
    act = gate * sig
    hidden = (act * up).astype(BF16)
    grad_feat = lax.all_gather(out_grad, "dp", axis=0, tiled=True)
    piece = lax.all_gather(out_grad, "fsdp", axis=1, tiled=True)
    hidden_all = lax.all_gather(hidden, "dp", axis=0, tiled=True)
    grad_gram = lax.psum(dot_nt(grad_feat, val_grad), "fsdp")
    grad_cols = lax.all_to_all(piece, "dp", split_axis=1, concat_axis=0, tiled=True)
    grad_hidden = dot_nt(piece, down_weight)
    grad_gate = (grad_hidden * up * sig * (1.0 + gate * (1.0 - sig))).astype(BF16)
    grad_up = (grad_hidden * act).astype(BF16)
    product = dot_nt(hidden_all, val_hidden) * grad_gram
    part = jnp.sum(product.reshape(n_dp * rows_here, toks // rows_here * VAL), axis=1)
    weight_grad = dot_tn(hidden_all, grad_cols).astype(BF16)
    scale = 1.0 / jnp.sqrt(F32(L) * VAL * FFW * D)
    scores = lax.all_gather(lax.psum(part, "fsdp"), "dp") * scale
    groups = lax.all_gather(assign, "dp", tiled=True)
    onehot = (groups[None, :] == jnp.arange(n_dp, dtype=jnp.int32)[:, None]).astype(F32)
    group_values = jnp.sum(onehot * scores, axis=1)
    row_scores = lax.dynamic_slice_in_dim(scores, me * rows_here, rows_here, axis=1).T
    return (grad_gate, grad_up, weight_grad, row_scores, group_values)


def solution(mesh):
    in_specs = (
        P("dp", "fsdp"),
        P("dp", "fsdp"),
        P("dp", "fsdp"),
        P("fsdp", None),
        P("dp", "fsdp"),
        P("dp", "fsdp"),
        P("dp"),
    )
    out_specs = (P("dp", "fsdp"), P("dp", "fsdp"), P("fsdp", "dp"), P("dp", None), P())
    n_dp, n_fs = mesh.shape["dp"], mesh.shape["fsdp"]
    fits = n_dp == 4 and n_fs == 2 * n_dp
    return jax.shard_map(
        per_device if fits else per_device_any,
        mesh=mesh, in_specs=in_specs, out_specs=out_specs, check_vma=False,
    )
```

time: 210 us -> 219 us (1.043)
  blocking collectives: 0 us -> 22.7 us
  other arithmetic: 20.4 us -> 7.84 us
  waiting for transfers between devices: 108 us -> 101 us
  Pallas kernels: 36.8 us -> 41 us
    ppermute x15 -> x11, waiting for transfers between devices: 104 us -> 52.6 us  [swap(): return lax.ppermute(x, axis, [(s, s ^ k) for s in range(n)])]
    ppermute x3, waiting for transfers between devices: 4.7 us -> 37.9 us  [shift(): return lax.ppermute(x, axis, [(s, (s + k) % n) for s in range(n)])]
    all_to_all x0 -> x1, blocking collectives: none -> 22.7 us  [gram_sum(): lax.all_to_all(pair, 'fsdp', split_axis=0, concat_axis=0, axis_index_grou...]
    another operation x8 -> x1, other arithmetic: 10 us -> 1.84 us  [over_dp(): near = swap(jnp.stack([x, far]), 'dp', 1)]
    all_to_all x0 -> x2, starting transfers between devices: none -> 8.16 us  [the longest x1 4.44 us: per_device(): lax.all_to_all(own, 'dp', split_axis=0, concat_axis=0, tiled=True)]
    all_to_all x2 -> x1, waiting for transfers between devices: 0.01 us -> 7.71 us  [gram_sum(): lax.all_to_all(pair, 'fsdp', split_axis=0, concat_axis=0, axis_index_grou...]
    pallas_call x4 -> x7, Pallas kernels: 36.8 us -> 41 us  [the longest x1 15.4 us: grads(): pl.pallas_call(grads_body, grid_spec=pltpu.PrefetchScalarGridSpec(num_sca...]
    all_to_all x2 -> x1, starting transfers between devices: 8.51 us -> 5.01 us  [gram_sum(): lax.all_to_all(pair, 'fsdp', split_axis=0, concat_axis=0, axis_index_grou...]
  transfers between devices with their start and end apart: 21 -> 18, of which waited for: 7 -> 10; matrix products, arithmetic and copies ran while one was open for 10% -> 4% of each run, Pallas kernels for 18% -> 18%
where the time goes in v3:
time: 219 us; the launch traced here: 218 us
  waiting for transfers between devices  101 us (46%)
  Pallas kernels  41 us (19%)
  starting transfers between devices  29.8 us (14%)
  blocking collectives  22.7 us (10%)
  local copies, waits for them, and re-layouts  14.4 us (7%)
  other arithmetic  7.84 us (4%)
    ppermute x11, waiting for transfers between devices, swap(): return lax.ppermute(x, axis, [(s, s ^ k) for s in range(n)])  52.6 us
    ppermute x3, waiting for transfers between devices, shift(): return lax.ppermute(x, axis, [(s, (s + k) % n) for s in range(n)])  37.9 us
    all_to_all x1, blocking collectives, gram_sum(): lax.all_to_all(pair, 'fsdp', split_axis=0, concat_axis=0, axis_index_grou...  22.7 us
    pallas_call x1, Pallas kernels, grads(): pl.pallas_call(grads_body, grid_spec=pltpu.PrefetchScalarGridSpec(num_sca...  15.4 us
    ppermute x11, starting transfers between devices, swap(): return lax.ppermute(x, axis, [(s, s ^ k) for s in range(n)])  12.2 us
    pallas_call x1, Pallas kernels, wgrad(): pl.pallas_call(wgrad_body, grid_spec=pltpu.PrefetchScalarGridSpec(num_sca...  11.7 us
    unnamed x27, local copies, waits for them, and re-layouts  9.07 us
    all_to_all x1, waiting for transfers between devices, gram_sum(): lax.all_to_all(pair, 'fsdp', split_axis=0, concat_axis=0, axis_index_grou...  7.71 us
  transfers between devices with their start and end apart: 18, of which 10 were waited for; matrix products, arithmetic and copies ran while one was open for 4% of the time, Pallas kernels for 18%

profile of v3, /device:TPU:0, one launch (start us, length us, event | category | flops | bytes accessed | tf_op | source)
XLA Modules:
  0.0 217.8 jit_solution(10072404558212329344)
XLA Ops:
  6.9 3.0 %collective-permute-start.8 = (bf16[1792,384]{1,0:T(8,128)(2,1)S(1)}, bf16[1792,384]{1,0:T(8,128)(2,1)S(1)}, u32[]{:S(2)}, u32[]{:S(2)}) collective-permute-start(bf16[1792,384]{1,0:T(8,128)(2,1)S(1)} %hidden.1.refs_0_), channel_id=1, source_target_pairs={{0,16},{8,24},{16,0},{24,8},{1,17},{9,25},{17,1},{25,9},{2,18},{10... | collective-permute-start | bytes 4128776 | tf_op jit(solution)/shard_map/ppermute | solution.py:30
  9.8 30.5 %collective-permute-done.8.refs_2_ = bf16[1792,384]{1,0:T(8,128)(2,1)S(1)} collective-permute-done((bf16[1792,384]{1,0:T(8,128)(2,1)S(1)}, bf16[1792,384]{1,0:T(8,128)(2,1)S(1)}, u32[]{:S(2)}, u32[]{:S(2)}) %collective-permute-start.8) | collective-permute-done | bytes 1376288 | tf_op jit(solution)/shard_map/ppermute | solution.py:30
  40.3 1.8 pad_maximum_fusion
  42.2 1.8 collective-permute-start
  44.0 13.9 %collective-permute-done.refs_1_ = bf16[384,640]{1,0:T(8,128)(2,1)S(1)} collective-permute-done((bf16[384,640]{1,0:T(8,128)(2,1)S(1)}, bf16[384,640]{1,0:T(8,128)(2,1)S(1)}, u32[]{:S(2)}, u32[]{:S(2)}) %collective-permute-start) | collective-permute-done | bytes 491552 | tf_op jit(solution)/shard_map/ppermute | solution.py:35
  60.9 11.9 %collective-permute-done.1.refs_2_ = bf16[384,640]{1,0:T(8,128)(2,1)} collective-permute-done((bf16[384,640]{1,0:T(8,128)(2,1)S(1)}, bf16[384,640]{1,0:T(8,128)(2,1)}, u32[]{:S(2)}, u32[]{:S(2)}) %collective-permute-start.1) | collective-permute-done | bytes 491552 | tf_op jit(solution)/shard_map/ppermute | solution.py:35
  75.1 12.1 %collective-permute-done.2.refs_3_ = bf16[384,640]{1,0:T(8,128)(2,1)} collective-permute-done((bf16[384,640]{1,0:T(8,128)(2,1)}, bf16[384,640]{1,0:T(8,128)(2,1)}, u32[]{:S(2)}, u32[]{:S(2)}) %collective-permute-start.2) | collective-permute-done | bytes 491552 | tf_op jit(solution)/shard_map/ppermute | solution.py:35
  89.4 2.7 %own_features.1.refs_4_.own_ref.refs_5_ = bf16[4,384,640]{2,1,0:T(8,128)(2,1)} custom-call(s32[4]{0:T(128)S(1)} %and_select_fusion.at_ref, bf16[384,640]{1,0:T(8,128)(2,1)S(1)} %copy-done, bf16[384,640]{1,0:T(8,128)(2,1)S(1)} %copy-done.9, bf16[384,640]{1,0:T(8,128)(2,1)} %collective-permute-done.1.refs_2_, bf16[384,640]{1,0:T(8,128)(2,1)} %collective-permute-done.2.refs_3_, ...), custom_call_target="tpu_custom_call" | custom-call | bytes 3932160 | tf_op jit(solution)/shard_map/own_features/pallas_call | solution.py:82
  92.1 4.4 %all-to-all-start = ((bf16[4,384,640]{2,1,0:T(8,128)(2,1)}), bf16[4,384,640]{2,1,0:T(8,128)(2,1)}, u32[]{:S(2)}, u32[]{:S(2)}) async-start(bf16[4,384,640]{2,1,0:T(8,128)(2,1)} %own_features.1.refs_4_.own_ref.refs_5_), calls=%async_computation | async-start | bytes 3932160 | tf_op jit(solution)/shard_map/all_to_all | solution.py:269
  98.5 2.3 %grad_gram.1 = f32[2,4,32,1536]{3,2,1,0:T(8,128)S(1)} custom-call(s32[4]{0:T(128)S(1)} %xor_multiply_fusion.offs_ref, bf16[384,640]{1,0:T(8,128)(2,1)S(1)} %copy-done, bf16[384,640]{1,0:T(8,128)(2,1)S(1)} %copy-done.2, bf16[384,640]{1,0:T(8,128)(2,1)} %collective-permute-done.11.refs_2_, bf16[384,640]{1,0:T(8,128)(2,1)} %collective-permute-done.12.refs_3_, ...), custom_call_target="tpu_custom_call" | custom-call | flops 503316480 | bytes 3866624 | tf_op jit(solution)/shard_map/grad_gram/pallas_call | solution.py:212
  101.8 6.7 %collective-permute-done.6.refs_3_ = bf16[384,640]{1,0:T(8,128)(2,1)} collective-permute-done((bf16[384,640]{1,0:T(8,128)(2,1)}, bf16[384,640]{1,0:T(8,128)(2,1)}, u32[]{:S(2)}, u32[]{:S(2)}) %collective-permute-start.6) | collective-permute-done | bytes 491552 | tf_op jit(solution)/shard_map/ppermute | solution.py:30
  108.4 2.9 %other_features.1.other_ref.refs_5_ = bf16[4,384,640]{2,1,0:T(8,128)(2,1)} custom-call(s32[4]{0:T(128)S(1)} %and_select_fusion.at_ref, bf16[384,640]{1,0:T(8,128)(2,1)} %collective-permute-done.3.refs_4_.refs_0_, bf16[384,640]{1,0:T(8,128)(2,1)} %collective-permute-done.4.refs_1_, bf16[384,640]{1,0:T(8,128)(2,1)} %collective-permute-done.5.refs_2_, ...), custom_call_target="tpu_custom_call" | custom-call | bytes 3932160 | tf_op jit(solution)/shard_map/other_features/pallas_call | solution.py:82
  111.3 3.2 %slice_bitcast_fusion = (bf16[1792,384]{1,0:T(8,128)(2,1)}, bf16[1792,384]{1,0:T(8,128)(2,1)S(1)}) fusion(bf16[2,1792,384]{2,1,0:T(8,128)(2,1)} %collective-permute-done.9), kind=kLoop, calls=%fused_computation.1 | loop fusion | bytes 5505024 | tf_op jit(solution)/shard_map/squeeze | solution.py:256
  114.5 4.8 %hidden_gram.1 = (f32[2,4,32,1536]{3,2,1,0:T(8,128)}, bf16[1792,1536]{1,0:T(8,128)(2,1)}) custom-call(s32[4]{0:T(128)S(1)} %xor_multiply_fusion.offs_ref, bf16[1792,384]{1,0:T(8,128)(2,1)S(1)} %hidden.1.refs_0_, bf16[1792,384]{1,0:T(8,128)(2,1)S(1)} %get-tuple-element.24.refs_1_, bf16[1792,384]{1,0:T(8,128)(2,1)S(1)} %collective-permute-done.8.refs_2_, ...), custom_call_target="tpu_custom_call" | custom-call | flops 1409286144 | bytes 13500416 | tf_op jit(solution)/shard_map/hidden_gram/pallas_call | solution.py:212
  122.0 3.2 %collective-permute-done.13 = f32[4,32,1536]{2,1,0:T(8,128)S(1)} collective-permute-done((f32[4,32,1536]{2,1,0:T(8,128)S(1)}, f32[4,32,1536]{2,1,0:T(8,128)S(1)}, u32[]{:S(2)}, u32[]{:S(2)}) %collective-permute-start.13) | collective-permute-done | bytes 786464 | tf_op jit(solution)/shard_map/ppermute | solution.py:30
  126.2 5.0 %all-to-all-start.3 = ((f32[4,32,1536]{2,1,0:T(8,128)}), f32[4,32,1536]{2,1,0:T(8,128)S(1)}, u32[]{:S(2)}, u32[]{:S(2)}) async-start(f32[4,32,1536]{2,1,0:T(8,128)} %bitcast_add_fusion), calls=%async_computation.3 | async-start | bytes 1572864 | tf_op jit(solution)/shard_map/all_to_all | solution.py:235
  131.2 10.5 %collective-permute-done.10 = f32[4,32,1536]{2,1,0:T(8,128)} collective-permute-done((f32[4,32,1536]{2,1,0:T(8,128)S(1)}, f32[4,32,1536]{2,1,0:T(8,128)}, u32[]{:S(2)}, u32[]{:S(2)}) %collective-permute-start.10) | collective-permute-done | bytes 786464 | tf_op jit(solution)/shard_map/ppermute | solution.py:30
  142.9 7.7 %all-to-all-done.3 = f32[4,32,1536]{2,1,0:T(8,128)S(1)} async-done(((f32[4,32,1536]{2,1,0:T(8,128)}), f32[4,32,1536]{2,1,0:T(8,128)S(1)}, u32[]{:S(2)}, u32[]{:S(2)}) %all-to-all-start.3) | async-done | bytes 786464 | tf_op jit(solution)/shard_map/all_to_all | solution.py:235
  150.6 22.7 %all_to_all.26 = f32[4,32,1536]{2,1,0:T(8,128)} all-to-all(f32[4,32,1536]{2,1,0:T(8,128)S(1)} %bitcast_add_fusion.1.order_ref), channel_id=1, replica_groups={{0,2,4,6},{1,3,5,7},{8,10,12,14},{9,11,13,15},{16,18,20,22},{17,19,21,2..., dimensions={0} | all-to-all | bytes 1572864 | tf_op jit(solution)/shard_map/all_to_all | solution.py:235
  173.3 3.7 %all-to-all-start.1 = ((bf16[4,384,640]{2,1,0:T(8,128)(2,1)}), bf16[4,384,640]{2,1,0:T(8,128)(2,1)S(1)}, u32[]{:S(2)}, u32[]{:S(2)}) async-start(bf16[4,384,640]{2,1,0:T(8,128)(2,1)} %other_features.1.other_ref.refs_5_), calls=%async_computation.1 | async-start | bytes 3932160 | tf_op jit(solution)/shard_map/all_to_all | solution.py:271
  179.8 15.4 %grads.1 = (bf16[384,1792]{1,0:T(8,128)(2,1)}, bf16[384,1792]{1,0:T(8,128)(2,1)}) custom-call(s32[2]{0:T(128)S(1)} %add_multiply_fusion.offs_ref, bf16[4,384,640]{2,1,0:T(8,128)(2,1)} %own_features.1.refs_4_.own_ref.refs_5_, bf16[4,384,640]{2,1,0:T(8,128)(2,1)} %other_features.1.other_ref.refs_5_, bf16[1792,5120]{1,0:T(8,128)(2,1)} %w_ref.1, ...), custom_call_target="tpu_custom_call" | custom-call | flops 7046430720 | bytes 27787264 | tf_op jit(solution)/shard_map/grads/pallas_call | solution.py:119
  198.3 3.0 %all-to-all-done.1.other_ref = bf16[4,384,640]{2,1,0:T(8,128)(2,1)S(1)} async-done(((bf16[4,384,640]{2,1,0:T(8,128)(2,1)}), bf16[4,384,640]{2,1,0:T(8,128)(2,1)S(1)}, u32[]{:S(2)}, u32[]{:S(2)}) %all-to-all-start.1) | async-done | bytes 1966112 | tf_op jit(solution)/shard_map/all_to_all | solution.py:271
  201.9 2.6 %all-to-all-start.4 = ((f32[32,1,128]{2,1,0:T(1,128)}), f32[32,1,128]{2,1,0:T(1,128)S(1)}, u32[]{:S(2)}, u32[]{:S(2)}) async-start(f32[32,1,128]{2,1,0:T(1,128)} %broadcast_in_dim.2), calls=%async_computation.4 | async-start | bytes 32768 | tf_op jit(solution)/shard_map/all_to_all | solution.py:296
  204.5 11.7 %wgrad.1 = bf16[1792,1280]{1,0:T(8,128)(2,1)} custom-call(s32[2]{0:T(128)S(1)} %add_multiply_fusion.offs_ref, bf16[1792,1536]{1,0:T(8,128)(2,1)} %get-tuple-element.11.hid_ref, bf16[4,384,640]{2,1,0:T(8,128)(2,1)} %all-to-all-done.own_ref, bf16[4,384,640]{2,1,0:T(8,128)(2,1)S(1)} %all-to-all-done.1.other_ref, f32[4,32,1536]{2,1,0:T(8,128)S(1)} %bitcast_add_fusion.1.order_ref), custom_call_target="tpu_custom_call" | custom-call | flops 7046430720 | bytes 14024704 | tf_op jit(solution)/shard_map/wgrad/pallas_call | solution.py:159
  (68 shorter events, 29.4 us)
Async XLA Ops:
  0.6 2.2 %collective-permute-start.7 = (bf16[384,640]{1,0:T(8,128)(2,1)}, bf16[384,640]{1,0:T(8,128)(2,1)S(1)}, u32[]{:S(2)}, u32[]{:S(2)}) collective-permute-start(bf16[384,640]{1,0:T(8,128)(2,1)} %refs_0_.3), channel_id=1, source_target_pairs={{0,8},{8,0},{16,24},{24,16},{1,9},{9,1},{17,25},{25,17},{2,10},{10... | collective-permute-start | bytes 1474568 | tf_op jit(solution)/shard_map/ppermute | solution.py:30
  6.9 33.4 %collective-permute-start.8 = (bf16[1792,384]{1,0:T(8,128)(2,1)S(1)}, bf16[1792,384]{1,0:T(8,128)(2,1)S(1)}, u32[]{:S(2)}, u32[]{:S(2)}) collective-permute-start(bf16[1792,384]{1,0:T(8,128)(2,1)S(1)} %hidden.1.refs_0_), channel_id=1, source_target_pairs={{0,16},{8,24},{16,0},{24,8},{1,17},{9,25},{17,1},{25,9},{2,18},{10... | collective-permute-start | bytes 4128776 | tf_op jit(solution)/shard_map/ppermute | solution.py:30
  40.3 1.8 copy-start
  42.2 69.2 %collective-permute-start.9 = (bf16[2,1792,384]{2,1,0:T(8,128)(2,1)}, bf16[2,1792,384]{2,1,0:T(8,128)(2,1)}, u32[]{:S(2)}, u32[]{:S(2)}) collective-permute-start(bf16[2,1792,384]{2,1,0:T(8,128)(2,1)} %pad_maximum_fusion), channel_id=1, source_target_pairs={{0,8},{8,0},{16,24},{24,16},{1,9},{9,1},{17,25},{25,17},{2,10},{10... | collective-permute-start | bytes 8257544 | tf_op jit(solution)/shard_map/ppermute | solution.py:30
  42.2 15.7 %collective-permute-start = (bf16[384,640]{1,0:T(8,128)(2,1)S(1)}, bf16[384,640]{1,0:T(8,128)(2,1)S(1)}, u32[]{:S(2)}, u32[]{:S(2)}) collective-permute-start(bf16[384,640]{1,0:T(8,128)(2,1)S(1)} %copy-done), channel_id=1, source_target_pairs={{0,2},{1,3},{2,4},{3,5},{4,6},{5,7},{6,0},{7,1},{8,10},{9,11},{10,... | collective-permute-start | bytes 1474568 | tf_op jit(solution)/shard_map/ppermute | solution.py:35
  57.9 15.0 %copy-start.8 = (bf16[384,640]{1,0:T(8,128)(2,1)}, bf16[384,640]{1,0:T(8,128)(2,1)S(1)}, u32[]{:S(2)}) copy-start(bf16[384,640]{1,0:T(8,128)(2,1)S(1)} %collective-permute-done.refs_1_) | copy-start | bytes 1474564
  57.9 15.0 %collective-permute-start.1 = (bf16[384,640]{1,0:T(8,128)(2,1)S(1)}, bf16[384,640]{1,0:T(8,128)(2,1)}, u32[]{:S(2)}, u32[]{:S(2)}) collective-permute-start(bf16[384,640]{1,0:T(8,128)(2,1)S(1)} %collective-permute-done.refs_1_), channel_id=1, source_target_pairs={{0,2},{1,3},{2,4},{3,5},{4,6},{5,7},{6,0},{7,1},{8,10},{9,11},{10,... | collective-permute-start | bytes 1474568 | tf_op jit(solution)/shard_map/ppermute | solution.py:35
  57.9 15.0 %collective-permute-start.11 = (bf16[384,640]{1,0:T(8,128)(2,1)S(1)}, bf16[384,640]{1,0:T(8,128)(2,1)}, u32[]{:S(2)}, u32[]{:S(2)}) collective-permute-start(bf16[384,640]{1,0:T(8,128)(2,1)S(1)} %copy-done), channel_id=1, source_target_pairs={{0,16},{8,24},{16,0},{24,8},{1,17},{9,25},{17,1},{25,9},{2,18},{10... | collective-permute-start | bytes 1474568 | tf_op jit(solution)/shard_map/ppermute | solution.py:30
  59.4 15.0 %collective-permute-start.3 = (bf16[384,640]{1,0:T(8,128)(2,1)S(1)}, bf16[384,640]{1,0:T(8,128)(2,1)}, u32[]{:S(2)}, u32[]{:S(2)}) collective-permute-start(bf16[384,640]{1,0:T(8,128)(2,1)S(1)} %copy-done), channel_id=1, source_target_pairs={{0,1},{1,0},{2,3},{3,2},{4,5},{5,4},{6,7},{7,6},{8,9},{9,8},{10,11... | collective-permute-start | bytes 1474568 | tf_op jit(solution)/shard_map/ppermute | solution.py:30
  72.8 14.3 %collective-permute-start.2 = (bf16[384,640]{1,0:T(8,128)(2,1)}, bf16[384,640]{1,0:T(8,128)(2,1)}, u32[]{:S(2)}, u32[]{:S(2)}) collective-permute-start(bf16[384,640]{1,0:T(8,128)(2,1)} %collective-permute-done.1.refs_2_), channel_id=1, source_target_pairs={{0,2},{1,3},{2,4},{3,5},{4,6},{5,7},{6,0},{7,1},{8,10},{9,11},{10,... | collective-permute-start | bytes 1474568 | tf_op jit(solution)/shard_map/ppermute | solution.py:35
  72.8 23.7 %collective-permute-start.12 = (bf16[384,640]{1,0:T(8,128)(2,1)}, bf16[384,640]{1,0:T(8,128)(2,1)}, u32[]{:S(2)}, u32[]{:S(2)}) collective-permute-start(bf16[384,640]{1,0:T(8,128)(2,1)} %collective-permute-done.11.refs_2_), channel_id=1, source_target_pairs={{0,8},{8,0},{16,24},{24,16},{1,9},{9,1},{17,25},{25,17},{2,10},{10... | collective-permute-start | bytes 1474568 | tf_op jit(solution)/shard_map/ppermute | solution.py:30
  73.0 28.8 %collective-permute-start.4 = (bf16[384,640]{1,0:T(8,128)(2,1)}, bf16[384,640]{1,0:T(8,128)(2,1)}, u32[]{:S(2)}, u32[]{:S(2)}) collective-permute-start(bf16[384,640]{1,0:T(8,128)(2,1)} %copy-done.8), channel_id=1, source_target_pairs={{0,1},{1,0},{2,3},{3,2},{4,5},{5,4},{6,7},{7,6},{8,9},{9,8},{10,11... | collective-permute-start | bytes 1474568 | tf_op jit(solution)/shard_map/ppermute | solution.py:30
  74.4 27.4 %collective-permute-start.5 = (bf16[384,640]{1,0:T(8,128)(2,1)}, bf16[384,640]{1,0:T(8,128)(2,1)}, u32[]{:S(2)}, u32[]{:S(2)}) collective-permute-start(bf16[384,640]{1,0:T(8,128)(2,1)} %collective-permute-done.1.refs_2_), channel_id=1, source_target_pairs={{0,1},{1,0},{2,3},{3,2},{4,5},{5,4},{6,7},{7,6},{8,9},{9,8},{10,11... | collective-permute-start | bytes 1474568 | tf_op jit(solution)/shard_map/ppermute | solution.py:30
  87.1 21.3 %collective-permute-start.6 = (bf16[384,640]{1,0:T(8,128)(2,1)}, bf16[384,640]{1,0:T(8,128)(2,1)}, u32[]{:S(2)}, u32[]{:S(2)}) collective-permute-start(bf16[384,640]{1,0:T(8,128)(2,1)} %collective-permute-done.2.refs_3_), channel_id=1, source_target_pairs={{0,1},{1,0},{2,3},{3,2},{4,5},{5,4},{6,7},{7,6},{8,9},{9,8},{10,11... | collective-permute-start | bytes 1474568 | tf_op jit(solution)/shard_map/ppermute | solution.py:30
  92.1 34.1 %all-to-all-start = ((bf16[4,384,640]{2,1,0:T(8,128)(2,1)}), bf16[4,384,640]{2,1,0:T(8,128)(2,1)}, u32[]{:S(2)}, u32[]{:S(2)}) async-start(bf16[4,384,640]{2,1,0:T(8,128)(2,1)} %own_features.1.refs_4_.own_ref.refs_5_), calls=%async_computation | async-start | bytes 3932160 | tf_op jit(solution)/shard_map/all_to_all | solution.py:269
  100.9 24.3 %collective-permute-start.13 = (f32[4,32,1536]{2,1,0:T(8,128)S(1)}, f32[4,32,1536]{2,1,0:T(8,128)S(1)}, u32[]{:S(2)}, u32[]{:S(2)}) collective-permute-start(f32[4,32,1536]{2,1,0:T(8,128)S(1)} %dynamic-slice_bitcast_fusion), channel_id=1, source_target_pairs={{0,1},{1,0},{2,3},{3,2},{4,5},{5,4},{6,7},{7,6},{8,9},{9,8},{10,11... | collective-permute-start | bytes 2359304 | tf_op jit(solution)/shard_map/ppermute | solution.py:30
  111.3 3.2 %copy-start.7 = (bf16[256,1792]{1,0:T(8,128)(2,1)S(1)}, bf16[256,1792]{1,0:T(8,128)(2,1)}, u32[]{:S(2)}) copy-start(bf16[256,1792]{1,0:T(8,128)(2,1)} %refs_4_.2) | copy-start | bytes 2752516
  120.5 21.1 %copy-start.11 = (f32[2,4,32,1536]{3,2,1,0:T(8,128)S(1)}, f32[2,4,32,1536]{3,2,1,0:T(8,128)}, u32[]{:S(2)}) copy-start(f32[2,4,32,1536]{3,2,1,0:T(8,128)} %get-tuple-element.12) | copy-start | bytes 4718596
  120.5 21.1 %collective-permute-start.10 = (f32[4,32,1536]{2,1,0:T(8,128)S(1)}, f32[4,32,1536]{2,1,0:T(8,128)}, u32[]{:S(2)}, u32[]{:S(2)}) collective-permute-start(f32[4,32,1536]{2,1,0:T(8,128)S(1)} %dynamic-slice_bitcast_fusion.1), channel_id=1, source_target_pairs={{0,1},{1,0},{2,3},{3,2},{4,5},{5,4},{6,7},{7,6},{8,9},{9,8},{10,11... | collective-permute-start | bytes 2359304 | tf_op jit(solution)/shard_map/ppermute | solution.py:30
  126.2 24.5 %all-to-all-start.3 = ((f32[4,32,1536]{2,1,0:T(8,128)}), f32[4,32,1536]{2,1,0:T(8,128)S(1)}, u32[]{:S(2)}, u32[]{:S(2)}) async-start(f32[4,32,1536]{2,1,0:T(8,128)} %bitcast_add_fusion), calls=%async_computation.3 | async-start | bytes 1572864 | tf_op jit(solution)/shard_map/all_to_all | solution.py:235
  173.3 3.7 %copy-start.12 = (s32[3]{0:T(128)S(1)}, s32[3]{0:T(128)}, u32[]{:S(2)}) copy-start(s32[3]{0:T(128)} %param.13) | copy-start | bytes 40
  173.3 28.0 %all-to-all-start.1 = ((bf16[4,384,640]{2,1,0:T(8,128)(2,1)}), bf16[4,384,640]{2,1,0:T(8,128)(2,1)S(1)}, u32[]{:S(2)}, u32[]{:S(2)}) async-start(bf16[4,384,640]{2,1,0:T(8,128)(2,1)} %other_features.1.other_ref.refs_5_), calls=%async_computation.1 | async-start | bytes 3932160 | tf_op jit(solution)/shard_map/all_to_all | solution.py:271
  177.2 1.3 copy-start.4
  201.9 14.3 %all-to-all-start.4 = ((f32[32,1,128]{2,1,0:T(1,128)}), f32[32,1,128]{2,1,0:T(1,128)S(1)}, u32[]{:S(2)}, u32[]{:S(2)}) async-start(f32[32,1,128]{2,1,0:T(1,128)} %broadcast_in_dim.2), calls=%async_computation.4 | async-start | bytes 32768 | tf_op jit(solution)/shard_map/all_to_all | solution.py:296
  (7 other events, 8.4 us)

commit v4 on v3

--- a/solution.py
+++ b/solution.py
@@ -46,20 +46,35 @@
     return pltpu.CompilerParams(vmem_limit_bytes=VMEM_LIMIT)
 
 
-def hidden_body(gate_ref, up_ref, order_ref, out_ref):
+def after_body(*refs):
+    pass
+
+
+def after(x, *order):
+    return pl.pallas_call(
+        after_body,
+        in_specs=[ANY] * (1 + len(order)),
+        out_specs=ANY,
+        out_shape=jax.ShapeDtypeStruct(x.shape, x.dtype),
+        input_output_aliases={0: 0},
+        name="after",
+    )(x, *order)
+
+
+def hidden_body(gate_ref, up_ref, out_ref):
     gate = gate_ref[...].astype(F32)
     up = up_ref[...].astype(F32)
     out_ref[...] = (gate * jax.nn.sigmoid(gate) * up).astype(BF16).T
 
 
-def hidden_units(gate, up, order):
+def hidden_units(gate, up):
     toks, units = gate.shape
     tile = 256
     cols = pl.BlockSpec((toks, tile), lambda i: (0, i))
     return pl.pallas_call(
         hidden_body,
         grid=(units // tile,),
-        in_specs=[cols, cols, ANY],
+        in_specs=[cols, cols],
         out_specs=pl.BlockSpec((tile, toks), lambda i: (i, 0)),
         out_shape=jax.ShapeDtypeStruct((units, toks), BF16),
         compiler_params=params(),
@@ -67,7 +82,7 @@
             flops=4 * toks * units, bytes_accessed=6 * toks * units, transcendentals=toks * units
         ),
         name="hidden",
-    )(gate, up, order)
+    )(gate, up)
 
 
 def arrange_body(n, at_ref, *refs):
@@ -92,7 +107,9 @@
     )(at, *blocks, order)
 
 
-def grads_body(offs_ref, own_ref, other_ref, w_ref, gate_ref, up_ref, gg_ref, gu_ref, piece):
+def grads_body(
+    offs_ref, own_ref, other_ref, w_ref, gate_ref, up_ref, order_ref, gg_ref, gu_ref, piece
+):
     n, toks, width = own_ref.shape
 
     @pl.when(pl.program_id(0) == 0)
@@ -110,7 +127,7 @@
     gu_ref[...] = (total * (gate * sig)).astype(BF16)
 
 
-def grads(offs, own, other, weight, gate, up):
+def grads(offs, own, other, weight, gate, up, order):
     n, toks, width = own.shape
     units, feats = weight.shape
     tile = 256
@@ -122,7 +139,7 @@
             num_scalar_prefetch=1,
             grid=(units // tile,),
             in_specs=[whole(own.shape)] * 2
-            + [pl.BlockSpec((tile, feats), lambda i, _: (i, 0)), cols, cols],
+            + [pl.BlockSpec((tile, feats), lambda i, _: (i, 0)), cols, cols, ANY],
             out_specs=[cols, cols],
             scratch_shapes=[pltpu.VMEM((toks, feats), BF16)],
         ),
@@ -134,7 +151,7 @@
             transcendentals=toks * units,
         ),
         name="grads",
-    )(offs, own, other, weight, gate, up)
+    )(offs, own, other, weight, gate, up, order)
 
 
 def wgrad_body(offs_ref, hid_ref, own_ref, other_ref, order_ref, out_ref, cols):
@@ -178,64 +195,117 @@
     )(offs, hid, own, other, order)
 
 
-def put_slices(part, out_ref):
-    inner, outer, size, _ = out_ref.shape
-    for p in range(inner * outer):
-        out_ref[p % inner, p // inner] = part[p * size : (p + 1) * size]
-
-
-def gram_shape(count, total, parts):
-    return jax.ShapeDtypeStruct((2, parts // 2, count // parts, total), F32)
-
-
-def grad_gram_body(offs_ref, *refs):
-    toks_refs, (val_ref, order_ref, out_ref, wide) = refs[:-4], refs[-4:]
+def put_slices(inner_ref, part, kept_ref, away_ref):
+    outer, size, _ = kept_ref.shape
+    for inner in range(2):
+
+        @pl.when(inner_ref[0] == inner)
+        def _():
+            for p in range(2 * outer):
+                out_ref = kept_ref if p % 2 == inner else away_ref
+                out_ref[p // 2] = part[p * size : (p + 1) * size]
+
+
+def grad_gram_body(inner_ref, offs_ref, *refs):
+    toks_refs, (val_ref, order_ref, kept_ref, away_ref, wide) = refs[:-5], refs[-5:]
     for k, ref in enumerate(toks_refs):
         toks = ref.shape[0]
         wide[:, pl.ds(pl.multiple_of(offs_ref[k], 128), toks)] = dot_nt(val_ref[...], ref[...])
-    put_slices(wide[...], out_ref)
-
-
-def hidden_gram_body(offs_ref, *refs):
-    hid, (val_ref, order_ref, out_ref, all_ref) = refs[:-4], refs[-4:]
+    put_slices(inner_ref, wide, kept_ref, away_ref)
+
+
+def hidden_gram_body(inner_ref, offs_ref, *refs):
+    hid, (val_ref, order_ref, kept_ref, away_ref, all_ref, wide) = refs[:-6], refs[-6:]
     for k, ref in enumerate(hid):
         toks = ref.shape[1]
         all_ref[:, pl.ds(pl.multiple_of(offs_ref[k], 128), toks)] = ref[...]
-    part = lax.dot_general(
+    wide[...] = lax.dot_general(
         val_ref[...], all_ref[...], (((1,), (0,)), ((), ())), preferred_element_type=F32
     )
-    put_slices(part, out_ref)
-
-
-def gram_call(body, offs, operands, order, shapes, scratch, flops, name):
+    put_slices(inner_ref, wide, kept_ref, away_ref)
+
+
+def gram_call(body, inner, offs, operands, order, parts, extra, name):
+    smem = pl.BlockSpec(memory_space=pltpu.SMEM)
     vmem = pl.BlockSpec(memory_space=pltpu.VMEM)
+    *toks, vals = operands
+    total = sum(x.size for x in toks) // vals.shape[1]
+    half = jax.ShapeDtypeStruct((parts // 2, vals.shape[0] // parts, total), F32)
+    shapes = [half, half, *extra]
     return pl.pallas_call(
         body,
-        in_specs=[pl.BlockSpec(memory_space=pltpu.SMEM)] + [vmem] * len(operands) + [ANY],
+        in_specs=[smem, smem] + [vmem] * len(operands) + [ANY],
         out_specs=[vmem] * len(shapes),
         out_shape=shapes,
-        scratch_shapes=scratch,
-        compiler_params=params(),
-        cost_estimate=pl.CostEstimate(
-            flops=flops,
+        scratch_shapes=[pltpu.VMEM((vals.shape[0], total), F32)],
+        compiler_params=params(),
+        cost_estimate=pl.CostEstimate(
+            flops=2 * vals.size * total,
             bytes_accessed=sum(x.size * x.dtype.itemsize for x in [*operands, *shapes]),
             transcendentals=0,
         ),
         name=name,
-    )(offs, *operands, order)
-
-
-def gram_sum(part):
+    )(inner, offs, *operands, order)
+
+
+def add_body(a_ref, b_ref, order_ref, out_ref):
+    out_ref[...] = a_ref[...] + b_ref[...]
+
+
+def add(a, b, order, name):
+    vmem = pl.BlockSpec(memory_space=pltpu.VMEM)
+    return pl.pallas_call(
+        add_body,
+        in_specs=[vmem, vmem, ANY],
+        out_specs=vmem,
+        out_shape=jax.ShapeDtypeStruct(a.shape, a.dtype),
+        compiler_params=params(),
+        cost_estimate=pl.CostEstimate(
+            flops=a.size, bytes_accessed=12 * a.size, transcendentals=0
+        ),
+        name=name,
+    )(a, b, order)
+
+
+def spread(pair):
     n_fs = lax.axis_size("fsdp")
-    inner = lax.axis_index("fsdp") % 2
-    away = lax.dynamic_index_in_dim(part, 1 - inner, axis=0, keepdims=False)
-    kept = lax.dynamic_index_in_dim(part, inner, axis=0, keepdims=False)
-    pair = kept + swap(away, "fsdp", 1)
     groups = [list(range(x, n_fs, 2)) for x in range(2)]
-    every = lax.all_to_all(
+    return lax.all_to_all(
         pair, "fsdp", split_axis=0, concat_axis=0, axis_index_groups=groups, tiled=True
     )
-    return jnp.sum(every, axis=0), pair
+
+
+def line_body(rows, assign_ref, hid_ref, grad_ref, out_ref):
+    n, _, total = hid_ref.shape
+    hid, grad = hid_ref[0], grad_ref[0]
+    for j in range(1, n):
+        hid += hid_ref[j]
+        grad += grad_ref[j]
+    by_tok = jnp.sum(hid * grad, axis=0, keepdims=True)
+    size = total // rows
+    lane = lax.broadcasted_iota(jnp.int32, (1, 128), 1)
+    line = jnp.zeros((1, 128), F32)
+    for r in range(rows):
+        row = jnp.sum(by_tok[:, r * size : (r + 1) * size], axis=1, keepdims=True)
+        line = jnp.where(lane == r, row, line)
+    for r in range(assign_ref.shape[0]):
+        line = jnp.where(lane == rows + r, assign_ref[r].astype(F32), line)
+    out_ref[...] = jnp.broadcast_to(line, out_ref.shape)
+
+
+def score_line(assign, hid, grad, rows, copies):
+    vmem = pl.BlockSpec(memory_space=pltpu.VMEM)
+    return pl.pallas_call(
+        functools.partial(line_body, rows),
+        in_specs=[pl.BlockSpec(memory_space=pltpu.SMEM), vmem, vmem],
+        out_specs=vmem,
+        out_shape=jax.ShapeDtypeStruct((copies, 128), F32),
+        compiler_params=params(),
+        cost_estimate=pl.CostEstimate(
+            flops=4 * hid.size, bytes_accessed=8 * hid.size, transcendentals=0
+        ),
+        name="score_line",
+    )(assign, hid, grad)
 
 
 def per_device(gate_act, up_act, out_grad, down_weight, val_hidden, val_grad, assign):
@@ -250,53 +320,55 @@
     n_out = n_fs // 2
     outer, inner = f // 2, f % 2
 
-    def over_dp(x):
-        far = swap(x, "dp", 2)
-        near = swap(jnp.stack([x, far]), "dp", 1)
-        return [x, near[0], far, near[1]]
-
-    ring = [out_grad]
-    for _ in range(n_out - 1):
-        ring.append(shift(ring[-1], "fsdp", 2))
-    others = [swap(own, "fsdp", 1) for own in ring]
-
+    first = shift(out_grad, "fsdp", 2)
+    others = [swap(out_grad, "fsdp", 1)]
     far = swap(out_grad, "dp", 2)
-    grad_dp = [out_grad, swap(out_grad, "dp", 1), far, swap(far, "dp", 1)]
-    hid_dp = over_dp(hidden_units(gate_act, up_act, grad_dp[1]))
+    near = swap(out_grad, "dp", 1)
+    first = after(first, others[0], far, near)
+    hidden = after(hidden_units(gate_act, up_act), first)
+    grad_dp = [out_grad, near, far, swap(far, "dp", 1)]
+    far = swap(hidden, "dp", 2)
+    ring = [out_grad, first]
+    for _ in range(n_out - 2):
+        others.append(swap(ring[-1], "fsdp", 1))
+        ring.append(after(shift(ring[-1], "fsdp", 2), others[-1]))
+    others.append(swap(ring[-1], "fsdp", 1))
 
     at = (outer - jnp.arange(n_out, dtype=jnp.int32)) % n_out
-    own = arrange(at, ring, others[0], "own_features")
+    own = arrange(at, ring, others[1], "own_features")
     own_cols = lax.all_to_all(own, "dp", split_axis=0, concat_axis=0, tiled=True)
-    other = arrange(at, others, own, "other_features")
+
+    tok_offs = (d ^ jnp.arange(n_dp, dtype=jnp.int32)) * toks
+    inner_at = inner.reshape(1).astype(jnp.int32)
+    grad_kept, away = gram_call(
+        grad_gram_body, inner_at, tok_offs, [*grad_dp, val_grad], own, n_fs, [], "grad_gram"
+    )
+    grad_came = swap(away, "fsdp", 1)
+
+    far = after(far, away, others[2])
+    hid_dp = [hidden, swap(hidden, "dp", 1), far, swap(far, "dp", 1)]
+
+    other = arrange(at, others, far, "other_features")
     other_cols = lax.all_to_all(other, "dp", split_axis=0, concat_axis=0, tiled=True)
 
-    tok_offs = (d ^ jnp.arange(n_dp, dtype=jnp.int32)) * toks
-    vals = val_grad.shape[0]
-    shape = gram_shape(vals, total, n_fs)
-    (part,) = gram_call(
-        grad_gram_body, tok_offs, [*grad_dp, val_grad], own, [shape],
-        [pltpu.VMEM((vals, total), F32)], 2 * vals * total * width, "grad_gram",
-    )
-    grad_gram, _ = gram_sum(part)
-    part, hid_all = gram_call(
-        hidden_gram_body, tok_offs, [*hid_dp, val_hidden], other,
-        [shape, jax.ShapeDtypeStruct((units, total), BF16)], [],
-        2 * vals * total * units, "hidden_gram",
-    )
-    hidden_gram, order = gram_sum(part)
-    by_row = jnp.sum(hidden_gram * grad_gram, axis=0)
-    by_row = jnp.sum(by_row.reshape(n_dp * rows_here, toks // rows_here), axis=1)
+    hid_kept, away, hid_all = gram_call(
+        hidden_gram_body, inner_at, tok_offs, [*hid_dp, val_hidden], other, n_fs,
+        [jax.ShapeDtypeStruct((units, total), BF16)], "hidden_gram",
+    )
+    hid_came = swap(away, "fsdp", 1)
+    grad_sums = spread(add(grad_kept, grad_came, away, "grad_pair"))
+    pair = add(hid_kept, hid_came, grad_came, "hidden_pair")
+    hid_sums = spread(pair)
 
     offs = (jnp.stack([inner, 1 - inner]) * width).astype(jnp.int32)
-    grad_gate, grad_up = grads(offs, own, other, down_weight, gate_act, up_act)
-    weight_grad = wgrad(offs, hid_all, own_cols, other_cols, order)
-
-    mine = jnp.concatenate([by_row, assign.astype(F32)])
-    mine = jnp.pad(mine, (0, 128 - mine.shape[0]))
+    grad_gate, grad_up = grads(offs, own, other, down_weight, gate_act, up_act, pair)
+
+    mine = score_line(assign, hid_sums, grad_sums, n_dp * rows_here, n_dp * n_fs)
     every = lax.all_to_all(
-        jnp.broadcast_to(mine[None], (n_dp * n_fs, 128)),
-        ("dp", "fsdp"), split_axis=0, concat_axis=0, tiled=True,
+        mine, ("dp", "fsdp"), split_axis=0, concat_axis=0, tiled=True
     ).reshape(n_dp, n_fs, 128)
+    weight_grad = wgrad(offs, hid_all, own_cols, other_cols, mine)
+
     rows = n_dp * rows_here
     scale = 1.0 / jnp.sqrt(F32(L) * VAL * FFW * D)
     scores = jnp.sum(every[:, :, :rows], axis=1) * scale

time: 219 us -> 199 us (0.909)
  waiting for transfers between devices: 101 us -> 78.7 us
  other arithmetic: 7.84 us -> 0.75 us
  Pallas kernels: 41 us -> 45.7 us
  local copies, waits for them, and re-layouts: 14.4 us -> 17.8 us
    ppermute x3, waiting for transfers between devices: 37.9 us -> 27.3 us  [shift(): return lax.ppermute(x, axis, [(s, (s + k) % n) for s in range(n)])]
    unnamed x27 -> x57, local copies, waits for them, and re-layouts: 9.07 us -> 17.5 us
    all_to_all x2, waiting for transfers between devices: 7.71 us -> 0.01 us  [the longest x1 0.01 us: spread(): lax.all_to_all(pair, 'fsdp', split_axis=0, concat_axis=0, axis_index_grou...]
    ppermute x11 -> x12, waiting for transfers between devices: 52.6 us -> 46.5 us  [swap(): return lax.ppermute(x, axis, [(s, s ^ k) for s in range(n)])]
    squeeze x3 -> x0, local copies, waits for them, and re-layouts: 4.43 us -> none  [the longest x1 3.19 us: over_dp(): return [x, near[0], far, near[1]]]
    pallas_call x3 -> x11, Pallas kernels: 8.38 us -> 12.7 us  [the longest x2 8.97 us: gram_call(): pl.pallas_call(body, in_specs=[smem, smem] + [vmem] * len(operands) + [AN...]
    reduce_sum x4 -> x0, other arithmetic: 2.98 us -> none  [the longest x2 1.91 us: gram_sum(): return (jnp.sum(every, axis=0), pair)]
    ppermute x3, starting transfers between devices: 1.8 us -> 4.66 us  [shift(): return lax.ppermute(x, axis, [(s, (s + k) % n) for s in range(n)])]
  transfers between devices with their start and end apart: 18 -> 19, of which waited for: 10 -> 7; matrix products, arithmetic and copies ran while one was open for 4% -> 0% of each run, Pallas kernels for 18% -> 23%
where the time goes in v4:
time: 199 us; the launch traced here: 198 us
  waiting for transfers between devices  78.7 us (40%)
  Pallas kernels  45.7 us (23%)
  starting transfers between devices  31.2 us (16%)
  blocking collectives  23.2 us (12%)
  local copies, waits for them, and re-layouts  17.8 us (9%)
    ppermute x12, waiting for transfers between devices, swap(): return lax.ppermute(x, axis, [(s, s ^ k) for s in range(n)])  46.5 us
    ppermute x3, waiting for transfers between devices, shift(): return lax.ppermute(x, axis, [(s, (s + k) % n) for s in range(n)])  27.3 us
    all_to_all x1, blocking collectives, spread(): lax.all_to_all(pair, 'fsdp', split_axis=0, concat_axis=0, axis_index_grou...  23.2 us
    unnamed x57, local copies, waits for them, and re-layouts  17.5 us
    pallas_call x1, Pallas kernels, grads(): pl.pallas_call(grads_body, grid_spec=pltpu.PrefetchScalarGridSpec(num_sca...  15.4 us
    pallas_call x1, Pallas kernels, wgrad(): pl.pallas_call(wgrad_body, grid_spec=pltpu.PrefetchScalarGridSpec(num_sca...  12.3 us
    ppermute x12, starting transfers between devices, swap(): return lax.ppermute(x, axis, [(s, s ^ k) for s in range(n)])  11 us
    pallas_call x2, Pallas kernels, gram_call(): pl.pallas_call(body, in_specs=[smem, smem] + [vmem] * len(operands) + [AN...  8.97 us
  transfers between devices with their start and end apart: 19, of which 7 were waited for; matrix products, arithmetic and copies ran while one was open for 0% of the time, Pallas kernels for 23%

profile of v4, /device:TPU:0, one launch (start us, length us, event | category | flops | bytes accessed | tf_op | source)
XLA Modules:
  0.0 198.1 jit_solution(10202426790248200827)
XLA Ops:
  0.6 3.1 %collective-permute-start = (bf16[384,640]{1,0:T(8,128)(2,1)}, bf16[384,640]{1,0:T(8,128)(2,1)S(1)}, u32[]{:S(2)}, u32[]{:S(2)}) collective-permute-start(bf16[384,640]{1,0:T(8,128)(2,1)} %refs_0_.3), channel_id=1, source_target_pairs={{0,2},{1,3},{2,4},{3,5},{4,6},{5,7},{6,0},{7,1},{8,10},{9,11},{10,... | collective-permute-start | bytes 1474568 | tf_op jit(solution)/shard_map/ppermute | solution.py:35
  3.7 1.5 collective-permute-start.1
  5.2 1.5 collective-permute-start.2
  11.8 5.4 %collective-permute-done.refs_0_ = bf16[384,640]{1,0:T(8,128)(2,1)S(1)} collective-permute-done((bf16[384,640]{1,0:T(8,128)(2,1)}, bf16[384,640]{1,0:T(8,128)(2,1)S(1)}, u32[]{:S(2)}, u32[]{:S(2)}) %collective-permute-start) | collective-permute-done | bytes 491552 | tf_op jit(solution)/shard_map/ppermute | solution.py:35
  19.5 1.5 collective-permute-start.9
  21.0 1.6 collective-permute-start.4
  23.1 11.3 %collective-permute-done.4.refs_0_ = bf16[384,640]{1,0:T(8,128)(2,1)S(1)} collective-permute-done((bf16[384,640]{1,0:T(8,128)(2,1)S(1)}, bf16[384,640]{1,0:T(8,128)(2,1)S(1)}, u32[]{:S(2)}, u32[]{:S(2)}) %collective-permute-start.4) | collective-permute-done | bytes 491552 | tf_op jit(solution)/shard_map/ppermute | solution.py:35
  37.2 10.7 %collective-permute-done.6.refs_0_ = bf16[384,640]{1,0:T(8,128)(2,1)} collective-permute-done((bf16[384,640]{1,0:T(8,128)(2,1)}, bf16[384,640]{1,0:T(8,128)(2,1)}, u32[]{:S(2)}, u32[]{:S(2)}) %collective-permute-start.6) | collective-permute-done | bytes 491552 | tf_op jit(solution)/shard_map/ppermute | solution.py:35
  50.0 2.6 %own_features.1.refs_5_.own_ref = bf16[4,384,640]{2,1,0:T(8,128)(2,1)} custom-call(s32[4]{0:T(128)S(1)} %and_select_fusion.at_ref, bf16[384,640]{1,0:T(8,128)(2,1)S(1)} %copy-done.10, bf16[384,640]{1,0:T(8,128)(2,1)S(1)} %copy-done.5, bf16[384,640]{1,0:T(8,128)(2,1)S(1)} %copy-done.13, bf16[384,640]{1,0:T(8,128)(2,1)} %after.7.refs_3_, ...), custom_call_target="tpu_custom_call" | custom-call | bytes 3932160 | tf_op jit(solution)/shard_map/own_features/pallas_call | solution.py:97
  52.6 2.1 %grad_gram.1 = (f32[4,32,1536]{2,1,0:T(8,128)S(1)}, f32[4,32,1536]{2,1,0:T(8,128)S(1)}) custom-call(s32[1]{0:T(128)} %bitcast.inner_ref, s32[4]{0:T(128)S(1)} %xor_multiply_fusion.offs_ref, bf16[384,640]{1,0:T(8,128)(2,1)S(1)} %copy-done.11, bf16[384,640]{1,0:T(8,128)(2,1)S(1)} %copy-done.9, bf16[384,640]{1,0:T(8,128)(2,1)S(1)} %copy-done.7, ...), custom_call_target="tpu_custom_call" | custom-call | flops 503316480 | bytes 3866624 | tf_op jit(solution)/shard_map/grad_gram/pallas_call | solution.py:235
  57.7 4.6 %all-to-all-start = ((bf16[4,384,640]{2,1,0:T(8,128)(2,1)}), bf16[4,384,640]{2,1,0:T(8,128)(2,1)}, u32[]{:S(2)}, u32[]{:S(2)}) async-start(bf16[4,384,640]{2,1,0:T(8,128)(2,1)} %own_features.1.refs_5_.own_ref), calls=%async_computation | async-start | bytes 3932160 | tf_op jit(solution)/shard_map/all_to_all | solution.py:339
  62.3 1.9 collective-permute-start.14
  64.4 28.5 %collective-permute-done.8.refs_3_ = bf16[384,640]{1,0:T(8,128)(2,1)S(1)} collective-permute-done((bf16[384,640]{1,0:T(8,128)(2,1)}, bf16[384,640]{1,0:T(8,128)(2,1)S(1)}, u32[]{:S(2)}, u32[]{:S(2)}) %collective-permute-start.8) | collective-permute-done | bytes 491552 | tf_op jit(solution)/shard_map/ppermute | solution.py:30
  94.0 2.8 %other_features.1.refs_5_.other_ref = bf16[4,384,640]{2,1,0:T(8,128)(2,1)} custom-call(s32[4]{0:T(128)S(1)} %and_select_fusion.at_ref, bf16[384,640]{1,0:T(8,128)(2,1)S(1)} %copy-done.15, bf16[384,640]{1,0:T(8,128)(2,1)} %collective-permute-done.5.refs_1_.refs_4_, bf16[384,640]{1,0:T(8,128)(2,1)} %collective-permute-done.7.refs_1_.refs_2_, ...), custom_call_target="tpu_custom_call" | custom-call | bytes 3932160 | tf_op jit(solution)/shard_map/other_features/pallas_call | solution.py:97
  96.8 6.8 %hidden_gram.1 = (f32[4,32,1536]{2,1,0:T(8,128)S(1)}, f32[4,32,1536]{2,1,0:T(8,128)S(1)}, bf16[1792,1536]{1,0:T(8,128)(2,1)}) custom-call(s32[1]{0:T(128)} %bitcast.inner_ref, s32[4]{0:T(128)S(1)} %xor_multiply_fusion.offs_ref, bf16[1792,384]{1,0:T(8,128)(2,1)S(1)} %copy-done.3, bf16[1792,384]{1,0:T(8,128)(2,1)} %collective-permute-done.11.refs_1_, ...), custom_call_target="tpu_custom_call" | custom-call | flops 1409286144 | bytes 13500416 | tf_op jit(solution)/shard_map/hidden_gram/pallas_call | solution.py:235
  105.5 3.5 %all-to-all-start.3 = ((f32[4,32,1536]{2,1,0:T(8,128)}), f32[4,32,1536]{2,1,0:T(8,128)S(1)}, u32[]{:S(2)}, u32[]{:S(2)}) async-start(f32[4,32,1536]{2,1,0:T(8,128)} %grad_pair.1), calls=%async_computation.3 | async-start | bytes 1572864 | tf_op jit(solution)/shard_map/all_to_all | solution.py:273
  109.0 1.8 collective-permute-start.13
  110.8 17.3 %collective-permute-done.13.b_ref = f32[4,32,1536]{2,1,0:T(8,128)S(1)} collective-permute-done((f32[4,32,1536]{2,1,0:T(8,128)S(1)}, f32[4,32,1536]{2,1,0:T(8,128)S(1)}, u32[]{:S(2)}, u32[]{:S(2)}) %collective-permute-start.13) | collective-permute-done | bytes 786464 | tf_op jit(solution)/shard_map/ppermute | solution.py:30
  129.3 23.2 %all_to_all.29.hid_ref = f32[4,32,1536]{2,1,0:T(8,128)S(1)} all-to-all(f32[4,32,1536]{2,1,0:T(8,128)S(1)} %hidden_pair.1.order_ref), channel_id=1, replica_groups={{0,2,4,6},{1,3,5,7},{8,10,12,14},{9,11,13,15},{16,18,20,22},{17,19,21,2..., dimensions={0} | all-to-all | bytes 1572864 | tf_op jit(solution)/shard_map/all_to_all | solution.py:273
  152.4 4.4 %all-to-all-start.1 = ((bf16[4,384,640]{2,1,0:T(8,128)(2,1)}), bf16[4,384,640]{2,1,0:T(8,128)(2,1)}, u32[]{:S(2)}, u32[]{:S(2)}) async-start(bf16[4,384,640]{2,1,0:T(8,128)(2,1)} %other_features.1.refs_5_.other_ref), calls=%async_computation.1 | async-start | bytes 3932160 | tf_op jit(solution)/shard_map/all_to_all | solution.py:352
  159.7 15.4 %grads.1 = (bf16[384,1792]{1,0:T(8,128)(2,1)}, bf16[384,1792]{1,0:T(8,128)(2,1)}) custom-call(s32[2]{0:T(128)S(1)} %add_multiply_fusion.offs_ref, bf16[4,384,640]{2,1,0:T(8,128)(2,1)} %own_features.1.refs_5_.own_ref, bf16[4,384,640]{2,1,0:T(8,128)(2,1)} %other_features.1.refs_5_.other_ref, bf16[1792,5120]{1,0:T(8,128)(2,1)} %w_ref.1, ...), custom_call_target="tpu_custom_call" | custom-call | flops 7046430720 | bytes 27787264 | tf_op jit(solution)/shard_map/grads/pallas_call | solution.py:136
  176.4 4.9 %all-to-all-done.1.other_ref = bf16[4,384,640]{2,1,0:T(8,128)(2,1)} async-done(((bf16[4,384,640]{2,1,0:T(8,128)(2,1)}), bf16[4,384,640]{2,1,0:T(8,128)(2,1)}, u32[]{:S(2)}, u32[]{:S(2)}) %all-to-all-start.1) | async-done | bytes 1966112 | tf_op jit(solution)/shard_map/all_to_all | solution.py:352
  181.2 3.0 %all-to-all-start.4 = ((f32[32,1,128]{2,1,0:T(1,128)}), f32[32,1,128]{2,1,0:T(1,128)S(1)}, u32[]{:S(2)}, u32[]{:S(2)}) async-start(f32[32,1,128]{2,1,0:T(1,128)} %bitcast.3), calls=%async_computation.4 | async-start | bytes 32768 | tf_op jit(solution)/shard_map/all_to_all | solution.py:367
  184.2 12.3 %wgrad.1 = bf16[1792,1280]{1,0:T(8,128)(2,1)} custom-call(s32[2]{0:T(128)S(1)} %add_multiply_fusion.offs_ref, bf16[1792,1536]{1,0:T(8,128)(2,1)} %get-tuple-element.17.hid_ref, bf16[4,384,640]{2,1,0:T(8,128)(2,1)} %all-to-all-done.own_ref, bf16[4,384,640]{2,1,0:T(8,128)(2,1)} %all-to-all-done.1.other_ref, f32[32,128]{1,0:T(8,128)} %score_line.1.order_ref), custom_call_target="tpu_custom_call" | custom-call | flops 7046430720 | bytes 14024704 | tf_op jit(solution)/shard_map/wgrad/pallas_call | solution.py:176
  (95 shorter events, 25.7 us)
Async XLA Ops:
  0.6 16.5 %collective-permute-start = (bf16[384,640]{1,0:T(8,128)(2,1)}, bf16[384,640]{1,0:T(8,128)(2,1)S(1)}, u32[]{:S(2)}, u32[]{:S(2)}) collective-permute-start(bf16[384,640]{1,0:T(8,128)(2,1)} %refs_0_.3), channel_id=1, source_target_pairs={{0,2},{1,3},{2,4},{3,5},{4,6},{5,7},{6,0},{7,1},{8,10},{9,11},{10,... | collective-permute-start | bytes 1474568 | tf_op jit(solution)/shard_map/ppermute | solution.py:35
  3.7 13.5 %collective-permute-start.1 = (bf16[384,640]{1,0:T(8,128)(2,1)}, bf16[384,640]{1,0:T(8,128)(2,1)S(1)}, u32[]{:S(2)}, u32[]{:S(2)}) collective-permute-start(bf16[384,640]{1,0:T(8,128)(2,1)} %refs_0_.3), channel_id=1, source_target_pairs={{0,1},{1,0},{2,3},{3,2},{4,5},{5,4},{6,7},{7,6},{8,9},{9,8},{10,11... | collective-permute-start | bytes 1474568 | tf_op jit(solution)/shard_map/ppermute | solution.py:30
  5.2 12.6 %collective-permute-start.2 = (bf16[384,640]{1,0:T(8,128)(2,1)}, bf16[384,640]{1,0:T(8,128)(2,1)S(1)}, u32[]{:S(2)}, u32[]{:S(2)}) collective-permute-start(bf16[384,640]{1,0:T(8,128)(2,1)} %refs_0_.3), channel_id=1, source_target_pairs={{0,16},{8,24},{16,0},{24,8},{1,17},{9,25},{17,1},{25,9},{2,18},{10... | collective-permute-start | bytes 1474568 | tf_op jit(solution)/shard_map/ppermute | solution.py:30
  6.7 11.1 %collective-permute-start.3 = (bf16[384,640]{1,0:T(8,128)(2,1)}, bf16[384,640]{1,0:T(8,128)(2,1)S(1)}, u32[]{:S(2)}, u32[]{:S(2)}) collective-permute-start(bf16[384,640]{1,0:T(8,128)(2,1)} %refs_0_.3), channel_id=1, source_target_pairs={{0,8},{8,0},{16,24},{24,16},{1,9},{9,1},{17,25},{25,17},{2,10},{10... | collective-permute-start | bytes 1474568 | tf_op jit(solution)/shard_map/ppermute | solution.py:30
  19.5 17.2 %copy-start.3 = (bf16[1792,384]{1,0:T(8,128)(2,1)S(1)}, bf16[1792,384]{1,0:T(8,128)(2,1)}, u32[]{:S(2)}) copy-start(bf16[1792,384]{1,0:T(8,128)(2,1)} %after.8.refs_0_) | copy-start | bytes 4128772
  19.5 37.1 %collective-permute-start.9 = (bf16[1792,384]{1,0:T(8,128)(2,1)}, bf16[1792,384]{1,0:T(8,128)(2,1)S(1)}, u32[]{:S(2)}, u32[]{:S(2)}) collective-permute-start(bf16[1792,384]{1,0:T(8,128)(2,1)} %after.8.refs_0_), channel_id=1, source_target_pairs={{0,16},{8,24},{16,0},{24,8},{1,17},{9,25},{17,1},{25,9},{2,18},{10... | collective-permute-start | bytes 4128776 | tf_op jit(solution)/shard_map/ppermute | solution.py:30
  21.0 13.4 %collective-permute-start.4 = (bf16[384,640]{1,0:T(8,128)(2,1)S(1)}, bf16[384,640]{1,0:T(8,128)(2,1)S(1)}, u32[]{:S(2)}, u32[]{:S(2)}) collective-permute-start(bf16[384,640]{1,0:T(8,128)(2,1)S(1)} %copy-done.5), channel_id=1, source_target_pairs={{0,2},{1,3},{2,4},{3,5},{4,6},{5,7},{6,0},{7,1},{8,10},{9,11},{10,... | collective-permute-start | bytes 1474568 | tf_op jit(solution)/shard_map/ppermute | solution.py:35
  22.6 12.6 %collective-permute-start.5 = (bf16[384,640]{1,0:T(8,128)(2,1)S(1)}, bf16[384,640]{1,0:T(8,128)(2,1)}, u32[]{:S(2)}, u32[]{:S(2)}) collective-permute-start(bf16[384,640]{1,0:T(8,128)(2,1)S(1)} %copy-done.5), channel_id=1, source_target_pairs={{0,1},{1,0},{2,3},{3,2},{4,5},{5,4},{6,7},{7,6},{8,9},{9,8},{10,11... | collective-permute-start | bytes 1474568 | tf_op jit(solution)/shard_map/ppermute | solution.py:30
  35.1 12.8 %collective-permute-start.6 = (bf16[384,640]{1,0:T(8,128)(2,1)}, bf16[384,640]{1,0:T(8,128)(2,1)}, u32[]{:S(2)}, u32[]{:S(2)}) collective-permute-start(bf16[384,640]{1,0:T(8,128)(2,1)} %after.6.refs_2_), channel_id=1, source_target_pairs={{0,2},{1,3},{2,4},{3,5},{4,6},{5,7},{6,0},{7,1},{8,10},{9,11},{10,... | collective-permute-start | bytes 1474568 | tf_op jit(solution)/shard_map/ppermute | solution.py:35
  35.2 12.8 %collective-permute-start.7 = (bf16[384,640]{1,0:T(8,128)(2,1)}, bf16[384,640]{1,0:T(8,128)(2,1)}, u32[]{:S(2)}, u32[]{:S(2)}) collective-permute-start(bf16[384,640]{1,0:T(8,128)(2,1)} %after.6.refs_2_), channel_id=1, source_target_pairs={{0,1},{1,0},{2,3},{3,2},{4,5},{5,4},{6,7},{7,6},{8,9},{9,8},{10,11... | collective-permute-start | bytes 1474568 | tf_op jit(solution)/shard_map/ppermute | solution.py:30
  36.6 16.0 %collective-permute-start.10 = (bf16[384,640]{1,0:T(8,128)(2,1)}, bf16[384,640]{1,0:T(8,128)(2,1)}, u32[]{:S(2)}, u32[]{:S(2)}) collective-permute-start(bf16[384,640]{1,0:T(8,128)(2,1)} %copy-done.6), channel_id=1, source_target_pairs={{0,8},{8,0},{16,24},{24,16},{1,9},{9,1},{17,25},{25,17},{2,10},{10... | collective-permute-start | bytes 1474568 | tf_op jit(solution)/shard_map/ppermute | solution.py:30
  36.7 60.1 %collective-permute-start.11 = (bf16[1792,384]{1,0:T(8,128)(2,1)S(1)}, bf16[1792,384]{1,0:T(8,128)(2,1)}, u32[]{:S(2)}, u32[]{:S(2)}) collective-permute-start(bf16[1792,384]{1,0:T(8,128)(2,1)S(1)} %copy-done.3), channel_id=1, source_target_pairs={{0,8},{8,0},{16,24},{24,16},{1,9},{9,1},{17,25},{25,17},{2,10},{10... | collective-permute-start | bytes 4128776 | tf_op jit(solution)/shard_map/ppermute | solution.py:30
  57.7 35.2 %copy-start.1 = (bf16[1792,384]{1,0:T(8,128)(2,1)S(1)}, bf16[1792,384]{1,0:T(8,128)(2,1)}, u32[]{:S(2)}) copy-start(bf16[1792,384]{1,0:T(8,128)(2,1)} %after.9.refs_4_.refs_2_) | copy-start | bytes 4128772
  57.7 39.1 %collective-permute-start.12 = (bf16[1792,384]{1,0:T(8,128)(2,1)}, bf16[1792,384]{1,0:T(8,128)(2,1)}, u32[]{:S(2)}, u32[]{:S(2)}) collective-permute-start(bf16[1792,384]{1,0:T(8,128)(2,1)} %after.9.refs_4_.refs_2_), channel_id=1, source_target_pairs={{0,8},{8,0},{16,24},{24,16},{1,9},{9,1},{17,25},{25,17},{2,10},{10... | collective-permute-start | bytes 4128776 | tf_op jit(solution)/shard_map/ppermute | solution.py:30
  57.7 47.8 %all-to-all-start = ((bf16[4,384,640]{2,1,0:T(8,128)(2,1)}), bf16[4,384,640]{2,1,0:T(8,128)(2,1)}, u32[]{:S(2)}, u32[]{:S(2)}) async-start(bf16[4,384,640]{2,1,0:T(8,128)(2,1)} %own_features.1.refs_5_.own_ref), calls=%async_computation | async-start | bytes 3932160 | tf_op jit(solution)/shard_map/all_to_all | solution.py:339
  62.3 42.2 %collective-permute-start.14 = (f32[4,32,1536]{2,1,0:T(8,128)}, f32[4,32,1536]{2,1,0:T(8,128)S(1)}, u32[]{:S(2)}, u32[]{:S(2)}) collective-permute-start(f32[4,32,1536]{2,1,0:T(8,128)} %copy-done.25), channel_id=1, source_target_pairs={{0,1},{1,0},{2,3},{3,2},{4,5},{5,4},{6,7},{7,6},{8,9},{9,8},{10,11... | collective-permute-start | bytes 2359304 | tf_op jit(solution)/shard_map/ppermute | solution.py:30
  64.1 28.8 %collective-permute-start.8 = (bf16[384,640]{1,0:T(8,128)(2,1)}, bf16[384,640]{1,0:T(8,128)(2,1)S(1)}, u32[]{:S(2)}, u32[]{:S(2)}) collective-permute-start(bf16[384,640]{1,0:T(8,128)(2,1)} %after.7.refs_3_), channel_id=1, source_target_pairs={{0,1},{1,0},{2,3},{3,2},{4,5},{5,4},{6,7},{7,6},{8,9},{9,8},{10,11... | collective-permute-start | bytes 1474568 | tf_op jit(solution)/shard_map/ppermute | solution.py:30
  94.0 2.8 %copy-start.20 = (bf16[256,1792]{1,0:T(8,128)(2,1)S(1)}, bf16[256,1792]{1,0:T(8,128)(2,1)}, u32[]{:S(2)}) copy-start(bf16[256,1792]{1,0:T(8,128)(2,1)} %refs_4_.3) | copy-start | bytes 2752516
  96.7 7.7 %copy-start.22 = (f32[4,32,1536]{2,1,0:T(8,128)S(1)}, f32[4,32,1536]{2,1,0:T(8,128)}, u32[]{:S(2)}) copy-start(f32[4,32,1536]{2,1,0:T(8,128)} %copy-done.21) | copy-start | bytes 2359300
  105.5 23.8 %all-to-all-start.3 = ((f32[4,32,1536]{2,1,0:T(8,128)}), f32[4,32,1536]{2,1,0:T(8,128)S(1)}, u32[]{:S(2)}, u32[]{:S(2)}) async-start(f32[4,32,1536]{2,1,0:T(8,128)} %grad_pair.1), calls=%async_computation.3 | async-start | bytes 1572864 | tf_op jit(solution)/shard_map/all_to_all | solution.py:273
  109.0 19.1 %collective-permute-start.13 = (f32[4,32,1536]{2,1,0:T(8,128)S(1)}, f32[4,32,1536]{2,1,0:T(8,128)S(1)}, u32[]{:S(2)}, u32[]{:S(2)}) collective-permute-start(f32[4,32,1536]{2,1,0:T(8,128)S(1)} %get-tuple-element.14.order_ref), channel_id=1, source_target_pairs={{0,1},{1,0},{2,3},{3,2},{4,5},{5,4},{6,7},{7,6},{8,9},{9,8},{10,11... | collective-permute-start | bytes 2359304 | tf_op jit(solution)/shard_map/ppermute | solution.py:30
  152.4 28.8 %all-to-all-start.1 = ((bf16[4,384,640]{2,1,0:T(8,128)(2,1)}), bf16[4,384,640]{2,1,0:T(8,128)(2,1)}, u32[]{:S(2)}, u32[]{:S(2)}) async-start(bf16[4,384,640]{2,1,0:T(8,128)(2,1)} %other_features.1.refs_5_.other_ref), calls=%async_computation.1 | async-start | bytes 3932160 | tf_op jit(solution)/shard_map/all_to_all | solution.py:352
  159.6 15.4 %copy-start.27 = (s32[3]{0:T(128)S(1)}, s32[3]{0:T(128)}, u32[]{:S(2)}) copy-start(s32[3]{0:T(128)} %assign_ref.1) | copy-start | bytes 40
  181.2 15.3 %all-to-all-start.4 = ((f32[32,1,128]{2,1,0:T(1,128)}), f32[32,1,128]{2,1,0:T(1,128)S(1)}, u32[]{:S(2)}, u32[]{:S(2)}) async-start(f32[32,1,128]{2,1,0:T(1,128)} %bitcast.3), calls=%async_computation.4 | async-start | bytes 32768 | tf_op jit(solution)/shard_map/all_to_all | solution.py:367
  (23 other events, 30.6 us)

commit v5 on v4

--- a/solution.py
+++ b/solution.py
@@ -40,6 +40,7 @@
 
 
 ANY = pl.BlockSpec(memory_space=pl.ANY)
+SMALL = pl.CostEstimate(flops=1024, bytes_accessed=1024, transcendentals=0)
 
 
 def params():
@@ -57,6 +58,7 @@
         out_specs=ANY,
         out_shape=jax.ShapeDtypeStruct(x.shape, x.dtype),
         input_output_aliases={0: 0},
+        cost_estimate=SMALL,
         name="after",
     )(x, *order)
 
@@ -78,9 +80,7 @@
         out_specs=pl.BlockSpec((tile, toks), lambda i: (i, 0)),
         out_shape=jax.ShapeDtypeStruct((units, toks), BF16),
         compiler_params=params(),
-        cost_estimate=pl.CostEstimate(
-            flops=4 * toks * units, bytes_accessed=6 * toks * units, transcendentals=toks * units
-        ),
+        cost_estimate=SMALL,
         name="hidden",
     )(gate, up)
 
@@ -100,9 +100,7 @@
         out_specs=vmem,
         out_shape=jax.ShapeDtypeStruct((n,) + blocks[0].shape, BF16),
         compiler_params=params(),
-        cost_estimate=pl.CostEstimate(
-            flops=0, bytes_accessed=4 * n * blocks[0].size, transcendentals=0
-        ),
+        cost_estimate=SMALL,
         name=name,
     )(at, *blocks, order)
 
@@ -145,11 +143,7 @@
         ),
         out_shape=(out, out),
         compiler_params=params(),
-        cost_estimate=pl.CostEstimate(
-            flops=2 * toks * units * feats,
-            bytes_accessed=2 * (units * feats + toks * feats + 4 * toks * units),
-            transcendentals=toks * units,
-        ),
+        cost_estimate=SMALL,
         name="grads",
     )(offs, own, other, weight, gate, up, order)
 
@@ -186,11 +180,7 @@
         ),
         out_shape=jax.ShapeDtypeStruct((units, 2 * width), BF16),
         compiler_params=params(),
-        cost_estimate=pl.CostEstimate(
-            flops=4 * total * units * width,
-            bytes_accessed=2 * (total * (units + 2 * width) + 2 * units * width),
-            transcendentals=0,
-        ),
+        cost_estimate=SMALL,
         name="wgrad",
     )(offs, hid, own, other, order)
 
@@ -239,11 +229,7 @@
         out_shape=shapes,
         scratch_shapes=[pltpu.VMEM((vals.shape[0], total), F32)],
         compiler_params=params(),
-        cost_estimate=pl.CostEstimate(
-            flops=2 * vals.size * total,
-            bytes_accessed=sum(x.size * x.dtype.itemsize for x in [*operands, *shapes]),
-            transcendentals=0,
-        ),
+        cost_estimate=SMALL,
         name=name,
     )(inner, offs, *operands, order)
 
@@ -260,9 +246,7 @@
         out_specs=vmem,
         out_shape=jax.ShapeDtypeStruct(a.shape, a.dtype),
         compiler_params=params(),
-        cost_estimate=pl.CostEstimate(
-            flops=a.size, bytes_accessed=12 * a.size, transcendentals=0
-        ),
+        cost_estimate=SMALL,
         name=name,
     )(a, b, order)
 
@@ -301,9 +285,7 @@
         out_specs=vmem,
         out_shape=jax.ShapeDtypeStruct((copies, 128), F32),
         compiler_params=params(),
-        cost_estimate=pl.CostEstimate(
-            flops=4 * hid.size, bytes_accessed=8 * hid.size, transcendentals=0
-        ),
+        cost_estimate=SMALL,
         name="score_line",
     )(assign, hid, grad)
 

time: 199 us -> 222 us (1.12)
  waiting for transfers between devices: 78.7 us -> 98 us
  local copies, waits for them, and re-layouts: 17.8 us -> 24.2 us
    all_to_all x1, waiting for transfers between devices: 4.88 us -> 21.8 us  [per_device(): lax.all_to_all(other, 'dp', split_axis=0, concat_axis=0, tiled=True)]
    unnamed x57 -> x65, local copies, waits for them, and re-layouts: 17.5 us -> 24 us
  transfers between devices with their start and end apart: 19 -> 19, of which waited for: 7 -> 8; matrix products, arithmetic and copies ran while one was open for 0% -> 0% of each run, Pallas kernels for 23% -> 20%
where the time goes in v5:
time: 222 us; the launch traced here: 221 us
  waiting for transfers between devices  98 us (44%)
  Pallas kernels  44.5 us (20%)
  starting transfers between devices  30.2 us (14%)
  local copies, waits for them, and re-layouts  24.2 us (11%)
  blocking collectives  22.7 us (10%)
    ppermute x12, waiting for transfers between devices, swap(): return lax.ppermute(x, axis, [(s, s ^ k) for s in range(n)])  46.8 us
    ppermute x3, waiting for transfers between devices, shift(): return lax.ppermute(x, axis, [(s, (s + k) % n) for s in range(n)])  28.4 us
    unnamed x65, local copies, waits for them, and re-layouts  24 us
    all_to_all x1, blocking collectives, spread(): lax.all_to_all(pair, 'fsdp', split_axis=0, concat_axis=0, axis_index_grou...  22.7 us
    all_to_all x1, waiting for transfers between devices, per_device(): lax.all_to_all(other, 'dp', split_axis=0, concat_axis=0, tiled=True)  21.8 us
    pallas_call x1, Pallas kernels, grads(): pl.pallas_call(grads_body, grid_spec=pltpu.PrefetchScalarGridSpec(num_sca...  15.4 us
    pallas_call x1, Pallas kernels, wgrad(): pl.pallas_call(wgrad_body, grid_spec=pltpu.PrefetchScalarGridSpec(num_sca...  11.7 us
    ppermute x12, starting transfers between devices, swap(): return lax.ppermute(x, axis, [(s, s ^ k) for s in range(n)])  11.1 us
  transfers between devices with their start and end apart: 19, of which 8 were waited for; matrix products, arithmetic and copies ran while one was open for 0% of the time, Pallas kernels for 20%

profile of v5, /device:TPU:0, one launch (start us, length us, event | category | flops | bytes accessed | tf_op | source)
XLA Modules:
  0.0 221.1 jit_solution(7073691859941842264)
XLA Ops:
  0.6 3.1 %collective-permute-start = (bf16[384,640]{1,0:T(8,128)(2,1)}, bf16[384,640]{1,0:T(8,128)(2,1)S(1)}, u32[]{:S(2)}, u32[]{:S(2)}) collective-permute-start(bf16[384,640]{1,0:T(8,128)(2,1)} %refs_0_.3), channel_id=1, source_target_pairs={{0,2},{1,3},{2,4},{3,5},{4,6},{5,7},{6,0},{7,1},{8,10},{9,11},{10,... | collective-permute-start | bytes 1474568 | tf_op jit(solution)/shard_map/ppermute | solution.py:35
  3.7 1.5 collective-permute-start.1
  5.2 1.5 collective-permute-start.2
  11.8 5.4 %collective-permute-done.refs_0_ = bf16[384,640]{1,0:T(8,128)(2,1)S(1)} collective-permute-done((bf16[384,640]{1,0:T(8,128)(2,1)}, bf16[384,640]{1,0:T(8,128)(2,1)S(1)}, u32[]{:S(2)}, u32[]{:S(2)}) %collective-permute-start) | collective-permute-done | bytes 491552 | tf_op jit(solution)/shard_map/ppermute | solution.py:35
  19.0 1.5 collective-permute-start.9
  22.8 11.5 %collective-permute-done.4.refs_0_ = bf16[384,640]{1,0:T(8,128)(2,1)} collective-permute-done((bf16[384,640]{1,0:T(8,128)(2,1)S(1)}, bf16[384,640]{1,0:T(8,128)(2,1)}, u32[]{:S(2)}, u32[]{:S(2)}) %collective-permute-start.4) | collective-permute-done | bytes 491552 | tf_op jit(solution)/shard_map/ppermute | solution.py:35
  35.1 1.5 collective-permute-start.7
  36.6 11.6 %collective-permute-done.6.refs_0_ = bf16[384,640]{1,0:T(8,128)(2,1)} collective-permute-done((bf16[384,640]{1,0:T(8,128)(2,1)}, bf16[384,640]{1,0:T(8,128)(2,1)}, u32[]{:S(2)}, u32[]{:S(2)}) %collective-permute-start.6) | collective-permute-done | bytes 491552 | tf_op jit(solution)/shard_map/ppermute | solution.py:35
  50.0 2.6 %own_features.1.refs_5_.own_ref = bf16[4,384,640]{2,1,0:T(8,128)(2,1)} custom-call(s32[4]{0:T(128)S(1)} %and_select_fusion.at_ref, bf16[384,640]{1,0:T(8,128)(2,1)S(1)} %copy-done.17, bf16[384,640]{1,0:T(8,128)(2,1)S(1)} %copy-done.9, bf16[384,640]{1,0:T(8,128)(2,1)} %after.6.refs_2_, bf16[384,640]{1,0:T(8,128)(2,1)} %after.7.refs_3_, ...), custom_call_target="tpu_custom_call" | custom-call | flops 1024 | bytes 1024 | tf_op jit(solution)/shard_map/own_features/pallas_call | solution.py:97
  52.6 4.6 %all-to-all-start = ((bf16[4,384,640]{2,1,0:T(8,128)(2,1)}), bf16[4,384,640]{2,1,0:T(8,128)(2,1)}, u32[]{:S(2)}, u32[]{:S(2)}) async-start(bf16[4,384,640]{2,1,0:T(8,128)(2,1)} %own_features.1.refs_5_.own_ref), calls=%async_computation | async-start | bytes 3932160 | tf_op jit(solution)/shard_map/all_to_all | solution.py:321
  60.7 2.3 %grad_gram.1 = (f32[4,32,1536]{2,1,0:T(8,128)S(1)}, f32[4,32,1536]{2,1,0:T(8,128)S(1)}) custom-call(s32[1]{0:T(128)} %bitcast.inner_ref, s32[4]{0:T(128)S(1)} %xor_multiply_fusion.offs_ref, bf16[384,640]{1,0:T(8,128)(2,1)S(1)} %copy-done.18, bf16[384,640]{1,0:T(8,128)(2,1)S(1)} %copy-done.16, bf16[384,640]{1,0:T(8,128)(2,1)} %collective-permute-done.2.refs_2_, ...), custom_call_target="tpu_custom_call" | custom-call | flops 1024 | bytes 1024 | tf_op jit(solution)/shard_map/grad_gram/pallas_call | solution.py:225
  66.0 1.4 collective-permute-start.14
  68.0 28.5 %collective-permute-done.8.refs_3_ = bf16[384,640]{1,0:T(8,128)(2,1)S(1)} collective-permute-done((bf16[384,640]{1,0:T(8,128)(2,1)}, bf16[384,640]{1,0:T(8,128)(2,1)S(1)}, u32[]{:S(2)}, u32[]{:S(2)}) %collective-permute-start.8) | collective-permute-done | bytes 491552 | tf_op jit(solution)/shard_map/ppermute | solution.py:30
  99.9 2.1 other_features.1.refs_5_.other_ref
  103.1 6.8 %hidden_gram.1 = (f32[4,32,1536]{2,1,0:T(8,128)S(1)}, f32[4,32,1536]{2,1,0:T(8,128)S(1)}, bf16[1792,1536]{1,0:T(8,128)(2,1)}) custom-call(s32[1]{0:T(128)} %bitcast.inner_ref, s32[4]{0:T(128)S(1)} %xor_multiply_fusion.offs_ref, bf16[1792,384]{1,0:T(8,128)(2,1)S(1)} %copy-done.3, bf16[1792,384]{1,0:T(8,128)(2,1)} %collective-permute-done.11.refs_1_, ...), custom_call_target="tpu_custom_call" | custom-call | flops 1024 | bytes 1024 | tf_op jit(solution)/shard_map/hidden_gram/pallas_call | solution.py:225
  112.6 3.6 %all-to-all-start.3 = ((f32[4,32,1536]{2,1,0:T(8,128)}), f32[4,32,1536]{2,1,0:T(8,128)S(1)}, u32[]{:S(2)}, u32[]{:S(2)}) async-start(f32[4,32,1536]{2,1,0:T(8,128)} %grad_pair.1), calls=%async_computation.3 | async-start | bytes 1572864 | tf_op jit(solution)/shard_map/all_to_all | solution.py:257
  116.3 1.5 collective-permute-start.13
  117.8 17.6 %collective-permute-done.13.b_ref = f32[4,32,1536]{2,1,0:T(8,128)S(1)} collective-permute-done((f32[4,32,1536]{2,1,0:T(8,128)S(1)}, f32[4,32,1536]{2,1,0:T(8,128)S(1)}, u32[]{:S(2)}, u32[]{:S(2)}) %collective-permute-start.13) | collective-permute-done | bytes 786464 | tf_op jit(solution)/shard_map/ppermute | solution.py:30
  136.3 22.7 %all_to_all.29.hid_ref = f32[4,32,1536]{2,1,0:T(8,128)} all-to-all(f32[4,32,1536]{2,1,0:T(8,128)S(1)} %hidden_pair.1.order_ref), channel_id=1, replica_groups={{0,2,4,6},{1,3,5,7},{8,10,12,14},{9,11,13,15},{16,18,20,22},{17,19,21,2..., dimensions={0} | all-to-all | bytes 1572864 | tf_op jit(solution)/shard_map/all_to_all | solution.py:257
  159.0 3.7 %all-to-all-start.1 = ((bf16[4,384,640]{2,1,0:T(8,128)(2,1)}), bf16[4,384,640]{2,1,0:T(8,128)(2,1)S(1)}, u32[]{:S(2)}, u32[]{:S(2)}) async-start(bf16[4,384,640]{2,1,0:T(8,128)(2,1)} %other_features.1.refs_5_.other_ref), calls=%async_computation.1 | async-start | bytes 3932160 | tf_op jit(solution)/shard_map/all_to_all | solution.py:334
  165.2 21.8 %all-to-all-done.1.other_ref = bf16[4,384,640]{2,1,0:T(8,128)(2,1)S(1)} async-done(((bf16[4,384,640]{2,1,0:T(8,128)(2,1)}), bf16[4,384,640]{2,1,0:T(8,128)(2,1)S(1)}, u32[]{:S(2)}, u32[]{:S(2)}) %all-to-all-start.1) | async-done | bytes 1966112 | tf_op jit(solution)/shard_map/all_to_all | solution.py:334
  187.0 2.7 %all-to-all-start.4 = ((f32[32,1,128]{2,1,0:T(1,128)}), f32[32,1,128]{2,1,0:T(1,128)S(1)}, u32[]{:S(2)}, u32[]{:S(2)}) async-start(f32[32,1,128]{2,1,0:T(1,128)} %bitcast.3), calls=%async_computation.4 | async-start | bytes 32768 | tf_op jit(solution)/shard_map/all_to_all | solution.py:349
  192.5 15.4 %grads.1 = (bf16[384,1792]{1,0:T(8,128)(2,1)}, bf16[384,1792]{1,0:T(8,128)(2,1)}) custom-call(s32[2]{0:T(128)S(1)} %add_multiply_fusion.offs_ref, bf16[4,384,640]{2,1,0:T(8,128)(2,1)} %own_features.1.refs_5_.own_ref, bf16[4,384,640]{2,1,0:T(8,128)(2,1)} %other_features.1.refs_5_.other_ref, bf16[1792,5120]{1,0:T(8,128)(2,1)} %w_ref.1, ...), custom_call_target="tpu_custom_call" | custom-call | flops 1024 | bytes 1024 | tf_op jit(solution)/shard_map/grads/pallas_call | solution.py:134
  207.9 11.7 %wgrad.1 = bf16[1792,1280]{1,0:T(8,128)(2,1)} custom-call(s32[2]{0:T(128)S(1)} %add_multiply_fusion.offs_ref, bf16[1792,1536]{1,0:T(8,128)(2,1)} %get-tuple-element.17.hid_ref, bf16[4,384,640]{2,1,0:T(8,128)(2,1)} %all-to-all-done.own_ref, bf16[4,384,640]{2,1,0:T(8,128)(2,1)S(1)} %all-to-all-done.1.other_ref, f32[32,128]{1,0:T(8,128)} %score_line.1.order_ref), custom_call_target="tpu_custom_call" | custom-call | flops 1024 | bytes 1024 | tf_op jit(solution)/shard_map/wgrad/pallas_call | solution.py:170
  (103 shorter events, 33.9 us)
Async XLA Ops:
  0.6 16.5 %collective-permute-start = (bf16[384,640]{1,0:T(8,128)(2,1)}, bf16[384,640]{1,0:T(8,128)(2,1)S(1)}, u32[]{:S(2)}, u32[]{:S(2)}) collective-permute-start(bf16[384,640]{1,0:T(8,128)(2,1)} %refs_0_.3), channel_id=1, source_target_pairs={{0,2},{1,3},{2,4},{3,5},{4,6},{5,7},{6,0},{7,1},{8,10},{9,11},{10,... | collective-permute-start | bytes 1474568 | tf_op jit(solution)/shard_map/ppermute | solution.py:35
  3.7 13.5 %collective-permute-start.1 = (bf16[384,640]{1,0:T(8,128)(2,1)}, bf16[384,640]{1,0:T(8,128)(2,1)S(1)}, u32[]{:S(2)}, u32[]{:S(2)}) collective-permute-start(bf16[384,640]{1,0:T(8,128)(2,1)} %refs_0_.3), channel_id=1, source_target_pairs={{0,1},{1,0},{2,3},{3,2},{4,5},{5,4},{6,7},{7,6},{8,9},{9,8},{10,11... | collective-permute-start | bytes 1474568 | tf_op jit(solution)/shard_map/ppermute | solution.py:30
  5.2 12.7 %collective-permute-start.2 = (bf16[384,640]{1,0:T(8,128)(2,1)}, bf16[384,640]{1,0:T(8,128)(2,1)}, u32[]{:S(2)}, u32[]{:S(2)}) collective-permute-start(bf16[384,640]{1,0:T(8,128)(2,1)} %refs_0_.3), channel_id=1, source_target_pairs={{0,16},{8,24},{16,0},{24,8},{1,17},{9,25},{17,1},{25,9},{2,18},{10... | collective-permute-start | bytes 1474568 | tf_op jit(solution)/shard_map/ppermute | solution.py:30
  6.7 11.2 %collective-permute-start.3 = (bf16[384,640]{1,0:T(8,128)(2,1)}, bf16[384,640]{1,0:T(8,128)(2,1)S(1)}, u32[]{:S(2)}, u32[]{:S(2)}) collective-permute-start(bf16[384,640]{1,0:T(8,128)(2,1)} %refs_0_.3), channel_id=1, source_target_pairs={{0,8},{8,0},{16,24},{24,16},{1,9},{9,1},{17,25},{25,17},{2,10},{10... | collective-permute-start | bytes 1474568 | tf_op jit(solution)/shard_map/ppermute | solution.py:30
  19.0 45.8 %collective-permute-start.9 = (bf16[1792,384]{1,0:T(8,128)(2,1)}, bf16[1792,384]{1,0:T(8,128)(2,1)S(1)}, u32[]{:S(2)}, u32[]{:S(2)}) collective-permute-start(bf16[1792,384]{1,0:T(8,128)(2,1)} %after.8.refs_0_), channel_id=1, source_target_pairs={{0,16},{8,24},{16,0},{24,8},{1,17},{9,25},{17,1},{25,9},{2,18},{10... | collective-permute-start | bytes 4128776 | tf_op jit(solution)/shard_map/ppermute | solution.py:30
  20.5 13.8 %collective-permute-start.4 = (bf16[384,640]{1,0:T(8,128)(2,1)S(1)}, bf16[384,640]{1,0:T(8,128)(2,1)}, u32[]{:S(2)}, u32[]{:S(2)}) collective-permute-start(bf16[384,640]{1,0:T(8,128)(2,1)S(1)} %copy-done.9), channel_id=1, source_target_pairs={{0,2},{1,3},{2,4},{3,5},{4,6},{5,7},{6,0},{7,1},{8,10},{9,11},{10,... | collective-permute-start | bytes 1474568 | tf_op jit(solution)/shard_map/ppermute | solution.py:35
  21.8 12.5 %collective-permute-start.5 = (bf16[384,640]{1,0:T(8,128)(2,1)S(1)}, bf16[384,640]{1,0:T(8,128)(2,1)S(1)}, u32[]{:S(2)}, u32[]{:S(2)}) collective-permute-start(bf16[384,640]{1,0:T(8,128)(2,1)S(1)} %copy-done.9), channel_id=1, source_target_pairs={{0,1},{1,0},{2,3},{3,2},{4,5},{5,4},{6,7},{7,6},{8,9},{9,8},{10,11... | collective-permute-start | bytes 1474568 | tf_op jit(solution)/shard_map/ppermute | solution.py:30
  35.1 13.9 %copy-start.11 = (bf16[384,640]{1,0:T(8,128)(2,1)S(1)}, bf16[384,640]{1,0:T(8,128)(2,1)}, u32[]{:S(2)}) copy-start(bf16[384,640]{1,0:T(8,128)(2,1)} %copy-done.10) | copy-start | bytes 1474564
  35.1 13.1 %collective-permute-start.6 = (bf16[384,640]{1,0:T(8,128)(2,1)}, bf16[384,640]{1,0:T(8,128)(2,1)}, u32[]{:S(2)}, u32[]{:S(2)}) collective-permute-start(bf16[384,640]{1,0:T(8,128)(2,1)} %after.6.refs_2_), channel_id=1, source_target_pairs={{0,2},{1,3},{2,4},{3,5},{4,6},{5,7},{6,0},{7,1},{8,10},{9,11},{10,... | collective-permute-start | bytes 1474568 | tf_op jit(solution)/shard_map/ppermute | solution.py:35
  35.1 13.1 %collective-permute-start.7 = (bf16[384,640]{1,0:T(8,128)(2,1)}, bf16[384,640]{1,0:T(8,128)(2,1)S(1)}, u32[]{:S(2)}, u32[]{:S(2)}) collective-permute-start(bf16[384,640]{1,0:T(8,128)(2,1)} %after.6.refs_2_), channel_id=1, source_target_pairs={{0,1},{1,0},{2,3},{3,2},{4,5},{5,4},{6,7},{7,6},{8,9},{9,8},{10,11... | collective-permute-start | bytes 1474568 | tf_op jit(solution)/shard_map/ppermute | solution.py:30
  36.6 21.1 %collective-permute-start.10 = (bf16[384,640]{1,0:T(8,128)(2,1)}, bf16[384,640]{1,0:T(8,128)(2,1)}, u32[]{:S(2)}, u32[]{:S(2)}) collective-permute-start(bf16[384,640]{1,0:T(8,128)(2,1)} %collective-permute-done.2.refs_2_), channel_id=1, source_target_pairs={{0,8},{8,0},{16,24},{24,16},{1,9},{9,1},{17,25},{25,17},{2,10},{10... | collective-permute-start | bytes 1474568 | tf_op jit(solution)/shard_map/ppermute | solution.py:30
  52.6 4.6 %copy-start.3 = (bf16[1792,384]{1,0:T(8,128)(2,1)S(1)}, bf16[1792,384]{1,0:T(8,128)(2,1)}, u32[]{:S(2)}) copy-start(bf16[1792,384]{1,0:T(8,128)(2,1)} %after.8.refs_0_) | copy-start | bytes 4128772
  52.6 60.0 %all-to-all-start = ((bf16[4,384,640]{2,1,0:T(8,128)(2,1)}), bf16[4,384,640]{2,1,0:T(8,128)(2,1)}, u32[]{:S(2)}, u32[]{:S(2)}) async-start(bf16[4,384,640]{2,1,0:T(8,128)(2,1)} %own_features.1.refs_5_.own_ref), calls=%async_computation | async-start | bytes 3932160 | tf_op jit(solution)/shard_map/all_to_all | solution.py:321
  57.2 44.8 %collective-permute-start.11 = (bf16[1792,384]{1,0:T(8,128)(2,1)S(1)}, bf16[1792,384]{1,0:T(8,128)(2,1)}, u32[]{:S(2)}, u32[]{:S(2)}) collective-permute-start(bf16[1792,384]{1,0:T(8,128)(2,1)S(1)} %copy-done.3), channel_id=1, source_target_pairs={{0,8},{8,0},{16,24},{24,16},{1,9},{9,1},{17,25},{25,17},{2,10},{10... | collective-permute-start | bytes 4128776 | tf_op jit(solution)/shard_map/ppermute | solution.py:30
  65.8 36.2 %collective-permute-start.12 = (bf16[1792,384]{1,0:T(8,128)(2,1)}, bf16[1792,384]{1,0:T(8,128)(2,1)S(1)}, u32[]{:S(2)}, u32[]{:S(2)}) collective-permute-start(bf16[1792,384]{1,0:T(8,128)(2,1)} %after.9.refs_4_.refs_2_), channel_id=1, source_target_pairs={{0,8},{8,0},{16,24},{24,16},{1,9},{9,1},{17,25},{25,17},{2,10},{10... | collective-permute-start | bytes 4128776 | tf_op jit(solution)/shard_map/ppermute | solution.py:30
  66.0 44.8 %collective-permute-start.14 = (f32[4,32,1536]{2,1,0:T(8,128)}, f32[4,32,1536]{2,1,0:T(8,128)S(1)}, u32[]{:S(2)}, u32[]{:S(2)}) collective-permute-start(f32[4,32,1536]{2,1,0:T(8,128)} %copy-done.28), channel_id=1, source_target_pairs={{0,1},{1,0},{2,3},{3,2},{4,5},{5,4},{6,7},{7,6},{8,9},{9,8},{10,11... | collective-permute-start | bytes 2359304 | tf_op jit(solution)/shard_map/ppermute | solution.py:30
  67.4 29.1 %collective-permute-start.8 = (bf16[384,640]{1,0:T(8,128)(2,1)}, bf16[384,640]{1,0:T(8,128)(2,1)S(1)}, u32[]{:S(2)}, u32[]{:S(2)}) collective-permute-start(bf16[384,640]{1,0:T(8,128)(2,1)} %after.7.refs_3_), channel_id=1, source_target_pairs={{0,1},{1,0},{2,3},{3,2},{4,5},{5,4},{6,7},{7,6},{8,9},{9,8},{10,11... | collective-permute-start | bytes 1474568 | tf_op jit(solution)/shard_map/ppermute | solution.py:30
  102.0 8.7 %copy-start.23 = (f32[4,32,1536]{2,1,0:T(8,128)S(1)}, f32[4,32,1536]{2,1,0:T(8,128)}, u32[]{:S(2)}) copy-start(f32[4,32,1536]{2,1,0:T(8,128)} %copy-done.22) | copy-start | bytes 2359300
  112.6 22.7 %copy-start.25 = (f32[4,32,1536]{2,1,0:T(8,128)S(1)}, f32[4,32,1536]{2,1,0:T(8,128)}, u32[]{:S(2)}) copy-start(f32[4,32,1536]{2,1,0:T(8,128)} %copy-done.24) | copy-start | bytes 2359300
  112.6 23.7 %all-to-all-start.3 = ((f32[4,32,1536]{2,1,0:T(8,128)}), f32[4,32,1536]{2,1,0:T(8,128)S(1)}, u32[]{:S(2)}, u32[]{:S(2)}) async-start(f32[4,32,1536]{2,1,0:T(8,128)} %grad_pair.1), calls=%async_computation.3 | async-start | bytes 1572864 | tf_op jit(solution)/shard_map/all_to_all | solution.py:257
  116.3 19.1 %collective-permute-start.13 = (f32[4,32,1536]{2,1,0:T(8,128)S(1)}, f32[4,32,1536]{2,1,0:T(8,128)S(1)}, u32[]{:S(2)}, u32[]{:S(2)}) collective-permute-start(f32[4,32,1536]{2,1,0:T(8,128)S(1)} %copy-done.27), channel_id=1, source_target_pairs={{0,1},{1,0},{2,3},{3,2},{4,5},{5,4},{6,7},{7,6},{8,9},{9,8},{10,11... | collective-permute-start | bytes 2359304 | tf_op jit(solution)/shard_map/ppermute | solution.py:30
  159.0 3.7 %copy-start.30 = (s32[3]{0:T(128)S(1)}, s32[3]{0:T(128)}, u32[]{:S(2)}) copy-start(s32[3]{0:T(128)} %assign_ref.1) | copy-start | bytes 40
  159.0 28.0 %all-to-all-start.1 = ((bf16[4,384,640]{2,1,0:T(8,128)(2,1)}), bf16[4,384,640]{2,1,0:T(8,128)(2,1)S(1)}, u32[]{:S(2)}, u32[]{:S(2)}) async-start(bf16[4,384,640]{2,1,0:T(8,128)(2,1)} %other_features.1.refs_5_.other_ref), calls=%async_computation.1 | async-start | bytes 3932160 | tf_op jit(solution)/shard_map/all_to_all | solution.py:334
  187.0 32.6 %all-to-all-start.4 = ((f32[32,1,128]{2,1,0:T(1,128)}), f32[32,1,128]{2,1,0:T(1,128)S(1)}, u32[]{:S(2)}, u32[]{:S(2)}) async-start(f32[32,1,128]{2,1,0:T(1,128)} %bitcast.3), calls=%async_computation.4 | async-start | bytes 32768 | tf_op jit(solution)/shard_map/all_to_all | solution.py:349
  (27 other events, 33.2 us)

commit v6 on v5

--- a/solution.py
+++ b/solution.py
@@ -14,7 +14,7 @@
 
 F32 = jnp.float32
 BF16 = jnp.bfloat16
-VMEM_LIMIT = 48 * 1024 * 1024
+VMEM_LIMIT = 32 * 1024 * 1024
 
 
 def dot_nt(a, b):
@@ -86,19 +86,24 @@
 
 
 def arrange_body(n, at_ref, *refs):
-    blocks, (order_ref, out_ref) = refs[:n], refs[n:]
-    for j in range(n):
-        out_ref[at_ref[j]] = blocks[j][...]
+    blocks, (order_ref, out_ref, sems) = refs[:n], refs[n:]
+    copies = [
+        pltpu.make_async_copy(blocks[j], out_ref.at[at_ref[j]], sems.at[j]) for j in range(n)
+    ]
+    for copy in copies:
+        copy.start()
+    for copy in copies:
+        copy.wait()
 
 
 def arrange(at, blocks, order, name):
     n = len(blocks)
-    vmem = pl.BlockSpec(memory_space=pltpu.VMEM)
     return pl.pallas_call(
         functools.partial(arrange_body, n),
-        in_specs=[pl.BlockSpec(memory_space=pltpu.SMEM)] + [vmem] * n + [ANY],
-        out_specs=vmem,
+        in_specs=[pl.BlockSpec(memory_space=pltpu.SMEM)] + [ANY] * (n + 1),
+        out_specs=ANY,
         out_shape=jax.ShapeDtypeStruct((n,) + blocks[0].shape, BF16),
+        scratch_shapes=[pltpu.SemaphoreType.DMA((n,))],
         compiler_params=params(),
         cost_estimate=SMALL,
         name=name,
@@ -143,7 +148,11 @@
         ),
         out_shape=(out, out),
         compiler_params=params(),
-        cost_estimate=SMALL,
+        cost_estimate=pl.CostEstimate(
+            flops=2 * toks * units * feats,
+            bytes_accessed=2 * (units * feats + toks * feats + 4 * toks * units),
+            transcendentals=toks * units,
+        ),
         name="grads",
     )(offs, own, other, weight, gate, up, order)
 
@@ -180,7 +189,11 @@
         ),
         out_shape=jax.ShapeDtypeStruct((units, 2 * width), BF16),
         compiler_params=params(),
-        cost_estimate=SMALL,
+        cost_estimate=pl.CostEstimate(
+            flops=4 * total * units * width,
+            bytes_accessed=2 * (total * (units + 2 * width) + 2 * units * width),
+            transcendentals=0,
+        ),
         name="wgrad",
     )(offs, hid, own, other, order)
 
@@ -234,39 +247,36 @@
     )(inner, offs, *operands, order)
 
 
-def add_body(a_ref, b_ref, order_ref, out_ref):
-    out_ref[...] = a_ref[...] + b_ref[...]
-
-
-def add(a, b, order, name):
+def pair_body(n, outer_ref, kept_ref, came_ref, order_ref, *out_refs):
+    for step in range(n):
+        at = lax.rem(outer_ref[0] + step, n)
+        out_refs[step][...] = kept_ref[at] + came_ref[at]
+
+
+def pair_sum(outer, kept, came, order, name):
+    n, *size = kept.shape
     vmem = pl.BlockSpec(memory_space=pltpu.VMEM)
     return pl.pallas_call(
-        add_body,
-        in_specs=[vmem, vmem, ANY],
-        out_specs=vmem,
-        out_shape=jax.ShapeDtypeStruct(a.shape, a.dtype),
+        functools.partial(pair_body, n),
+        in_specs=[pl.BlockSpec(memory_space=pltpu.SMEM), vmem, vmem, ANY],
+        out_specs=[vmem] * n,
+        out_shape=[jax.ShapeDtypeStruct(size, F32)] * n,
         compiler_params=params(),
         cost_estimate=SMALL,
         name=name,
-    )(a, b, order)
-
-
-def spread(pair):
-    n_fs = lax.axis_size("fsdp")
-    groups = [list(range(x, n_fs, 2)) for x in range(2)]
-    return lax.all_to_all(
-        pair, "fsdp", split_axis=0, concat_axis=0, axis_index_groups=groups, tiled=True
-    )
-
-
-def line_body(rows, assign_ref, hid_ref, grad_ref, out_ref):
-    n, _, total = hid_ref.shape
-    hid, grad = hid_ref[0], grad_ref[0]
-    for j in range(1, n):
-        hid += hid_ref[j]
-        grad += grad_ref[j]
-    by_tok = jnp.sum(hid * grad, axis=0, keepdims=True)
-    size = total // rows
+    )(outer, kept, came, order)
+
+
+def spread(slices):
+    return [x if j == 0 else shift(x, "fsdp", 2 * j) for j, x in enumerate(slices)]
+
+
+def line_body(rows, n, assign_ref, *refs):
+    hid, grad, (order_ref, out_ref) = refs[:n], refs[n : 2 * n], refs[2 * n :]
+    hid_sum = sum(ref[...] for ref in hid)
+    grad_sum = sum(ref[...] for ref in grad)
+    by_tok = jnp.sum(hid_sum * grad_sum, axis=0, keepdims=True)
+    size = by_tok.shape[1] // rows
     lane = lax.broadcasted_iota(jnp.int32, (1, 128), 1)
     line = jnp.zeros((1, 128), F32)
     for r in range(rows):
@@ -277,17 +287,18 @@
     out_ref[...] = jnp.broadcast_to(line, out_ref.shape)
 
 
-def score_line(assign, hid, grad, rows, copies):
+def score_line(assign, hid, grad, order, rows, copies):
+    n = len(hid)
     vmem = pl.BlockSpec(memory_space=pltpu.VMEM)
     return pl.pallas_call(
-        functools.partial(line_body, rows),
-        in_specs=[pl.BlockSpec(memory_space=pltpu.SMEM), vmem, vmem],
+        functools.partial(line_body, rows, n),
+        in_specs=[pl.BlockSpec(memory_space=pltpu.SMEM)] + [vmem] * (2 * n) + [ANY],
         out_specs=vmem,
         out_shape=jax.ShapeDtypeStruct((copies, 128), F32),
         compiler_params=params(),
         cost_estimate=SMALL,
         name="score_line",
-    )(assign, hid, grad)
+    )(assign, *hid, *grad, order)
 
 
 def per_device(gate_act, up_act, out_grad, down_weight, val_hidden, val_grad, assign):
@@ -302,6 +313,11 @@
     n_out = n_fs // 2
     outer, inner = f // 2, f % 2
 
+    at = (outer - jnp.arange(n_out, dtype=jnp.int32)) % n_out
+    tok_offs = (d ^ jnp.arange(n_dp, dtype=jnp.int32)) * toks
+    inner_at = inner.reshape(1).astype(jnp.int32)
+    outer_at = outer.reshape(1).astype(jnp.int32)
+
     first = shift(out_grad, "fsdp", 2)
     others = [swap(out_grad, "fsdp", 1)]
     far = swap(out_grad, "dp", 2)
@@ -310,42 +326,41 @@
     hidden = after(hidden_units(gate_act, up_act), first)
     grad_dp = [out_grad, near, far, swap(far, "dp", 1)]
     far = swap(hidden, "dp", 2)
+    near = swap(hidden, "dp", 1)
+
+    grad_kept, away = gram_call(
+        grad_gram_body, inner_at, tok_offs, [*grad_dp, val_grad], first, n_fs, [], "grad_gram"
+    )
+    grad_came = swap(away, "fsdp", 1)
     ring = [out_grad, first]
     for _ in range(n_out - 2):
         others.append(swap(ring[-1], "fsdp", 1))
-        ring.append(after(shift(ring[-1], "fsdp", 2), others[-1]))
+        ring.append(after(shift(ring[-1], "fsdp", 2), others[-1], away))
     others.append(swap(ring[-1], "fsdp", 1))
 
-    at = (outer - jnp.arange(n_out, dtype=jnp.int32)) % n_out
-    own = arrange(at, ring, others[1], "own_features")
+    far = after(far, ring[-1])
+    hid_dp = [hidden, near, far, swap(far, "dp", 1)]
+    own = arrange(at, ring, far, "own_features")
     own_cols = lax.all_to_all(own, "dp", split_axis=0, concat_axis=0, tiled=True)
-
-    tok_offs = (d ^ jnp.arange(n_dp, dtype=jnp.int32)) * toks
-    inner_at = inner.reshape(1).astype(jnp.int32)
-    grad_kept, away = gram_call(
-        grad_gram_body, inner_at, tok_offs, [*grad_dp, val_grad], own, n_fs, [], "grad_gram"
-    )
-    grad_came = swap(away, "fsdp", 1)
-
-    far = after(far, away, others[2])
-    hid_dp = [hidden, swap(hidden, "dp", 1), far, swap(far, "dp", 1)]
-
-    other = arrange(at, others, far, "other_features")
+    grad_pair = pair_sum(outer_at, grad_kept, grad_came, own, "grad_pair")
+    grad_sums = spread(grad_pair)
+
+    hid_kept, away, hid_all = gram_call(
+        hidden_gram_body, inner_at, tok_offs, [*hid_dp, val_hidden], grad_pair[0], n_fs,
+        [jax.ShapeDtypeStruct((units, total), BF16)], "hidden_gram",
+    )
+    hid_came = swap(away, "fsdp", 1)
+    other = arrange(at, others, away, "other_features")
     other_cols = lax.all_to_all(other, "dp", split_axis=0, concat_axis=0, tiled=True)
-
-    hid_kept, away, hid_all = gram_call(
-        hidden_gram_body, inner_at, tok_offs, [*hid_dp, val_hidden], other, n_fs,
-        [jax.ShapeDtypeStruct((units, total), BF16)], "hidden_gram",
-    )
-    hid_came = swap(away, "fsdp", 1)
-    grad_sums = spread(add(grad_kept, grad_came, away, "grad_pair"))
-    pair = add(hid_kept, hid_came, grad_came, "hidden_pair")
-    hid_sums = spread(pair)
+    hid_pair = pair_sum(outer_at, hid_kept, hid_came, other, "hidden_pair")
+    hid_sums = spread(hid_pair)
 
     offs = (jnp.stack([inner, 1 - inner]) * width).astype(jnp.int32)
-    grad_gate, grad_up = grads(offs, own, other, down_weight, gate_act, up_act, pair)
-
-    mine = score_line(assign, hid_sums, grad_sums, n_dp * rows_here, n_dp * n_fs)
+    grad_gate, grad_up = grads(offs, own, other, down_weight, gate_act, up_act, hid_pair[0])
+
+    mine = score_line(
+        assign, hid_sums, grad_sums, grad_up, n_dp * rows_here, n_dp * n_fs
+    )
     every = lax.all_to_all(
         mine, ("dp", "fsdp"), split_axis=0, concat_axis=0, tiled=True
     ).reshape(n_dp, n_fs, 128)

time: 222 us -> 241 us (1.086)
  Pallas kernels: 44.5 us -> 99.9 us
  waiting for transfers between devices: 98 us -> 80.2 us
  blocking collectives: 22.7 us -> 11.2 us
  local copies, waits for them, and re-layouts: 24.2 us -> 20.1 us
  starting transfers between devices: 30.2 us -> 27.3 us
    pallas_call x2, Pallas kernels: 4.67 us -> 62.9 us  [arrange(): pl.pallas_call(functools.partial(arrange_body, n), in_specs=[pl.BlockSpec...]
    all_to_all x1, blocking collectives: 22.7 us -> 11.2 us  [per_device(): lax.all_to_all(mine, ('dp', 'fsdp'), split_axis=0, concat_axis=0, tiled=T...]
    ppermute x3 -> x9, waiting for transfers between devices: 28.4 us -> 19.3 us  [shift(): return lax.ppermute(x, axis, [(s, (s + k) % n) for s in range(n)])]
    ppermute x12, waiting for transfers between devices: 46.8 us -> 38.2 us  [swap(): return lax.ppermute(x, axis, [(s, s ^ k) for s in range(n)])]
    all_to_all x2 -> x0, starting transfers between devices: 6.34 us -> none  [the longest x1 3.63 us: spread(): lax.all_to_all(pair, 'fsdp', split_axis=0, concat_axis=0, axis_index_grou...]
    ppermute x3 -> x9, starting transfers between devices: 4.43 us -> 9.35 us  [shift(): return lax.ppermute(x, axis, [(s, (s + k) % n) for s in range(n)])]
    unnamed x65 -> x63, local copies, waits for them, and re-layouts: 24 us -> 19.9 us
    pallas_call x2, Pallas kernels: 9.03 us -> 6.11 us  [gram_call(): pl.pallas_call(body, in_specs=[smem, smem] + [vmem] * len(operands) + [AN...]
  transfers between devices with their start and end apart: 19 -> 23, of which waited for: 8 -> 10; matrix products, arithmetic and copies ran while one was open for 0% -> 1% of each run, Pallas kernels for 20% -> 37%
where the time goes in v6:
time: 241 us; the launch traced here: 240 us
  Pallas kernels  99.9 us (41%)
  waiting for transfers between devices  80.2 us (33%)
  starting transfers between devices  27.3 us (11%)
  local copies, waits for them, and re-layouts  20.1 us (8%)
  blocking collectives  11.2 us (5%)
    pallas_call x2, Pallas kernels, arrange(): pl.pallas_call(functools.partial(arrange_body, n), in_specs=[pl.BlockSpec...  62.9 us
    ppermute x12, waiting for transfers between devices, swap(): return lax.ppermute(x, axis, [(s, s ^ k) for s in range(n)])  38.2 us
    all_to_all x1, waiting for transfers between devices, per_device(): lax.all_to_all(other, 'dp', split_axis=0, concat_axis=0, tiled=True)  22.7 us
    unnamed x63, local copies, waits for them, and re-layouts  19.9 us
    ppermute x9, waiting for transfers between devices, shift(): return lax.ppermute(x, axis, [(s, (s + k) % n) for s in range(n)])  19.3 us
    pallas_call x1, Pallas kernels, grads(): pl.pallas_call(grads_body, grid_spec=pltpu.PrefetchScalarGridSpec(num_sca...  15.4 us
    pallas_call x1, Pallas kernels, wgrad(): pl.pallas_call(wgrad_body, grid_spec=pltpu.PrefetchScalarGridSpec(num_sca...  11.3 us
    all_to_all x1, blocking collectives, per_device(): lax.all_to_all(mine, ('dp', 'fsdp'), split_axis=0, concat_axis=0, tiled=T...  11.2 us
  transfers between devices with their start and end apart: 23, of which 10 were waited for; matrix products, arithmetic and copies ran while one was open for 1% of the time, Pallas kernels for 37%

profile of v6, /device:TPU:0, one launch (start us, length us, event | category | flops | bytes accessed | tf_op | source)
XLA Modules:
  0.0 240.5 jit_solution(13884209162895183633)
XLA Ops:
  0.6 3.0 %collective-permute-start.2 = (bf16[384,640]{1,0:T(8,128)(2,1)}, bf16[384,640]{1,0:T(8,128)(2,1)S(1)}, u32[]{:S(2)}, u32[]{:S(2)}) collective-permute-start(bf16[384,640]{1,0:T(8,128)(2,1)} %refs_0_.3), channel_id=1, source_target_pairs={{0,16},{8,24},{16,0},{24,8},{1,17},{9,25},{17,1},{25,9},{2,18},{10... | collective-permute-start | bytes 1474568 | tf_op jit(solution)/shard_map/ppermute | solution.py:30
  5.2 1.6 collective-permute-start
  11.8 3.3 %collective-permute-done.2.refs_2_ = bf16[384,640]{1,0:T(8,128)(2,1)S(1)} collective-permute-done((bf16[384,640]{1,0:T(8,128)(2,1)}, bf16[384,640]{1,0:T(8,128)(2,1)S(1)}, u32[]{:S(2)}, u32[]{:S(2)}) %collective-permute-start.2) | collective-permute-done | bytes 491552 | tf_op jit(solution)/shard_map/ppermute | solution.py:30
  16.6 4.3 %collective-permute-done.refs_0_ = bf16[384,640]{1,0:T(8,128)(2,1)S(1)} collective-permute-done((bf16[384,640]{1,0:T(8,128)(2,1)}, bf16[384,640]{1,0:T(8,128)(2,1)S(1)}, u32[]{:S(2)}, u32[]{:S(2)}) %collective-permute-start) | collective-permute-done | bytes 491552 | tf_op jit(solution)/shard_map/ppermute | solution.py:35
  25.7 2.1 grad_gram.1
  29.6 6.9 %collective-permute-done.5.refs_1_ = bf16[384,640]{1,0:T(8,128)(2,1)} collective-permute-done((bf16[384,640]{1,0:T(8,128)(2,1)S(1)}, bf16[384,640]{1,0:T(8,128)(2,1)}, u32[]{:S(2)}, u32[]{:S(2)}) %collective-permute-start.5) | collective-permute-done | bytes 491552 | tf_op jit(solution)/shard_map/ppermute | solution.py:30
  36.4 2.1 collective-permute-done.4.refs_0_
  40.0 13.0 %collective-permute-done.7.refs_0_ = bf16[384,640]{1,0:T(8,128)(2,1)} collective-permute-done((bf16[384,640]{1,0:T(8,128)(2,1)}, bf16[384,640]{1,0:T(8,128)(2,1)}, u32[]{:S(2)}, u32[]{:S(2)}) %collective-permute-start.7) | collective-permute-done | bytes 491552 | tf_op jit(solution)/shard_map/ppermute | solution.py:35
  57.9 31.5 %own_features.1.order_ref.own_ref = bf16[4,384,640]{2,1,0:T(8,128)(2,1)} custom-call(s32[4]{0:T(128)S(1)} %and_select_fusion.at_ref, bf16[384,640]{1,0:T(8,128)(2,1)S(1)} %copy-done.15, bf16[384,640]{1,0:T(8,128)(2,1)S(1)} %copy-done.6, bf16[384,640]{1,0:T(8,128)(2,1)} %after.6.refs_2_, bf16[384,640]{1,0:T(8,128)(2,1)} %after.7.refs_1_.refs_3_, ...), custom_call_target="tpu_custom_call" | custom-call | flops 1024 | bytes 1024 | tf_op jit(solution)/shard_map/own_features/pallas_call | solution.py:101
  89.4 4.6 %all-to-all-start = ((bf16[4,384,640]{2,1,0:T(8,128)(2,1)}), bf16[4,384,640]{2,1,0:T(8,128)(2,1)}, u32[]{:S(2)}, u32[]{:S(2)}) async-start(bf16[4,384,640]{2,1,0:T(8,128)(2,1)} %own_features.1.order_ref.own_ref), calls=%async_computation | async-start | bytes 3932160 | tf_op jit(solution)/shard_map/all_to_all | solution.py:344
  94.0 2.0 grad_pair.1
  96.8 4.0 %hidden_gram.1 = (f32[4,32,1536]{2,1,0:T(8,128)S(1)}, f32[4,32,1536]{2,1,0:T(8,128)S(1)}, bf16[1792,1536]{1,0:T(8,128)(2,1)S(1)}) custom-call(s32[1]{0:T(128)} %bitcast.inner_ref, s32[4]{0:T(128)S(1)} %xor_multiply_fusion.offs_ref, bf16[1792,384]{1,0:T(8,128)(2,1)S(1)} %copy-done.4, bf16[1792,384]{1,0:T(8,128)(2,1)} %collective-permute-done.11.refs_1_, ...), custom_call_target="tpu_custom_call" | custom-call | flops 1024 | bytes 1024 | tf_op jit(solution)/shard_map/hidden_gram/pallas_call | solution.py:238
  101.6 2.4 %copy-done.28 = bf16[1792,1536]{1,0:T(8,128)(2,1)} copy-done((bf16[1792,1536]{1,0:T(8,128)(2,1)}, bf16[1792,1536]{1,0:T(8,128)(2,1)S(1)}, u32[]{:S(2)}) %copy-start.28) | copy-done | bytes 5505048
  106.2 2.3 collective-permute-start.19
  108.5 1.6 collective-permute-start.20
  110.1 24.4 %collective-permute-done.10.refs_3_ = bf16[384,640]{1,0:T(8,128)(2,1)S(1)} collective-permute-done((bf16[384,640]{1,0:T(8,128)(2,1)}, bf16[384,640]{1,0:T(8,128)(2,1)S(1)}, u32[]{:S(2)}, u32[]{:S(2)}) %collective-permute-start.10) | collective-permute-done | bytes 491552 | tf_op jit(solution)/shard_map/ppermute | solution.py:30
  134.5 31.5 %other_features.1.order_ref.other_ref = bf16[4,384,640]{2,1,0:T(8,128)(2,1)} custom-call(s32[4]{0:T(128)S(1)} %and_select_fusion.at_ref, bf16[384,640]{1,0:T(8,128)(2,1)S(1)} %copy-done.13, bf16[384,640]{1,0:T(8,128)(2,1)} %collective-permute-done.5.refs_1_, bf16[384,640]{1,0:T(8,128)(2,1)} %collective-permute-done.8.refs_1_.refs_2_, ...), custom_call_target="tpu_custom_call" | custom-call | flops 1024 | bytes 1024 | tf_op jit(solution)/shard_map/other_features/pallas_call | solution.py:101
  166.2 2.3 collective-permute-start.16
  170.0 15.4 %grads.1 = (bf16[384,1792]{1,0:T(8,128)(2,1)}, bf16[384,1792]{1,0:T(8,128)(2,1)}) custom-call(s32[2]{0:T(128)S(1)} %add_multiply_fusion.offs_ref, bf16[4,384,640]{2,1,0:T(8,128)(2,1)} %own_features.1.order_ref.own_ref, bf16[4,384,640]{2,1,0:T(8,128)(2,1)} %other_features.1.order_ref.other_ref, bf16[1792,5120]{1,0:T(8,128)(2,1)} %w_ref.1, ...), custom_call_target="tpu_custom_call" | custom-call | flops 7046430720 | bytes 27787264 | tf_op jit(solution)/shard_map/grads/pallas_call | solution.py:139
  187.5 11.2 %all_to_all.19 = f32[32,1,128]{2,1,0:T(1,128)S(1)} all-to-all(f32[32,1,128]{2,1,0:T(1,128)S(1)} %bitcast.12), channel_id=1, replica_groups=mesh['dp'=4,'fsdp'=8] {'dp','fsdp'}, dimensions={0} | all-to-all | bytes 32768 | tf_op jit(solution)/shard_map/all_to_all | solution.py:364
  198.8 3.6 %all-to-all-start.1 = ((bf16[4,384,640]{2,1,0:T(8,128)(2,1)}), bf16[4,384,640]{2,1,0:T(8,128)(2,1)S(1)}, u32[]{:S(2)}, u32[]{:S(2)}) async-start(bf16[4,384,640]{2,1,0:T(8,128)(2,1)} %other_features.1.order_ref.other_ref), calls=%async_computation.1 | async-start | bytes 3932160 | tf_op jit(solution)/shard_map/all_to_all | solution.py:354
  203.9 22.7 %all-to-all-done.1.other_ref = bf16[4,384,640]{2,1,0:T(8,128)(2,1)S(1)} async-done(((bf16[4,384,640]{2,1,0:T(8,128)(2,1)}), bf16[4,384,640]{2,1,0:T(8,128)(2,1)S(1)}, u32[]{:S(2)}, u32[]{:S(2)}) %all-to-all-start.1) | async-done | bytes 1966112 | tf_op jit(solution)/shard_map/all_to_all | solution.py:354
  226.6 2.6 %copy-done.29 = bf16[1792,1536]{1,0:T(8,128)(2,1)S(1)} copy-done((bf16[1792,1536]{1,0:T(8,128)(2,1)S(1)}, bf16[1792,1536]{1,0:T(8,128)(2,1)}, u32[]{:S(2)}) %copy-start.29) | copy-done | bytes 5505048
  229.2 11.3 %wgrad.1 = bf16[1792,1280]{1,0:T(8,128)(2,1)} custom-call(s32[2]{0:T(128)S(1)} %add_multiply_fusion.offs_ref, bf16[1792,1536]{1,0:T(8,128)(2,1)S(1)} %copy-done.29, bf16[4,384,640]{2,1,0:T(8,128)(2,1)} %all-to-all-done.own_ref, bf16[4,384,640]{2,1,0:T(8,128)(2,1)S(1)} %all-to-all-done.1.other_ref, f32[32,128]{1,0:T(8,128)S(1)} %score_line.1.order_ref), custom_call_target="tpu_custom_call" | custom-call | flops 7046430720 | bytes 14024704 | tf_op jit(solution)/shard_map/wgrad/pallas_call | solution.py:179
  (109 shorter events, 30.0 us)
Async XLA Ops:
  0.6 14.5 %collective-permute-start.2 = (bf16[384,640]{1,0:T(8,128)(2,1)}, bf16[384,640]{1,0:T(8,128)(2,1)S(1)}, u32[]{:S(2)}, u32[]{:S(2)}) collective-permute-start(bf16[384,640]{1,0:T(8,128)(2,1)} %refs_0_.3), channel_id=1, source_target_pairs={{0,16},{8,24},{16,0},{24,8},{1,17},{9,25},{17,1},{25,9},{2,18},{10... | collective-permute-start | bytes 1474568 | tf_op jit(solution)/shard_map/ppermute | solution.py:30
  3.7 12.9 %collective-permute-start.1 = (bf16[384,640]{1,0:T(8,128)(2,1)}, bf16[384,640]{1,0:T(8,128)(2,1)S(1)}, u32[]{:S(2)}, u32[]{:S(2)}) collective-permute-start(bf16[384,640]{1,0:T(8,128)(2,1)} %refs_0_.3), channel_id=1, source_target_pairs={{0,1},{1,0},{2,3},{3,2},{4,5},{5,4},{6,7},{7,6},{8,9},{9,8},{10,11... | collective-permute-start | bytes 1474568 | tf_op jit(solution)/shard_map/ppermute | solution.py:30
  5.2 11.4 %collective-permute-start.3 = (bf16[384,640]{1,0:T(8,128)(2,1)}, bf16[384,640]{1,0:T(8,128)(2,1)S(1)}, u32[]{:S(2)}, u32[]{:S(2)}) collective-permute-start(bf16[384,640]{1,0:T(8,128)(2,1)} %refs_0_.3), channel_id=1, source_target_pairs={{0,8},{8,0},{16,24},{24,16},{1,9},{9,1},{17,25},{25,17},{2,10},{10... | collective-permute-start | bytes 1474568 | tf_op jit(solution)/shard_map/ppermute | solution.py:30
  5.2 15.7 %collective-permute-start = (bf16[384,640]{1,0:T(8,128)(2,1)}, bf16[384,640]{1,0:T(8,128)(2,1)S(1)}, u32[]{:S(2)}, u32[]{:S(2)}) collective-permute-start(bf16[384,640]{1,0:T(8,128)(2,1)} %refs_0_.3), channel_id=1, source_target_pairs={{0,2},{1,3},{2,4},{3,5},{4,6},{5,7},{6,0},{7,1},{8,10},{9,11},{10,... | collective-permute-start | bytes 1474568 | tf_op jit(solution)/shard_map/ppermute | solution.py:35
  21.7 32.2 %collective-permute-start.9 = (bf16[1792,384]{1,0:T(8,128)(2,1)}, bf16[1792,384]{1,0:T(8,128)(2,1)S(1)}, u32[]{:S(2)}, u32[]{:S(2)}) collective-permute-start(bf16[1792,384]{1,0:T(8,128)(2,1)} %after.8.refs_0_), channel_id=1, source_target_pairs={{0,16},{8,24},{16,0},{24,8},{1,17},{9,25},{17,1},{25,9},{2,18},{10... | collective-permute-start | bytes 4128776 | tf_op jit(solution)/shard_map/ppermute | solution.py:30
  22.7 2.0 collective-permute-start.6
  22.8 13.6 %collective-permute-start.5 = (bf16[384,640]{1,0:T(8,128)(2,1)S(1)}, bf16[384,640]{1,0:T(8,128)(2,1)}, u32[]{:S(2)}, u32[]{:S(2)}) collective-permute-start(bf16[384,640]{1,0:T(8,128)(2,1)S(1)} %copy-done.6), channel_id=1, source_target_pairs={{0,1},{1,0},{2,3},{3,2},{4,5},{5,4},{6,7},{7,6},{8,9},{9,8},{10,11... | collective-permute-start | bytes 1474568 | tf_op jit(solution)/shard_map/ppermute | solution.py:30
  23.4 15.1 %collective-permute-start.4 = (bf16[384,640]{1,0:T(8,128)(2,1)S(1)}, bf16[384,640]{1,0:T(8,128)(2,1)}, u32[]{:S(2)}, u32[]{:S(2)}) collective-permute-start(bf16[384,640]{1,0:T(8,128)(2,1)S(1)} %copy-done.6), channel_id=1, source_target_pairs={{0,2},{1,3},{2,4},{3,5},{4,6},{5,7},{6,0},{7,1},{8,10},{9,11},{10,... | collective-permute-start | bytes 1474568 | tf_op jit(solution)/shard_map/ppermute | solution.py:35
  38.5 14.5 %collective-permute-start.7 = (bf16[384,640]{1,0:T(8,128)(2,1)}, bf16[384,640]{1,0:T(8,128)(2,1)}, u32[]{:S(2)}, u32[]{:S(2)}) collective-permute-start(bf16[384,640]{1,0:T(8,128)(2,1)} %after.6.refs_2_), channel_id=1, source_target_pairs={{0,2},{1,3},{2,4},{3,5},{4,6},{5,7},{6,0},{7,1},{8,10},{9,11},{10,... | collective-permute-start | bytes 1474568 | tf_op jit(solution)/shard_map/ppermute | solution.py:35
  38.5 14.5 %collective-permute-start.8 = (bf16[384,640]{1,0:T(8,128)(2,1)}, bf16[384,640]{1,0:T(8,128)(2,1)}, u32[]{:S(2)}, u32[]{:S(2)}) collective-permute-start(bf16[384,640]{1,0:T(8,128)(2,1)} %after.6.refs_2_), channel_id=1, source_target_pairs={{0,1},{1,0},{2,3},{3,2},{4,5},{5,4},{6,7},{7,6},{8,9},{9,8},{10,11... | collective-permute-start | bytes 1474568 | tf_op jit(solution)/shard_map/ppermute | solution.py:30
  40.0 56.1 %collective-permute-start.11 = (bf16[1792,384]{1,0:T(8,128)(2,1)S(1)}, bf16[1792,384]{1,0:T(8,128)(2,1)}, u32[]{:S(2)}, u32[]{:S(2)}) collective-permute-start(bf16[1792,384]{1,0:T(8,128)(2,1)S(1)} %copy-done.4), channel_id=1, source_target_pairs={{0,8},{8,0},{16,24},{24,16},{1,9},{9,1},{17,25},{25,17},{2,10},{10... | collective-permute-start | bytes 4128776 | tf_op jit(solution)/shard_map/ppermute | solution.py:30
  54.9 41.2 %collective-permute-start.12 = (bf16[1792,384]{1,0:T(8,128)(2,1)}, bf16[1792,384]{1,0:T(8,128)(2,1)}, u32[]{:S(2)}, u32[]{:S(2)}) collective-permute-start(bf16[1792,384]{1,0:T(8,128)(2,1)} %after.9.refs_4_.refs_2_), channel_id=1, source_target_pairs={{0,8},{8,0},{16,24},{24,16},{1,9},{9,1},{17,25},{25,17},{2,10},{10... | collective-permute-start | bytes 4128776 | tf_op jit(solution)/shard_map/ppermute | solution.py:30
  54.9 39.1 %collective-permute-start.13 = (f32[4,32,1536]{2,1,0:T(8,128)}, f32[4,32,1536]{2,1,0:T(8,128)}, u32[]{:S(2)}, u32[]{:S(2)}) collective-permute-start(f32[4,32,1536]{2,1,0:T(8,128)} %copy-done.7), channel_id=1, source_target_pairs={{0,1},{1,0},{2,3},{3,2},{4,5},{5,4},{6,7},{7,6},{8,9},{9,8},{10,11... | collective-permute-start | bytes 2359304 | tf_op jit(solution)/shard_map/ppermute | solution.py:30
  89.4 98.1 %all-to-all-start = ((bf16[4,384,640]{2,1,0:T(8,128)(2,1)}), bf16[4,384,640]{2,1,0:T(8,128)(2,1)}, u32[]{:S(2)}, u32[]{:S(2)}) async-start(bf16[4,384,640]{2,1,0:T(8,128)(2,1)} %own_features.1.order_ref.own_ref), calls=%async_computation | async-start | bytes 3932160 | tf_op jit(solution)/shard_map/all_to_all | solution.py:344
  104.1 61.9 %collective-permute-start.14 = (f32[4,32,1536]{2,1,0:T(8,128)S(1)}, f32[4,32,1536]{2,1,0:T(8,128)S(1)}, u32[]{:S(2)}, u32[]{:S(2)}) collective-permute-start(f32[4,32,1536]{2,1,0:T(8,128)S(1)} %get-tuple-element.23.refs_4_), channel_id=1, source_target_pairs={{0,1},{1,0},{2,3},{3,2},{4,5},{5,4},{6,7},{7,6},{8,9},{9,8},{10,11... | collective-permute-start | bytes 2359304 | tf_op jit(solution)/shard_map/ppermute | solution.py:30
  105.5 29.0 %collective-permute-start.10 = (bf16[384,640]{1,0:T(8,128)(2,1)}, bf16[384,640]{1,0:T(8,128)(2,1)S(1)}, u32[]{:S(2)}, u32[]{:S(2)}) collective-permute-start(bf16[384,640]{1,0:T(8,128)(2,1)} %after.7.refs_1_.refs_3_), channel_id=1, source_target_pairs={{0,1},{1,0},{2,3},{3,2},{4,5},{5,4},{6,7},{7,6},{8,9},{9,8},{10,11... | collective-permute-start | bytes 1474568 | tf_op jit(solution)/shard_map/ppermute | solution.py:30
  106.1 62.4 %collective-permute-start.18 = (f32[32,1536]{1,0:T(8,128)}, f32[32,1536]{1,0:T(8,128)S(1)}, u32[]{:S(2)}, u32[]{:S(2)}) collective-permute-start(f32[32,1536]{1,0:T(8,128)} %get-tuple-element.32), channel_id=1, source_target_pairs={{0,2},{1,3},{2,4},{3,5},{4,6},{5,7},{6,0},{7,1},{8,10},{9,11},{10,... | collective-permute-start | bytes 589832 | tf_op jit(solution)/shard_map/ppermute | solution.py:35
  106.2 79.2 %collective-permute-start.19 = (f32[32,1536]{1,0:T(8,128)}, f32[32,1536]{1,0:T(8,128)S(1)}, u32[]{:S(2)}, u32[]{:S(2)}) collective-permute-start(f32[32,1536]{1,0:T(8,128)} %copy-done.30), channel_id=1, source_target_pairs={{0,4},{1,5},{2,6},{3,7},{4,0},{5,1},{6,2},{7,3},{8,12},{9,13},{10,... | collective-permute-start | bytes 589832 | tf_op jit(solution)/shard_map/ppermute | solution.py:35
  108.5 57.5 %copy-start.25 = (f32[4,32,1536]{2,1,0:T(8,128)S(1)}, f32[4,32,1536]{2,1,0:T(8,128)}, u32[]{:S(2)}) copy-start(f32[4,32,1536]{2,1,0:T(8,128)} %copy-done.24) | copy-start | bytes 2359300
  108.5 76.9 %collective-permute-start.20 = (f32[32,1536]{1,0:T(8,128)S(1)}, f32[32,1536]{1,0:T(8,128)S(1)}, u32[]{:S(2)}, u32[]{:S(2)}) collective-permute-start(f32[32,1536]{1,0:T(8,128)S(1)} %get-tuple-element.34), channel_id=1, source_target_pairs={{0,6},{1,7},{2,0},{3,1},{4,2},{5,3},{6,4},{7,5},{8,14},{9,15},{10,... | collective-permute-start | bytes 589832 | tf_op jit(solution)/shard_map/ppermute | solution.py:35
  166.1 19.3 %collective-permute-start.15 = (f32[32,1536]{1,0:T(8,128)S(1)}, f32[32,1536]{1,0:T(8,128)S(1)}, u32[]{:S(2)}, u32[]{:S(2)}) collective-permute-start(f32[32,1536]{1,0:T(8,128)S(1)} %get-tuple-element.29), channel_id=1, source_target_pairs={{0,2},{1,3},{2,4},{3,5},{4,6},{5,7},{6,0},{7,1},{8,10},{9,11},{10,... | collective-permute-start | bytes 589832 | tf_op jit(solution)/shard_map/ppermute | solution.py:35
  166.2 19.2 %collective-permute-start.16 = (f32[32,1536]{1,0:T(8,128)S(1)}, f32[32,1536]{1,0:T(8,128)S(1)}, u32[]{:S(2)}, u32[]{:S(2)}) collective-permute-start(f32[32,1536]{1,0:T(8,128)S(1)} %get-tuple-element.30), channel_id=1, source_target_pairs={{0,4},{1,5},{2,6},{3,7},{4,0},{5,1},{6,2},{7,3},{8,12},{9,13},{10,... | collective-permute-start | bytes 589832 | tf_op jit(solution)/shard_map/ppermute | solution.py:35
  168.5 17.0 %collective-permute-start.17 = (f32[32,1536]{1,0:T(8,128)S(1)}, f32[32,1536]{1,0:T(8,128)S(1)}, u32[]{:S(2)}, u32[]{:S(2)}) collective-permute-start(f32[32,1536]{1,0:T(8,128)S(1)} %get-tuple-element.31), channel_id=1, source_target_pairs={{0,6},{1,7},{2,0},{3,1},{4,2},{5,3},{6,4},{7,5},{8,14},{9,15},{10,... | collective-permute-start | bytes 589832 | tf_op jit(solution)/shard_map/ppermute | solution.py:35
  198.8 27.9 %all-to-all-start.1 = ((bf16[4,384,640]{2,1,0:T(8,128)(2,1)}), bf16[4,384,640]{2,1,0:T(8,128)(2,1)S(1)}, u32[]{:S(2)}, u32[]{:S(2)}) async-start(bf16[4,384,640]{2,1,0:T(8,128)(2,1)} %other_features.1.order_ref.other_ref), calls=%async_computation.1 | async-start | bytes 3932160 | tf_op jit(solution)/shard_map/all_to_all | solution.py:354
  (30 other events, 122.9 us)

commit v7 on v6

--- a/solution.py
+++ b/solution.py
@@ -63,10 +63,14 @@
     )(x, *order)
 
 
-def hidden_body(gate_ref, up_ref, out_ref):
+def hidden_body(gate_ref, up_ref, hid_ref, by_gate_ref, by_up_ref):
     gate = gate_ref[...].astype(F32)
     up = up_ref[...].astype(F32)
-    out_ref[...] = (gate * jax.nn.sigmoid(gate) * up).astype(BF16).T
+    sig = jax.nn.sigmoid(gate)
+    act = gate * sig
+    hid_ref[...] = (act * up).astype(BF16).T
+    by_gate_ref[...] = (up * sig * (1.0 + gate * (1.0 - sig))).astype(BF16)
+    by_up_ref[...] = act.astype(BF16)
 
 
 def hidden_units(gate, up):
@@ -77,8 +81,12 @@
         hidden_body,
         grid=(units // tile,),
         in_specs=[cols, cols],
-        out_specs=pl.BlockSpec((tile, toks), lambda i: (i, 0)),
-        out_shape=jax.ShapeDtypeStruct((units, toks), BF16),
+        out_specs=[pl.BlockSpec((tile, toks), lambda i: (i, 0)), cols, cols],
+        out_shape=[
+            jax.ShapeDtypeStruct((units, toks), BF16),
+            jax.ShapeDtypeStruct((toks, units), BF16),
+            jax.ShapeDtypeStruct((toks, units), BF16),
+        ],
         compiler_params=params(),
         cost_estimate=SMALL,
         name="hidden",
@@ -101,7 +109,7 @@
     return pl.pallas_call(
         functools.partial(arrange_body, n),
         in_specs=[pl.BlockSpec(memory_space=pltpu.SMEM)] + [ANY] * (n + 1),
-        out_specs=ANY,
+        out_specs=pl.BlockSpec(memory_space=pltpu.VMEM),
         out_shape=jax.ShapeDtypeStruct((n,) + blocks[0].shape, BF16),
         scratch_shapes=[pltpu.SemaphoreType.DMA((n,))],
         compiler_params=params(),
@@ -111,7 +119,7 @@
 
 
 def grads_body(
-    offs_ref, own_ref, other_ref, w_ref, gate_ref, up_ref, order_ref, gg_ref, gu_ref, piece
+    offs_ref, own_ref, other_ref, w_ref, by_gate_ref, by_up_ref, order_ref, gg_ref, gu_ref, piece
 ):
     n, toks, width = own_ref.shape
 
@@ -123,14 +131,11 @@
                 piece[:, pl.ds(place, width)] = ref[j]
 
     total = dot_nt(piece[...], w_ref[...])
-    gate = gate_ref[...].astype(F32)
-    up = up_ref[...].astype(F32)
-    sig = jax.nn.sigmoid(gate)
-    gg_ref[...] = (total * up * sig * (1.0 + gate * (1.0 - sig))).astype(BF16)
-    gu_ref[...] = (total * (gate * sig)).astype(BF16)
-
-
-def grads(offs, own, other, weight, gate, up, order):
+    gg_ref[...] = (total * by_gate_ref[...]).astype(BF16)
+    gu_ref[...] = (total * by_up_ref[...]).astype(BF16)
+
+
+def grads(offs, own, other, weight, by_gate, by_up, order):
     n, toks, width = own.shape
     units, feats = weight.shape
     tile = 256
@@ -148,13 +153,9 @@
         ),
         out_shape=(out, out),
         compiler_params=params(),
-        cost_estimate=pl.CostEstimate(
-            flops=2 * toks * units * feats,
-            bytes_accessed=2 * (units * feats + toks * feats + 4 * toks * units),
-            transcendentals=toks * units,
-        ),
+        cost_estimate=SMALL,
         name="grads",
-    )(offs, own, other, weight, gate, up, order)
+    )(offs, own, other, weight, by_gate, by_up, order)
 
 
 def wgrad_body(offs_ref, hid_ref, own_ref, other_ref, order_ref, out_ref, cols):
@@ -272,7 +273,7 @@
 
 
 def line_body(rows, n, assign_ref, *refs):
-    hid, grad, (order_ref, out_ref) = refs[:n], refs[n : 2 * n], refs[2 * n :]
+    hid, grad, out_ref = refs[:n], refs[n : 2 * n], refs[-1]
     hid_sum = sum(ref[...] for ref in hid)
     grad_sum = sum(ref[...] for ref in grad)
     by_tok = jnp.sum(hid_sum * grad_sum, axis=0, keepdims=True)
@@ -292,13 +293,13 @@
     vmem = pl.BlockSpec(memory_space=pltpu.VMEM)
     return pl.pallas_call(
         functools.partial(line_body, rows, n),
-        in_specs=[pl.BlockSpec(memory_space=pltpu.SMEM)] + [vmem] * (2 * n) + [ANY],
+        in_specs=[pl.BlockSpec(memory_space=pltpu.SMEM)] + [vmem] * (2 * n) + [ANY] * len(order),
         out_specs=vmem,
         out_shape=jax.ShapeDtypeStruct((copies, 128), F32),
         compiler_params=params(),
         cost_estimate=SMALL,
         name="score_line",
-    )(assign, *hid, *grad, order)
+    )(assign, *hid, *grad, *order)
 
 
 def per_device(gate_act, up_act, out_grad, down_weight, val_hidden, val_grad, assign):
@@ -323,7 +324,8 @@
     far = swap(out_grad, "dp", 2)
     near = swap(out_grad, "dp", 1)
     first = after(first, others[0], far, near)
-    hidden = after(hidden_units(gate_act, up_act), first)
+    hidden, by_gate, by_up = hidden_units(gate_act, up_act)
+    hidden = after(hidden, first)
     grad_dp = [out_grad, near, far, swap(far, "dp", 1)]
     far = swap(hidden, "dp", 2)
     near = swap(hidden, "dp", 1)
@@ -336,30 +338,29 @@
     for _ in range(n_out - 2):
         others.append(swap(ring[-1], "fsdp", 1))
         ring.append(after(shift(ring[-1], "fsdp", 2), others[-1], away))
-    others.append(swap(ring[-1], "fsdp", 1))
+    others.append(shift(others[-1], "fsdp", 2))
 
     far = after(far, ring[-1])
     hid_dp = [hidden, near, far, swap(far, "dp", 1)]
     own = arrange(at, ring, far, "own_features")
     own_cols = lax.all_to_all(own, "dp", split_axis=0, concat_axis=0, tiled=True)
-    grad_pair = pair_sum(outer_at, grad_kept, grad_came, own, "grad_pair")
-    grad_sums = spread(grad_pair)
-
     hid_kept, away, hid_all = gram_call(
-        hidden_gram_body, inner_at, tok_offs, [*hid_dp, val_hidden], grad_pair[0], n_fs,
+        hidden_gram_body, inner_at, tok_offs, [*hid_dp, val_hidden], own, n_fs,
         [jax.ShapeDtypeStruct((units, total), BF16)], "hidden_gram",
     )
     hid_came = swap(away, "fsdp", 1)
     other = arrange(at, others, away, "other_features")
     other_cols = lax.all_to_all(other, "dp", split_axis=0, concat_axis=0, tiled=True)
-    hid_pair = pair_sum(outer_at, hid_kept, hid_came, other, "hidden_pair")
+    grad_pair = pair_sum(outer_at, grad_kept, grad_came, other, "grad_pair")
+    grad_sums = spread(grad_pair)
+    hid_pair = pair_sum(outer_at, hid_kept, hid_came, grad_pair[0], "hidden_pair")
     hid_sums = spread(hid_pair)
 
     offs = (jnp.stack([inner, 1 - inner]) * width).astype(jnp.int32)
-    grad_gate, grad_up = grads(offs, own, other, down_weight, gate_act, up_act, hid_pair[0])
+    grad_gate, grad_up = grads(offs, own, other, down_weight, by_gate, by_up, hid_pair[0])
 
     mine = score_line(
-        assign, hid_sums, grad_sums, grad_up, n_dp * rows_here, n_dp * n_fs
+        assign, hid_sums, grad_sums, [grad_up, other_cols], n_dp * rows_here, n_dp * n_fs
     )
     every = lax.all_to_all(
         mine, ("dp", "fsdp"), split_axis=0, concat_axis=0, tiled=True

time: 241 us -> 188 us (0.78)
  Pallas kernels: 99.9 us -> 44.4 us
  waiting for transfers between devices: 80.2 us -> 62.9 us
  blocking collectives: 11.2 us -> 27.6 us
  local copies, waits for them, and re-layouts: 20.1 us -> 23.5 us
    pallas_call x2, Pallas kernels: 62.9 us -> 5.87 us  [arrange(): pl.pallas_call(functools.partial(arrange_body, n), in_specs=[pl.BlockSpec...]
    all_to_all x1, waiting for transfers between devices: 22.7 us -> 0.01 us  [per_device(): lax.all_to_all(mine, ('dp', 'fsdp'), split_axis=0, concat_axis=0, tiled=T...]
    all_to_all x1, blocking collectives: 11.2 us -> 27.6 us  [per_device(): lax.all_to_all(other, 'dp', split_axis=0, concat_axis=0, tiled=True)]
    unnamed x63 -> x79, local copies, waits for them, and re-layouts: 19.9 us -> 23.2 us
    ppermute x9 -> x10, waiting for transfers between devices: 19.3 us -> 22.1 us  [shift(): return lax.ppermute(x, axis, [(s, (s + k) % n) for s in range(n)])]
    ppermute x12 -> x11, waiting for transfers between devices: 38.2 us -> 40.8 us  [swap(): return lax.ppermute(x, axis, [(s, s ^ k) for s in range(n)])]
    ppermute x12 -> x11, starting transfers between devices: 9.79 us -> 9.26 us  [swap(): return lax.ppermute(x, axis, [(s, s ^ k) for s in range(n)])]
    ppermute x9 -> x10, starting transfers between devices: 9.35 us -> 9.24 us  [shift(): return lax.ppermute(x, axis, [(s, (s + k) % n) for s in range(n)])]
  transfers between devices with their start and end apart: 23 -> 23, of which waited for: 10 -> 11; matrix products, arithmetic and copies ran while one was open for 1% -> 0% of each run, Pallas kernels for 37% -> 23%
where the time goes in v7:
time: 188 us; the launch traced here: 187 us
  waiting for transfers between devices  62.9 us (33%)
  Pallas kernels  44.4 us (24%)
  blocking collectives  27.6 us (15%)
  starting transfers between devices  26.6 us (14%)
  local copies, waits for them, and re-layouts  23.5 us (12%)
    ppermute x11, waiting for transfers between devices, swap(): return lax.ppermute(x, axis, [(s, s ^ k) for s in range(n)])  40.8 us
    all_to_all x1, blocking collectives, per_device(): lax.all_to_all(other, 'dp', split_axis=0, concat_axis=0, tiled=True)  27.6 us
    unnamed x79, local copies, waits for them, and re-layouts  23.2 us
    ppermute x10, waiting for transfers between devices, shift(): return lax.ppermute(x, axis, [(s, (s + k) % n) for s in range(n)])  22.1 us
    pallas_call x1, Pallas kernels, grads(): pl.pallas_call(grads_body, grid_spec=pltpu.PrefetchScalarGridSpec(num_sca...  14.7 us
    pallas_call x1, Pallas kernels, wgrad(): pl.pallas_call(wgrad_body, grid_spec=pltpu.PrefetchScalarGridSpec(num_sca...  11.3 us
    ppermute x11, starting transfers between devices, swap(): return lax.ppermute(x, axis, [(s, s ^ k) for s in range(n)])  9.26 us
    ppermute x10, starting transfers between devices, shift(): return lax.ppermute(x, axis, [(s, (s + k) % n) for s in range(n)])  9.24 us
  transfers between devices with their start and end apart: 23, of which 11 were waited for; matrix products, arithmetic and copies ran while one was open for 0% of the time, Pallas kernels for 23%

profile of v7, /device:TPU:0, one launch (start us, length us, event | category | flops | bytes accessed | tf_op | source)
XLA Modules:
  0.0 186.6 jit_solution(13167600233387603709)
XLA Ops:
  0.6 3.0 %collective-permute-start.2 = (bf16[384,640]{1,0:T(8,128)(2,1)}, bf16[384,640]{1,0:T(8,128)(2,1)S(1)}, u32[]{:S(2)}, u32[]{:S(2)}) collective-permute-start(bf16[384,640]{1,0:T(8,128)(2,1)} %refs_0_.3), channel_id=1, source_target_pairs={{0,16},{8,24},{16,0},{24,8},{1,17},{9,25},{17,1},{25,9},{2,18},{10... | collective-permute-start | bytes 1474568 | tf_op jit(solution)/shard_map/ppermute | solution.py:30
  9.4 2.0 %hidden.1 = (bf16[1792,384]{1,0:T(8,128)(2,1)S(1)}, bf16[384,1792]{1,0:T(8,128)(2,1)S(1)}, bf16[384,1792]{1,0:T(8,128)(2,1)S(1)}) custom-call(bf16[384,1792]{1,0:T(8,128)(2,1)S(1)} %copy-done.20, bf16[384,1792]{1,0:T(8,128)(2,1)S(1)} %copy-done.21), custom_call_target="tpu_custom_call" | custom-call | flops 1024 | bytes 1024 | tf_op jit(solution)/shard_map/hidden/pallas_call | solution.py:80
  16.6 4.3 %collective-permute-done.refs_0_ = bf16[384,640]{1,0:T(8,128)(2,1)S(1)} collective-permute-done((bf16[384,640]{1,0:T(8,128)(2,1)}, bf16[384,640]{1,0:T(8,128)(2,1)S(1)}, u32[]{:S(2)}, u32[]{:S(2)}) %collective-permute-start) | collective-permute-done | bytes 491552 | tf_op jit(solution)/shard_map/ppermute | solution.py:35
  25.7 2.1 %grad_gram.1 = (f32[4,32,1536]{2,1,0:T(8,128)S(1)}, f32[4,32,1536]{2,1,0:T(8,128)S(1)}) custom-call(s32[1]{0:T(128)} %bitcast.inner_ref, s32[4]{0:T(128)S(1)} %xor_multiply_fusion.offs_ref, bf16[384,640]{1,0:T(8,128)(2,1)S(1)} %copy-done.17, bf16[384,640]{1,0:T(8,128)(2,1)S(1)} %copy-done.14, bf16[384,640]{1,0:T(8,128)(2,1)S(1)} %copy-done.12, ...), custom_call_target="tpu_custom_call" | custom-call | flops 1024 | bytes 1024 | tf_op jit(solution)/shard_map/grad_gram/pallas_call | solution.py:239
  29.6 6.8 %collective-permute-done.5.refs_1_ = bf16[384,640]{1,0:T(8,128)(2,1)} collective-permute-done((bf16[384,640]{1,0:T(8,128)(2,1)S(1)}, bf16[384,640]{1,0:T(8,128)(2,1)}, u32[]{:S(2)}, u32[]{:S(2)}) %collective-permute-start.5) | collective-permute-done | bytes 491552 | tf_op jit(solution)/shard_map/ppermute | solution.py:30
  36.4 2.1 %collective-permute-done.4.refs_0_ = bf16[384,640]{1,0:T(8,128)(2,1)} collective-permute-done((bf16[384,640]{1,0:T(8,128)(2,1)S(1)}, bf16[384,640]{1,0:T(8,128)(2,1)}, u32[]{:S(2)}, u32[]{:S(2)}) %collective-permute-start.4) | collective-permute-done | bytes 491552 | tf_op jit(solution)/shard_map/ppermute | solution.py:35
  40.0 13.0 %collective-permute-done.7.refs_0_ = bf16[384,640]{1,0:T(8,128)(2,1)} collective-permute-done((bf16[384,640]{1,0:T(8,128)(2,1)}, bf16[384,640]{1,0:T(8,128)(2,1)}, u32[]{:S(2)}, u32[]{:S(2)}) %collective-permute-start.7) | collective-permute-done | bytes 491552 | tf_op jit(solution)/shard_map/ppermute | solution.py:35
  57.3 3.7 %own_features.1.refs_5_.own_ref = bf16[4,384,640]{2,1,0:T(8,128)(2,1)} custom-call(s32[4]{0:T(128)S(1)} %and_select_fusion.at_ref, bf16[384,640]{1,0:T(8,128)(2,1)S(1)} %copy-done.18, bf16[384,640]{1,0:T(8,128)(2,1)S(1)} %copy-done.4, bf16[384,640]{1,0:T(8,128)(2,1)} %after.6.refs_2_, bf16[384,640]{1,0:T(8,128)(2,1)} %after.7.refs_1_.refs_3_, ...), custom_call_target="tpu_custom_call" | custom-call | flops 1024 | bytes 1024 | tf_op jit(solution)/shard_map/own_features/pallas_call | solution.py:109
  61.0 4.5 %hidden_gram.1 = (f32[4,32,1536]{2,1,0:T(8,128)S(1)}, f32[4,32,1536]{2,1,0:T(8,128)}, bf16[1792,1536]{1,0:T(8,128)(2,1)S(1)}) custom-call(s32[1]{0:T(128)} %bitcast.inner_ref, s32[4]{0:T(128)S(1)} %xor_multiply_fusion.offs_ref, bf16[1792,384]{1,0:T(8,128)(2,1)S(1)} %copy-done.8, bf16[1792,384]{1,0:T(8,128)(2,1)} %collective-permute-done.11.refs_1_, ...), custom_call_target="tpu_custom_call" | custom-call | flops 1024 | bytes 1024 | tf_op jit(solution)/shard_map/hidden_gram/pallas_call | solution.py:239
  65.5 2.4 %copy-done.37 = bf16[1792,1536]{1,0:T(8,128)(2,1)} copy-done((bf16[1792,1536]{1,0:T(8,128)(2,1)}, bf16[1792,1536]{1,0:T(8,128)(2,1)S(1)}, u32[]{:S(2)}) %copy-start.37) | copy-done | bytes 5505048
  67.9 2.8 %collective-permute-done.10.refs_3_ = bf16[384,640]{1,0:T(8,128)(2,1)} collective-permute-done((bf16[384,640]{1,0:T(8,128)(2,1)}, bf16[384,640]{1,0:T(8,128)(2,1)}, u32[]{:S(2)}, u32[]{:S(2)}) %collective-permute-start.10) | collective-permute-done | bytes 491552 | tf_op jit(solution)/shard_map/ppermute | solution.py:35
  70.7 2.2 %other_features.1.order_ref.other_ref = bf16[4,384,640]{2,1,0:T(8,128)(2,1)S(1)} custom-call(s32[4]{0:T(128)S(1)} %and_select_fusion.at_ref, bf16[384,640]{1,0:T(8,128)(2,1)S(1)} %copy-done.16, bf16[384,640]{1,0:T(8,128)(2,1)} %collective-permute-done.5.refs_1_, bf16[384,640]{1,0:T(8,128)(2,1)} %collective-permute-done.8.refs_1_.refs_2_, ...), custom_call_target="tpu_custom_call" | custom-call | flops 1024 | bytes 1024 | tf_op jit(solution)/shard_map/other_features/pallas_call | solution.py:109
  72.9 27.6 %all_to_all.19.refs_9_.other_ref = bf16[4,384,640]{2,1,0:T(8,128)(2,1)} all-to-all(bf16[4,384,640]{2,1,0:T(8,128)(2,1)S(1)} %other_features.1.order_ref.other_ref), channel_id=1, replica_groups=mesh['dp'=4,'fsdp'=8] {'dp'}, dimensions={0} | all-to-all | bytes 3932160 | tf_op jit(solution)/shard_map/all_to_all | solution.py:353
  100.5 4.6 %all-to-all-start = ((bf16[4,384,640]{2,1,0:T(8,128)(2,1)}), bf16[4,384,640]{2,1,0:T(8,128)(2,1)}, u32[]{:S(2)}, u32[]{:S(2)}) async-start(bf16[4,384,640]{2,1,0:T(8,128)(2,1)} %own_features.1.refs_5_.own_ref), calls=%async_computation | async-start | bytes 3932160 | tf_op jit(solution)/shard_map/all_to_all | solution.py:346
  107.2 18.3 %collective-permute-done.14.came_ref = f32[4,32,1536]{2,1,0:T(8,128)S(1)} collective-permute-done((f32[4,32,1536]{2,1,0:T(8,128)S(1)}, f32[4,32,1536]{2,1,0:T(8,128)S(1)}, u32[]{:S(2)}, u32[]{:S(2)}) %collective-permute-start.14) | collective-permute-done | bytes 786464 | tf_op jit(solution)/shard_map/ppermute | solution.py:30
  126.4 1.6 collective-permute-start.19
  128.0 2.2 %collective-permute-start.20 = (f32[32,1536]{1,0:T(8,128)}, f32[32,1536]{1,0:T(8,128)}, u32[]{:S(2)}, u32[]{:S(2)}) collective-permute-start(f32[32,1536]{1,0:T(8,128)} %get-tuple-element.40), channel_id=1, source_target_pairs={{0,6},{1,7},{2,0},{3,1},{4,2},{5,3},{6,4},{7,5},{8,14},{9,15},{10,... | collective-permute-start | bytes 589832 | tf_op jit(solution)/shard_map/ppermute | solution.py:35
  130.2 11.6 %collective-permute-done.13.came_ref = f32[4,32,1536]{2,1,0:T(8,128)S(1)} collective-permute-done((f32[4,32,1536]{2,1,0:T(8,128)}, f32[4,32,1536]{2,1,0:T(8,128)S(1)}, u32[]{:S(2)}, u32[]{:S(2)}) %collective-permute-start.13) | collective-permute-done | bytes 786464 | tf_op jit(solution)/shard_map/ppermute | solution.py:30
  145.7 2.2 %collective-permute-start.17 = (f32[32,1536]{1,0:T(8,128)}, f32[32,1536]{1,0:T(8,128)}, u32[]{:S(2)}, u32[]{:S(2)}) collective-permute-start(f32[32,1536]{1,0:T(8,128)} %get-tuple-element.37), channel_id=1, source_target_pairs={{0,6},{1,7},{2,0},{3,1},{4,2},{5,3},{6,4},{7,5},{8,14},{9,15},{10,... | collective-permute-start | bytes 589832 | tf_op jit(solution)/shard_map/ppermute | solution.py:35
  149.3 14.7 %grads.1 = (bf16[384,1792]{1,0:T(8,128)(2,1)}, bf16[384,1792]{1,0:T(8,128)(2,1)}) custom-call(s32[2]{0:T(128)S(1)} %add_multiply_fusion.offs_ref, bf16[4,384,640]{2,1,0:T(8,128)(2,1)} %own_features.1.refs_5_.own_ref, bf16[4,384,640]{2,1,0:T(8,128)(2,1)S(1)} %other_features.1.order_ref.other_ref, bf16[1792,5120]{1,0:T(8,128)(2,1)} %w_ref.1, ...), custom_call_target="tpu_custom_call" | custom-call | flops 1024 | bytes 1024 | tf_op jit(solution)/shard_map/grads/pallas_call | solution.py:144
  165.5 2.2 %score_line.1.order_ref = f32[32,128]{1,0:T(8,128)} custom-call(s32[3]{0:T(128)S(1)} %copy-done.36, f32[32,1536]{1,0:T(8,128)S(1)} %get-tuple-element.31.order_ref.refs_0_, f32[32,1536]{1,0:T(8,128)} %collective-permute-done.15.refs_1_, f32[32,1536]{1,0:T(8,128)} %collective-permute-done.16.refs_2_, f32[32,1536]{1,0:T(8,128)} %collective-permute-done.17.refs_3_, ...), custom_call_target="tpu_custom_call" | custom-call | flops 1024 | bytes 1024 | tf_op jit(solution)/shard_map/score_line/pallas_call | solution.py:294
  167.7 3.6 %all-to-all-start.2 = ((f32[32,1,128]{2,1,0:T(1,128)}), f32[32,1,128]{2,1,0:T(1,128)S(1)}, u32[]{:S(2)}, u32[]{:S(2)}) async-start(f32[32,1,128]{2,1,0:T(1,128)} %bitcast.4), calls=%async_computation.2 | async-start | bytes 32768 | tf_op jit(solution)/shard_map/all_to_all | solution.py:365
  171.3 2.6 %copy-done.38 = bf16[1792,1536]{1,0:T(8,128)(2,1)S(1)} copy-done((bf16[1792,1536]{1,0:T(8,128)(2,1)S(1)}, bf16[1792,1536]{1,0:T(8,128)(2,1)}, u32[]{:S(2)}) %copy-start.38) | copy-done | bytes 5505048
  173.8 11.3 %wgrad.1 = bf16[1792,1280]{1,0:T(8,128)(2,1)} custom-call(s32[2]{0:T(128)S(1)} %add_multiply_fusion.offs_ref, bf16[1792,1536]{1,0:T(8,128)(2,1)S(1)} %copy-done.38, bf16[4,384,640]{2,1,0:T(8,128)(2,1)} %all-to-all-done.own_ref, bf16[4,384,640]{2,1,0:T(8,128)(2,1)S(1)} %copy-done.6, f32[32,128]{1,0:T(8,128)} %score_line.1.order_ref), custom_call_target="tpu_custom_call" | custom-call | flops 7046430720 | bytes 14024704 | tf_op jit(solution)/shard_map/wgrad/pallas_call | solution.py:180
  (125 shorter events, 34.5 us)
Async XLA Ops:
  0.6 14.5 %collective-permute-start.2 = (bf16[384,640]{1,0:T(8,128)(2,1)}, bf16[384,640]{1,0:T(8,128)(2,1)S(1)}, u32[]{:S(2)}, u32[]{:S(2)}) collective-permute-start(bf16[384,640]{1,0:T(8,128)(2,1)} %refs_0_.3), channel_id=1, source_target_pairs={{0,16},{8,24},{16,0},{24,8},{1,17},{9,25},{17,1},{25,9},{2,18},{10... | collective-permute-start | bytes 1474568 | tf_op jit(solution)/shard_map/ppermute | solution.py:30
  3.7 12.9 %collective-permute-start.1 = (bf16[384,640]{1,0:T(8,128)(2,1)}, bf16[384,640]{1,0:T(8,128)(2,1)S(1)}, u32[]{:S(2)}, u32[]{:S(2)}) collective-permute-start(bf16[384,640]{1,0:T(8,128)(2,1)} %refs_0_.3), channel_id=1, source_target_pairs={{0,1},{1,0},{2,3},{3,2},{4,5},{5,4},{6,7},{7,6},{8,9},{9,8},{10,11... | collective-permute-start | bytes 1474568 | tf_op jit(solution)/shard_map/ppermute | solution.py:30
  5.2 11.4 %collective-permute-start.3 = (bf16[384,640]{1,0:T(8,128)(2,1)}, bf16[384,640]{1,0:T(8,128)(2,1)S(1)}, u32[]{:S(2)}, u32[]{:S(2)}) collective-permute-start(bf16[384,640]{1,0:T(8,128)(2,1)} %refs_0_.3), channel_id=1, source_target_pairs={{0,8},{8,0},{16,24},{24,16},{1,9},{9,1},{17,25},{25,17},{2,10},{10... | collective-permute-start | bytes 1474568 | tf_op jit(solution)/shard_map/ppermute | solution.py:30
  5.2 15.7 %collective-permute-start = (bf16[384,640]{1,0:T(8,128)(2,1)}, bf16[384,640]{1,0:T(8,128)(2,1)S(1)}, u32[]{:S(2)}, u32[]{:S(2)}) collective-permute-start(bf16[384,640]{1,0:T(8,128)(2,1)} %refs_0_.3), channel_id=1, source_target_pairs={{0,2},{1,3},{2,4},{3,5},{4,6},{5,7},{6,0},{7,1},{8,10},{9,11},{10,... | collective-permute-start | bytes 1474568 | tf_op jit(solution)/shard_map/ppermute | solution.py:35
  21.7 32.2 %collective-permute-start.9 = (bf16[1792,384]{1,0:T(8,128)(2,1)}, bf16[1792,384]{1,0:T(8,128)(2,1)S(1)}, u32[]{:S(2)}, u32[]{:S(2)}) collective-permute-start(bf16[1792,384]{1,0:T(8,128)(2,1)} %after.8.refs_0_), channel_id=1, source_target_pairs={{0,16},{8,24},{16,0},{24,8},{1,17},{9,25},{17,1},{25,9},{2,18},{10... | collective-permute-start | bytes 4128776 | tf_op jit(solution)/shard_map/ppermute | solution.py:30
  22.7 2.0 %collective-permute-start.6 = (bf16[384,640]{1,0:T(8,128)(2,1)S(1)}, bf16[384,640]{1,0:T(8,128)(2,1)}, u32[]{:S(2)}, u32[]{:S(2)}) collective-permute-start(bf16[384,640]{1,0:T(8,128)(2,1)S(1)} %copy-done.12), channel_id=1, source_target_pairs={{0,8},{8,0},{16,24},{24,16},{1,9},{9,1},{17,25},{25,17},{2,10},{10... | collective-permute-start | bytes 1474568 | tf_op jit(solution)/shard_map/ppermute | solution.py:30
  22.8 13.6 %collective-permute-start.5 = (bf16[384,640]{1,0:T(8,128)(2,1)S(1)}, bf16[384,640]{1,0:T(8,128)(2,1)}, u32[]{:S(2)}, u32[]{:S(2)}) collective-permute-start(bf16[384,640]{1,0:T(8,128)(2,1)S(1)} %copy-done.4), channel_id=1, source_target_pairs={{0,1},{1,0},{2,3},{3,2},{4,5},{5,4},{6,7},{7,6},{8,9},{9,8},{10,11... | collective-permute-start | bytes 1474568 | tf_op jit(solution)/shard_map/ppermute | solution.py:30
  23.4 15.1 %collective-permute-start.4 = (bf16[384,640]{1,0:T(8,128)(2,1)S(1)}, bf16[384,640]{1,0:T(8,128)(2,1)}, u32[]{:S(2)}, u32[]{:S(2)}) collective-permute-start(bf16[384,640]{1,0:T(8,128)(2,1)S(1)} %copy-done.4), channel_id=1, source_target_pairs={{0,2},{1,3},{2,4},{3,5},{4,6},{5,7},{6,0},{7,1},{8,10},{9,11},{10,... | collective-permute-start | bytes 1474568 | tf_op jit(solution)/shard_map/ppermute | solution.py:35
  38.5 14.5 %collective-permute-start.7 = (bf16[384,640]{1,0:T(8,128)(2,1)}, bf16[384,640]{1,0:T(8,128)(2,1)}, u32[]{:S(2)}, u32[]{:S(2)}) collective-permute-start(bf16[384,640]{1,0:T(8,128)(2,1)} %after.6.refs_2_), channel_id=1, source_target_pairs={{0,2},{1,3},{2,4},{3,5},{4,6},{5,7},{6,0},{7,1},{8,10},{9,11},{10,... | collective-permute-start | bytes 1474568 | tf_op jit(solution)/shard_map/ppermute | solution.py:35
  38.5 14.5 %collective-permute-start.8 = (bf16[384,640]{1,0:T(8,128)(2,1)}, bf16[384,640]{1,0:T(8,128)(2,1)}, u32[]{:S(2)}, u32[]{:S(2)}) collective-permute-start(bf16[384,640]{1,0:T(8,128)(2,1)} %after.6.refs_2_), channel_id=1, source_target_pairs={{0,1},{1,0},{2,3},{3,2},{4,5},{5,4},{6,7},{7,6},{8,9},{9,8},{10,11... | collective-permute-start | bytes 1474568 | tf_op jit(solution)/shard_map/ppermute | solution.py:30
  40.0 21.0 %collective-permute-start.11 = (bf16[1792,384]{1,0:T(8,128)(2,1)S(1)}, bf16[1792,384]{1,0:T(8,128)(2,1)}, u32[]{:S(2)}, u32[]{:S(2)}) collective-permute-start(bf16[1792,384]{1,0:T(8,128)(2,1)S(1)} %copy-done.8), channel_id=1, source_target_pairs={{0,8},{8,0},{16,24},{24,16},{1,9},{9,1},{17,25},{25,17},{2,10},{10... | collective-permute-start | bytes 4128776 | tf_op jit(solution)/shard_map/ppermute | solution.py:30
  54.9 6.1 %collective-permute-start.12 = (bf16[1792,384]{1,0:T(8,128)(2,1)}, bf16[1792,384]{1,0:T(8,128)(2,1)S(1)}, u32[]{:S(2)}, u32[]{:S(2)}) collective-permute-start(bf16[1792,384]{1,0:T(8,128)(2,1)} %after.9.refs_4_.refs_2_), channel_id=1, source_target_pairs={{0,8},{8,0},{16,24},{24,16},{1,9},{9,1},{17,25},{25,17},{2,10},{10... | collective-permute-start | bytes 4128776 | tf_op jit(solution)/shard_map/ppermute | solution.py:30
  54.9 15.7 %collective-permute-start.10 = (bf16[384,640]{1,0:T(8,128)(2,1)}, bf16[384,640]{1,0:T(8,128)(2,1)}, u32[]{:S(2)}, u32[]{:S(2)}) collective-permute-start(bf16[384,640]{1,0:T(8,128)(2,1)} %collective-permute-done.8.refs_1_.refs_2_), channel_id=1, source_target_pairs={{0,2},{1,3},{2,4},{3,5},{4,6},{5,7},{6,0},{7,1},{8,10},{9,11},{10,... | collective-permute-start | bytes 1474568 | tf_op jit(solution)/shard_map/ppermute | solution.py:35
  100.5 25.0 %copy-start.32 = (f32[4,32,1536]{2,1,0:T(8,128)S(1)}, f32[4,32,1536]{2,1,0:T(8,128)}, u32[]{:S(2)}) copy-start(f32[4,32,1536]{2,1,0:T(8,128)} %copy-done.31) | copy-start | bytes 2359300
  100.5 67.2 %all-to-all-start = ((bf16[4,384,640]{2,1,0:T(8,128)(2,1)}), bf16[4,384,640]{2,1,0:T(8,128)(2,1)}, u32[]{:S(2)}, u32[]{:S(2)}) async-start(bf16[4,384,640]{2,1,0:T(8,128)(2,1)} %own_features.1.refs_5_.own_ref), calls=%async_computation | async-start | bytes 3932160 | tf_op jit(solution)/shard_map/all_to_all | solution.py:346
  105.1 20.4 %collective-permute-start.14 = (f32[4,32,1536]{2,1,0:T(8,128)S(1)}, f32[4,32,1536]{2,1,0:T(8,128)S(1)}, u32[]{:S(2)}, u32[]{:S(2)}) collective-permute-start(f32[4,32,1536]{2,1,0:T(8,128)S(1)} %copy-done.10), channel_id=1, source_target_pairs={{0,1},{1,0},{2,3},{3,2},{4,5},{5,4},{6,7},{7,6},{8,9},{9,8},{10,11... | collective-permute-start | bytes 2359304 | tf_op jit(solution)/shard_map/ppermute | solution.py:30
  105.8 36.0 %collective-permute-start.13 = (f32[4,32,1536]{2,1,0:T(8,128)}, f32[4,32,1536]{2,1,0:T(8,128)S(1)}, u32[]{:S(2)}, u32[]{:S(2)}) collective-permute-start(f32[4,32,1536]{2,1,0:T(8,128)} %get-tuple-element.25.refs_4_), channel_id=1, source_target_pairs={{0,1},{1,0},{2,3},{3,2},{4,5},{5,4},{6,7},{7,6},{8,9},{9,8},{10,11... | collective-permute-start | bytes 2359304 | tf_op jit(solution)/shard_map/ppermute | solution.py:30
  126.4 18.7 %collective-permute-start.18 = (f32[32,1536]{1,0:T(8,128)S(1)}, f32[32,1536]{1,0:T(8,128)S(1)}, u32[]{:S(2)}, u32[]{:S(2)}) collective-permute-start(f32[32,1536]{1,0:T(8,128)S(1)} %get-tuple-element.38), channel_id=1, source_target_pairs={{0,2},{1,3},{2,4},{3,5},{4,6},{5,7},{6,0},{7,1},{8,10},{9,11},{10,... | collective-permute-start | bytes 589832 | tf_op jit(solution)/shard_map/ppermute | solution.py:35
  126.4 37.7 %collective-permute-start.19 = (f32[32,1536]{1,0:T(8,128)}, f32[32,1536]{1,0:T(8,128)}, u32[]{:S(2)}, u32[]{:S(2)}) collective-permute-start(f32[32,1536]{1,0:T(8,128)} %get-tuple-element.39), channel_id=1, source_target_pairs={{0,4},{1,5},{2,6},{3,7},{4,0},{5,1},{6,2},{7,3},{8,12},{9,13},{10,... | collective-permute-start | bytes 589832 | tf_op jit(solution)/shard_map/ppermute | solution.py:35
  128.0 36.1 %collective-permute-start.20 = (f32[32,1536]{1,0:T(8,128)}, f32[32,1536]{1,0:T(8,128)}, u32[]{:S(2)}, u32[]{:S(2)}) collective-permute-start(f32[32,1536]{1,0:T(8,128)} %get-tuple-element.40), channel_id=1, source_target_pairs={{0,6},{1,7},{2,0},{3,1},{4,2},{5,3},{6,4},{7,5},{8,14},{9,15},{10,... | collective-permute-start | bytes 589832 | tf_op jit(solution)/shard_map/ppermute | solution.py:35
  143.4 20.7 %collective-permute-start.15 = (f32[32,1536]{1,0:T(8,128)}, f32[32,1536]{1,0:T(8,128)}, u32[]{:S(2)}, u32[]{:S(2)}) collective-permute-start(f32[32,1536]{1,0:T(8,128)} %get-tuple-element.35), channel_id=1, source_target_pairs={{0,2},{1,3},{2,4},{3,5},{4,6},{5,7},{6,0},{7,1},{8,10},{9,11},{10,... | collective-permute-start | bytes 589832 | tf_op jit(solution)/shard_map/ppermute | solution.py:35
  143.4 20.7 %collective-permute-start.16 = (f32[32,1536]{1,0:T(8,128)}, f32[32,1536]{1,0:T(8,128)}, u32[]{:S(2)}, u32[]{:S(2)}) collective-permute-start(f32[32,1536]{1,0:T(8,128)} %get-tuple-element.36), channel_id=1, source_target_pairs={{0,4},{1,5},{2,6},{3,7},{4,0},{5,1},{6,2},{7,3},{8,12},{9,13},{10,... | collective-permute-start | bytes 589832 | tf_op jit(solution)/shard_map/ppermute | solution.py:35
  145.7 18.4 %collective-permute-start.17 = (f32[32,1536]{1,0:T(8,128)}, f32[32,1536]{1,0:T(8,128)}, u32[]{:S(2)}, u32[]{:S(2)}) collective-permute-start(f32[32,1536]{1,0:T(8,128)} %get-tuple-element.37), channel_id=1, source_target_pairs={{0,6},{1,7},{2,0},{3,1},{4,2},{5,3},{6,4},{7,5},{8,14},{9,15},{10,... | collective-permute-start | bytes 589832 | tf_op jit(solution)/shard_map/ppermute | solution.py:35
  167.7 17.4 %all-to-all-start.2 = ((f32[32,1,128]{2,1,0:T(1,128)}), f32[32,1,128]{2,1,0:T(1,128)S(1)}, u32[]{:S(2)}, u32[]{:S(2)}) async-start(f32[32,1,128]{2,1,0:T(1,128)} %bitcast.4), calls=%async_computation.2 | async-start | bytes 32768 | tf_op jit(solution)/shard_map/all_to_all | solution.py:365
  (38 other events, 184.6 us)

commit v8 on v7

--- a/solution.py
+++ b/solution.py
@@ -93,60 +93,60 @@
     )(gate, up)
 
 
-def arrange_body(n, at_ref, *refs):
-    blocks, (order_ref, out_ref, sems) = refs[:n], refs[n:]
-    copies = [
-        pltpu.make_async_copy(blocks[j], out_ref.at[at_ref[j]], sems.at[j]) for j in range(n)
-    ]
-    for copy in copies:
-        copy.start()
-    for copy in copies:
-        copy.wait()
-
-
-def arrange(at, blocks, order, name):
+def arrange_body(n, to_ref, *refs):
+    blocks, outs, sems = refs[:n], refs[-n - 1 : -1], refs[-1]
+    for j in range(n):
+        for k in range(n):
+
+            @pl.when(to_ref[j] == k)
+            def _():
+                pltpu.make_async_copy(blocks[j], outs[k], sems.at[j]).start()
+
+    for j in range(n):
+        pltpu.make_async_copy(blocks[j], outs[0], sems.at[j]).wait()
+
+
+def arrange(to, blocks, order, name):
     n = len(blocks)
     return pl.pallas_call(
         functools.partial(arrange_body, n),
-        in_specs=[pl.BlockSpec(memory_space=pltpu.SMEM)] + [ANY] * (n + 1),
-        out_specs=pl.BlockSpec(memory_space=pltpu.VMEM),
-        out_shape=jax.ShapeDtypeStruct((n,) + blocks[0].shape, BF16),
+        in_specs=[pl.BlockSpec(memory_space=pltpu.SMEM)] + [ANY] * (n + len(order)),
+        out_specs=[pl.BlockSpec(memory_space=pltpu.VMEM)] * n,
+        out_shape=[jax.ShapeDtypeStruct(blocks[0].shape, BF16)] * n,
         scratch_shapes=[pltpu.SemaphoreType.DMA((n,))],
         compiler_params=params(),
         cost_estimate=SMALL,
         name=name,
-    )(at, *blocks, order)
-
-
-def grads_body(
-    offs_ref, own_ref, other_ref, w_ref, by_gate_ref, by_up_ref, order_ref, gg_ref, gu_ref, piece
-):
-    n, toks, width = own_ref.shape
+    )(to, *blocks, *order)
+
+
+def grads_body(n, offs_ref, *refs):
+    blocks, (w_ref, by_gate_ref, by_up_ref, order_ref, gg_ref, gu_ref, piece) = refs[:n], refs[n:]
+    width = blocks[0].shape[1]
 
     @pl.when(pl.program_id(0) == 0)
     def _():
-        for half, ref in enumerate((own_ref, other_ref)):
-            for j in range(n):
-                place = pl.multiple_of(offs_ref[half] + 2 * j * width, 128)
-                piece[:, pl.ds(place, width)] = ref[j]
+        for j in range(n):
+            piece[:, pl.ds(pl.multiple_of(offs_ref[j], 128), width)] = blocks[j][...]
 
     total = dot_nt(piece[...], w_ref[...])
     gg_ref[...] = (total * by_gate_ref[...]).astype(BF16)
     gu_ref[...] = (total * by_up_ref[...]).astype(BF16)
 
 
-def grads(offs, own, other, weight, by_gate, by_up, order):
-    n, toks, width = own.shape
+def grads(offs, blocks, weight, by_gate, by_up, order):
+    n = len(blocks)
+    toks, width = blocks[0].shape
     units, feats = weight.shape
     tile = 256
     cols = pl.BlockSpec((toks, tile), lambda i, _: (0, i))
     out = jax.ShapeDtypeStruct((toks, units), BF16)
     return pl.pallas_call(
-        grads_body,
+        functools.partial(grads_body, n),
         grid_spec=pltpu.PrefetchScalarGridSpec(
             num_scalar_prefetch=1,
             grid=(units // tile,),
-            in_specs=[whole(own.shape)] * 2
+            in_specs=[whole((toks, width))] * n
             + [pl.BlockSpec((tile, feats), lambda i, _: (i, 0)), cols, cols, ANY],
             out_specs=[cols, cols],
             scratch_shapes=[pltpu.VMEM((toks, feats), BF16)],
@@ -155,37 +155,40 @@
         compiler_params=params(),
         cost_estimate=SMALL,
         name="grads",
-    )(offs, own, other, weight, by_gate, by_up, order)
-
-
-def wgrad_body(offs_ref, hid_ref, own_ref, other_ref, order_ref, out_ref, cols):
-    n, toks, width = own_ref.shape
+    )(offs, *blocks, weight, by_gate, by_up, order)
+
+
+def wgrad_body(n, offs_ref, toks_ref, hid_ref, *refs):
+    blocks, (order_ref, out_ref, cols) = refs[: 2 * n], refs[2 * n :]
+    toks, width = blocks[0].shape
 
     @pl.when(pl.program_id(0) == 0)
     def _():
-        for half, ref in enumerate((own_ref, other_ref)):
+        for half in range(2):
             place = pl.ds(pl.multiple_of(offs_ref[half], 128), width)
             for k in range(n):
-                cols[k * toks : (k + 1) * toks, place] = ref[k]
+                rows = pl.ds(pl.multiple_of(toks_ref[k], 128), toks)
+                cols[rows, place] = blocks[half * n + k][...]
 
     out_ref[...] = lax.dot_general(
         hid_ref[...], cols[...], (((1,), (0,)), ((), ())), preferred_element_type=F32
     ).astype(BF16)
 
 
-def wgrad(offs, hid, own, other, order):
+def wgrad(offs, tok_offs, hid, blocks, order):
     units, total = hid.shape
-    width = own.shape[2]
+    toks, width = blocks[0].shape
+    n = total // toks
     tile = units // 4
     return pl.pallas_call(
-        wgrad_body,
+        functools.partial(wgrad_body, n),
         grid_spec=pltpu.PrefetchScalarGridSpec(
-            num_scalar_prefetch=1,
+            num_scalar_prefetch=2,
             grid=(units // tile,),
-            in_specs=[pl.BlockSpec((tile, total), lambda i, _: (i, 0))]
-            + [whole(own.shape)] * 2
+            in_specs=[pl.BlockSpec((tile, total), lambda i, *_: (i, 0))]
+            + [whole((toks, width))] * (2 * n)
             + [ANY],
-            out_specs=pl.BlockSpec((tile, 2 * width), lambda i, _: (i, 0)),
+            out_specs=pl.BlockSpec((tile, 2 * width), lambda i, *_: (i, 0)),
             scratch_shapes=[pltpu.VMEM((total, 2 * width), BF16)],
         ),
         out_shape=jax.ShapeDtypeStruct((units, 2 * width), BF16),
@@ -196,7 +199,7 @@
             transcendentals=0,
         ),
         name="wgrad",
-    )(offs, hid, own, other, order)
+    )(offs, tok_offs, hid, *blocks, order)
 
 
 def put_slices(inner_ref, part, kept_ref, away_ref):
@@ -248,34 +251,36 @@
     )(inner, offs, *operands, order)
 
 
-def pair_body(n, outer_ref, kept_ref, came_ref, order_ref, *out_refs):
-    for step in range(n):
-        at = lax.rem(outer_ref[0] + step, n)
-        out_refs[step][...] = kept_ref[at] + came_ref[at]
-
-
-def pair_sum(outer, kept, came, order, name):
-    n, *size = kept.shape
+def pair_body(kept_ref, came_ref, *refs):
+    refs[-1][...] = kept_ref[...] + came_ref[...]
+
+
+def pair_sum(kept, came, order, name):
     vmem = pl.BlockSpec(memory_space=pltpu.VMEM)
     return pl.pallas_call(
-        functools.partial(pair_body, n),
-        in_specs=[pl.BlockSpec(memory_space=pltpu.SMEM), vmem, vmem, ANY],
-        out_specs=[vmem] * n,
-        out_shape=[jax.ShapeDtypeStruct(size, F32)] * n,
+        pair_body,
+        in_specs=[vmem, vmem] + [ANY] * len(order),
+        out_specs=vmem,
+        out_shape=jax.ShapeDtypeStruct(kept.shape, F32),
         compiler_params=params(),
         cost_estimate=SMALL,
         name=name,
-    )(outer, kept, came, order)
-
-
-def spread(slices):
-    return [x if j == 0 else shift(x, "fsdp", 2 * j) for j, x in enumerate(slices)]
-
-
-def line_body(rows, n, assign_ref, *refs):
-    hid, grad, out_ref = refs[:n], refs[n : 2 * n], refs[-1]
-    hid_sum = sum(ref[...] for ref in hid)
-    grad_sum = sum(ref[...] for ref in grad)
+    )(kept, came, *order)
+
+
+def spread(pair):
+    n_fs = lax.axis_size("fsdp")
+    groups = [list(range(x, n_fs, 2)) for x in range(2)]
+    return lax.all_to_all(
+        pair, "fsdp", split_axis=0, concat_axis=0, axis_index_groups=groups, tiled=True
+    )
+
+
+def line_body(rows, assign_ref, hid_ref, grad_ref, *refs):
+    out_ref = refs[-1]
+    n = hid_ref.shape[0]
+    hid_sum = sum(hid_ref[j] for j in range(n))
+    grad_sum = sum(grad_ref[j] for j in range(n))
     by_tok = jnp.sum(hid_sum * grad_sum, axis=0, keepdims=True)
     size = by_tok.shape[1] // rows
     lane = lax.broadcasted_iota(jnp.int32, (1, 128), 1)
@@ -289,17 +294,16 @@
 
 
 def score_line(assign, hid, grad, order, rows, copies):
-    n = len(hid)
     vmem = pl.BlockSpec(memory_space=pltpu.VMEM)
     return pl.pallas_call(
-        functools.partial(line_body, rows, n),
-        in_specs=[pl.BlockSpec(memory_space=pltpu.SMEM)] + [vmem] * (2 * n) + [ANY] * len(order),
+        functools.partial(line_body, rows),
+        in_specs=[pl.BlockSpec(memory_space=pltpu.SMEM), vmem, vmem] + [ANY] * len(order),
         out_specs=vmem,
         out_shape=jax.ShapeDtypeStruct((copies, 128), F32),
         compiler_params=params(),
         cost_estimate=SMALL,
         name="score_line",
-    )(assign, *hid, *grad, *order)
+    )(assign, hid, grad, *order)
 
 
 def per_device(gate_act, up_act, out_grad, down_weight, val_hidden, val_grad, assign):
@@ -317,7 +321,7 @@
     at = (outer - jnp.arange(n_out, dtype=jnp.int32)) % n_out
     tok_offs = (d ^ jnp.arange(n_dp, dtype=jnp.int32)) * toks
     inner_at = inner.reshape(1).astype(jnp.int32)
-    outer_at = outer.reshape(1).astype(jnp.int32)
+    to = at ^ d
 
     first = shift(out_grad, "fsdp", 2)
     others = [swap(out_grad, "fsdp", 1)]
@@ -340,32 +344,36 @@
         ring.append(after(shift(ring[-1], "fsdp", 2), others[-1], away))
     others.append(shift(others[-1], "fsdp", 2))
 
+    def over_columns(blocks):
+        return [x if k == 0 else swap(x, "dp", k) for k, x in enumerate(blocks)]
+
     far = after(far, ring[-1])
     hid_dp = [hidden, near, far, swap(far, "dp", 1)]
-    own = arrange(at, ring, far, "own_features")
-    own_cols = lax.all_to_all(own, "dp", split_axis=0, concat_axis=0, tiled=True)
+    own = arrange(to, ring, [far], "own_features")
+    own_cols = over_columns(own)
     hid_kept, away, hid_all = gram_call(
-        hidden_gram_body, inner_at, tok_offs, [*hid_dp, val_hidden], own, n_fs,
+        hidden_gram_body, inner_at, tok_offs, [*hid_dp, val_hidden], own[0], n_fs,
         [jax.ShapeDtypeStruct((units, total), BF16)], "hidden_gram",
     )
     hid_came = swap(away, "fsdp", 1)
-    other = arrange(at, others, away, "other_features")
-    other_cols = lax.all_to_all(other, "dp", split_axis=0, concat_axis=0, tiled=True)
-    grad_pair = pair_sum(outer_at, grad_kept, grad_came, other, "grad_pair")
+    other = arrange(to, others, [away, grad_came], "other_features")
+    other_cols = over_columns(other)
+    grad_pair = pair_sum(grad_kept, grad_came, [other[0]], "grad_pair")
     grad_sums = spread(grad_pair)
-    hid_pair = pair_sum(outer_at, hid_kept, hid_came, grad_pair[0], "hidden_pair")
+    hid_pair = pair_sum(hid_kept, hid_came, [grad_pair, *own_cols], "hidden_pair")
     hid_sums = spread(hid_pair)
 
     offs = (jnp.stack([inner, 1 - inner]) * width).astype(jnp.int32)
-    grad_gate, grad_up = grads(offs, own, other, down_weight, by_gate, by_up, hid_pair[0])
+    places = (offs[:, None] + at[None, :] * (2 * width)).reshape(-1)
+    grad_gate, grad_up = grads(places, [*ring, *others], down_weight, by_gate, by_up, hid_pair)
 
     mine = score_line(
-        assign, hid_sums, grad_sums, [grad_up, other_cols], n_dp * rows_here, n_dp * n_fs
+        assign, hid_sums, grad_sums, [grad_up, *other_cols], n_dp * rows_here, n_dp * n_fs
     )
     every = lax.all_to_all(
         mine, ("dp", "fsdp"), split_axis=0, concat_axis=0, tiled=True
     ).reshape(n_dp, n_fs, 128)
-    weight_grad = wgrad(offs, hid_all, own_cols, other_cols, mine)
+    weight_grad = wgrad(offs, tok_offs, hid_all, [*own_cols, *other_cols], mine)
 
     rows = n_dp * rows_here
     scale = 1.0 / jnp.sqrt(F32(L) * VAL * FFW * D)

time: 188 us -> 175 us (0.931)
  blocking collectives: 27.6 us -> 0 us
  local copies, waits for them, and re-layouts: 23.5 us -> 40.5 us
  waiting for transfers between devices: 62.9 us -> 58.1 us
  starting transfers between devices: 26.6 us -> 30.1 us
    all_to_all x1 -> x0, blocking collectives: 27.6 us -> none  [per_device(): lax.all_to_all(other, 'dp', split_axis=0, concat_axis=0, tiled=True)]
    unnamed x79 -> x117, local copies, waits for them, and re-layouts: 23.2 us -> 40.2 us
    ppermute x10 -> x4, starting transfers between devices: 9.24 us -> 1.58 us  [shift(): return lax.ppermute(x, axis, [(s, (s + k) % n) for s in range(n)])]
    ppermute x11 -> x17, starting transfers between devices: 9.26 us -> 14.2 us  [swap(): return lax.ppermute(x, axis, [(s, s ^ k) for s in range(n)])]
    all_to_all x1 -> x2, starting transfers between devices: 4.57 us -> 9.17 us  [spread(): lax.all_to_all(pair, 'fsdp', split_axis=0, concat_axis=0, axis_index_grou...]
    ppermute x10 -> x4, waiting for transfers between devices: 22.1 us -> 18.7 us  [shift(): return lax.ppermute(x, axis, [(s, (s + k) % n) for s in range(n)])]
    ppermute x11 -> x17, waiting for transfers between devices: 40.8 us -> 39.3 us  [swap(): return lax.ppermute(x, axis, [(s, s ^ k) for s in range(n)])]
  transfers between devices with their start and end apart: 23 -> 24, of which waited for: 11 -> 11; matrix products, arithmetic and copies ran while one was open for 0% -> 0% of each run, Pallas kernels for 23% -> 21%
where the time goes in v8:
time: 175 us; the launch traced here: 174 us
  waiting for transfers between devices  58.1 us (33%)
  Pallas kernels  43.1 us (25%)
  local copies, waits for them, and re-layouts  40.5 us (23%)
  starting transfers between devices  30.1 us (17%)
    unnamed x117, local copies, waits for them, and re-layouts  40.2 us
    ppermute x17, waiting for transfers between devices, swap(): return lax.ppermute(x, axis, [(s, s ^ k) for s in range(n)])  39.3 us
    ppermute x4, waiting for transfers between devices, shift(): return lax.ppermute(x, axis, [(s, (s + k) % n) for s in range(n)])  18.7 us
    ppermute x17, starting transfers between devices, swap(): return lax.ppermute(x, axis, [(s, s ^ k) for s in range(n)])  14.2 us
    pallas_call x1, Pallas kernels, grads(): pl.pallas_call(functools.partial(grads_body, n), grid_spec=pltpu.Prefetch...  14.1 us
    pallas_call x1, Pallas kernels, wgrad(): pl.pallas_call(functools.partial(wgrad_body, n), grid_spec=pltpu.Prefetch...  11.1 us
    all_to_all x2, starting transfers between devices, spread(): lax.all_to_all(pair, 'fsdp', split_axis=0, concat_axis=0, axis_index_grou...  9.17 us
    pallas_call x2, Pallas kernels, gram_call(): pl.pallas_call(body, in_specs=[smem, smem] + [vmem] * len(operands) + [AN...  5.9 us
  transfers between devices with their start and end apart: 24, of which 11 were waited for; matrix products, arithmetic and copies ran while one was open for 0% of the time, Pallas kernels for 21%

profile of v8, /device:TPU:0, one launch (start us, length us, event | category | flops | bytes accessed | tf_op | source)
XLA Modules:
  0.0 173.6 jit_solution(8231216888837889126)
XLA Ops:
  0.6 3.0 %collective-permute-start.1 = (bf16[384,640]{1,0:T(8,128)(2,1)}, bf16[384,640]{1,0:T(8,128)(2,1)S(1)}, u32[]{:S(2)}, u32[]{:S(2)}) collective-permute-start(bf16[384,640]{1,0:T(8,128)(2,1)} %refs_0_.5), channel_id=1, source_target_pairs={{0,1},{1,0},{2,3},{3,2},{4,5},{5,4},{6,7},{7,6},{8,9},{9,8},{10,11... | collective-permute-start | bytes 1474568 | tf_op jit(solution)/shard_map/ppermute | solution.py:30
  9.4 2.0 %hidden.1 = (bf16[1792,384]{1,0:T(8,128)(2,1)S(1)}, bf16[384,1792]{1,0:T(8,128)(2,1)S(1)}, bf16[384,1792]{1,0:T(8,128)(2,1)S(1)}) custom-call(bf16[384,1792]{1,0:T(8,128)(2,1)S(1)} %copy-done.28, bf16[384,1792]{1,0:T(8,128)(2,1)S(1)} %copy-done.29), custom_call_target="tpu_custom_call" | custom-call | flops 1024 | bytes 1024 | tf_op jit(solution)/shard_map/hidden/pallas_call | solution.py:80
  16.6 4.2 %collective-permute-done.refs_0_ = bf16[384,640]{1,0:T(8,128)(2,1)S(1)} collective-permute-done((bf16[384,640]{1,0:T(8,128)(2,1)}, bf16[384,640]{1,0:T(8,128)(2,1)S(1)}, u32[]{:S(2)}, u32[]{:S(2)}) %collective-permute-start) | collective-permute-done | bytes 491552 | tf_op jit(solution)/shard_map/ppermute | solution.py:35
  26.4 2.3 %grad_gram.1 = (f32[4,32,1536]{2,1,0:T(8,128)S(1)}, f32[4,32,1536]{2,1,0:T(8,128)S(1)}) custom-call(s32[1]{0:T(128)} %bitcast.inner_ref, s32[4]{0:T(128)S(1)} %xor_multiply_fusion.offs_ref.toks_ref, bf16[384,640]{1,0:T(8,128)(2,1)S(1)} %copy-done.9, bf16[384,640]{1,0:T(8,128)(2,1)S(1)} %copy-done.20, bf16[384,640]{1,0:T(8,128)(2,1)} %collective-permute-done.2.refs_2_, ...), custom_call_target="tpu_custom_call" | custom-call | flops 1024 | bytes 1024 | tf_op jit(solution)/shard_map/grad_gram/pallas_call | solution.py:242
  30.5 5.3 %collective-permute-done.5.refs_1_.refs_5_ = bf16[384,640]{1,0:T(8,128)(2,1)S(1)} collective-permute-done((bf16[384,640]{1,0:T(8,128)(2,1)S(1)}, bf16[384,640]{1,0:T(8,128)(2,1)S(1)}, u32[]{:S(2)}, u32[]{:S(2)}) %collective-permute-start.5) | collective-permute-done | bytes 491552 | tf_op jit(solution)/shard_map/ppermute | solution.py:30
  35.8 2.1 %collective-permute-done.4.refs_0_ = bf16[384,640]{1,0:T(8,128)(2,1)S(1)} collective-permute-done((bf16[384,640]{1,0:T(8,128)(2,1)S(1)}, bf16[384,640]{1,0:T(8,128)(2,1)S(1)}, u32[]{:S(2)}, u32[]{:S(2)}) %collective-permute-start.4) | collective-permute-done | bytes 491552 | tf_op jit(solution)/shard_map/ppermute | solution.py:35
  40.1 12.5 %collective-permute-done.7.refs_0_ = bf16[384,640]{1,0:T(8,128)(2,1)S(1)} collective-permute-done((bf16[384,640]{1,0:T(8,128)(2,1)}, bf16[384,640]{1,0:T(8,128)(2,1)S(1)}, u32[]{:S(2)}, u32[]{:S(2)}) %collective-permute-start.7) | collective-permute-done | bytes 491552 | tf_op jit(solution)/shard_map/ppermute | solution.py:35
  58.2 2.0 %own_features.1 = (bf16[384,640]{1,0:T(8,128)(2,1)S(1)}, bf16[384,640]{1,0:T(8,128)(2,1)S(1)}, bf16[384,640]{1,0:T(8,128)(2,1)S(1)}, bf16[384,640]{1,0:T(8,128)(2,1)S(1)}) custom-call(s32[4]{0:T(128)S(1)} %broadcast_xor_fusion.to_ref, bf16[384,640]{1,0:T(8,128)(2,1)S(1)} %copy-done.9, bf16[384,640]{1,0:T(8,128)(2,1)S(1)} %copy-done.4, ...), custom_call_target="tpu_custom_call" | custom-call | flops 1024 | bytes 1024 | tf_op jit(solution)/shard_map/own_features/pallas_call | solution.py:111
  66.2 3.6 %hidden_gram.1 = (f32[4,32,1536]{2,1,0:T(8,128)S(1)}, f32[4,32,1536]{2,1,0:T(8,128)S(1)}, bf16[1792,1536]{1,0:T(8,128)(2,1)S(1)}) custom-call(s32[1]{0:T(128)} %bitcast.inner_ref, s32[4]{0:T(128)S(1)} %xor_multiply_fusion.offs_ref.toks_ref, bf16[1792,384]{1,0:T(8,128)(2,1)S(1)} %copy-done.8, bf16[1792,384]{1,0:T(8,128)(2,1)} %collective-permute-done.10.refs_1_, ...), custom_call_target="tpu_custom_call" | custom-call | flops 1024 | bytes 1024 | tf_op jit(solution)/shard_map/hidden_gram/pallas_call | solution.py:242
  69.9 2.4 %copy-done.50 = bf16[1792,1536]{1,0:T(8,128)(2,1)} copy-done((bf16[1792,1536]{1,0:T(8,128)(2,1)}, bf16[1792,1536]{1,0:T(8,128)(2,1)S(1)}, u32[]{:S(2)}) %copy-start.50) | copy-done | bytes 5505048
  72.3 3.3 %collective-permute-done.14.refs_5_.came_ref = f32[4,32,1536]{2,1,0:T(8,128)} collective-permute-done((f32[4,32,1536]{2,1,0:T(8,128)}, f32[4,32,1536]{2,1,0:T(8,128)}, u32[]{:S(2)}, u32[]{:S(2)}) %collective-permute-start.14) | collective-permute-done | bytes 786464 | tf_op jit(solution)/shard_map/ppermute | solution.py:30
  75.6 2.6 %other_features.1 = (bf16[384,640]{1,0:T(8,128)(2,1)S(1)}, bf16[384,640]{1,0:T(8,128)(2,1)S(1)}, bf16[384,640]{1,0:T(8,128)(2,1)S(1)}, bf16[384,640]{1,0:T(8,128)(2,1)S(1)}) custom-call(s32[4]{0:T(128)S(1)} %broadcast_xor_fusion.to_ref, bf16[384,640]{1,0:T(8,128)(2,1)S(1)} %copy-done.11, bf16[384,640]{1,0:T(8,128)(2,1)S(1)} %copy-done.15, ...), custom_call_target="tpu_custom_call" | custom-call | flops 1024 | bytes 1024 | tf_op jit(solution)/shard_map/other_features/pallas_call | solution.py:111
  80.6 2.1 %grad_pair.1.refs_0_ = f32[4,32,1536]{2,1,0:T(8,128)} custom-call(f32[4,32,1536]{2,1,0:T(8,128)S(1)} %copy-done.40, f32[4,32,1536]{2,1,0:T(8,128)} %collective-permute-done.14.refs_5_.came_ref, bf16[384,640]{1,0:T(8,128)(2,1)S(1)} %get-tuple-element.31.refs_0_.refs_1_.refs_4_), custom_call_target="tpu_custom_call" | custom-call | flops 1024 | bytes 1024 | tf_op jit(solution)/shard_map/grad_pair/pallas_call | solution.py:260
  83.6 4.2 %all-to-all-start.1 = ((f32[4,32,1536]{2,1,0:T(8,128)}), f32[4,32,1536]{2,1,0:T(8,128)}, u32[]{:S(2)}, u32[]{:S(2)}) async-start(f32[4,32,1536]{2,1,0:T(8,128)} %grad_pair.1.refs_0_), calls=%async_computation.1 | async-start | bytes 1572864 | tf_op jit(solution)/shard_map/all_to_all | solution.py:274
  89.3 2.1 %collective-permute-start.16 = (bf16[384,640]{1,0:T(8,128)(2,1)}, bf16[384,640]{1,0:T(8,128)(2,1)S(1)}, u32[]{:S(2)}, u32[]{:S(2)}) collective-permute-start(bf16[384,640]{1,0:T(8,128)(2,1)} %copy-done.56), channel_id=1, source_target_pairs={{0,16},{8,24},{16,0},{24,8},{1,17},{9,25},{17,1},{25,9},{2,18},{10... | collective-permute-start | bytes 1474568 | tf_op jit(solution)/shard_map/ppermute | solution.py:30
  91.6 12.1 %collective-permute-done.16.refs_3_.refs_2_ = bf16[384,640]{1,0:T(8,128)(2,1)S(1)} collective-permute-done((bf16[384,640]{1,0:T(8,128)(2,1)}, bf16[384,640]{1,0:T(8,128)(2,1)S(1)}, u32[]{:S(2)}, u32[]{:S(2)}) %collective-permute-start.16) | collective-permute-done | bytes 491552 | tf_op jit(solution)/shard_map/ppermute | solution.py:30
  103.7 10.2 %collective-permute-done.17.refs_4_.refs_3_ = bf16[384,640]{1,0:T(8,128)(2,1)S(1)} collective-permute-done((bf16[384,640]{1,0:T(8,128)(2,1)}, bf16[384,640]{1,0:T(8,128)(2,1)S(1)}, u32[]{:S(2)}, u32[]{:S(2)}) %collective-permute-start.17) | collective-permute-done | bytes 491552 | tf_op jit(solution)/shard_map/ppermute | solution.py:30
  119.4 5.0 %all-to-all-start = ((f32[4,32,1536]{2,1,0:T(8,128)}), f32[4,32,1536]{2,1,0:T(8,128)}, u32[]{:S(2)}, u32[]{:S(2)}) async-start(f32[4,32,1536]{2,1,0:T(8,128)} %hidden_pair.1.refs_11_), calls=%async_computation | async-start | bytes 1572864 | tf_op jit(solution)/shard_map/all_to_all | solution.py:274
  129.2 14.1 %grads.1 = (bf16[384,1792]{1,0:T(8,128)(2,1)}, bf16[384,1792]{1,0:T(8,128)(2,1)}) custom-call(s32[8]{0:T(128)S(1)} %add.40.offs_ref, bf16[384,640]{1,0:T(8,128)(2,1)S(1)} %copy-done.9, bf16[384,640]{1,0:T(8,128)(2,1)S(1)} %copy-done.4, bf16[384,640]{1,0:T(8,128)(2,1)S(1)} %copy-done.13, bf16[384,640]{1,0:T(8,128)(2,1)S(1)} %copy-done.6, ...), custom_call_target="tpu_custom_call" | custom-call | flops 1024 | bytes 1024 | tf_op jit(solution)/shard_map/grads/pallas_call | solution.py:144
  143.3 5.2 %collective-permute-done.20.refs_4_.refs_7_ = bf16[384,640]{1,0:T(8,128)(2,1)} collective-permute-done((bf16[384,640]{1,0:T(8,128)(2,1)}, bf16[384,640]{1,0:T(8,128)(2,1)}, u32[]{:S(2)}, u32[]{:S(2)}) %collective-permute-start.20) | collective-permute-done | bytes 491552 | tf_op jit(solution)/shard_map/ppermute | solution.py:30
  150.9 2.3 %score_line.1.refs_8_ = f32[32,128]{1,0:T(8,128)} custom-call(s32[3]{0:T(128)S(1)} %copy-done.49, f32[4,32,1536]{2,1,0:T(8,128)} %all-to-all-done.hid_ref, f32[4,32,1536]{2,1,0:T(8,128)} %all-to-all-done.1.grad_ref, bf16[384,1792]{1,0:T(8,128)(2,1)S(1)} %copy-done.27, bf16[384,640]{1,0:T(8,128)(2,1)S(1)} %copy-done.25, ...), custom_call_target="tpu_custom_call" | custom-call | flops 1024 | bytes 1024 | tf_op jit(solution)/shard_map/score_line/pallas_call | solution.py:298
  153.2 5.2 %all-to-all-start.2 = ((f32[32,1,128]{2,1,0:T(1,128)}), f32[32,1,128]{2,1,0:T(1,128)S(1)}, u32[]{:S(2)}, u32[]{:S(2)}) async-start(f32[32,1,128]{2,1,0:T(1,128)} %bitcast.3), calls=%async_computation.2 | async-start | bytes 32768 | tf_op jit(solution)/shard_map/all_to_all | solution.py:373
  158.4 2.6 %copy-done.51 = bf16[1792,1536]{1,0:T(8,128)(2,1)S(1)} copy-done((bf16[1792,1536]{1,0:T(8,128)(2,1)S(1)}, bf16[1792,1536]{1,0:T(8,128)(2,1)}, u32[]{:S(2)}) %copy-start.51) | copy-done | bytes 5505048
  161.0 11.1 %wgrad.1 = bf16[1792,1280]{1,0:T(8,128)(2,1)} custom-call(s32[2]{0:T(128)S(1)} %add_multiply_fusion.offs_ref, s32[4]{0:T(128)S(1)} %xor_multiply_fusion.offs_ref.toks_ref, bf16[1792,1536]{1,0:T(8,128)(2,1)S(1)} %copy-done.51, bf16[384,640]{1,0:T(8,128)(2,1)S(1)} %copy-done.23, bf16[384,640]{1,0:T(8,128)(2,1)S(1)} %copy-done.43, ...), custom_call_target="tpu_custom_call" | custom-call | flops 7046430720 | bytes 14024704 | tf_op jit(solution)/shard_map/wgrad/pallas_call | solution.py:183
  (167 shorter events, 51.3 us)
Async XLA Ops:
  0.6 14.4 %collective-permute-start.1 = (bf16[384,640]{1,0:T(8,128)(2,1)}, bf16[384,640]{1,0:T(8,128)(2,1)S(1)}, u32[]{:S(2)}, u32[]{:S(2)}) collective-permute-start(bf16[384,640]{1,0:T(8,128)(2,1)} %refs_0_.5), channel_id=1, source_target_pairs={{0,1},{1,0},{2,3},{3,2},{4,5},{5,4},{6,7},{7,6},{8,9},{9,8},{10,11... | collective-permute-start | bytes 1474568 | tf_op jit(solution)/shard_map/ppermute | solution.py:30
  3.6 13.0 %collective-permute-start.2 = (bf16[384,640]{1,0:T(8,128)(2,1)}, bf16[384,640]{1,0:T(8,128)(2,1)}, u32[]{:S(2)}, u32[]{:S(2)}) collective-permute-start(bf16[384,640]{1,0:T(8,128)(2,1)} %refs_0_.5), channel_id=1, source_target_pairs={{0,16},{8,24},{16,0},{24,8},{1,17},{9,25},{17,1},{25,9},{2,18},{10... | collective-permute-start | bytes 1474568 | tf_op jit(solution)/shard_map/ppermute | solution.py:30
  5.2 11.5 %collective-permute-start.3 = (bf16[384,640]{1,0:T(8,128)(2,1)}, bf16[384,640]{1,0:T(8,128)(2,1)S(1)}, u32[]{:S(2)}, u32[]{:S(2)}) collective-permute-start(bf16[384,640]{1,0:T(8,128)(2,1)} %refs_0_.5), channel_id=1, source_target_pairs={{0,8},{8,0},{16,24},{24,16},{1,9},{9,1},{17,25},{25,17},{2,10},{10... | collective-permute-start | bytes 1474568 | tf_op jit(solution)/shard_map/ppermute | solution.py:30
  5.2 15.7 %collective-permute-start = (bf16[384,640]{1,0:T(8,128)(2,1)}, bf16[384,640]{1,0:T(8,128)(2,1)S(1)}, u32[]{:S(2)}, u32[]{:S(2)}) collective-permute-start(bf16[384,640]{1,0:T(8,128)(2,1)} %refs_0_.5), channel_id=1, source_target_pairs={{0,2},{1,3},{2,4},{3,5},{4,6},{5,7},{6,0},{7,1},{8,10},{9,11},{10,... | collective-permute-start | bytes 1474568 | tf_op jit(solution)/shard_map/ppermute | solution.py:35
  21.7 32.6 %collective-permute-start.11 = (bf16[1792,384]{1,0:T(8,128)(2,1)}, bf16[1792,384]{1,0:T(8,128)(2,1)S(1)}, u32[]{:S(2)}, u32[]{:S(2)}) collective-permute-start(bf16[1792,384]{1,0:T(8,128)(2,1)} %after.8.refs_0_), channel_id=1, source_target_pairs={{0,16},{8,24},{16,0},{24,8},{1,17},{9,25},{17,1},{25,9},{2,18},{10... | collective-permute-start | bytes 4128776 | tf_op jit(solution)/shard_map/ppermute | solution.py:30
  22.2 2.2 %collective-permute-start.6 = (bf16[384,640]{1,0:T(8,128)(2,1)}, bf16[384,640]{1,0:T(8,128)(2,1)}, u32[]{:S(2)}, u32[]{:S(2)}) collective-permute-start(bf16[384,640]{1,0:T(8,128)(2,1)} %collective-permute-done.2.refs_2_), channel_id=1, source_target_pairs={{0,8},{8,0},{16,24},{24,16},{1,9},{9,1},{17,25},{25,17},{2,10},{10... | collective-permute-start | bytes 1474568 | tf_op jit(solution)/shard_map/ppermute | solution.py:30
  22.7 13.1 %collective-permute-start.5 = (bf16[384,640]{1,0:T(8,128)(2,1)S(1)}, bf16[384,640]{1,0:T(8,128)(2,1)S(1)}, u32[]{:S(2)}, u32[]{:S(2)}) collective-permute-start(bf16[384,640]{1,0:T(8,128)(2,1)S(1)} %copy-done.4), channel_id=1, source_target_pairs={{0,1},{1,0},{2,3},{3,2},{4,5},{5,4},{6,7},{7,6},{8,9},{9,8},{10,11... | collective-permute-start | bytes 1474568 | tf_op jit(solution)/shard_map/ppermute | solution.py:30
  23.2 14.6 %collective-permute-start.4 = (bf16[384,640]{1,0:T(8,128)(2,1)S(1)}, bf16[384,640]{1,0:T(8,128)(2,1)S(1)}, u32[]{:S(2)}, u32[]{:S(2)}) collective-permute-start(bf16[384,640]{1,0:T(8,128)(2,1)S(1)} %copy-done.4), channel_id=1, source_target_pairs={{0,2},{1,3},{2,4},{3,5},{4,6},{5,7},{6,0},{7,1},{8,10},{9,11},{10,... | collective-permute-start | bytes 1474568 | tf_op jit(solution)/shard_map/ppermute | solution.py:35
  38.7 14.0 %collective-permute-start.7 = (bf16[384,640]{1,0:T(8,128)(2,1)}, bf16[384,640]{1,0:T(8,128)(2,1)S(1)}, u32[]{:S(2)}, u32[]{:S(2)}) collective-permute-start(bf16[384,640]{1,0:T(8,128)(2,1)} %after.6.refs_2_), channel_id=1, source_target_pairs={{0,2},{1,3},{2,4},{3,5},{4,6},{5,7},{6,0},{7,1},{8,10},{9,11},{10,... | collective-permute-start | bytes 1474568 | tf_op jit(solution)/shard_map/ppermute | solution.py:35
  38.7 14.0 %collective-permute-start.8 = (bf16[384,640]{1,0:T(8,128)(2,1)}, bf16[384,640]{1,0:T(8,128)(2,1)S(1)}, u32[]{:S(2)}, u32[]{:S(2)}) collective-permute-start(bf16[384,640]{1,0:T(8,128)(2,1)} %after.6.refs_2_), channel_id=1, source_target_pairs={{0,1},{1,0},{2,3},{3,2},{4,5},{5,4},{6,7},{7,6},{8,9},{9,8},{10,11... | collective-permute-start | bytes 1474568 | tf_op jit(solution)/shard_map/ppermute | solution.py:30
  40.1 22.4 %collective-permute-start.10 = (bf16[1792,384]{1,0:T(8,128)(2,1)}, bf16[1792,384]{1,0:T(8,128)(2,1)}, u32[]{:S(2)}, u32[]{:S(2)}) collective-permute-start(bf16[1792,384]{1,0:T(8,128)(2,1)} %after.8.refs_0_), channel_id=1, source_target_pairs={{0,8},{8,0},{16,24},{24,16},{1,9},{9,1},{17,25},{25,17},{2,10},{10... | collective-permute-start | bytes 4128776 | tf_op jit(solution)/shard_map/ppermute | solution.py:30
  55.3 7.2 %collective-permute-start.12 = (bf16[1792,384]{1,0:T(8,128)(2,1)}, bf16[1792,384]{1,0:T(8,128)(2,1)S(1)}, u32[]{:S(2)}, u32[]{:S(2)}) collective-permute-start(bf16[1792,384]{1,0:T(8,128)(2,1)} %after.9.refs_4_.refs_2_), channel_id=1, source_target_pairs={{0,8},{8,0},{16,24},{24,16},{1,9},{9,1},{17,25},{25,17},{2,10},{10... | collective-permute-start | bytes 4128776 | tf_op jit(solution)/shard_map/ppermute | solution.py:30
  55.3 20.3 %collective-permute-start.14 = (f32[4,32,1536]{2,1,0:T(8,128)}, f32[4,32,1536]{2,1,0:T(8,128)}, u32[]{:S(2)}, u32[]{:S(2)}) collective-permute-start(f32[4,32,1536]{2,1,0:T(8,128)} %copy-done.18), channel_id=1, source_target_pairs={{0,1},{1,0},{2,3},{3,2},{4,5},{5,4},{6,7},{7,6},{8,9},{9,8},{10,11... | collective-permute-start | bytes 2359304 | tf_op jit(solution)/shard_map/ppermute | solution.py:30
  56.8 18.8 %collective-permute-start.9 = (bf16[384,640]{1,0:T(8,128)(2,1)}, bf16[384,640]{1,0:T(8,128)(2,1)}, u32[]{:S(2)}, u32[]{:S(2)}) collective-permute-start(bf16[384,640]{1,0:T(8,128)(2,1)} %copy-done.16), channel_id=1, source_target_pairs={{0,2},{1,3},{2,4},{3,5},{4,6},{5,7},{6,0},{7,1},{8,10},{9,11},{10,... | collective-permute-start | bytes 1474568 | tf_op jit(solution)/shard_map/ppermute | solution.py:35
  83.6 35.8 %all-to-all-start.1 = ((f32[4,32,1536]{2,1,0:T(8,128)}), f32[4,32,1536]{2,1,0:T(8,128)}, u32[]{:S(2)}, u32[]{:S(2)}) async-start(f32[4,32,1536]{2,1,0:T(8,128)} %grad_pair.1.refs_0_), calls=%async_computation.1 | async-start | bytes 1572864 | tf_op jit(solution)/shard_map/all_to_all | solution.py:274
  87.8 26.1 %collective-permute-start.13 = (f32[4,32,1536]{2,1,0:T(8,128)}, f32[4,32,1536]{2,1,0:T(8,128)S(1)}, u32[]{:S(2)}, u32[]{:S(2)}) collective-permute-start(f32[4,32,1536]{2,1,0:T(8,128)} %copy-done.41), channel_id=1, source_target_pairs={{0,1},{1,0},{2,3},{3,2},{4,5},{5,4},{6,7},{7,6},{8,9},{9,8},{10,11... | collective-permute-start | bytes 2359304 | tf_op jit(solution)/shard_map/ppermute | solution.py:30
  89.3 2.3 %collective-permute-start.15 = (bf16[384,640]{1,0:T(8,128)(2,1)}, bf16[384,640]{1,0:T(8,128)(2,1)S(1)}, u32[]{:S(2)}, u32[]{:S(2)}) collective-permute-start(bf16[384,640]{1,0:T(8,128)(2,1)} %copy-done.57), channel_id=1, source_target_pairs={{0,8},{8,0},{16,24},{24,16},{1,9},{9,1},{17,25},{25,17},{2,10},{10... | collective-permute-start | bytes 1474568 | tf_op jit(solution)/shard_map/ppermute | solution.py:30
  89.3 14.4 %collective-permute-start.16 = (bf16[384,640]{1,0:T(8,128)(2,1)}, bf16[384,640]{1,0:T(8,128)(2,1)S(1)}, u32[]{:S(2)}, u32[]{:S(2)}) collective-permute-start(bf16[384,640]{1,0:T(8,128)(2,1)} %copy-done.56), channel_id=1, source_target_pairs={{0,16},{8,24},{16,0},{24,8},{1,17},{9,25},{17,1},{25,9},{2,18},{10... | collective-permute-start | bytes 1474568 | tf_op jit(solution)/shard_map/ppermute | solution.py:30
  91.4 22.4 %collective-permute-start.17 = (bf16[384,640]{1,0:T(8,128)(2,1)}, bf16[384,640]{1,0:T(8,128)(2,1)S(1)}, u32[]{:S(2)}, u32[]{:S(2)}) collective-permute-start(bf16[384,640]{1,0:T(8,128)(2,1)} %copy-done.55), channel_id=1, source_target_pairs={{0,24},{8,16},{16,8},{24,0},{1,25},{9,17},{17,9},{25,1},{2,26},{10... | collective-permute-start | bytes 1474568 | tf_op jit(solution)/shard_map/ppermute | solution.py:30
  119.4 29.1 %all-to-all-start = ((f32[4,32,1536]{2,1,0:T(8,128)}), f32[4,32,1536]{2,1,0:T(8,128)}, u32[]{:S(2)}, u32[]{:S(2)}) async-start(f32[4,32,1536]{2,1,0:T(8,128)} %hidden_pair.1.refs_11_), calls=%async_computation | async-start | bytes 1572864 | tf_op jit(solution)/shard_map/all_to_all | solution.py:274
  124.4 18.9 %collective-permute-start.18 = (bf16[384,640]{1,0:T(8,128)(2,1)}, bf16[384,640]{1,0:T(8,128)(2,1)}, u32[]{:S(2)}, u32[]{:S(2)}) collective-permute-start(bf16[384,640]{1,0:T(8,128)(2,1)} %copy-done.54), channel_id=1, source_target_pairs={{0,8},{8,0},{16,24},{24,16},{1,9},{9,1},{17,25},{25,17},{2,10},{10... | collective-permute-start | bytes 1474568 | tf_op jit(solution)/shard_map/ppermute | solution.py:30
  124.4 18.9 %collective-permute-start.19 = (bf16[384,640]{1,0:T(8,128)(2,1)}, bf16[384,640]{1,0:T(8,128)(2,1)}, u32[]{:S(2)}, u32[]{:S(2)}) collective-permute-start(bf16[384,640]{1,0:T(8,128)(2,1)} %copy-done.53), channel_id=1, source_target_pairs={{0,16},{8,24},{16,0},{24,8},{1,17},{9,25},{17,1},{25,9},{2,18},{10... | collective-permute-start | bytes 1474568 | tf_op jit(solution)/shard_map/ppermute | solution.py:30
  125.9 22.6 %collective-permute-start.20 = (bf16[384,640]{1,0:T(8,128)(2,1)}, bf16[384,640]{1,0:T(8,128)(2,1)}, u32[]{:S(2)}, u32[]{:S(2)}) collective-permute-start(bf16[384,640]{1,0:T(8,128)(2,1)} %copy-done.52), channel_id=1, source_target_pairs={{0,24},{8,16},{16,8},{24,0},{1,25},{9,17},{17,9},{25,1},{2,26},{10... | collective-permute-start | bytes 1474568 | tf_op jit(solution)/shard_map/ppermute | solution.py:30
  153.2 18.8 %all-to-all-start.2 = ((f32[32,1,128]{2,1,0:T(1,128)}), f32[32,1,128]{2,1,0:T(1,128)S(1)}, u32[]{:S(2)}, u32[]{:S(2)}) async-start(f32[32,1,128]{2,1,0:T(1,128)} %bitcast.3), calls=%async_computation.2 | async-start | bytes 32768 | tf_op jit(solution)/shard_map/all_to_all | solution.py:373
  (58 other events, 180.5 us)

commit v9 on v8

--- a/solution.py
+++ b/solution.py
@@ -14,7 +14,7 @@
 
 F32 = jnp.float32
 BF16 = jnp.bfloat16
-VMEM_LIMIT = 32 * 1024 * 1024
+MIB = 1024 * 1024
 
 
 def dot_nt(a, b):
@@ -40,11 +40,12 @@
 
 
 ANY = pl.BlockSpec(memory_space=pl.ANY)
+HBM = pl.BlockSpec(memory_space=pltpu.HBM)
 SMALL = pl.CostEstimate(flops=1024, bytes_accessed=1024, transcendentals=0)
 
 
-def params():
-    return pltpu.CompilerParams(vmem_limit_bytes=VMEM_LIMIT)
+def params(mib):
+    return pltpu.CompilerParams(vmem_limit_bytes=mib * MIB)
 
 
 def after_body(*refs):
@@ -58,6 +59,7 @@
         out_specs=ANY,
         out_shape=jax.ShapeDtypeStruct(x.shape, x.dtype),
         input_output_aliases={0: 0},
+        compiler_params=params(1),
         cost_estimate=SMALL,
         name="after",
     )(x, *order)
@@ -87,10 +89,35 @@
             jax.ShapeDtypeStruct((toks, units), BF16),
             jax.ShapeDtypeStruct((toks, units), BF16),
         ],
-        compiler_params=params(),
+        compiler_params=params(12),
         cost_estimate=SMALL,
         name="hidden",
     )(gate, up)
+
+
+def stack_body(n, at_ref, *refs):
+    blocks, out_ref, sems = refs[:n], refs[-2], refs[-1]
+    copies = [
+        pltpu.make_async_copy(blocks[j], out_ref.at[at_ref[j]], sems.at[j]) for j in range(n)
+    ]
+    for copy in copies:
+        copy.start()
+    for copy in copies:
+        copy.wait()
+
+
+def stack(at, blocks, order, name):
+    n = len(blocks)
+    return pl.pallas_call(
+        functools.partial(stack_body, n),
+        in_specs=[pl.BlockSpec(memory_space=pltpu.SMEM)] + [ANY] * (n + len(order)),
+        out_specs=pl.BlockSpec(memory_space=pltpu.VMEM),
+        out_shape=jax.ShapeDtypeStruct((n,) + blocks[0].shape, BF16),
+        scratch_shapes=[pltpu.SemaphoreType.DMA((n,))],
+        compiler_params=params(8),
+        cost_estimate=SMALL,
+        name=name,
+    )(at, *blocks, *order)
 
 
 def arrange_body(n, to_ref, *refs):
@@ -114,20 +141,21 @@
         out_specs=[pl.BlockSpec(memory_space=pltpu.VMEM)] * n,
         out_shape=[jax.ShapeDtypeStruct(blocks[0].shape, BF16)] * n,
         scratch_shapes=[pltpu.SemaphoreType.DMA((n,))],
-        compiler_params=params(),
+        compiler_params=params(8),
         cost_estimate=SMALL,
         name=name,
     )(to, *blocks, *order)
 
 
 def grads_body(n, offs_ref, *refs):
-    blocks, (w_ref, by_gate_ref, by_up_ref, order_ref, gg_ref, gu_ref, piece) = refs[:n], refs[n:]
+    blocks, (w_ref, by_gate_ref, by_up_ref, _, gg_ref, gu_ref, done_ref, piece) = refs[:n], refs[n:]
     width = blocks[0].shape[1]
 
     @pl.when(pl.program_id(0) == 0)
     def _():
         for j in range(n):
             piece[:, pl.ds(pl.multiple_of(offs_ref[j], 128), width)] = blocks[j][...]
+        done_ref[...] = jnp.zeros_like(done_ref)
 
     total = dot_nt(piece[...], w_ref[...])
     gg_ref[...] = (total * by_gate_ref[...]).astype(BF16)
@@ -148,58 +176,75 @@
             grid=(units // tile,),
             in_specs=[whole((toks, width))] * n
             + [pl.BlockSpec((tile, feats), lambda i, _: (i, 0)), cols, cols, ANY],
-            out_specs=[cols, cols],
+            out_specs=[cols, cols, whole((8, 128))],
             scratch_shapes=[pltpu.VMEM((toks, feats), BF16)],
         ),
-        out_shape=(out, out),
-        compiler_params=params(),
+        out_shape=(out, out, jax.ShapeDtypeStruct((8, 128), F32)),
+        compiler_params=params(24),
         cost_estimate=SMALL,
         name="grads",
     )(offs, *blocks, weight, by_gate, by_up, order)
 
 
-def wgrad_body(n, offs_ref, toks_ref, hid_ref, *refs):
-    blocks, (order_ref, out_ref, cols) = refs[: 2 * n], refs[2 * n :]
-    toks, width = blocks[0].shape
-
-    @pl.when(pl.program_id(0) == 0)
-    def _():
-        for half in range(2):
-            place = pl.ds(pl.multiple_of(offs_ref[half], 128), width)
-            for k in range(n):
-                rows = pl.ds(pl.multiple_of(toks_ref[k], 128), toks)
-                cols[rows, place] = blocks[half * n + k][...]
-
-    out_ref[...] = lax.dot_general(
-        hid_ref[...], cols[...], (((1,), (0,)), ((), ())), preferred_element_type=F32
-    ).astype(BF16)
-
-
-def wgrad(offs, tok_offs, hid, blocks, order):
+def wgrad_body(n, offs_ref, toks_ref, hid_ref, own_ref, *refs):
+    others, (order_ref, out_ref, hid, cols, outs, hid_sems, col_sems, out_sems) = refs[:n], refs[n:]
+    _, toks, width = own_ref.shape
+    steps, tile, _ = hid.shape
+    own, other = (pl.ds(pl.multiple_of(offs_ref[half], 128), width) for half in range(2))
+    came = []
+    for k in range(n):
+        rows = pl.ds(pl.multiple_of(toks_ref[k], 128), toks)
+        came.append((own_ref.at[k], cols.at[k * toks : (k + 1) * toks, own]))
+        came.append((others[k], cols.at[rows, other]))
+    came = [pltpu.make_async_copy(a, b, col_sems.at[j]) for j, (a, b) in enumerate(came)]
+    came += [
+        pltpu.make_async_copy(hid_ref.at[i * tile : (i + 1) * tile], hid.at[i], hid_sems.at[i])
+        for i in range(steps)
+    ]
+    for copy in came:
+        copy.start()
+    for copy in came[:-steps]:
+        copy.wait()
+    gone = []
+    for i in range(steps):
+        came[i - steps].wait()
+        outs[i] = lax.dot_general(
+            hid[i], cols[...], (((1,), (0,)), ((), ())), preferred_element_type=F32
+        ).astype(BF16)
+        rows = out_ref.at[i * tile : (i + 1) * tile]
+        gone.append(pltpu.make_async_copy(outs.at[i], rows, out_sems.at[i]))
+        gone[-1].start()
+    for copy in gone:
+        copy.wait()
+
+
+def wgrad(offs, tok_offs, hid, own, others, order):
     units, total = hid.shape
-    toks, width = blocks[0].shape
-    n = total // toks
-    tile = units // 4
+    n, toks, width = own.shape
+    steps = 4
+    tile = units // steps
+    smem = pl.BlockSpec(memory_space=pltpu.SMEM)
     return pl.pallas_call(
         functools.partial(wgrad_body, n),
-        grid_spec=pltpu.PrefetchScalarGridSpec(
-            num_scalar_prefetch=2,
-            grid=(units // tile,),
-            in_specs=[pl.BlockSpec((tile, total), lambda i, *_: (i, 0))]
-            + [whole((toks, width))] * (2 * n)
-            + [ANY],
-            out_specs=pl.BlockSpec((tile, 2 * width), lambda i, *_: (i, 0)),
-            scratch_shapes=[pltpu.VMEM((total, 2 * width), BF16)],
-        ),
+        in_specs=[smem, smem, HBM] + [ANY] * (n + 2),
+        out_specs=HBM,
         out_shape=jax.ShapeDtypeStruct((units, 2 * width), BF16),
-        compiler_params=params(),
+        scratch_shapes=[
+            pltpu.VMEM((steps, tile, total), BF16),
+            pltpu.VMEM((total, 2 * width), BF16),
+            pltpu.VMEM((steps, tile, 2 * width), BF16),
+            pltpu.SemaphoreType.DMA((steps,)),
+            pltpu.SemaphoreType.DMA((2 * n,)),
+            pltpu.SemaphoreType.DMA((steps,)),
+        ],
+        compiler_params=params(28),
         cost_estimate=pl.CostEstimate(
             flops=4 * total * units * width,
             bytes_accessed=2 * (total * (units + 2 * width) + 2 * units * width),
             transcendentals=0,
         ),
         name="wgrad",
-    )(offs, tok_offs, hid, *blocks, order)
+    )(offs, tok_offs, hid, own, *others, order)
 
 
 def put_slices(inner_ref, part, kept_ref, away_ref):
@@ -222,14 +267,17 @@
 
 
 def hidden_gram_body(inner_ref, offs_ref, *refs):
-    hid, (val_ref, order_ref, kept_ref, away_ref, all_ref, wide) = refs[:-6], refs[-6:]
+    hid, (val_ref, order_ref, kept_ref, away_ref, all_ref, wide, held, sem) = refs[:-8], refs[-8:]
     for k, ref in enumerate(hid):
         toks = ref.shape[1]
-        all_ref[:, pl.ds(pl.multiple_of(offs_ref[k], 128), toks)] = ref[...]
+        held[:, pl.ds(pl.multiple_of(offs_ref[k], 128), toks)] = ref[...]
+    copy = pltpu.make_async_copy(held, all_ref, sem)
+    copy.start()
     wide[...] = lax.dot_general(
-        val_ref[...], all_ref[...], (((1,), (0,)), ((), ())), preferred_element_type=F32
+        val_ref[...], held[...], (((1,), (0,)), ((), ())), preferred_element_type=F32
     )
     put_slices(inner_ref, wide, kept_ref, away_ref)
+    copy.wait()
 
 
 def gram_call(body, inner, offs, operands, order, parts, extra, name):
@@ -242,10 +290,11 @@
     return pl.pallas_call(
         body,
         in_specs=[smem, smem] + [vmem] * len(operands) + [ANY],
-        out_specs=[vmem] * len(shapes),
+        out_specs=[vmem, vmem] + [HBM] * len(extra),
         out_shape=shapes,
-        scratch_shapes=[pltpu.VMEM((vals.shape[0], total), F32)],
-        compiler_params=params(),
+        scratch_shapes=[pltpu.VMEM((vals.shape[0], total), F32)]
+        + [y for x in extra for y in (pltpu.VMEM(x.shape, x.dtype), pltpu.SemaphoreType.DMA)],
+        compiler_params=params(20),
         cost_estimate=SMALL,
         name=name,
     )(inner, offs, *operands, order)
@@ -262,7 +311,7 @@
         in_specs=[vmem, vmem] + [ANY] * len(order),
         out_specs=vmem,
         out_shape=jax.ShapeDtypeStruct(kept.shape, F32),
-        compiler_params=params(),
+        compiler_params=params(8),
         cost_estimate=SMALL,
         name=name,
     )(kept, came, *order)
@@ -300,7 +349,7 @@
         in_specs=[pl.BlockSpec(memory_space=pltpu.SMEM), vmem, vmem] + [ANY] * len(order),
         out_specs=vmem,
         out_shape=jax.ShapeDtypeStruct((copies, 128), F32),
-        compiler_params=params(),
+        compiler_params=params(8),
         cost_estimate=SMALL,
         name="score_line",
     )(assign, hid, grad, *order)
@@ -341,7 +390,8 @@
     ring = [out_grad, first]
     for _ in range(n_out - 2):
         others.append(swap(ring[-1], "fsdp", 1))
-        ring.append(after(shift(ring[-1], "fsdp", 2), others[-1], away))
+        order = away if len(ring) == 2 else near
+        ring.append(after(shift(ring[-1], "fsdp", 2), others[-1], order))
     others.append(shift(others[-1], "fsdp", 2))
 
     def over_columns(blocks):
@@ -349,10 +399,10 @@
 
     far = after(far, ring[-1])
     hid_dp = [hidden, near, far, swap(far, "dp", 1)]
-    own = arrange(to, ring, [far], "own_features")
-    own_cols = over_columns(own)
+    own = stack(at, ring, [far], "own_features")
+    own_cols = lax.all_to_all(own, "dp", split_axis=0, concat_axis=0, tiled=True)
     hid_kept, away, hid_all = gram_call(
-        hidden_gram_body, inner_at, tok_offs, [*hid_dp, val_hidden], own[0], n_fs,
+        hidden_gram_body, inner_at, tok_offs, [*hid_dp, val_hidden], own, n_fs,
         [jax.ShapeDtypeStruct((units, total), BF16)], "hidden_gram",
     )
     hid_came = swap(away, "fsdp", 1)
@@ -360,20 +410,22 @@
     other_cols = over_columns(other)
     grad_pair = pair_sum(grad_kept, grad_came, [other[0]], "grad_pair")
     grad_sums = spread(grad_pair)
-    hid_pair = pair_sum(hid_kept, hid_came, [grad_pair, *own_cols], "hidden_pair")
+    hid_pair = pair_sum(hid_kept, hid_came, [grad_pair, own_cols], "hidden_pair")
     hid_sums = spread(hid_pair)
 
     offs = (jnp.stack([inner, 1 - inner]) * width).astype(jnp.int32)
     places = (offs[:, None] + at[None, :] * (2 * width)).reshape(-1)
-    grad_gate, grad_up = grads(places, [*ring, *others], down_weight, by_gate, by_up, hid_pair)
+    grad_gate, grad_up, done = grads(
+        places, [*ring, *others], down_weight, by_gate, by_up, hid_pair
+    )
 
     mine = score_line(
-        assign, hid_sums, grad_sums, [grad_up, *other_cols], n_dp * rows_here, n_dp * n_fs
+        assign, hid_sums, grad_sums, [done, *other_cols], n_dp * rows_here, n_dp * n_fs
     )
     every = lax.all_to_all(
         mine, ("dp", "fsdp"), split_axis=0, concat_axis=0, tiled=True
     ).reshape(n_dp, n_fs, 128)
-    weight_grad = wgrad(offs, tok_offs, hid_all, [*own_cols, *other_cols], mine)
+    weight_grad = wgrad(offs, tok_offs, hid_all, own_cols, other_cols, mine)
 
     rows = n_dp * rows_here
     scale = 1.0 / jnp.sqrt(F32(L) * VAL * FFW * D)

time: 175 us -> 169 us (0.966)
  local copies, waits for them, and re-layouts: 40.5 us -> 27.9 us
  waiting for transfers between devices: 58.1 us -> 62.7 us
    unnamed x117 -> x67, local copies, waits for them, and re-layouts: 40.2 us -> 27.5 us
    pallas_call x1 -> x2, Pallas kernels: 11.1 us -> 16.3 us  [the longest x1 12.8 us: wgrad(): pl.pallas_call(functools.partial(wgrad_body, n), in_specs=[smem, smem, HB...]
    all_to_all x0 -> x1, starting transfers between devices: none -> 4.44 us  [per_device(): lax.all_to_all(own, 'dp', split_axis=0, concat_axis=0, tiled=True)]
    ppermute x17 -> x14, waiting for transfers between devices: 39.3 us -> 43.4 us  [swap(): return lax.ppermute(x, axis, [(s, s ^ k) for s in range(n)])]
    ppermute x17 -> x14, starting transfers between devices: 14.2 us -> 11.3 us  [swap(): return lax.ppermute(x, axis, [(s, s ^ k) for s in range(n)])]
    pallas_call x1, Pallas kernels: 14.1 us -> 11.7 us  [grads(): pl.pallas_call(functools.partial(grads_body, n), grid_spec=pltpu.Prefetch...]
    pallas_call x2 -> x1, Pallas kernels: 4.6 us -> 2.3 us  [arrange(): pl.pallas_call(functools.partial(arrange_body, n), in_specs=[pl.BlockSpec...]
    pallas_call x1, Pallas kernels: 1.99 us -> 3.74 us  [hidden_units(): pl.pallas_call(hidden_body, grid=(units // tile,), in_specs=[cols, cols],...]
  transfers between devices with their start and end apart: 24 -> 22, of which waited for: 11 -> 12; matrix products, arithmetic and copies ran while one was open for 0% -> 0% of each run, Pallas kernels for 21% -> 23%
where the time goes in v9:
time: 169 us; the launch traced here: 168 us
  waiting for transfers between devices  62.7 us (37%)
  Pallas kernels  44.7 us (26%)
  starting transfers between devices  31.1 us (18%)
  local copies, waits for them, and re-layouts  27.9 us (17%)
    ppermute x14, waiting for transfers between devices, swap(): return lax.ppermute(x, axis, [(s, s ^ k) for s in range(n)])  43.4 us
    unnamed x67, local copies, waits for them, and re-layouts  27.5 us
    ppermute x4, waiting for transfers between devices, shift(): return lax.ppermute(x, axis, [(s, (s + k) % n) for s in range(n)])  19.2 us
    pallas_call x1, Pallas kernels, wgrad(): pl.pallas_call(functools.partial(wgrad_body, n), in_specs=[smem, smem, HB...  12.8 us
    pallas_call x1, Pallas kernels, grads(): pl.pallas_call(functools.partial(grads_body, n), grid_spec=pltpu.Prefetch...  11.7 us
    ppermute x14, starting transfers between devices, swap(): return lax.ppermute(x, axis, [(s, s ^ k) for s in range(n)])  11.3 us
    all_to_all x2, starting transfers between devices, spread(): lax.all_to_all(pair, 'fsdp', split_axis=0, concat_axis=0, axis_index_grou...  8.46 us
    pallas_call x2, Pallas kernels, gram_call(): pl.pallas_call(body, in_specs=[smem, smem] + [vmem] * len(operands) + [AN...  6.63 us
  transfers between devices with their start and end apart: 22, of which 12 were waited for; matrix products, arithmetic and copies ran while one was open for 0% of the time, Pallas kernels for 23%

profile of v9, /device:TPU:0, one launch (start us, length us, event | category | flops | bytes accessed | tf_op | source)
XLA Modules:
  0.0 168.0 jit_solution(16703160395212001237)
XLA Ops:
  0.6 3.0 %collective-permute-start.1 = (bf16[384,640]{1,0:T(8,128)(2,1)}, bf16[384,640]{1,0:T(8,128)(2,1)S(1)}, u32[]{:S(2)}, u32[]{:S(2)}) collective-permute-start(bf16[384,640]{1,0:T(8,128)(2,1)} %refs_0_.5), channel_id=1, source_target_pairs={{0,1},{1,0},{2,3},{3,2},{4,5},{5,4},{6,7},{7,6},{8,9},{9,8},{10,11... | collective-permute-start | bytes 1474568 | tf_op jit(solution)/shard_map/ppermute | solution.py:30
  9.4 3.7 %hidden.1 = (bf16[1792,384]{1,0:T(8,128)(2,1)}, bf16[384,1792]{1,0:T(8,128)(2,1)S(1)}, bf16[384,1792]{1,0:T(8,128)(2,1)S(1)}) custom-call(bf16[384,1792]{1,0:T(8,128)(2,1)S(1)} %copy-done.12, bf16[384,1792]{1,0:T(8,128)(2,1)S(1)} %copy-done.13), custom_call_target="tpu_custom_call" | custom-call | flops 1024 | bytes 1024 | tf_op jit(solution)/shard_map/hidden/pallas_call | solution.py:82
  16.6 4.2 %collective-permute-done.refs_0_ = bf16[384,640]{1,0:T(8,128)(2,1)S(1)} collective-permute-done((bf16[384,640]{1,0:T(8,128)(2,1)}, bf16[384,640]{1,0:T(8,128)(2,1)S(1)}, u32[]{:S(2)}, u32[]{:S(2)}) %collective-permute-start) | collective-permute-done | bytes 491552 | tf_op jit(solution)/shard_map/ppermute | solution.py:35
  22.2 2.9 %collective-permute-done.6.refs_3_ = bf16[384,640]{1,0:T(8,128)(2,1)} collective-permute-done((bf16[384,640]{1,0:T(8,128)(2,1)}, bf16[384,640]{1,0:T(8,128)(2,1)}, u32[]{:S(2)}, u32[]{:S(2)}) %collective-permute-start.6) | collective-permute-done | bytes 491552 | tf_op jit(solution)/shard_map/ppermute | solution.py:30
  27.1 2.3 %grad_gram.1 = (f32[4,32,1536]{2,1,0:T(8,128)S(1)}, f32[4,32,1536]{2,1,0:T(8,128)S(1)}) custom-call(s32[1]{0:T(128)} %bitcast.inner_ref, s32[4]{0:T(128)S(1)} %xor_multiply_fusion.offs_ref.toks_ref, bf16[384,640]{1,0:T(8,128)(2,1)S(1)} %copy-done.1, bf16[384,640]{1,0:T(8,128)(2,1)S(1)} %copy-done.6, bf16[384,640]{1,0:T(8,128)(2,1)} %collective-permute-done.2.refs_2_, ...), custom_call_target="tpu_custom_call" | custom-call | flops 1024 | bytes 1024 | tf_op jit(solution)/shard_map/grad_gram/pallas_call | solution.py:290
  29.4 5.7 %collective-permute-done.5.refs_1_.refs_5_ = bf16[384,640]{1,0:T(8,128)(2,1)S(1)} collective-permute-done((bf16[384,640]{1,0:T(8,128)(2,1)S(1)}, bf16[384,640]{1,0:T(8,128)(2,1)S(1)}, u32[]{:S(2)}, u32[]{:S(2)}) %collective-permute-start.5) | collective-permute-done | bytes 491552 | tf_op jit(solution)/shard_map/ppermute | solution.py:30
  35.2 2.2 %collective-permute-done.4.refs_0_ = bf16[384,640]{1,0:T(8,128)(2,1)} collective-permute-done((bf16[384,640]{1,0:T(8,128)(2,1)S(1)}, bf16[384,640]{1,0:T(8,128)(2,1)}, u32[]{:S(2)}, u32[]{:S(2)}) %collective-permute-start.4) | collective-permute-done | bytes 491552 | tf_op jit(solution)/shard_map/ppermute | solution.py:35
  39.6 12.9 %collective-permute-done.7.refs_0_ = bf16[384,640]{1,0:T(8,128)(2,1)S(1)} collective-permute-done((bf16[384,640]{1,0:T(8,128)(2,1)}, bf16[384,640]{1,0:T(8,128)(2,1)S(1)}, u32[]{:S(2)}, u32[]{:S(2)}) %collective-permute-start.7) | collective-permute-done | bytes 491552 | tf_op jit(solution)/shard_map/ppermute | solution.py:35
  53.8 3.5 %own_features.1.refs_5_ = bf16[4,384,640]{2,1,0:T(8,128)(2,1)} custom-call(s32[4]{0:T(128)S(1)} %and_select_fusion.at_ref, bf16[384,640]{1,0:T(8,128)(2,1)S(1)} %copy-done.1, bf16[384,640]{1,0:T(8,128)(2,1)S(1)} %after.5.refs_5_.refs_1_, bf16[384,640]{1,0:T(8,128)(2,1)} %after.6.refs_2_, bf16[384,640]{1,0:T(8,128)(2,1)S(1)} %after.8.refs_1_.refs_3_, ...), custom_call_target="tpu_custom_call" | custom-call | flops 1024 | bytes 1024 | tf_op jit(solution)/shard_map/own_features/pallas_call | solution.py:111
  57.3 4.4 %all-to-all-start = ((bf16[4,384,640]{2,1,0:T(8,128)(2,1)}), bf16[4,384,640]{2,1,0:T(8,128)(2,1)}, u32[]{:S(2)}, u32[]{:S(2)}) async-start(bf16[4,384,640]{2,1,0:T(8,128)(2,1)} %own_features.1.refs_5_), calls=%async_computation | async-start | bytes 3932160 | tf_op jit(solution)/shard_map/all_to_all | solution.py:403
  62.8 2.8 %collective-permute-done.12.refs_3_ = bf16[1792,384]{1,0:T(8,128)(2,1)S(1)} collective-permute-done((bf16[1792,384]{1,0:T(8,128)(2,1)S(1)}, bf16[1792,384]{1,0:T(8,128)(2,1)S(1)}, u32[]{:S(2)}, u32[]{:S(2)}) %collective-permute-start.12) | collective-permute-done | bytes 1376288 | tf_op jit(solution)/shard_map/ppermute | solution.py:30
  66.7 4.4 %hidden_gram.1 = (f32[4,32,1536]{2,1,0:T(8,128)S(1)}, f32[4,32,1536]{2,1,0:T(8,128)S(1)}, bf16[1792,1536]{1,0:T(8,128)(2,1)S(1)}) custom-call(s32[1]{0:T(128)} %bitcast.inner_ref, s32[4]{0:T(128)S(1)} %xor_multiply_fusion.offs_ref.toks_ref, bf16[1792,384]{1,0:T(8,128)(2,1)} %after.7.refs_0_, bf16[1792,384]{1,0:T(8,128)(2,1)} %collective-permute-done.9.refs_2_.refs_1_, ...), custom_call_target="tpu_custom_call" | custom-call | flops 1024 | bytes 1024 | tf_op jit(solution)/shard_map/hidden_gram/pallas_call | solution.py:290
  71.1 2.4 %copy-done.28 = bf16[1792,1536]{1,0:T(8,128)(2,1)} copy-done((bf16[1792,1536]{1,0:T(8,128)(2,1)}, bf16[1792,1536]{1,0:T(8,128)(2,1)S(1)}, u32[]{:S(2)}) %copy-start.28) | copy-done | bytes 5505048
  73.5 8.5 %collective-permute-done.14.refs_5_.came_ref = f32[4,32,1536]{2,1,0:T(8,128)S(1)} collective-permute-done((f32[4,32,1536]{2,1,0:T(8,128)}, f32[4,32,1536]{2,1,0:T(8,128)S(1)}, u32[]{:S(2)}, u32[]{:S(2)}) %collective-permute-start.14) | collective-permute-done | bytes 786464 | tf_op jit(solution)/shard_map/ppermute | solution.py:30
  82.0 2.3 %other_features.1 = (bf16[384,640]{1,0:T(8,128)(2,1)S(1)}, bf16[384,640]{1,0:T(8,128)(2,1)S(1)}, bf16[384,640]{1,0:T(8,128)(2,1)S(1)}, bf16[384,640]{1,0:T(8,128)(2,1)S(1)}) custom-call(s32[4]{0:T(128)S(1)} %broadcast_xor_fusion.to_ref, bf16[384,640]{1,0:T(8,128)(2,1)S(1)} %collective-permute-done.1.refs_1_.refs_0_.refs_4_, bf16[384,640]{1,0:T(8,128)(2,1)S(1)} %copy-done.3, ...), custom_call_target="tpu_custom_call" | custom-call | flops 1024 | bytes 1024 | tf_op jit(solution)/shard_map/other_features/pallas_call | solution.py:138
  88.5 3.6 %all-to-all-start.2 = ((f32[4,32,1536]{2,1,0:T(8,128)}), f32[4,32,1536]{2,1,0:T(8,128)S(1)}, u32[]{:S(2)}, u32[]{:S(2)}) async-start(f32[4,32,1536]{2,1,0:T(8,128)} %grad_pair.1.refs_0_), calls=%async_computation.2 | async-start | bytes 1572864 | tf_op jit(solution)/shard_map/all_to_all | solution.py:323
  92.7 18.3 %collective-permute-done.13.came_ref = f32[4,32,1536]{2,1,0:T(8,128)S(1)} collective-permute-done((f32[4,32,1536]{2,1,0:T(8,128)S(1)}, f32[4,32,1536]{2,1,0:T(8,128)S(1)}, u32[]{:S(2)}, u32[]{:S(2)}) %collective-permute-start.13) | collective-permute-done | bytes 786464 | tf_op jit(solution)/shard_map/ppermute | solution.py:30
  113.1 4.8 %all-to-all-start.1 = ((f32[4,32,1536]{2,1,0:T(8,128)}), f32[4,32,1536]{2,1,0:T(8,128)}, u32[]{:S(2)}, u32[]{:S(2)}) async-start(f32[4,32,1536]{2,1,0:T(8,128)} %hidden_pair.1.refs_11_), calls=%async_computation.1 | async-start | bytes 1572864 | tf_op jit(solution)/shard_map/all_to_all | solution.py:323
  118.0 2.2 %collective-permute-start.16 = (bf16[384,640]{1,0:T(8,128)(2,1)}, bf16[384,640]{1,0:T(8,128)(2,1)}, u32[]{:S(2)}, u32[]{:S(2)}) collective-permute-start(bf16[384,640]{1,0:T(8,128)(2,1)} %copy-done.31), channel_id=1, source_target_pairs={{0,16},{8,24},{16,0},{24,8},{1,17},{9,25},{17,1},{25,9},{2,18},{10... | collective-permute-start | bytes 1474568 | tf_op jit(solution)/shard_map/ppermute | solution.py:30
  120.6 6.2 %copy-done = bf16[1792,5120]{1,0:T(8,128)(2,1)S(1)} copy-done((bf16[1792,5120]{1,0:T(8,128)(2,1)S(1)}, bf16[1792,5120]{1,0:T(8,128)(2,1)}, u32[]{:S(2)}) %copy-start) | copy-done | bytes 18350104
  130.5 11.7 %grads.1 = (bf16[384,1792]{1,0:T(8,128)(2,1)}, bf16[384,1792]{1,0:T(8,128)(2,1)}, f32[8,128]{1,0:T(8,128)S(1)}) custom-call(s32[8]{0:T(128)S(1)} %add.40.offs_ref, bf16[384,640]{1,0:T(8,128)(2,1)S(1)} %copy-done.1, bf16[384,640]{1,0:T(8,128)(2,1)S(1)} %after.5.refs_5_.refs_1_, bf16[384,640]{1,0:T(8,128)(2,1)} %after.6.refs_2_, ...), custom_call_target="tpu_custom_call" | custom-call | flops 1024 | bytes 1024 | tf_op jit(solution)/shard_map/grads/pallas_call | solution.py:172
  145.8 5.3 %all-to-all-start.3 = ((f32[32,1,128]{2,1,0:T(1,128)}), f32[32,1,128]{2,1,0:T(1,128)S(1)}, u32[]{:S(2)}, u32[]{:S(2)}) async-start(f32[32,1,128]{2,1,0:T(1,128)} %bitcast.3), calls=%async_computation.3 | async-start | bytes 32768 | tf_op jit(solution)/shard_map/all_to_all | solution.py:425
  151.1 2.6 %copy-done.29 = bf16[1792,1536]{1,0:T(8,128)(2,1)S(1)} copy-done((bf16[1792,1536]{1,0:T(8,128)(2,1)S(1)}, bf16[1792,1536]{1,0:T(8,128)(2,1)}, u32[]{:S(2)}) %copy-start.29) | copy-done | bytes 5505048
  153.7 12.8 %wgrad.1 = bf16[1792,1280]{1,0:T(8,128)(2,1)} custom-call(s32[2]{0:T(128)S(1)} %add_multiply_fusion.offs_ref, s32[4]{0:T(128)S(1)} %xor_multiply_fusion.offs_ref.toks_ref, bf16[1792,1536]{1,0:T(8,128)(2,1)S(1)} %copy-done.29, bf16[4,384,640]{2,1,0:T(8,128)(2,1)} %all-to-all-done.refs_1_.own_ref, bf16[384,640]{1,0:T(8,128)(2,1)S(1)} %copy-done.9, ...), custom_call_target="tpu_custom_call" | custom-call | flops 7046430720 | bytes 14024704 | tf_op jit(solution)/shard_map/wgrad/pallas_call | solution.py:227
  (114 shorter events, 34.5 us)
Async XLA Ops:
  0.6 14.4 %collective-permute-start.1 = (bf16[384,640]{1,0:T(8,128)(2,1)}, bf16[384,640]{1,0:T(8,128)(2,1)S(1)}, u32[]{:S(2)}, u32[]{:S(2)}) collective-permute-start(bf16[384,640]{1,0:T(8,128)(2,1)} %refs_0_.5), channel_id=1, source_target_pairs={{0,1},{1,0},{2,3},{3,2},{4,5},{5,4},{6,7},{7,6},{8,9},{9,8},{10,11... | collective-permute-start | bytes 1474568 | tf_op jit(solution)/shard_map/ppermute | solution.py:30
  3.6 13.0 %collective-permute-start.2 = (bf16[384,640]{1,0:T(8,128)(2,1)}, bf16[384,640]{1,0:T(8,128)(2,1)}, u32[]{:S(2)}, u32[]{:S(2)}) collective-permute-start(bf16[384,640]{1,0:T(8,128)(2,1)} %refs_0_.5), channel_id=1, source_target_pairs={{0,16},{8,24},{16,0},{24,8},{1,17},{9,25},{17,1},{25,9},{2,18},{10... | collective-permute-start | bytes 1474568 | tf_op jit(solution)/shard_map/ppermute | solution.py:30
  5.2 11.5 %collective-permute-start.3 = (bf16[384,640]{1,0:T(8,128)(2,1)}, bf16[384,640]{1,0:T(8,128)(2,1)S(1)}, u32[]{:S(2)}, u32[]{:S(2)}) collective-permute-start(bf16[384,640]{1,0:T(8,128)(2,1)} %refs_0_.5), channel_id=1, source_target_pairs={{0,8},{8,0},{16,24},{24,16},{1,9},{9,1},{17,25},{25,17},{2,10},{10... | collective-permute-start | bytes 1474568 | tf_op jit(solution)/shard_map/ppermute | solution.py:30
  5.2 15.7 %collective-permute-start = (bf16[384,640]{1,0:T(8,128)(2,1)}, bf16[384,640]{1,0:T(8,128)(2,1)S(1)}, u32[]{:S(2)}, u32[]{:S(2)}) collective-permute-start(bf16[384,640]{1,0:T(8,128)(2,1)} %refs_0_.5), channel_id=1, source_target_pairs={{0,2},{1,3},{2,4},{3,5},{4,6},{5,7},{6,0},{7,1},{8,10},{9,11},{10,... | collective-permute-start | bytes 1474568 | tf_op jit(solution)/shard_map/ppermute | solution.py:35
  20.9 31.6 %collective-permute-start.9 = (bf16[1792,384]{1,0:T(8,128)(2,1)}, bf16[1792,384]{1,0:T(8,128)(2,1)}, u32[]{:S(2)}, u32[]{:S(2)}) collective-permute-start(bf16[1792,384]{1,0:T(8,128)(2,1)} %after.7.refs_0_), channel_id=1, source_target_pairs={{0,8},{8,0},{16,24},{24,16},{1,9},{9,1},{17,25},{25,17},{2,10},{10... | collective-permute-start | bytes 4128776 | tf_op jit(solution)/shard_map/ppermute | solution.py:30
  21.0 32.8 %collective-permute-start.11 = (bf16[1792,384]{1,0:T(8,128)(2,1)}, bf16[1792,384]{1,0:T(8,128)(2,1)S(1)}, u32[]{:S(2)}, u32[]{:S(2)}) collective-permute-start(bf16[1792,384]{1,0:T(8,128)(2,1)} %after.7.refs_0_), channel_id=1, source_target_pairs={{0,16},{8,24},{16,0},{24,8},{1,17},{9,25},{17,1},{25,9},{2,18},{10... | collective-permute-start | bytes 4128776 | tf_op jit(solution)/shard_map/ppermute | solution.py:30
  21.5 3.6 %collective-permute-start.6 = (bf16[384,640]{1,0:T(8,128)(2,1)}, bf16[384,640]{1,0:T(8,128)(2,1)}, u32[]{:S(2)}, u32[]{:S(2)}) collective-permute-start(bf16[384,640]{1,0:T(8,128)(2,1)} %collective-permute-done.2.refs_2_), channel_id=1, source_target_pairs={{0,8},{8,0},{16,24},{24,16},{1,9},{9,1},{17,25},{25,17},{2,10},{10... | collective-permute-start | bytes 1474568 | tf_op jit(solution)/shard_map/ppermute | solution.py:30
  21.7 13.5 %collective-permute-start.5 = (bf16[384,640]{1,0:T(8,128)(2,1)S(1)}, bf16[384,640]{1,0:T(8,128)(2,1)S(1)}, u32[]{:S(2)}, u32[]{:S(2)}) collective-permute-start(bf16[384,640]{1,0:T(8,128)(2,1)S(1)} %after.5.refs_5_.refs_1_), channel_id=1, source_target_pairs={{0,1},{1,0},{2,3},{3,2},{4,5},{5,4},{6,7},{7,6},{8,9},{9,8},{10,11... | collective-permute-start | bytes 1474568 | tf_op jit(solution)/shard_map/ppermute | solution.py:30
  22.2 15.1 %collective-permute-start.4 = (bf16[384,640]{1,0:T(8,128)(2,1)S(1)}, bf16[384,640]{1,0:T(8,128)(2,1)}, u32[]{:S(2)}, u32[]{:S(2)}) collective-permute-start(bf16[384,640]{1,0:T(8,128)(2,1)S(1)} %after.5.refs_5_.refs_1_), channel_id=1, source_target_pairs={{0,2},{1,3},{2,4},{3,5},{4,6},{5,7},{6,0},{7,1},{8,10},{9,11},{10,... | collective-permute-start | bytes 1474568 | tf_op jit(solution)/shard_map/ppermute | solution.py:35
  38.1 14.4 %collective-permute-start.7 = (bf16[384,640]{1,0:T(8,128)(2,1)}, bf16[384,640]{1,0:T(8,128)(2,1)S(1)}, u32[]{:S(2)}, u32[]{:S(2)}) collective-permute-start(bf16[384,640]{1,0:T(8,128)(2,1)} %after.6.refs_2_), channel_id=1, source_target_pairs={{0,2},{1,3},{2,4},{3,5},{4,6},{5,7},{6,0},{7,1},{8,10},{9,11},{10,... | collective-permute-start | bytes 1474568 | tf_op jit(solution)/shard_map/ppermute | solution.py:35
  38.1 14.4 %collective-permute-start.8 = (bf16[384,640]{1,0:T(8,128)(2,1)}, bf16[384,640]{1,0:T(8,128)(2,1)}, u32[]{:S(2)}, u32[]{:S(2)}) collective-permute-start(bf16[384,640]{1,0:T(8,128)(2,1)} %after.6.refs_2_), channel_id=1, source_target_pairs={{0,1},{1,0},{2,3},{3,2},{4,5},{5,4},{6,7},{7,6},{8,9},{9,8},{10,11... | collective-permute-start | bytes 1474568 | tf_op jit(solution)/shard_map/ppermute | solution.py:30
  57.3 31.2 %all-to-all-start = ((bf16[4,384,640]{2,1,0:T(8,128)(2,1)}), bf16[4,384,640]{2,1,0:T(8,128)(2,1)}, u32[]{:S(2)}, u32[]{:S(2)}) async-start(bf16[4,384,640]{2,1,0:T(8,128)(2,1)} %own_features.1.refs_5_), calls=%async_computation | async-start | bytes 3932160 | tf_op jit(solution)/shard_map/all_to_all | solution.py:403
  61.7 3.8 %collective-permute-start.12 = (bf16[1792,384]{1,0:T(8,128)(2,1)S(1)}, bf16[1792,384]{1,0:T(8,128)(2,1)S(1)}, u32[]{:S(2)}, u32[]{:S(2)}) collective-permute-start(bf16[1792,384]{1,0:T(8,128)(2,1)S(1)} %after.9.refs_4_.refs_2_), channel_id=1, source_target_pairs={{0,8},{8,0},{16,24},{24,16},{1,9},{9,1},{17,25},{25,17},{2,10},{10... | collective-permute-start | bytes 4128776 | tf_op jit(solution)/shard_map/ppermute | solution.py:30
  62.2 19.8 %collective-permute-start.14 = (f32[4,32,1536]{2,1,0:T(8,128)}, f32[4,32,1536]{2,1,0:T(8,128)S(1)}, u32[]{:S(2)}, u32[]{:S(2)}) collective-permute-start(f32[4,32,1536]{2,1,0:T(8,128)} %copy-done.21), channel_id=1, source_target_pairs={{0,1},{1,0},{2,3},{3,2},{4,5},{5,4},{6,7},{7,6},{8,9},{9,8},{10,11... | collective-permute-start | bytes 2359304 | tf_op jit(solution)/shard_map/ppermute | solution.py:30
  62.7 19.2 %collective-permute-start.10 = (bf16[384,640]{1,0:T(8,128)(2,1)}, bf16[384,640]{1,0:T(8,128)(2,1)S(1)}, u32[]{:S(2)}, u32[]{:S(2)}) collective-permute-start(bf16[384,640]{1,0:T(8,128)(2,1)} %collective-permute-done.8.refs_1_.refs_2_.refs_6_), channel_id=1, source_target_pairs={{0,2},{1,3},{2,4},{3,5},{4,6},{5,7},{6,0},{7,1},{8,10},{9,11},{10,... | collective-permute-start | bytes 1474568 | tf_op jit(solution)/shard_map/ppermute | solution.py:35
  62.7 19.2 %copy-start.3 = (bf16[384,640]{1,0:T(8,128)(2,1)S(1)}, bf16[384,640]{1,0:T(8,128)(2,1)}, u32[]{:S(2)}) copy-start(bf16[384,640]{1,0:T(8,128)(2,1)} %copy-done.2) | copy-start | bytes 1474564
  88.5 24.6 %all-to-all-start.2 = ((f32[4,32,1536]{2,1,0:T(8,128)}), f32[4,32,1536]{2,1,0:T(8,128)S(1)}, u32[]{:S(2)}, u32[]{:S(2)}) async-start(f32[4,32,1536]{2,1,0:T(8,128)} %grad_pair.1.refs_0_), calls=%async_computation.2 | async-start | bytes 1572864 | tf_op jit(solution)/shard_map/all_to_all | solution.py:323
  92.1 18.9 %collective-permute-start.13 = (f32[4,32,1536]{2,1,0:T(8,128)S(1)}, f32[4,32,1536]{2,1,0:T(8,128)S(1)}, u32[]{:S(2)}, u32[]{:S(2)}) collective-permute-start(f32[4,32,1536]{2,1,0:T(8,128)S(1)} %copy-done.25), channel_id=1, source_target_pairs={{0,1},{1,0},{2,3},{3,2},{4,5},{5,4},{6,7},{7,6},{8,9},{9,8},{10,11... | collective-permute-start | bytes 2359304 | tf_op jit(solution)/shard_map/ppermute | solution.py:30
  113.1 29.6 %all-to-all-start.1 = ((f32[4,32,1536]{2,1,0:T(8,128)}), f32[4,32,1536]{2,1,0:T(8,128)}, u32[]{:S(2)}, u32[]{:S(2)}) async-start(f32[4,32,1536]{2,1,0:T(8,128)} %hidden_pair.1.refs_11_), calls=%async_computation.1 | async-start | bytes 1572864 | tf_op jit(solution)/shard_map/all_to_all | solution.py:323
  118.0 24.2 %collective-permute-start.15 = (bf16[384,640]{1,0:T(8,128)(2,1)}, bf16[384,640]{1,0:T(8,128)(2,1)}, u32[]{:S(2)}, u32[]{:S(2)}) collective-permute-start(bf16[384,640]{1,0:T(8,128)(2,1)} %copy-done.32), channel_id=1, source_target_pairs={{0,8},{8,0},{16,24},{24,16},{1,9},{9,1},{17,25},{25,17},{2,10},{10... | collective-permute-start | bytes 1474568 | tf_op jit(solution)/shard_map/ppermute | solution.py:30
  118.0 24.2 %collective-permute-start.16 = (bf16[384,640]{1,0:T(8,128)(2,1)}, bf16[384,640]{1,0:T(8,128)(2,1)}, u32[]{:S(2)}, u32[]{:S(2)}) collective-permute-start(bf16[384,640]{1,0:T(8,128)(2,1)} %copy-done.31), channel_id=1, source_target_pairs={{0,16},{8,24},{16,0},{24,8},{1,17},{9,25},{17,1},{25,9},{2,18},{10... | collective-permute-start | bytes 1474568 | tf_op jit(solution)/shard_map/ppermute | solution.py:30
  120.2 22.6 %collective-permute-start.17 = (bf16[384,640]{1,0:T(8,128)(2,1)}, bf16[384,640]{1,0:T(8,128)(2,1)}, u32[]{:S(2)}, u32[]{:S(2)}) collective-permute-start(bf16[384,640]{1,0:T(8,128)(2,1)} %copy-done.30), channel_id=1, source_target_pairs={{0,24},{8,16},{16,8},{24,0},{1,25},{9,17},{17,9},{25,1},{2,26},{10... | collective-permute-start | bytes 1474568 | tf_op jit(solution)/shard_map/ppermute | solution.py:30
  130.5 12.2 %copy-start.27 = (s32[3]{0:T(128)S(1)}, s32[3]{0:T(128)}, u32[]{:S(2)}) copy-start(s32[3]{0:T(128)} %assign_ref.1) | copy-start | bytes 40
  145.8 20.7 %all-to-all-start.3 = ((f32[32,1,128]{2,1,0:T(1,128)}), f32[32,1,128]{2,1,0:T(1,128)S(1)}, u32[]{:S(2)}, u32[]{:S(2)}) async-start(f32[32,1,128]{2,1,0:T(1,128)} %bitcast.3), calls=%async_computation.3 | async-start | bytes 32768 | tf_op jit(solution)/shard_map/all_to_all | solution.py:425
  (31 other events, 114.6 us)

commit v10 on v9

--- a/solution.py
+++ b/solution.py
@@ -37,6 +37,10 @@
 
 def whole(shape):
     return pl.BlockSpec(shape, lambda *_: (0,) * len(shape))
+
+
+def each(arrays):
+    return [whole(x.shape) for x in arrays]
 
 
 ANY = pl.BlockSpec(memory_space=pl.ANY)
@@ -108,11 +112,13 @@
 
 def stack(at, blocks, order, name):
     n = len(blocks)
+    shape = (n,) + blocks[0].shape
     return pl.pallas_call(
         functools.partial(stack_body, n),
+        grid=(1,),
         in_specs=[pl.BlockSpec(memory_space=pltpu.SMEM)] + [ANY] * (n + len(order)),
-        out_specs=pl.BlockSpec(memory_space=pltpu.VMEM),
-        out_shape=jax.ShapeDtypeStruct((n,) + blocks[0].shape, BF16),
+        out_specs=whole(shape),
+        out_shape=jax.ShapeDtypeStruct(shape, BF16),
         scratch_shapes=[pltpu.SemaphoreType.DMA((n,))],
         compiler_params=params(8),
         cost_estimate=SMALL,
@@ -137,9 +143,10 @@
     n = len(blocks)
     return pl.pallas_call(
         functools.partial(arrange_body, n),
+        grid=(1,),
         in_specs=[pl.BlockSpec(memory_space=pltpu.SMEM)] + [ANY] * (n + len(order)),
-        out_specs=[pl.BlockSpec(memory_space=pltpu.VMEM)] * n,
-        out_shape=[jax.ShapeDtypeStruct(blocks[0].shape, BF16)] * n,
+        out_specs=each(blocks),
+        out_shape=[jax.ShapeDtypeStruct(x.shape, BF16) for x in blocks],
         scratch_shapes=[pltpu.SemaphoreType.DMA((n,))],
         compiler_params=params(8),
         cost_estimate=SMALL,
@@ -180,16 +187,18 @@
             scratch_shapes=[pltpu.VMEM((toks, feats), BF16)],
         ),
         out_shape=(out, out, jax.ShapeDtypeStruct((8, 128), F32)),
-        compiler_params=params(24),
+        compiler_params=params(48),
         cost_estimate=SMALL,
         name="grads",
     )(offs, *blocks, weight, by_gate, by_up, order)
 
 
-def wgrad_body(n, offs_ref, toks_ref, hid_ref, own_ref, *refs):
-    others, (order_ref, out_ref, hid, cols, outs, hid_sems, col_sems, out_sems) = refs[:n], refs[n:]
+def wgrad_body(n, offs_ref, toks_ref, own_ref, *refs):
+    others, hids = refs[:n], refs[n : 2 * n]
+    out_ref, done_ref, hid, cols, outs, hid_sems, col_sems, out_sems = refs[-8:]
+    done_ref[...] = jnp.zeros_like(done_ref)
     _, toks, width = own_ref.shape
-    steps, tile, _ = hid.shape
+    steps, tile, _ = outs.shape
     own, other = (pl.ds(pl.multiple_of(offs_ref[half], 128), width) for half in range(2))
     came = []
     for k in range(n):
@@ -197,124 +206,138 @@
         came.append((own_ref.at[k], cols.at[k * toks : (k + 1) * toks, own]))
         came.append((others[k], cols.at[rows, other]))
     came = [pltpu.make_async_copy(a, b, col_sems.at[j]) for j, (a, b) in enumerate(came)]
-    came += [
-        pltpu.make_async_copy(hid_ref.at[i * tile : (i + 1) * tile], hid.at[i], hid_sems.at[i])
-        for i in range(steps)
-    ]
+    units = []
+    for i in range(steps):
+        part = slice(i * tile, (i + 1) * tile)
+        for k in range(n):
+            place = pl.ds(pl.multiple_of(toks_ref[k], 128), toks)
+            units.append(
+                pltpu.make_async_copy(
+                    hids[k].at[part], hid.at[part, place], hid_sems.at[i * n + k]
+                )
+            )
+    for copy in [*units[:n], *came, *units[n:]]:
+        copy.start()
     for copy in came:
-        copy.start()
-    for copy in came[:-steps]:
         copy.wait()
     gone = []
     for i in range(steps):
-        came[i - steps].wait()
+        for copy in units[i * n : (i + 1) * n]:
+            copy.wait()
+        part = slice(i * tile, (i + 1) * tile)
         outs[i] = lax.dot_general(
-            hid[i], cols[...], (((1,), (0,)), ((), ())), preferred_element_type=F32
+            hid[part], cols[...], (((1,), (0,)), ((), ())), preferred_element_type=F32
         ).astype(BF16)
-        rows = out_ref.at[i * tile : (i + 1) * tile]
-        gone.append(pltpu.make_async_copy(outs.at[i], rows, out_sems.at[i]))
+        gone.append(pltpu.make_async_copy(outs.at[i], out_ref.at[part], out_sems.at[i]))
         gone[-1].start()
     for copy in gone:
         copy.wait()
 
 
-def wgrad(offs, tok_offs, hid, own, others, order):
-    units, total = hid.shape
+def wgrad(offs, tok_offs, own, others, hids, order):
     n, toks, width = own.shape
+    units = hids[0].shape[0]
+    total = n * toks
     steps = 4
-    tile = units // steps
     smem = pl.BlockSpec(memory_space=pltpu.SMEM)
     return pl.pallas_call(
         functools.partial(wgrad_body, n),
-        in_specs=[smem, smem, HBM] + [ANY] * (n + 2),
-        out_specs=HBM,
-        out_shape=jax.ShapeDtypeStruct((units, 2 * width), BF16),
+        in_specs=[smem, smem] + [ANY] * (2 * n + 1 + len(order)),
+        out_specs=[ANY, pl.BlockSpec(memory_space=pltpu.VMEM)],
+        out_shape=[
+            jax.ShapeDtypeStruct((units, 2 * width), BF16),
+            jax.ShapeDtypeStruct((8, 128), F32),
+        ],
         scratch_shapes=[
-            pltpu.VMEM((steps, tile, total), BF16),
+            pltpu.VMEM((units, total), BF16),
             pltpu.VMEM((total, 2 * width), BF16),
-            pltpu.VMEM((steps, tile, 2 * width), BF16),
-            pltpu.SemaphoreType.DMA((steps,)),
+            pltpu.VMEM((steps, units // steps, 2 * width), BF16),
+            pltpu.SemaphoreType.DMA((steps * n,)),
             pltpu.SemaphoreType.DMA((2 * n,)),
             pltpu.SemaphoreType.DMA((steps,)),
         ],
-        compiler_params=params(28),
-        cost_estimate=pl.CostEstimate(
-            flops=4 * total * units * width,
-            bytes_accessed=2 * (total * (units + 2 * width) + 2 * units * width),
-            transcendentals=0,
-        ),
+        compiler_params=params(24),
+        cost_estimate=SMALL,
         name="wgrad",
-    )(offs, tok_offs, hid, own, *others, order)
-
-
-def put_slices(inner_ref, part, kept_ref, away_ref):
-    outer, size, _ = kept_ref.shape
+    )(offs, tok_offs, own, *others, *hids, *order)
+
+
+def put_slices(inner_ref, part, kept_ref, away_refs):
+    outer, size, total = kept_ref.shape
+    half = total // 2
     for inner in range(2):
 
         @pl.when(inner_ref[0] == inner)
         def _():
             for p in range(2 * outer):
-                out_ref = kept_ref if p % 2 == inner else away_ref
-                out_ref[p // 2] = part[p * size : (p + 1) * size]
+                rows = part[p * size : (p + 1) * size]
+                if p % 2 == inner:
+                    kept_ref[p // 2] = rows
+                else:
+                    for h in range(2):
+                        away_refs[h][p // 2] = rows[:, h * half : (h + 1) * half]
 
 
 def grad_gram_body(inner_ref, offs_ref, *refs):
-    toks_refs, (val_ref, order_ref, kept_ref, away_ref, wide) = refs[:-5], refs[-5:]
+    n = len(refs) - 6
+    toks_refs, (val_ref, _, kept_ref, *away_refs, wide) = refs[:n], refs[n:]
     for k, ref in enumerate(toks_refs):
         toks = ref.shape[0]
         wide[:, pl.ds(pl.multiple_of(offs_ref[k], 128), toks)] = dot_nt(val_ref[...], ref[...])
-    put_slices(inner_ref, wide, kept_ref, away_ref)
+    put_slices(inner_ref, wide, kept_ref, away_refs)
 
 
 def hidden_gram_body(inner_ref, offs_ref, *refs):
-    hid, (val_ref, order_ref, kept_ref, away_ref, all_ref, wide, held, sem) = refs[:-8], refs[-8:]
+    n = len(refs) - 6
+    hid, (val_ref, _, kept_ref, *away_refs, wide) = refs[:n], refs[n:]
     for k, ref in enumerate(hid):
         toks = ref.shape[1]
-        held[:, pl.ds(pl.multiple_of(offs_ref[k], 128), toks)] = ref[...]
-    copy = pltpu.make_async_copy(held, all_ref, sem)
-    copy.start()
-    wide[...] = lax.dot_general(
-        val_ref[...], held[...], (((1,), (0,)), ((), ())), preferred_element_type=F32
-    )
-    put_slices(inner_ref, wide, kept_ref, away_ref)
-    copy.wait()
-
-
-def gram_call(body, inner, offs, operands, order, parts, extra, name):
+        wide[:, pl.ds(pl.multiple_of(offs_ref[k], 128), toks)] = lax.dot_general(
+            val_ref[...], ref[...], (((1,), (0,)), ((), ())), preferred_element_type=F32
+        )
+    put_slices(inner_ref, wide, kept_ref, away_refs)
+
+
+def gram(body, inner, offs, operands, order, parts, name):
     smem = pl.BlockSpec(memory_space=pltpu.SMEM)
-    vmem = pl.BlockSpec(memory_space=pltpu.VMEM)
     *toks, vals = operands
     total = sum(x.size for x in toks) // vals.shape[1]
-    half = jax.ShapeDtypeStruct((parts // 2, vals.shape[0] // parts, total), F32)
-    shapes = [half, half, *extra]
-    return pl.pallas_call(
+    kept = jax.ShapeDtypeStruct((parts // 2, vals.shape[0] // parts, total), F32)
+    away = jax.ShapeDtypeStruct((parts // 2, vals.shape[0] // parts, total // 2), F32)
+    shapes = [kept, away, away]
+    kept, *away = pl.pallas_call(
         body,
-        in_specs=[smem, smem] + [vmem] * len(operands) + [ANY],
-        out_specs=[vmem, vmem] + [HBM] * len(extra),
+        grid=(1,),
+        in_specs=[smem, smem] + each(operands) + [ANY],
+        out_specs=each(shapes),
         out_shape=shapes,
-        scratch_shapes=[pltpu.VMEM((vals.shape[0], total), F32)]
-        + [y for x in extra for y in (pltpu.VMEM(x.shape, x.dtype), pltpu.SemaphoreType.DMA)],
-        compiler_params=params(20),
+        scratch_shapes=[pltpu.VMEM((vals.shape[0], total), F32)],
+        compiler_params=params(28),
         cost_estimate=SMALL,
         name=name,
     )(inner, offs, *operands, order)
-
-
-def pair_body(kept_ref, came_ref, *refs):
-    refs[-1][...] = kept_ref[...] + came_ref[...]
+    return kept, away, [swap(x, "fsdp", 1) for x in away]
+
+
+def pair_body(kept_ref, *refs):
+    came_refs, out_ref = refs[:2], refs[-1]
+    half = came_refs[0].shape[2]
+    for h in range(2):
+        cols = slice(h * half, (h + 1) * half)
+        out_ref[:, :, cols] = kept_ref[:, :, cols] + came_refs[h][...]
 
 
 def pair_sum(kept, came, order, name):
-    vmem = pl.BlockSpec(memory_space=pltpu.VMEM)
     return pl.pallas_call(
         pair_body,
-        in_specs=[vmem, vmem] + [ANY] * len(order),
-        out_specs=vmem,
+        grid=(1,),
+        in_specs=each([kept, *came]) + [ANY] * len(order),
+        out_specs=whole(kept.shape),
         out_shape=jax.ShapeDtypeStruct(kept.shape, F32),
-        compiler_params=params(8),
+        compiler_params=params(16),
         cost_estimate=SMALL,
         name=name,
-    )(kept, came, *order)
+    )(kept, *came, *order)
 
 
 def spread(pair):
@@ -343,11 +366,11 @@
 
 
 def score_line(assign, hid, grad, order, rows, copies):
-    vmem = pl.BlockSpec(memory_space=pltpu.VMEM)
     return pl.pallas_call(
         functools.partial(line_body, rows),
-        in_specs=[pl.BlockSpec(memory_space=pltpu.SMEM), vmem, vmem] + [ANY] * len(order),
-        out_specs=vmem,
+        grid=(1,),
+        in_specs=[pl.BlockSpec(memory_space=pltpu.SMEM)] + each([hid, grad]) + [ANY] * len(order),
+        out_specs=whole((copies, 128)),
         out_shape=jax.ShapeDtypeStruct((copies, 128), F32),
         compiler_params=params(8),
         cost_estimate=SMALL,
@@ -383,49 +406,46 @@
     far = swap(hidden, "dp", 2)
     near = swap(hidden, "dp", 1)
 
-    grad_kept, away = gram_call(
-        grad_gram_body, inner_at, tok_offs, [*grad_dp, val_grad], first, n_fs, [], "grad_gram"
-    )
-    grad_came = swap(away, "fsdp", 1)
+    grad_kept, away, grad_came = gram(
+        grad_gram_body, inner_at, tok_offs, [*grad_dp, val_grad], first, n_fs, "grad_gram"
+    )
     ring = [out_grad, first]
-    for _ in range(n_out - 2):
-        others.append(swap(ring[-1], "fsdp", 1))
-        order = away if len(ring) == 2 else near
-        ring.append(after(shift(ring[-1], "fsdp", 2), others[-1], order))
-    others.append(shift(others[-1], "fsdp", 2))
+    others.append(swap(ring[1], "fsdp", 1))
+    ring.append(after(shift(ring[1], "fsdp", 2), others[1], grad_came[0]))
+    others.append(swap(ring[2], "fsdp", 1))
+    ring.append(after(shift(ring[2], "fsdp", 2), near))
+    others.append(shift(others[2], "fsdp", 2))
 
     def over_columns(blocks):
         return [x if k == 0 else swap(x, "dp", k) for k, x in enumerate(blocks)]
 
-    far = after(far, ring[-1])
+    far = after(far, ring[3])
     hid_dp = [hidden, near, far, swap(far, "dp", 1)]
     own = stack(at, ring, [far], "own_features")
     own_cols = lax.all_to_all(own, "dp", split_axis=0, concat_axis=0, tiled=True)
-    hid_kept, away, hid_all = gram_call(
-        hidden_gram_body, inner_at, tok_offs, [*hid_dp, val_hidden], own, n_fs,
-        [jax.ShapeDtypeStruct((units, total), BF16)], "hidden_gram",
-    )
-    hid_came = swap(away, "fsdp", 1)
-    other = arrange(to, others, [away, grad_came], "other_features")
+    hid_kept, away, hid_came = gram(
+        hidden_gram_body, inner_at, tok_offs, [*hid_dp, val_hidden], own, n_fs, "hidden_gram"
+    )
+    grad_pair = pair_sum(grad_kept, grad_came, away, "grad_pair")
+    other = arrange(to, others, [grad_pair, hid_came[0]], "other_features")
     other_cols = over_columns(other)
-    grad_pair = pair_sum(grad_kept, grad_came, [other[0]], "grad_pair")
     grad_sums = spread(grad_pair)
-    hid_pair = pair_sum(hid_kept, hid_came, [grad_pair, own_cols], "hidden_pair")
-    hid_sums = spread(hid_pair)
 
     offs = (jnp.stack([inner, 1 - inner]) * width).astype(jnp.int32)
     places = (offs[:, None] + at[None, :] * (2 * width)).reshape(-1)
     grad_gate, grad_up, done = grads(
-        places, [*ring, *others], down_weight, by_gate, by_up, hid_pair
-    )
+        places, [*ring, *others], down_weight, by_gate, by_up, other[0]
+    )
+    hid_pair = pair_sum(hid_kept, hid_came, [done, own_cols], "hidden_pair")
+    hid_sums = spread(hid_pair)
+    weight_grad, done = wgrad(offs, tok_offs, own_cols, other_cols, hid_dp, [hid_pair])
 
     mine = score_line(
-        assign, hid_sums, grad_sums, [done, *other_cols], n_dp * rows_here, n_dp * n_fs
+        assign, hid_sums, grad_sums, [done], n_dp * rows_here, n_dp * n_fs
     )
     every = lax.all_to_all(
         mine, ("dp", "fsdp"), split_axis=0, concat_axis=0, tiled=True
     ).reshape(n_dp, n_fs, 128)
-    weight_grad = wgrad(offs, tok_offs, hid_all, own_cols, other_cols, mine)
 
     rows = n_dp * rows_here
     scale = 1.0 / jnp.sqrt(F32(L) * VAL * FFW * D)

time: 169 us -> 218 us (1.29)
  waiting for transfers between devices: 62.7 us -> 95.4 us
  starting transfers between devices: 31.1 us -> 41.4 us
  local copies, waits for them, and re-layouts: 27.9 us -> 32.9 us
    ppermute x14 -> x16, waiting for transfers between devices: 43.4 us -> 54.4 us  [swap(): return lax.ppermute(x, axis, [(s, s ^ k) for s in range(n)])]
    all_to_all x1, waiting for transfers between devices: 0.01 us -> 8.88 us  [per_device(): lax.all_to_all(own, 'dp', split_axis=0, concat_axis=0, tiled=True)]
    all_to_all x1, waiting for transfers between devices: 0.01 us -> 7.12 us  [per_device(): lax.all_to_all(mine, ('dp', 'fsdp'), split_axis=0, concat_axis=0, tiled=T...]
    ppermute x4, waiting for transfers between devices: 19.2 us -> 24.9 us  [shift(): return lax.ppermute(x, axis, [(s, (s + k) % n) for s in range(n)])]
    ppermute x14 -> x16, starting transfers between devices: 11.3 us -> 16.3 us  [swap(): return lax.ppermute(x, axis, [(s, s ^ k) for s in range(n)])]
    unnamed x67 -> x93, local copies, waits for them, and re-layouts: 27.5 us -> 32.5 us
    ppermute x4, starting transfers between devices: 1.58 us -> 6.36 us  [shift(): return lax.ppermute(x, axis, [(s, (s + k) % n) for s in range(n)])]
    pallas_call x1, Pallas kernels: 11.7 us -> 14.6 us  [grads(): pl.pallas_call(functools.partial(grads_body, n), grid_spec=pltpu.Prefetch...]
  transfers between devices with their start and end apart: 22 -> 24, of which waited for: 12 -> 13; matrix products, arithmetic and copies ran while one was open for 0% -> 0% of each run, Pallas kernels for 23% -> 19%
where the time goes in v10:
time: 218 us; the launch traced here: 216 us
  waiting for transfers between devices  95.4 us (44%)
  Pallas kernels  44.9 us (21%)
  starting transfers between devices  41.4 us (19%)
  local copies, waits for them, and re-layouts  32.9 us (15%)
    ppermute x16, waiting for transfers between devices, swap(): return lax.ppermute(x, axis, [(s, s ^ k) for s in range(n)])  54.4 us
    unnamed x93, local copies, waits for them, and re-layouts  32.5 us
    ppermute x4, waiting for transfers between devices, shift(): return lax.ppermute(x, axis, [(s, (s + k) % n) for s in range(n)])  24.9 us
    ppermute x16, starting transfers between devices, swap(): return lax.ppermute(x, axis, [(s, s ^ k) for s in range(n)])  16.3 us
    pallas_call x1, Pallas kernels, grads(): pl.pallas_call(functools.partial(grads_body, n), grid_spec=pltpu.Prefetch...  14.6 us
    pallas_call x1, Pallas kernels, wgrad(): pl.pallas_call(functools.partial(wgrad_body, n), in_specs=[smem, smem] +...  11.9 us
    all_to_all x2, starting transfers between devices, spread(): lax.all_to_all(pair, 'fsdp', split_axis=0, concat_axis=0, axis_index_grou...  9.61 us
    all_to_all x1, waiting for transfers between devices, per_device(): lax.all_to_all(own, 'dp', split_axis=0, concat_axis=0, tiled=True)  8.88 us
  transfers between devices with their start and end apart: 24, of which 13 were waited for; matrix products, arithmetic and copies ran while one was open for 0% of the time, Pallas kernels for 19%

profile of v10, /device:TPU:0, one launch (start us, length us, event | category | flops | bytes accessed | tf_op | source)
XLA Modules:
  0.0 216.3 jit_solution(1162606317531673731)
XLA Ops:
  0.6 3.0 %collective-permute-start.2 = (bf16[384,640]{1,0:T(8,128)(2,1)}, bf16[384,640]{1,0:T(8,128)(2,1)}, u32[]{:S(2)}, u32[]{:S(2)}) collective-permute-start(bf16[384,640]{1,0:T(8,128)(2,1)} %refs_0_.5), channel_id=1, source_target_pairs={{0,16},{8,24},{16,0},{24,8},{1,17},{9,25},{17,1},{25,9},{2,18},{10... | collective-permute-start | bytes 1474568 | tf_op jit(solution)/shard_map/ppermute | solution.py:30
  6.7 8.5 %collective-permute-done.2.refs_2_ = bf16[384,640]{1,0:T(8,128)(2,1)} collective-permute-done((bf16[384,640]{1,0:T(8,128)(2,1)}, bf16[384,640]{1,0:T(8,128)(2,1)}, u32[]{:S(2)}, u32[]{:S(2)}) %collective-permute-start.2) | collective-permute-done | bytes 491552 | tf_op jit(solution)/shard_map/ppermute | solution.py:30
  17.9 3.7 %hidden.1 = (bf16[1792,384]{1,0:T(8,128)(2,1)}, bf16[384,1792]{1,0:T(8,128)(2,1)S(1)}, bf16[384,1792]{1,0:T(8,128)(2,1)S(1)}) custom-call(bf16[384,1792]{1,0:T(8,128)(2,1)S(1)} %copy-done.28, bf16[384,1792]{1,0:T(8,128)(2,1)S(1)} %copy-done.29), custom_call_target="tpu_custom_call" | custom-call | flops 1024 | bytes 1024 | tf_op jit(solution)/shard_map/hidden/pallas_call | solution.py:86
  31.8 2.3 %grad_gram.1 = (f32[4,32,1536]{2,1,0:T(8,128)S(1)}, f32[4,32,768]{2,1,0:T(8,128)S(1)}, f32[4,32,768]{2,1,0:T(8,128)S(1)}) custom-call(s32[1]{0:T(128)} %bitcast.inner_ref, s32[4]{0:T(128)S(1)} %xor_multiply_fusion.offs_ref.toks_ref, bf16[384,640]{1,0:T(8,128)(2,1)S(1)} %copy-done.19, bf16[384,640]{1,0:T(8,128)(2,1)S(1)} %copy-done.23, ...), custom_call_target="tpu_custom_call" | custom-call | flops 1024 | bytes 1024 | tf_op jit(solution)/shard_map/grad_gram/pallas_call | solution.py:308
  34.7 5.1 %collective-permute-done.5.refs_1_.refs_5_ = bf16[384,640]{1,0:T(8,128)(2,1)S(1)} collective-permute-done((bf16[384,640]{1,0:T(8,128)(2,1)S(1)}, bf16[384,640]{1,0:T(8,128)(2,1)S(1)}, u32[]{:S(2)}, u32[]{:S(2)}) %collective-permute-start.5) | collective-permute-done | bytes 491552 | tf_op jit(solution)/shard_map/ppermute | solution.py:30
  39.9 1.9 collective-permute-done.4.refs_0_
  41.8 5.3 %collective-permute-done.7.refs_2_.refs_0_ = f32[4,32,768]{2,1,0:T(8,128)S(1)} collective-permute-done((f32[4,32,768]{2,1,0:T(8,128)S(1)}, f32[4,32,768]{2,1,0:T(8,128)S(1)}, u32[]{:S(2)}, u32[]{:S(2)}) %collective-permute-start.7) | collective-permute-done | bytes 393248 | tf_op jit(solution)/shard_map/ppermute | solution.py:30
  50.1 12.5 %collective-permute-done.8.refs_0_ = bf16[384,640]{1,0:T(8,128)(2,1)} collective-permute-done((bf16[384,640]{1,0:T(8,128)(2,1)}, bf16[384,640]{1,0:T(8,128)(2,1)}, u32[]{:S(2)}, u32[]{:S(2)}) %collective-permute-start.8) | collective-permute-done | bytes 491552 | tf_op jit(solution)/shard_map/ppermute | solution.py:35
  64.0 2.4 %own_features.1.refs_5_ = bf16[4,384,640]{2,1,0:T(8,128)(2,1)S(1)} custom-call(s32[4]{0:T(128)S(1)} %and_select_fusion.at_ref, bf16[384,640]{1,0:T(8,128)(2,1)S(1)} %copy-done.20, bf16[384,640]{1,0:T(8,128)(2,1)S(1)} %after.5.refs_5_.refs_1_, bf16[384,640]{1,0:T(8,128)(2,1)} %after.6.refs_2_, bf16[384,640]{1,0:T(8,128)(2,1)} %after.8.refs_1_.refs_3_, ...), custom_call_target="tpu_custom_call" | custom-call | flops 1024 | bytes 1024 | tf_op jit(solution)/shard_map/own_features/pallas_call | solution.py:116
  67.7 3.6 %all-to-all-start = ((bf16[4,384,640]{2,1,0:T(8,128)(2,1)}), bf16[4,384,640]{2,1,0:T(8,128)(2,1)S(1)}, u32[]{:S(2)}, u32[]{:S(2)}) async-start(bf16[4,384,640]{2,1,0:T(8,128)(2,1)} %copy-done), calls=%async_computation | async-start | bytes 3932160 | tf_op jit(solution)/shard_map/all_to_all | solution.py:425
  79.2 4.1 %hidden_gram.1 = (f32[4,32,1536]{2,1,0:T(8,128)S(1)}, f32[4,32,768]{2,1,0:T(8,128)S(1)}, f32[4,32,768]{2,1,0:T(8,128)S(1)}) custom-call(s32[1]{0:T(128)} %bitcast.inner_ref, s32[4]{0:T(128)S(1)} %xor_multiply_fusion.offs_ref.toks_ref, bf16[1792,384]{1,0:T(8,128)(2,1)} %after.7.refs_0_.refs_4_, bf16[1792,384]{1,0:T(8,128)(2,1)S(1)} %copy-done.3, ...), custom_call_target="tpu_custom_call" | custom-call | flops 1024 | bytes 1024 | tf_op jit(solution)/shard_map/hidden_gram/pallas_call | solution.py:308
  86.7 8.9 %all-to-all-done.refs_3_.own_ref = bf16[4,384,640]{2,1,0:T(8,128)(2,1)S(1)} async-done(((bf16[4,384,640]{2,1,0:T(8,128)(2,1)}), bf16[4,384,640]{2,1,0:T(8,128)(2,1)S(1)}, u32[]{:S(2)}, u32[]{:S(2)}) %all-to-all-start) | async-done | bytes 1966112 | tf_op jit(solution)/shard_map/all_to_all | solution.py:425
  95.6 4.2 %all-to-all-start.2 = ((f32[4,32,1536]{2,1,0:T(8,128)}), f32[4,32,1536]{2,1,0:T(8,128)}, u32[]{:S(2)}, u32[]{:S(2)}) async-start(f32[4,32,1536]{2,1,0:T(8,128)} %copy-done.7), calls=%async_computation.2 | async-start | bytes 1572864 | tf_op jit(solution)/shard_map/all_to_all | solution.py:346
  101.3 11.6 %collective-permute-done.10.refs_2_.refs_6_ = bf16[384,640]{1,0:T(8,128)(2,1)} collective-permute-done((bf16[384,640]{1,0:T(8,128)(2,1)}, bf16[384,640]{1,0:T(8,128)(2,1)}, u32[]{:S(2)}, u32[]{:S(2)}) %collective-permute-start.10) | collective-permute-done | bytes 491552 | tf_op jit(solution)/shard_map/ppermute | solution.py:30
  116.9 10.5 %collective-permute-done.11.refs_3_.refs_7_ = bf16[384,640]{1,0:T(8,128)(2,1)} collective-permute-done((bf16[384,640]{1,0:T(8,128)(2,1)}, bf16[384,640]{1,0:T(8,128)(2,1)}, u32[]{:S(2)}, u32[]{:S(2)}) %collective-permute-start.11) | collective-permute-done | bytes 491552 | tf_op jit(solution)/shard_map/ppermute | solution.py:35
  130.6 2.4 %other_features.1 = (bf16[384,640]{1,0:T(8,128)(2,1)S(1)}, bf16[384,640]{1,0:T(8,128)(2,1)S(1)}, bf16[384,640]{1,0:T(8,128)(2,1)S(1)}, bf16[384,640]{1,0:T(8,128)(2,1)S(1)}) custom-call(s32[4]{0:T(128)S(1)} %broadcast_xor_fusion.to_ref, bf16[384,640]{1,0:T(8,128)(2,1)S(1)} %copy-done.14, bf16[384,640]{1,0:T(8,128)(2,1)S(1)} %copy-done.17, ...), custom_call_target="tpu_custom_call" | custom-call | flops 1024 | bytes 1024 | tf_op jit(solution)/shard_map/other_features/pallas_call | solution.py:144
  136.9 14.6 %grads.1 = (bf16[384,1792]{1,0:T(8,128)(2,1)}, bf16[384,1792]{1,0:T(8,128)(2,1)}, f32[8,128]{1,0:T(8,128)S(1)}) custom-call(s32[8]{0:T(128)S(1)} %add.40.offs_ref, bf16[384,640]{1,0:T(8,128)(2,1)S(1)} %copy-done.21, bf16[384,640]{1,0:T(8,128)(2,1)S(1)} %copy-done.6, bf16[384,640]{1,0:T(8,128)(2,1)} %after.6.refs_2_, bf16[384,640]{1,0:T(8,128)(2,1)} %after.8.refs_1_.refs_3_, ...), custom_call_target="tpu_custom_call" | custom-call | flops 1024 | bytes 1024 | tf_op jit(solution)/shard_map/grads/pallas_call | solution.py:179
  153.7 5.4 %all-to-all-start.1 = ((f32[4,32,1536]{2,1,0:T(8,128)}), f32[4,32,1536]{2,1,0:T(8,128)}, u32[]{:S(2)}, u32[]{:S(2)}) async-start(f32[4,32,1536]{2,1,0:T(8,128)} %copy-done.9), calls=%async_computation.1 | async-start | bytes 1572864 | tf_op jit(solution)/shard_map/all_to_all | solution.py:346
  161.2 12.2 %collective-permute-done.17.refs_2_ = bf16[384,640]{1,0:T(8,128)(2,1)S(1)} collective-permute-done((bf16[384,640]{1,0:T(8,128)(2,1)}, bf16[384,640]{1,0:T(8,128)(2,1)S(1)}, u32[]{:S(2)}, u32[]{:S(2)}) %collective-permute-start.17) | collective-permute-done | bytes 491552 | tf_op jit(solution)/shard_map/ppermute | solution.py:30
  173.4 9.8 %collective-permute-done.18.refs_3_ = bf16[384,640]{1,0:T(8,128)(2,1)S(1)} collective-permute-done((bf16[384,640]{1,0:T(8,128)(2,1)}, bf16[384,640]{1,0:T(8,128)(2,1)S(1)}, u32[]{:S(2)}, u32[]{:S(2)}) %collective-permute-start.18) | collective-permute-done | bytes 491552 | tf_op jit(solution)/shard_map/ppermute | solution.py:30
  188.0 11.9 %wgrad.1 = (bf16[1792,1280]{1,0:T(8,128)(2,1)}, f32[8,128]{1,0:T(8,128)S(1)}) custom-call(s32[2]{0:T(128)S(1)} %add_multiply_fusion.offs_ref, s32[4]{0:T(128)S(1)} %xor_multiply_fusion.offs_ref.toks_ref, bf16[4,384,640]{2,1,0:T(8,128)(2,1)S(1)} %all-to-all-done.refs_3_.own_ref, bf16[384,640]{1,0:T(8,128)(2,1)S(1)} %copy-done.25, ...), custom_call_target="tpu_custom_call" | custom-call | flops 1024 | bytes 1024 | tf_op jit(solution)/shard_map/wgrad/pallas_call | solution.py:243
  200.0 2.2 score_line.1
  202.1 5.5 %all-to-all-start.3 = ((f32[32,1,128]{2,1,0:T(1,128)}), f32[32,1,128]{2,1,0:T(1,128)S(1)}, u32[]{:S(2)}, u32[]{:S(2)}) async-start(f32[32,1,128]{2,1,0:T(1,128)} %bitcast.3), calls=%async_computation.3 | async-start | bytes 32768 | tf_op jit(solution)/shard_map/all_to_all | solution.py:446
  207.6 7.1 %all-to-all-done.3 = f32[32,1,128]{2,1,0:T(1,128)S(1)} async-done(((f32[32,1,128]{2,1,0:T(1,128)}), f32[32,1,128]{2,1,0:T(1,128)S(1)}, u32[]{:S(2)}, u32[]{:S(2)}) %all-to-all-start.3) | async-done | bytes 16416 | tf_op jit(solution)/shard_map/all_to_all | solution.py:446
  (144 shorter events, 56.7 us)
Async XLA Ops:
  0.6 14.6 %collective-permute-start.2 = (bf16[384,640]{1,0:T(8,128)(2,1)}, bf16[384,640]{1,0:T(8,128)(2,1)}, u32[]{:S(2)}, u32[]{:S(2)}) collective-permute-start(bf16[384,640]{1,0:T(8,128)(2,1)} %refs_0_.5), channel_id=1, source_target_pairs={{0,16},{8,24},{16,0},{24,8},{1,17},{9,25},{17,1},{25,9},{2,18},{10... | collective-permute-start | bytes 1474568 | tf_op jit(solution)/shard_map/ppermute | solution.py:30
  3.7 18.0 %collective-permute-start.3 = (bf16[384,640]{1,0:T(8,128)(2,1)}, bf16[384,640]{1,0:T(8,128)(2,1)S(1)}, u32[]{:S(2)}, u32[]{:S(2)}) collective-permute-start(bf16[384,640]{1,0:T(8,128)(2,1)} %refs_0_.5), channel_id=1, source_target_pairs={{0,8},{8,0},{16,24},{24,16},{1,9},{9,1},{17,25},{25,17},{2,10},{10... | collective-permute-start | bytes 1474568 | tf_op jit(solution)/shard_map/ppermute | solution.py:30
  3.7 18.0 %collective-permute-start.1 = (bf16[384,640]{1,0:T(8,128)(2,1)}, bf16[384,640]{1,0:T(8,128)(2,1)S(1)}, u32[]{:S(2)}, u32[]{:S(2)}) collective-permute-start(bf16[384,640]{1,0:T(8,128)(2,1)} %refs_0_.5), channel_id=1, source_target_pairs={{0,1},{1,0},{2,3},{3,2},{4,5},{5,4},{6,7},{7,6},{8,9},{9,8},{10,11... | collective-permute-start | bytes 1474568 | tf_op jit(solution)/shard_map/ppermute | solution.py:30
  5.2 16.5 %collective-permute-start = (bf16[384,640]{1,0:T(8,128)(2,1)}, bf16[384,640]{1,0:T(8,128)(2,1)S(1)}, u32[]{:S(2)}, u32[]{:S(2)}) collective-permute-start(bf16[384,640]{1,0:T(8,128)(2,1)} %refs_0_.5), channel_id=1, source_target_pairs={{0,2},{1,3},{2,4},{3,5},{4,6},{5,7},{6,0},{7,1},{8,10},{9,11},{10,... | collective-permute-start | bytes 1474568 | tf_op jit(solution)/shard_map/ppermute | solution.py:35
  15.2 13.6 %collective-permute-start.6 = (bf16[384,640]{1,0:T(8,128)(2,1)}, bf16[384,640]{1,0:T(8,128)(2,1)}, u32[]{:S(2)}, u32[]{:S(2)}) collective-permute-start(bf16[384,640]{1,0:T(8,128)(2,1)} %collective-permute-done.2.refs_2_), channel_id=1, source_target_pairs={{0,8},{8,0},{16,24},{24,16},{1,9},{9,1},{17,25},{25,17},{2,10},{10... | collective-permute-start | bytes 1474568 | tf_op jit(solution)/shard_map/ppermute | solution.py:30
  23.5 39.2 %collective-permute-start.9 = (bf16[1792,384]{1,0:T(8,128)(2,1)}, bf16[1792,384]{1,0:T(8,128)(2,1)S(1)}, u32[]{:S(2)}, u32[]{:S(2)}) collective-permute-start(bf16[1792,384]{1,0:T(8,128)(2,1)} %after.7.refs_0_.refs_4_), channel_id=1, source_target_pairs={{0,8},{8,0},{16,24},{24,16},{1,9},{9,1},{17,25},{25,17},{2,10},{10... | collective-permute-start | bytes 4128776 | tf_op jit(solution)/shard_map/ppermute | solution.py:30
  24.0 38.7 %collective-permute-start.13 = (bf16[1792,384]{1,0:T(8,128)(2,1)}, bf16[1792,384]{1,0:T(8,128)(2,1)S(1)}, u32[]{:S(2)}, u32[]{:S(2)}) collective-permute-start(bf16[1792,384]{1,0:T(8,128)(2,1)} %after.7.refs_0_.refs_4_), channel_id=1, source_target_pairs={{0,16},{8,24},{16,0},{24,8},{1,17},{9,25},{17,1},{25,9},{2,18},{10... | collective-permute-start | bytes 4128776 | tf_op jit(solution)/shard_map/ppermute | solution.py:30
  25.7 14.1 %collective-permute-start.5 = (bf16[384,640]{1,0:T(8,128)(2,1)S(1)}, bf16[384,640]{1,0:T(8,128)(2,1)S(1)}, u32[]{:S(2)}, u32[]{:S(2)}) collective-permute-start(bf16[384,640]{1,0:T(8,128)(2,1)S(1)} %after.5.refs_5_.refs_1_), channel_id=1, source_target_pairs={{0,1},{1,0},{2,3},{3,2},{4,5},{5,4},{6,7},{7,6},{8,9},{9,8},{10,11... | collective-permute-start | bytes 1474568 | tf_op jit(solution)/shard_map/ppermute | solution.py:30
  27.2 14.5 %collective-permute-start.4 = (bf16[384,640]{1,0:T(8,128)(2,1)S(1)}, bf16[384,640]{1,0:T(8,128)(2,1)}, u32[]{:S(2)}, u32[]{:S(2)}) collective-permute-start(bf16[384,640]{1,0:T(8,128)(2,1)S(1)} %after.5.refs_5_.refs_1_), channel_id=1, source_target_pairs={{0,2},{1,3},{2,4},{3,5},{4,6},{5,7},{6,0},{7,1},{8,10},{9,11},{10,... | collective-permute-start | bytes 1474568 | tf_op jit(solution)/shard_map/ppermute | solution.py:35
  34.1 12.9 %collective-permute-start.7 = (f32[4,32,768]{2,1,0:T(8,128)S(1)}, f32[4,32,768]{2,1,0:T(8,128)S(1)}, u32[]{:S(2)}, u32[]{:S(2)}) collective-permute-start(f32[4,32,768]{2,1,0:T(8,128)S(1)} %get-tuple-element.23), channel_id=1, source_target_pairs={{0,1},{1,0},{2,3},{3,2},{4,5},{5,4},{6,7},{7,6},{8,9},{9,8},{10,11... | collective-permute-start | bytes 1179656 | tf_op jit(solution)/shard_map/ppermute | solution.py:30
  48.5 14.1 %collective-permute-start.8 = (bf16[384,640]{1,0:T(8,128)(2,1)}, bf16[384,640]{1,0:T(8,128)(2,1)}, u32[]{:S(2)}, u32[]{:S(2)}) collective-permute-start(bf16[384,640]{1,0:T(8,128)(2,1)} %after.6.refs_2_), channel_id=1, source_target_pairs={{0,2},{1,3},{2,4},{3,5},{4,6},{5,7},{6,0},{7,1},{8,10},{9,11},{10,... | collective-permute-start | bytes 1474568 | tf_op jit(solution)/shard_map/ppermute | solution.py:35
  67.7 27.9 %all-to-all-start = ((bf16[4,384,640]{2,1,0:T(8,128)(2,1)}), bf16[4,384,640]{2,1,0:T(8,128)(2,1)S(1)}, u32[]{:S(2)}, u32[]{:S(2)}) async-start(bf16[4,384,640]{2,1,0:T(8,128)(2,1)} %copy-done), calls=%async_computation | async-start | bytes 3932160 | tf_op jit(solution)/shard_map/all_to_all | solution.py:425
  71.3 3.8 %collective-permute-start.14 = (bf16[1792,384]{1,0:T(8,128)(2,1)S(1)}, bf16[1792,384]{1,0:T(8,128)(2,1)S(1)}, u32[]{:S(2)}, u32[]{:S(2)}) collective-permute-start(bf16[1792,384]{1,0:T(8,128)(2,1)S(1)} %after.9.refs_4_.refs_2_.refs_6_), channel_id=1, source_target_pairs={{0,8},{8,0},{16,24},{24,16},{1,9},{9,1},{17,25},{25,17},{2,10},{10... | collective-permute-start | bytes 4128776 | tf_op jit(solution)/shard_map/ppermute | solution.py:30
  71.8 12.4 %collective-permute-start.12 = (f32[4,32,768]{2,1,0:T(8,128)}, f32[4,32,768]{2,1,0:T(8,128)S(1)}, u32[]{:S(2)}, u32[]{:S(2)}) collective-permute-start(f32[4,32,768]{2,1,0:T(8,128)} %copy-done.45), channel_id=1, source_target_pairs={{0,1},{1,0},{2,3},{3,2},{4,5},{5,4},{6,7},{7,6},{8,9},{9,8},{10,11... | collective-permute-start | bytes 1179656 | tf_op jit(solution)/shard_map/ppermute | solution.py:30
  95.6 58.2 %all-to-all-start.2 = ((f32[4,32,1536]{2,1,0:T(8,128)}), f32[4,32,1536]{2,1,0:T(8,128)}, u32[]{:S(2)}, u32[]{:S(2)}) async-start(f32[4,32,1536]{2,1,0:T(8,128)} %copy-done.7), calls=%async_computation.2 | async-start | bytes 1572864 | tf_op jit(solution)/shard_map/all_to_all | solution.py:346
  99.8 13.1 %collective-permute-start.10 = (bf16[384,640]{1,0:T(8,128)(2,1)}, bf16[384,640]{1,0:T(8,128)(2,1)}, u32[]{:S(2)}, u32[]{:S(2)}) collective-permute-start(bf16[384,640]{1,0:T(8,128)(2,1)} %after.6.refs_2_), channel_id=1, source_target_pairs={{0,1},{1,0},{2,3},{3,2},{4,5},{5,4},{6,7},{7,6},{8,9},{9,8},{10,11... | collective-permute-start | bytes 1474568 | tf_op jit(solution)/shard_map/ppermute | solution.py:30
  112.9 14.5 %collective-permute-start.11 = (bf16[384,640]{1,0:T(8,128)(2,1)}, bf16[384,640]{1,0:T(8,128)(2,1)}, u32[]{:S(2)}, u32[]{:S(2)}) collective-permute-start(bf16[384,640]{1,0:T(8,128)(2,1)} %collective-permute-done.10.refs_2_.refs_6_), channel_id=1, source_target_pairs={{0,2},{1,3},{2,4},{3,5},{4,6},{5,7},{6,0},{7,1},{8,10},{9,11},{10,... | collective-permute-start | bytes 1474568 | tf_op jit(solution)/shard_map/ppermute | solution.py:35
  114.6 12.8 %collective-permute-start.15 = (f32[4,32,768]{2,1,0:T(8,128)}, f32[4,32,768]{2,1,0:T(8,128)}, u32[]{:S(2)}, u32[]{:S(2)}) collective-permute-start(f32[4,32,768]{2,1,0:T(8,128)} %copy-done.39), channel_id=1, source_target_pairs={{0,1},{1,0},{2,3},{3,2},{4,5},{5,4},{6,7},{7,6},{8,9},{9,8},{10,11... | collective-permute-start | bytes 1179656 | tf_op jit(solution)/shard_map/ppermute | solution.py:30
  116.1 35.5 %collective-permute-start.19 = (f32[4,32,768]{2,1,0:T(8,128)}, f32[4,32,768]{2,1,0:T(8,128)}, u32[]{:S(2)}, u32[]{:S(2)}) collective-permute-start(f32[4,32,768]{2,1,0:T(8,128)} %copy-done.38), channel_id=1, source_target_pairs={{0,1},{1,0},{2,3},{3,2},{4,5},{5,4},{6,7},{7,6},{8,9},{9,8},{10,11... | collective-permute-start | bytes 1179656 | tf_op jit(solution)/shard_map/ppermute | solution.py:30
  153.7 46.2 %all-to-all-start.1 = ((f32[4,32,1536]{2,1,0:T(8,128)}), f32[4,32,1536]{2,1,0:T(8,128)}, u32[]{:S(2)}, u32[]{:S(2)}) async-start(f32[4,32,1536]{2,1,0:T(8,128)} %copy-done.9), calls=%async_computation.1 | async-start | bytes 1572864 | tf_op jit(solution)/shard_map/all_to_all | solution.py:346
  159.2 2.1 collective-permute-start.16
  159.2 14.2 %collective-permute-start.17 = (bf16[384,640]{1,0:T(8,128)(2,1)}, bf16[384,640]{1,0:T(8,128)(2,1)S(1)}, u32[]{:S(2)}, u32[]{:S(2)}) collective-permute-start(bf16[384,640]{1,0:T(8,128)(2,1)} %copy-done.43), channel_id=1, source_target_pairs={{0,16},{8,24},{16,0},{24,8},{1,17},{9,25},{17,1},{25,9},{2,18},{10... | collective-permute-start | bytes 1474568 | tf_op jit(solution)/shard_map/ppermute | solution.py:30
  160.1 23.0 %collective-permute-start.18 = (bf16[384,640]{1,0:T(8,128)(2,1)}, bf16[384,640]{1,0:T(8,128)(2,1)S(1)}, u32[]{:S(2)}, u32[]{:S(2)}) collective-permute-start(bf16[384,640]{1,0:T(8,128)(2,1)} %copy-done.42), channel_id=1, source_target_pairs={{0,24},{8,16},{16,8},{24,0},{1,25},{9,17},{17,9},{25,1},{2,26},{10... | collective-permute-start | bytes 1474568 | tf_op jit(solution)/shard_map/ppermute | solution.py:30
  202.1 12.6 %all-to-all-start.3 = ((f32[32,1,128]{2,1,0:T(1,128)}), f32[32,1,128]{2,1,0:T(1,128)S(1)}, u32[]{:S(2)}, u32[]{:S(2)}) async-start(f32[32,1,128]{2,1,0:T(1,128)} %bitcast.3), calls=%async_computation.3 | async-start | bytes 32768 | tf_op jit(solution)/shard_map/all_to_all | solution.py:446
  (46 other events, 222.0 us)

commit v11 on v10

--- a/solution.py
+++ b/solution.py
@@ -14,7 +14,7 @@
 
 F32 = jnp.float32
 BF16 = jnp.bfloat16
-MIB = 1024 * 1024
+VMEM_LIMIT = 63 * 1024 * 1024
 
 
 def dot_nt(a, b):
@@ -48,8 +48,8 @@
 SMALL = pl.CostEstimate(flops=1024, bytes_accessed=1024, transcendentals=0)
 
 
-def params(mib):
-    return pltpu.CompilerParams(vmem_limit_bytes=mib * MIB)
+def params():
+    return pltpu.CompilerParams(vmem_limit_bytes=VMEM_LIMIT)
 
 
 def after_body(*refs):
@@ -63,7 +63,7 @@
         out_specs=ANY,
         out_shape=jax.ShapeDtypeStruct(x.shape, x.dtype),
         input_output_aliases={0: 0},
-        compiler_params=params(1),
+        compiler_params=params(),
         cost_estimate=SMALL,
         name="after",
     )(x, *order)
@@ -93,7 +93,7 @@
             jax.ShapeDtypeStruct((toks, units), BF16),
             jax.ShapeDtypeStruct((toks, units), BF16),
         ],
-        compiler_params=params(12),
+        compiler_params=params(),
         cost_estimate=SMALL,
         name="hidden",
     )(gate, up)
@@ -120,7 +120,7 @@
         out_specs=whole(shape),
         out_shape=jax.ShapeDtypeStruct(shape, BF16),
         scratch_shapes=[pltpu.SemaphoreType.DMA((n,))],
-        compiler_params=params(8),
+        compiler_params=params(),
         cost_estimate=SMALL,
         name=name,
     )(at, *blocks, *order)
@@ -148,14 +148,16 @@
         out_specs=each(blocks),
         out_shape=[jax.ShapeDtypeStruct(x.shape, BF16) for x in blocks],
         scratch_shapes=[pltpu.SemaphoreType.DMA((n,))],
-        compiler_params=params(8),
+        compiler_params=params(),
         cost_estimate=SMALL,
         name=name,
     )(to, *blocks, *order)
 
 
 def grads_body(n, offs_ref, *refs):
-    blocks, (w_ref, by_gate_ref, by_up_ref, _, gg_ref, gu_ref, done_ref, piece) = refs[:n], refs[n:]
+    blocks, (w_ref, by_gate_ref, by_up_ref), (gg_ref, gu_ref, done_ref, piece) = (
+        refs[:n], refs[n : n + 3], refs[-4:]
+    )
     width = blocks[0].shape[1]
 
     @pl.when(pl.program_id(0) == 0)
@@ -169,36 +171,45 @@
     gu_ref[...] = (total * by_up_ref[...]).astype(BF16)
 
 
-def grads(offs, blocks, weight, by_gate, by_up, order):
+def grads(offs, blocks, weight, by_gate, by_up, order, tiles, made, name):
     n = len(blocks)
     toks, width = blocks[0].shape
     units, feats = weight.shape
     tile = 256
-    cols = pl.BlockSpec((toks, tile), lambda i, _: (0, i))
+    first, count = tiles
+    cols = pl.BlockSpec((toks, tile), lambda i, _: (0, first + i))
     out = jax.ShapeDtypeStruct((toks, units), BF16)
+    operands = [offs, *blocks, weight, by_gate, by_up, *order, *made]
     return pl.pallas_call(
         functools.partial(grads_body, n),
         grid_spec=pltpu.PrefetchScalarGridSpec(
             num_scalar_prefetch=1,
-            grid=(units // tile,),
+            grid=(count,),
             in_specs=[whole((toks, width))] * n
-            + [pl.BlockSpec((tile, feats), lambda i, _: (i, 0)), cols, cols, ANY],
+            + [pl.BlockSpec((tile, feats), lambda i, _: (first + i, 0)), cols, cols]
+            + [ANY] * (len(order) + len(made)),
             out_specs=[cols, cols, whole((8, 128))],
             scratch_shapes=[pltpu.VMEM((toks, feats), BF16)],
         ),
         out_shape=(out, out, jax.ShapeDtypeStruct((8, 128), F32)),
-        compiler_params=params(48),
-        cost_estimate=SMALL,
-        name="grads",
-    )(offs, *blocks, weight, by_gate, by_up, order)
-
-
-def wgrad_body(n, offs_ref, toks_ref, own_ref, *refs):
+        input_output_aliases={len(operands) - len(made) + k: k for k in range(len(made))},
+        compiler_params=params(),
+        cost_estimate=pl.CostEstimate(
+            flops=2 * toks * tile * count * feats,
+            bytes_accessed=2 * (tile * count * feats + toks * feats + 4 * toks * tile * count),
+            transcendentals=0,
+        ),
+        name=name,
+    )(*operands)
+
+
+def wgrad_body(n, first, offs_ref, toks_ref, own_ref, *refs):
     others, hids = refs[:n], refs[n : 2 * n]
     out_ref, done_ref, hid, cols, outs, hid_sems, col_sems, out_sems = refs[-8:]
     done_ref[...] = jnp.zeros_like(done_ref)
     _, toks, width = own_ref.shape
     steps, tile, _ = outs.shape
+    base = first * tile
     own, other = (pl.ds(pl.multiple_of(offs_ref[half], 128), width) for half in range(2))
     came = []
     for k in range(n):
@@ -209,11 +220,12 @@
     units = []
     for i in range(steps):
         part = slice(i * tile, (i + 1) * tile)
+        taken = slice(base + i * tile, base + (i + 1) * tile)
         for k in range(n):
             place = pl.ds(pl.multiple_of(toks_ref[k], 128), toks)
             units.append(
                 pltpu.make_async_copy(
-                    hids[k].at[part], hid.at[part, place], hid_sems.at[i * n + k]
+                    hids[k].at[taken], hid.at[part, place], hid_sems.at[i * n + k]
                 )
             )
     for copy in [*units[:n], *came, *units[n:]]:
@@ -228,43 +240,51 @@
         outs[i] = lax.dot_general(
             hid[part], cols[...], (((1,), (0,)), ((), ())), preferred_element_type=F32
         ).astype(BF16)
-        gone.append(pltpu.make_async_copy(outs.at[i], out_ref.at[part], out_sems.at[i]))
+        made = out_ref.at[base + i * tile : base + (i + 1) * tile]
+        gone.append(pltpu.make_async_copy(outs.at[i], made, out_sems.at[i]))
         gone[-1].start()
     for copy in gone:
         copy.wait()
 
 
-def wgrad(offs, tok_offs, own, others, hids, order):
+def wgrad(offs, tok_offs, own, others, hids, order, parts, made, name):
     n, toks, width = own.shape
     units = hids[0].shape[0]
     total = n * toks
-    steps = 4
+    first, steps = parts
+    tile = units // 4
     smem = pl.BlockSpec(memory_space=pltpu.SMEM)
-    return pl.pallas_call(
-        functools.partial(wgrad_body, n),
-        in_specs=[smem, smem] + [ANY] * (2 * n + 1 + len(order)),
+    operands = [offs, tok_offs, own, *others, *hids, *order, *made]
+    return pl.pallas_call(
+        functools.partial(wgrad_body, n, first),
+        in_specs=[smem, smem] + [ANY] * (len(operands) - 2),
         out_specs=[ANY, pl.BlockSpec(memory_space=pltpu.VMEM)],
         out_shape=[
             jax.ShapeDtypeStruct((units, 2 * width), BF16),
             jax.ShapeDtypeStruct((8, 128), F32),
         ],
         scratch_shapes=[
-            pltpu.VMEM((units, total), BF16),
+            pltpu.VMEM((steps * tile, total), BF16),
             pltpu.VMEM((total, 2 * width), BF16),
-            pltpu.VMEM((steps, units // steps, 2 * width), BF16),
+            pltpu.VMEM((steps, tile, 2 * width), BF16),
             pltpu.SemaphoreType.DMA((steps * n,)),
             pltpu.SemaphoreType.DMA((2 * n,)),
             pltpu.SemaphoreType.DMA((steps,)),
         ],
-        compiler_params=params(24),
-        cost_estimate=SMALL,
-        name="wgrad",
-    )(offs, tok_offs, own, *others, *hids, *order)
+        input_output_aliases={len(operands) - len(made) + k: k for k in range(len(made))},
+        compiler_params=params(),
+        cost_estimate=pl.CostEstimate(
+            flops=4 * total * steps * tile * width,
+            bytes_accessed=2 * (total * (steps * tile + 2 * width) + 2 * steps * tile * width),
+            transcendentals=0,
+        ),
+        name=name,
+    )(*operands)
 
 
 def put_slices(inner_ref, part, kept_ref, away_refs):
     outer, size, total = kept_ref.shape
-    half = total // 2
+    cut = total // len(away_refs)
     for inner in range(2):
 
         @pl.when(inner_ref[0] == inner)
@@ -274,22 +294,20 @@
                 if p % 2 == inner:
                     kept_ref[p // 2] = rows
                 else:
-                    for h in range(2):
-                        away_refs[h][p // 2] = rows[:, h * half : (h + 1) * half]
-
-
-def grad_gram_body(inner_ref, offs_ref, *refs):
-    n = len(refs) - 6
-    toks_refs, (val_ref, _, kept_ref, *away_refs, wide) = refs[:n], refs[n:]
+                    for h, away_ref in enumerate(away_refs):
+                        away_ref[p // 2] = rows[:, h * cut : (h + 1) * cut]
+
+
+def grad_gram_body(n, cuts, inner_ref, offs_ref, *refs):
+    toks_refs, val_ref, (kept_ref, *away_refs, wide) = refs[:n], refs[n], refs[-2 - cuts :]
     for k, ref in enumerate(toks_refs):
         toks = ref.shape[0]
         wide[:, pl.ds(pl.multiple_of(offs_ref[k], 128), toks)] = dot_nt(val_ref[...], ref[...])
     put_slices(inner_ref, wide, kept_ref, away_refs)
 
 
-def hidden_gram_body(inner_ref, offs_ref, *refs):
-    n = len(refs) - 6
-    hid, (val_ref, _, kept_ref, *away_refs, wide) = refs[:n], refs[n:]
+def hidden_gram_body(n, cuts, inner_ref, offs_ref, *refs):
+    hid, val_ref, (kept_ref, *away_refs, wide) = refs[:n], refs[n], refs[-2 - cuts :]
     for k, ref in enumerate(hid):
         toks = ref.shape[1]
         wide[:, pl.ds(pl.multiple_of(offs_ref[k], 128), toks)] = lax.dot_general(
@@ -298,43 +316,43 @@
     put_slices(inner_ref, wide, kept_ref, away_refs)
 
 
-def gram(body, inner, offs, operands, order, parts, name):
+def gram(body, inner, offs, operands, order, parts, cuts, name):
     smem = pl.BlockSpec(memory_space=pltpu.SMEM)
     *toks, vals = operands
     total = sum(x.size for x in toks) // vals.shape[1]
     kept = jax.ShapeDtypeStruct((parts // 2, vals.shape[0] // parts, total), F32)
-    away = jax.ShapeDtypeStruct((parts // 2, vals.shape[0] // parts, total // 2), F32)
-    shapes = [kept, away, away]
+    away = jax.ShapeDtypeStruct((parts // 2, vals.shape[0] // parts, total // cuts), F32)
+    shapes = [kept] + [away] * cuts
     kept, *away = pl.pallas_call(
-        body,
+        functools.partial(body, len(toks), cuts),
         grid=(1,),
-        in_specs=[smem, smem] + each(operands) + [ANY],
+        in_specs=[smem, smem] + each(operands) + [ANY] * len(order),
         out_specs=each(shapes),
         out_shape=shapes,
         scratch_shapes=[pltpu.VMEM((vals.shape[0], total), F32)],
-        compiler_params=params(28),
+        compiler_params=params(),
         cost_estimate=SMALL,
         name=name,
-    )(inner, offs, *operands, order)
+    )(inner, offs, *operands, *order)
     return kept, away, [swap(x, "fsdp", 1) for x in away]
 
 
-def pair_body(kept_ref, *refs):
-    came_refs, out_ref = refs[:2], refs[-1]
-    half = came_refs[0].shape[2]
-    for h in range(2):
-        cols = slice(h * half, (h + 1) * half)
+def pair_body(cuts, kept_ref, *refs):
+    came_refs, out_ref = refs[:cuts], refs[-1]
+    cut = kept_ref.shape[2] // cuts
+    for h in range(cuts):
+        cols = slice(h * cut, (h + 1) * cut)
         out_ref[:, :, cols] = kept_ref[:, :, cols] + came_refs[h][...]
 
 
 def pair_sum(kept, came, order, name):
     return pl.pallas_call(
-        pair_body,
+        functools.partial(pair_body, len(came)),
         grid=(1,),
         in_specs=each([kept, *came]) + [ANY] * len(order),
         out_specs=whole(kept.shape),
         out_shape=jax.ShapeDtypeStruct(kept.shape, F32),
-        compiler_params=params(16),
+        compiler_params=params(),
         cost_estimate=SMALL,
         name=name,
     )(kept, *came, *order)
@@ -372,7 +390,7 @@
         in_specs=[pl.BlockSpec(memory_space=pltpu.SMEM)] + each([hid, grad]) + [ANY] * len(order),
         out_specs=whole((copies, 128)),
         out_shape=jax.ShapeDtypeStruct((copies, 128), F32),
-        compiler_params=params(8),
+        compiler_params=params(),
         cost_estimate=SMALL,
         name="score_line",
     )(assign, hid, grad, *order)
@@ -407,13 +425,13 @@
     near = swap(hidden, "dp", 1)
 
     grad_kept, away, grad_came = gram(
-        grad_gram_body, inner_at, tok_offs, [*grad_dp, val_grad], first, n_fs, "grad_gram"
+        grad_gram_body, inner_at, tok_offs, [*grad_dp, val_grad], [first], n_fs, 1, "grad_gram"
     )
     ring = [out_grad, first]
     others.append(swap(ring[1], "fsdp", 1))
-    ring.append(after(shift(ring[1], "fsdp", 2), others[1], grad_came[0]))
+    ring.append(after(shift(ring[1], "fsdp", 2), others[1], *away))
     others.append(swap(ring[2], "fsdp", 1))
-    ring.append(after(shift(ring[2], "fsdp", 2), near))
+    ring.append(after(shift(ring[2], "fsdp", 2), others[2], near))
     others.append(shift(others[2], "fsdp", 2))
 
     def over_columns(blocks):
@@ -424,21 +442,29 @@
     own = stack(at, ring, [far], "own_features")
     own_cols = lax.all_to_all(own, "dp", split_axis=0, concat_axis=0, tiled=True)
     hid_kept, away, hid_came = gram(
-        hidden_gram_body, inner_at, tok_offs, [*hid_dp, val_hidden], own, n_fs, "hidden_gram"
-    )
-    grad_pair = pair_sum(grad_kept, grad_came, away, "grad_pair")
-    other = arrange(to, others, [grad_pair, hid_came[0]], "other_features")
-    other_cols = over_columns(other)
-    grad_sums = spread(grad_pair)
-
+        hidden_gram_body, inner_at, tok_offs, [*hid_dp, val_hidden], [own, others[3]], n_fs, 2,
+        "hidden_gram",
+    )
     offs = (jnp.stack([inner, 1 - inner]) * width).astype(jnp.int32)
     places = (offs[:, None] + at[None, :] * (2 * width)).reshape(-1)
+    tiles = units // 256
+    *made, done = grads(
+        places, [*ring, *others], down_weight, by_gate, by_up, away, (0, tiles // 2 + 1), [],
+        "grads_first",
+    )
+    grad_pair = pair_sum(grad_kept, grad_came, [done, hid_came[0]], "grad_pair")
+    grad_sums = spread(grad_pair)
+    other = arrange(to, others, [grad_pair], "other_features")
+    other_cols = over_columns(other)
     grad_gate, grad_up, done = grads(
-        places, [*ring, *others], down_weight, by_gate, by_up, other[0]
-    )
-    hid_pair = pair_sum(hid_kept, hid_came, [done, own_cols], "hidden_pair")
+        places, [*ring, *others], down_weight, by_gate, by_up, [other[0]],
+        (tiles // 2 + 1, tiles - tiles // 2 - 1), made, "grads_last",
+    )
+    hid_pair = pair_sum(hid_kept, hid_came, [done, *other_cols[1:3]], "hidden_pair")
     hid_sums = spread(hid_pair)
-    weight_grad, done = wgrad(offs, tok_offs, own_cols, other_cols, hid_dp, [hid_pair])
+    made, done = wgrad(
+        offs, tok_offs, own_cols, other_cols, hid_dp, [hid_pair], (0, 2), [], "wgrad_first"
+    )
 
     mine = score_line(
         assign, hid_sums, grad_sums, [done], n_dp * rows_here, n_dp * n_fs
@@ -446,6 +472,9 @@
     every = lax.all_to_all(
         mine, ("dp", "fsdp"), split_axis=0, concat_axis=0, tiled=True
     ).reshape(n_dp, n_fs, 128)
+    weight_grad, _ = wgrad(
+        offs, tok_offs, own_cols, other_cols, hid_dp, [mine], (2, 2), [made], "wgrad_last"
+    )
 
     rows = n_dp * rows_here
     scale = 1.0 / jnp.sqrt(F32(L) * VAL * FFW * D)

time: 218 us -> 173 us (0.79)
  waiting for transfers between devices: 95.4 us -> 60.5 us
  local copies, waits for them, and re-layouts: 32.9 us -> 4.92 us
  Pallas kernels: 44.9 us -> 70 us
  starting transfers between devices: 41.4 us -> 33.2 us
    unnamed x93 -> x25, local copies, waits for them, and re-layouts: 32.5 us -> 4.1 us
    ppermute x16 -> x15, waiting for transfers between devices: 54.4 us -> 37.6 us  [swap(): return lax.ppermute(x, axis, [(s, s ^ k) for s in range(n)])]
    pallas_call x5 -> x6, Pallas kernels: 19.6 us -> 34.4 us  [the longest x2 19.7 us: wgrad(): pl.pallas_call(functools.partial(wgrad_body, n, first), in_specs=[smem, s...]
    all_to_all x1, waiting for transfers between devices: 8.88 us -> 0.01 us  [per_device(): lax.all_to_all(own, 'dp', split_axis=0, concat_axis=0, tiled=True)]
    all_to_all x1, waiting for transfers between devices: 7.12 us -> 0.01 us  [per_device(): lax.all_to_all(mine, ('dp', 'fsdp'), split_axis=0, concat_axis=0, tiled=T...]
    pallas_call x1 -> x2, Pallas kernels: 14.6 us -> 19.9 us  [grads(): pl.pallas_call(functools.partial(grads_body, n), grid_spec=pltpu.Prefetch...]
    ppermute x4, starting transfers between devices: 6.36 us -> 1.85 us  [shift(): return lax.ppermute(x, axis, [(s, (s + k) % n) for s in range(n)])]
    ppermute x16 -> x15, starting transfers between devices: 16.3 us -> 12.4 us  [swap(): return lax.ppermute(x, axis, [(s, s ^ k) for s in range(n)])]
  transfers between devices with their start and end apart: 24 -> 23, of which waited for: 13 -> 13; matrix products, arithmetic and copies ran while one was open for 0% -> 1% of each run, Pallas kernels for 19% -> 39%
where the time goes in v11:
time: 173 us; the launch traced here: 172 us
  Pallas kernels  70 us (40%)
  waiting for transfers between devices  60.5 us (35%)
  starting transfers between devices  33.2 us (19%)
  local copies, waits for them, and re-layouts  4.92 us (3%)
  other arithmetic  2.43 us (1%)
    ppermute x15, waiting for transfers between devices, swap(): return lax.ppermute(x, axis, [(s, s ^ k) for s in range(n)])  37.6 us
    ppermute x4, waiting for transfers between devices, shift(): return lax.ppermute(x, axis, [(s, (s + k) % n) for s in range(n)])  22.8 us
    pallas_call x2, Pallas kernels, grads(): pl.pallas_call(functools.partial(grads_body, n), grid_spec=pltpu.Prefetch...  19.9 us
    pallas_call x2, Pallas kernels, wgrad(): pl.pallas_call(functools.partial(wgrad_body, n, first), in_specs=[smem, s...  19.7 us
    ppermute x15, starting transfers between devices, swap(): return lax.ppermute(x, axis, [(s, s ^ k) for s in range(n)])  12.4 us
    pallas_call x2, Pallas kernels, gram(): pl.pallas_call(functools.partial(body, len(toks), cuts), grid=(1,), in_sp...  10 us
    all_to_all x2, starting transfers between devices, spread(): lax.all_to_all(pair, 'fsdp', split_axis=0, concat_axis=0, axis_index_grou...  8.69 us
    pallas_call x1, Pallas kernels, hidden_units(): pl.pallas_call(hidden_body, grid=(units // tile,), in_specs=[cols, cols],...  6.63 us
  transfers between devices with their start and end apart: 23, of which 13 were waited for; matrix products, arithmetic and copies ran while one was open for 1% of the time, Pallas kernels for 39%

profile of v11, /device:TPU:0, one launch (start us, length us, event | category | flops | bytes accessed | tf_op | source)
XLA Modules:
  0.0 171.8 jit_solution(4206128023124704312)
XLA Ops:
  1.1 2.6 %collective-permute-start.2 = (bf16[384,640]{1,0:T(8,128)(2,1)}, bf16[384,640]{1,0:T(8,128)(2,1)}, u32[]{:S(2)}, u32[]{:S(2)}) collective-permute-start(bf16[384,640]{1,0:T(8,128)(2,1)} %refs_0_.7), channel_id=1, source_target_pairs={{0,16},{8,24},{16,0},{24,8},{1,17},{9,25},{17,1},{25,9},{2,18},{10... | collective-permute-start | bytes 1474568 | tf_op jit(solution)/shard_map/ppermute | solution.py:30
  6.8 6.6 %hidden.1 = (bf16[1792,384]{1,0:T(8,128)(2,1)}, bf16[384,1792]{1,0:T(8,128)(2,1)}, bf16[384,1792]{1,0:T(8,128)(2,1)}) custom-call(bf16[384,1792]{1,0:T(8,128)(2,1)} %gate_ref.1, bf16[384,1792]{1,0:T(8,128)(2,1)} %up_ref.1), custom_call_target="tpu_custom_call" | custom-call | flops 1024 | bytes 1024 | tf_op jit(solution)/shard_map/hidden/pallas_call | solution.py:86
  13.4 2.4 %collective-permute-done.2.refs_2_ = bf16[384,640]{1,0:T(8,128)(2,1)} collective-permute-done((bf16[384,640]{1,0:T(8,128)(2,1)}, bf16[384,640]{1,0:T(8,128)(2,1)}, u32[]{:S(2)}, u32[]{:S(2)}) %collective-permute-start.2) | collective-permute-done | bytes 491552 | tf_op jit(solution)/shard_map/ppermute | solution.py:30
  17.2 3.1 %collective-permute-done.refs_0_ = bf16[384,640]{1,0:T(8,128)(2,1)S(1)} collective-permute-done((bf16[384,640]{1,0:T(8,128)(2,1)}, bf16[384,640]{1,0:T(8,128)(2,1)S(1)}, u32[]{:S(2)}, u32[]{:S(2)}) %collective-permute-start) | collective-permute-done | bytes 491552 | tf_op jit(solution)/shard_map/ppermute | solution.py:35
  25.3 3.8 %grad_gram.1 = (f32[4,32,1536]{2,1,0:T(8,128)}, f32[4,32,1536]{2,1,0:T(8,128)}) custom-call(s32[1]{0:T(128)} %bitcast.inner_ref, s32[4]{0:T(128)} %xor_multiply_fusion.offs_ref.toks_ref, bf16[384,640]{1,0:T(8,128)(2,1)} %refs_0_.7, bf16[384,640]{1,0:T(8,128)(2,1)} %collective-permute-done.3.refs_3_.refs_1_, bf16[384,640]{1,0:T(8,128)(2,1)} %collective-permute-done.2.refs_2_, ...), custom_call_target="tpu_custom_call" | custom-call | flops 1024 | bytes 1024 | tf_op jit(solution)/shard_map/grad_gram/pallas_call | solution.py:326
  29.2 6.1 %collective-permute-done.5.refs_1_.refs_5_ = bf16[384,640]{1,0:T(8,128)(2,1)S(1)} collective-permute-done((bf16[384,640]{1,0:T(8,128)(2,1)S(1)}, bf16[384,640]{1,0:T(8,128)(2,1)S(1)}, u32[]{:S(2)}, u32[]{:S(2)}) %collective-permute-start.5) | collective-permute-done | bytes 491552 | tf_op jit(solution)/shard_map/ppermute | solution.py:30
  35.3 2.2 %collective-permute-done.4.refs_0_ = bf16[384,640]{1,0:T(8,128)(2,1)} collective-permute-done((bf16[384,640]{1,0:T(8,128)(2,1)S(1)}, bf16[384,640]{1,0:T(8,128)(2,1)}, u32[]{:S(2)}, u32[]{:S(2)}) %collective-permute-start.4) | collective-permute-done | bytes 491552 | tf_op jit(solution)/shard_map/ppermute | solution.py:35
  39.0 10.7 %collective-permute-done.8.refs_1_.refs_6_.refs_2_ = bf16[384,640]{1,0:T(8,128)(2,1)S(1)} collective-permute-done((bf16[384,640]{1,0:T(8,128)(2,1)}, bf16[384,640]{1,0:T(8,128)(2,1)S(1)}, u32[]{:S(2)}, u32[]{:S(2)}) %collective-permute-start.8) | collective-permute-done | bytes 491552 | tf_op jit(solution)/shard_map/ppermute | solution.py:30
  49.6 3.0 %collective-permute-done.7.refs_0_ = bf16[384,640]{1,0:T(8,128)(2,1)S(1)} collective-permute-done((bf16[384,640]{1,0:T(8,128)(2,1)}, bf16[384,640]{1,0:T(8,128)(2,1)S(1)}, u32[]{:S(2)}, u32[]{:S(2)}) %collective-permute-start.7) | collective-permute-done | bytes 491552 | tf_op jit(solution)/shard_map/ppermute | solution.py:35
  54.6 3.4 %own_features.1.refs_5_ = bf16[4,384,640]{2,1,0:T(8,128)(2,1)} custom-call(s32[4]{0:T(128)} %and_select_fusion.at_ref, bf16[384,640]{1,0:T(8,128)(2,1)} %refs_0_.7, bf16[384,640]{1,0:T(8,128)(2,1)} %after.5.refs_5_.refs_1_, bf16[384,640]{1,0:T(8,128)(2,1)} %after.6.refs_2_, bf16[384,640]{1,0:T(8,128)(2,1)} %after.8.refs_1_.refs_3_, ...), custom_call_target="tpu_custom_call" | custom-call | flops 1024 | bytes 1024 | tf_op jit(solution)/shard_map/own_features/pallas_call | solution.py:116
  58.1 4.6 %all-to-all-start = ((bf16[4,384,640]{2,1,0:T(8,128)(2,1)}), bf16[4,384,640]{2,1,0:T(8,128)(2,1)}, u32[]{:S(2)}, u32[]{:S(2)}) async-start(bf16[4,384,640]{2,1,0:T(8,128)(2,1)} %own_features.1.refs_5_), calls=%async_computation | async-start | bytes 3932160 | tf_op jit(solution)/shard_map/all_to_all | solution.py:443
  63.6 14.6 %collective-permute-done.10.refs_6_.refs_7_.refs_3_ = bf16[384,640]{1,0:T(8,128)(2,1)S(1)} collective-permute-done((bf16[384,640]{1,0:T(8,128)(2,1)S(1)}, bf16[384,640]{1,0:T(8,128)(2,1)S(1)}, u32[]{:S(2)}, u32[]{:S(2)}) %collective-permute-start.10) | collective-permute-done | bytes 491552 | tf_op jit(solution)/shard_map/ppermute | solution.py:35
  78.9 6.2 %hidden_gram.1 = (f32[4,32,1536]{2,1,0:T(8,128)}, f32[4,32,768]{2,1,0:T(8,128)}, f32[4,32,768]{2,1,0:T(8,128)}) custom-call(s32[1]{0:T(128)} %bitcast.inner_ref, s32[4]{0:T(128)} %xor_multiply_fusion.offs_ref.toks_ref, bf16[1792,384]{1,0:T(8,128)(2,1)} %after.7.refs_0_.refs_4_, bf16[1792,384]{1,0:T(8,128)(2,1)} %collective-permute-done.9.refs_2_.refs_1_.refs_5_, ...), custom_call_target="tpu_custom_call" | custom-call | flops 1024 | bytes 1024 | tf_op jit(solution)/shard_map/hidden_gram/pallas_call | solution.py:326
  86.3 10.7 %grads_first.1 = (bf16[384,1792]{1,0:T(8,128)(2,1)}, bf16[384,1792]{1,0:T(8,128)(2,1)}, f32[8,128]{1,0:T(8,128)}) custom-call(s32[8]{0:T(128)} %add.40.offs_ref, bf16[384,640]{1,0:T(8,128)(2,1)} %refs_0_.7, bf16[384,640]{1,0:T(8,128)(2,1)} %after.5.refs_5_.refs_1_, bf16[384,640]{1,0:T(8,128)(2,1)} %after.6.refs_2_, bf16[384,640]{1,0:T(8,128)(2,1)} %after.8.refs_1_.refs_3_, ...), custom_call_target="tpu_custom_call" | custom-call | flops 4026531840 | bytes 17563648 | tf_op jit(solution)/shard_map/grads_first/pallas_call | solution.py:183
  97.8 2.3 %grad_pair.1.refs_4_ = f32[4,32,1536]{2,1,0:T(8,128)} custom-call(f32[4,32,1536]{2,1,0:T(8,128)} %get-tuple-element.30.kept_ref, f32[4,32,1536]{2,1,0:T(8,128)} %collective-permute-done.11.refs_0_, f32[8,128]{1,0:T(8,128)} %get-tuple-element.33.refs_1_, f32[4,32,768]{2,1,0:T(8,128)} %copy-done.9), custom_call_target="tpu_custom_call" | custom-call | flops 1024 | bytes 1024 | tf_op jit(solution)/shard_map/grad_pair/pallas_call | solution.py:349
  100.1 3.5 %all-to-all-start.2 = ((f32[4,32,1536]{2,1,0:T(8,128)}), f32[4,32,1536]{2,1,0:T(8,128)S(1)}, u32[]{:S(2)}, u32[]{:S(2)}) async-start(f32[4,32,1536]{2,1,0:T(8,128)} %grad_pair.1.refs_4_), calls=%async_computation.2 | async-start | bytes 1572864 | tf_op jit(solution)/shard_map/all_to_all | solution.py:364
  104.1 3.5 %other_features.1 = (bf16[384,640]{1,0:T(8,128)(2,1)}, bf16[384,640]{1,0:T(8,128)(2,1)}, bf16[384,640]{1,0:T(8,128)(2,1)}, bf16[384,640]{1,0:T(8,128)(2,1)}) custom-call(s32[4]{0:T(128)} %broadcast_xor_fusion.to_ref, bf16[384,640]{1,0:T(8,128)(2,1)} %copy-done.3, bf16[384,640]{1,0:T(8,128)(2,1)} %copy-done.4, bf16[384,640]{1,0:T(8,128)(2,1)} %copy-done.5, ...), custom_call_target="tpu_custom_call" | custom-call | flops 1024 | bytes 1024 | tf_op jit(solution)/shard_map/other_features/pallas_call | solution.py:144
  110.8 9.2 %grads_last.1 = (bf16[384,1792]{1,0:T(8,128)(2,1)}, bf16[384,1792]{1,0:T(8,128)(2,1)}, f32[8,128]{1,0:T(8,128)}) custom-call(s32[8]{0:T(128)} %add.40.offs_ref, bf16[384,640]{1,0:T(8,128)(2,1)} %refs_0_.7, bf16[384,640]{1,0:T(8,128)(2,1)} %after.5.refs_5_.refs_1_, bf16[384,640]{1,0:T(8,128)(2,1)} %after.6.refs_2_, ...), custom_call_target="tpu_custom_call", output_to_operand_aliasing={{0}: (13, {}), {1}: (14, {})} | custom-call | flops 3019898880 | bytes 14155776 | tf_op jit(solution)/shard_map/grads_last/pallas_call | solution.py:183
  121.6 2.3 %hidden_pair.1.refs_8_ = f32[4,32,1536]{2,1,0:T(8,128)} custom-call(f32[4,32,1536]{2,1,0:T(8,128)} %get-tuple-element.42.kept_ref, f32[4,32,768]{2,1,0:T(8,128)} %copy-done.9, f32[4,32,768]{2,1,0:T(8,128)} %collective-permute-done.18.refs_1_, f32[8,128]{1,0:T(8,128)} %get-tuple-element.43.refs_2_, bf16[384,640]{1,0:T(8,128)(2,1)} %collective-permute-done.15.refs_3_.refs_1_, ...), custom_call_target="tpu_custom_call" | custom-call | flops 1024 | bytes 1024 | tf_op jit(solution)/shard_map/hidden_pair/pallas_call | solution.py:349
  123.9 5.2 %all-to-all-start.1 = ((f32[4,32,1536]{2,1,0:T(8,128)}), f32[4,32,1536]{2,1,0:T(8,128)}, u32[]{:S(2)}, u32[]{:S(2)}) async-start(f32[4,32,1536]{2,1,0:T(8,128)} %hidden_pair.1.refs_8_), calls=%async_computation.1 | async-start | bytes 1572864 | tf_op jit(solution)/shard_map/all_to_all | solution.py:364
  129.7 13.0 %collective-permute-done.17.refs_3_ = bf16[384,640]{1,0:T(8,128)(2,1)} collective-permute-done((bf16[384,640]{1,0:T(8,128)(2,1)S(1)}, bf16[384,640]{1,0:T(8,128)(2,1)}, u32[]{:S(2)}, u32[]{:S(2)}) %collective-permute-start.17) | collective-permute-done | bytes 491552 | tf_op jit(solution)/shard_map/ppermute | solution.py:30
  142.7 9.9 %wgrad_first.1 = (bf16[1792,1280]{1,0:T(8,128)(2,1)}, f32[8,128]{1,0:T(8,128)}) custom-call(s32[2]{0:T(128)} %copy-done.10, s32[4]{0:T(128)} %xor_multiply_fusion.offs_ref.toks_ref, bf16[4,384,640]{2,1,0:T(8,128)(2,1)} %all-to-all-done.own_ref, bf16[384,640]{1,0:T(8,128)(2,1)} %get-tuple-element.34.refs_11_.refs_0_, ...), custom_call_target="tpu_custom_call" | custom-call | flops 3523215360 | bytes 8978432 | tf_op jit(solution)/shard_map/wgrad_first/pallas_call | solution.py:258
  154.7 5.7 %all-to-all-start.3 = ((f32[32,1,128]{2,1,0:T(1,128)}), f32[32,1,128]{2,1,0:T(1,128)S(1)}, u32[]{:S(2)}, u32[]{:S(2)}) async-start(f32[32,1,128]{2,1,0:T(1,128)} %bitcast.11), calls=%async_computation.3 | async-start | bytes 32768 | tf_op jit(solution)/shard_map/all_to_all | solution.py:472
  160.4 9.8 %wgrad_last.1 = (bf16[1792,1280]{1,0:T(8,128)(2,1)}, f32[8,128]{1,0:T(8,128)}) custom-call(s32[2]{0:T(128)} %copy-done.10, s32[4]{0:T(128)} %xor_multiply_fusion.offs_ref.toks_ref, bf16[4,384,640]{2,1,0:T(8,128)(2,1)} %all-to-all-done.own_ref, bf16[384,640]{1,0:T(8,128)(2,1)} %get-tuple-element.34.refs_11_.refs_0_, ...), custom_call_target="tpu_custom_call", output_to_operand_aliasing={{0}: (12, {})} | custom-call | flops 3523215360 | bytes 8978432 | tf_op jit(solution)/shard_map/wgrad_last/pallas_call | solution.py:258
  (76 shorter events, 26.6 us)
Async XLA Ops:
  0.6 12.8 %collective-permute-start.3 = (bf16[384,640]{1,0:T(8,128)(2,1)}, bf16[384,640]{1,0:T(8,128)(2,1)}, u32[]{:S(2)}, u32[]{:S(2)}) collective-permute-start(bf16[384,640]{1,0:T(8,128)(2,1)} %refs_0_.7), channel_id=1, source_target_pairs={{0,8},{8,0},{16,24},{24,16},{1,9},{9,1},{17,25},{25,17},{2,10},{10... | collective-permute-start | bytes 1474568 | tf_op jit(solution)/shard_map/ppermute | solution.py:30
  1.1 14.7 %collective-permute-start.2 = (bf16[384,640]{1,0:T(8,128)(2,1)}, bf16[384,640]{1,0:T(8,128)(2,1)}, u32[]{:S(2)}, u32[]{:S(2)}) collective-permute-start(bf16[384,640]{1,0:T(8,128)(2,1)} %refs_0_.7), channel_id=1, source_target_pairs={{0,16},{8,24},{16,0},{24,8},{1,17},{9,25},{17,1},{25,9},{2,18},{10... | collective-permute-start | bytes 1474568 | tf_op jit(solution)/shard_map/ppermute | solution.py:30
  3.7 13.5 %collective-permute-start.1 = (bf16[384,640]{1,0:T(8,128)(2,1)}, bf16[384,640]{1,0:T(8,128)(2,1)S(1)}, u32[]{:S(2)}, u32[]{:S(2)}) collective-permute-start(bf16[384,640]{1,0:T(8,128)(2,1)} %refs_0_.7), channel_id=1, source_target_pairs={{0,1},{1,0},{2,3},{3,2},{4,5},{5,4},{6,7},{7,6},{8,9},{9,8},{10,11... | collective-permute-start | bytes 1474568 | tf_op jit(solution)/shard_map/ppermute | solution.py:30
  5.2 15.1 %collective-permute-start = (bf16[384,640]{1,0:T(8,128)(2,1)}, bf16[384,640]{1,0:T(8,128)(2,1)S(1)}, u32[]{:S(2)}, u32[]{:S(2)}) collective-permute-start(bf16[384,640]{1,0:T(8,128)(2,1)} %refs_0_.7), channel_id=1, source_target_pairs={{0,2},{1,3},{2,4},{3,5},{4,6},{5,7},{6,0},{7,1},{8,10},{9,11},{10,... | collective-permute-start | bytes 1474568 | tf_op jit(solution)/shard_map/ppermute | solution.py:35
  21.2 31.5 %collective-permute-start.9 = (bf16[1792,384]{1,0:T(8,128)(2,1)}, bf16[1792,384]{1,0:T(8,128)(2,1)}, u32[]{:S(2)}, u32[]{:S(2)}) collective-permute-start(bf16[1792,384]{1,0:T(8,128)(2,1)} %after.7.refs_0_.refs_4_), channel_id=1, source_target_pairs={{0,8},{8,0},{16,24},{24,16},{1,9},{9,1},{17,25},{25,17},{2,10},{10... | collective-permute-start | bytes 4128776 | tf_op jit(solution)/shard_map/ppermute | solution.py:30
  21.2 32.9 %collective-permute-start.12 = (bf16[1792,384]{1,0:T(8,128)(2,1)}, bf16[1792,384]{1,0:T(8,128)(2,1)}, u32[]{:S(2)}, u32[]{:S(2)}) collective-permute-start(bf16[1792,384]{1,0:T(8,128)(2,1)} %after.7.refs_0_.refs_4_), channel_id=1, source_target_pairs={{0,16},{8,24},{16,0},{24,8},{1,17},{9,25},{17,1},{25,9},{2,18},{10... | collective-permute-start | bytes 4128776 | tf_op jit(solution)/shard_map/ppermute | solution.py:30
  21.7 3.7 %collective-permute-start.6 = (bf16[384,640]{1,0:T(8,128)(2,1)}, bf16[384,640]{1,0:T(8,128)(2,1)}, u32[]{:S(2)}, u32[]{:S(2)}) collective-permute-start(bf16[384,640]{1,0:T(8,128)(2,1)} %collective-permute-done.2.refs_2_), channel_id=1, source_target_pairs={{0,8},{8,0},{16,24},{24,16},{1,9},{9,1},{17,25},{25,17},{2,10},{10... | collective-permute-start | bytes 1474568 | tf_op jit(solution)/shard_map/ppermute | solution.py:30
  22.2 13.1 %collective-permute-start.5 = (bf16[384,640]{1,0:T(8,128)(2,1)S(1)}, bf16[384,640]{1,0:T(8,128)(2,1)S(1)}, u32[]{:S(2)}, u32[]{:S(2)}) collective-permute-start(bf16[384,640]{1,0:T(8,128)(2,1)S(1)} %copy-done.1), channel_id=1, source_target_pairs={{0,1},{1,0},{2,3},{3,2},{4,5},{5,4},{6,7},{7,6},{8,9},{9,8},{10,11... | collective-permute-start | bytes 1474568 | tf_op jit(solution)/shard_map/ppermute | solution.py:30
  22.7 14.7 %collective-permute-start.4 = (bf16[384,640]{1,0:T(8,128)(2,1)S(1)}, bf16[384,640]{1,0:T(8,128)(2,1)}, u32[]{:S(2)}, u32[]{:S(2)}) collective-permute-start(bf16[384,640]{1,0:T(8,128)(2,1)S(1)} %copy-done.1), channel_id=1, source_target_pairs={{0,2},{1,3},{2,4},{3,5},{4,6},{5,7},{6,0},{7,1},{8,10},{9,11},{10,... | collective-permute-start | bytes 1474568 | tf_op jit(solution)/shard_map/ppermute | solution.py:35
  37.5 12.2 %collective-permute-start.8 = (bf16[384,640]{1,0:T(8,128)(2,1)}, bf16[384,640]{1,0:T(8,128)(2,1)S(1)}, u32[]{:S(2)}, u32[]{:S(2)}) collective-permute-start(bf16[384,640]{1,0:T(8,128)(2,1)} %after.6.refs_2_), channel_id=1, source_target_pairs={{0,1},{1,0},{2,3},{3,2},{4,5},{5,4},{6,7},{7,6},{8,9},{9,8},{10,11... | collective-permute-start | bytes 1474568 | tf_op jit(solution)/shard_map/ppermute | solution.py:30
  39.0 13.7 %collective-permute-start.7 = (bf16[384,640]{1,0:T(8,128)(2,1)}, bf16[384,640]{1,0:T(8,128)(2,1)S(1)}, u32[]{:S(2)}, u32[]{:S(2)}) collective-permute-start(bf16[384,640]{1,0:T(8,128)(2,1)} %after.6.refs_2_), channel_id=1, source_target_pairs={{0,2},{1,3},{2,4},{3,5},{4,6},{5,7},{6,0},{7,1},{8,10},{9,11},{10,... | collective-permute-start | bytes 1474568 | tf_op jit(solution)/shard_map/ppermute | solution.py:35
  54.1 24.1 %collective-permute-start.13 = (bf16[1792,384]{1,0:T(8,128)(2,1)}, bf16[1792,384]{1,0:T(8,128)(2,1)}, u32[]{:S(2)}, u32[]{:S(2)}) collective-permute-start(bf16[1792,384]{1,0:T(8,128)(2,1)} %after.9.refs_4_.refs_2_.refs_6_), channel_id=1, source_target_pairs={{0,8},{8,0},{16,24},{24,16},{1,9},{9,1},{17,25},{25,17},{2,10},{10... | collective-permute-start | bytes 4128776 | tf_op jit(solution)/shard_map/ppermute | solution.py:30
  58.1 42.0 %all-to-all-start = ((bf16[4,384,640]{2,1,0:T(8,128)(2,1)}), bf16[4,384,640]{2,1,0:T(8,128)(2,1)}, u32[]{:S(2)}, u32[]{:S(2)}) async-start(bf16[4,384,640]{2,1,0:T(8,128)(2,1)} %own_features.1.refs_5_), calls=%async_computation | async-start | bytes 3932160 | tf_op jit(solution)/shard_map/all_to_all | solution.py:443
  62.7 15.5 %collective-permute-start.10 = (bf16[384,640]{1,0:T(8,128)(2,1)S(1)}, bf16[384,640]{1,0:T(8,128)(2,1)S(1)}, u32[]{:S(2)}, u32[]{:S(2)}) collective-permute-start(bf16[384,640]{1,0:T(8,128)(2,1)S(1)} %copy-done.6), channel_id=1, source_target_pairs={{0,2},{1,3},{2,4},{3,5},{4,6},{5,7},{6,0},{7,1},{8,10},{9,11},{10,... | collective-permute-start | bytes 1474568 | tf_op jit(solution)/shard_map/ppermute | solution.py:35
  62.7 34.3 %collective-permute-start.11 = (f32[4,32,1536]{2,1,0:T(8,128)}, f32[4,32,1536]{2,1,0:T(8,128)}, u32[]{:S(2)}, u32[]{:S(2)}) collective-permute-start(f32[4,32,1536]{2,1,0:T(8,128)} %get-tuple-element.26.refs_2_), channel_id=1, source_target_pairs={{0,1},{1,0},{2,3},{3,2},{4,5},{5,4},{6,7},{7,6},{8,9},{9,8},{10,11... | collective-permute-start | bytes 2359304 | tf_op jit(solution)/shard_map/ppermute | solution.py:30
  85.1 11.9 %collective-permute-start.14 = (f32[4,32,768]{2,1,0:T(8,128)}, f32[4,32,768]{2,1,0:T(8,128)S(1)}, u32[]{:S(2)}, u32[]{:S(2)}) collective-permute-start(f32[4,32,768]{2,1,0:T(8,128)} %get-tuple-element.31.refs_11_), channel_id=1, source_target_pairs={{0,1},{1,0},{2,3},{3,2},{4,5},{5,4},{6,7},{7,6},{8,9},{9,8},{10,11... | collective-permute-start | bytes 1179656 | tf_op jit(solution)/shard_map/ppermute | solution.py:30
  100.1 23.8 %all-to-all-start.2 = ((f32[4,32,1536]{2,1,0:T(8,128)}), f32[4,32,1536]{2,1,0:T(8,128)S(1)}, u32[]{:S(2)}, u32[]{:S(2)}) async-start(f32[4,32,1536]{2,1,0:T(8,128)} %grad_pair.1.refs_4_), calls=%async_computation.2 | async-start | bytes 1572864 | tf_op jit(solution)/shard_map/all_to_all | solution.py:364
  107.6 13.2 %collective-permute-start.15 = (bf16[384,640]{1,0:T(8,128)(2,1)}, bf16[384,640]{1,0:T(8,128)(2,1)}, u32[]{:S(2)}, u32[]{:S(2)}) collective-permute-start(bf16[384,640]{1,0:T(8,128)(2,1)} %get-tuple-element.39), channel_id=1, source_target_pairs={{0,8},{8,0},{16,24},{24,16},{1,9},{9,1},{17,25},{25,17},{2,10},{10... | collective-permute-start | bytes 1474568 | tf_op jit(solution)/shard_map/ppermute | solution.py:30
  107.7 14.0 %collective-permute-start.16 = (bf16[384,640]{1,0:T(8,128)(2,1)}, bf16[384,640]{1,0:T(8,128)(2,1)}, u32[]{:S(2)}, u32[]{:S(2)}) collective-permute-start(bf16[384,640]{1,0:T(8,128)(2,1)} %get-tuple-element.40), channel_id=1, source_target_pairs={{0,16},{8,24},{16,0},{24,8},{1,17},{9,25},{17,1},{25,9},{2,18},{10... | collective-permute-start | bytes 1474568 | tf_op jit(solution)/shard_map/ppermute | solution.py:30
  109.3 11.5 %collective-permute-start.18 = (f32[4,32,768]{2,1,0:T(8,128)}, f32[4,32,768]{2,1,0:T(8,128)}, u32[]{:S(2)}, u32[]{:S(2)}) collective-permute-start(f32[4,32,768]{2,1,0:T(8,128)} %get-tuple-element.32.refs_12_), channel_id=1, source_target_pairs={{0,1},{1,0},{2,3},{3,2},{4,5},{5,4},{6,7},{7,6},{8,9},{9,8},{10,11... | collective-permute-start | bytes 1179656 | tf_op jit(solution)/shard_map/ppermute | solution.py:30
  123.9 28.6 %copy-start.8 = (f32[4,32,1536]{2,1,0:T(8,128)}, f32[4,32,1536]{2,1,0:T(8,128)S(1)}, u32[]{:S(2)}) copy-start(f32[4,32,1536]{2,1,0:T(8,128)S(1)} %all-to-all-done.2.grad_ref) | copy-start | bytes 2359300
  123.9 28.6 %all-to-all-start.1 = ((f32[4,32,1536]{2,1,0:T(8,128)}), f32[4,32,1536]{2,1,0:T(8,128)}, u32[]{:S(2)}, u32[]{:S(2)}) async-start(f32[4,32,1536]{2,1,0:T(8,128)} %hidden_pair.1.refs_8_), calls=%async_computation.1 | async-start | bytes 1572864 | tf_op jit(solution)/shard_map/all_to_all | solution.py:364
  129.2 13.5 %collective-permute-start.17 = (bf16[384,640]{1,0:T(8,128)(2,1)S(1)}, bf16[384,640]{1,0:T(8,128)(2,1)}, u32[]{:S(2)}, u32[]{:S(2)}) collective-permute-start(bf16[384,640]{1,0:T(8,128)(2,1)S(1)} %copy-done.11), channel_id=1, source_target_pairs={{0,24},{8,16},{16,8},{24,0},{1,25},{9,17},{17,9},{25,1},{2,26},{10... | collective-permute-start | bytes 1474568 | tf_op jit(solution)/shard_map/ppermute | solution.py:30
  154.7 15.5 %all-to-all-start.3 = ((f32[32,1,128]{2,1,0:T(1,128)}), f32[32,1,128]{2,1,0:T(1,128)S(1)}, u32[]{:S(2)}, u32[]{:S(2)}) async-start(f32[32,1,128]{2,1,0:T(1,128)} %bitcast.11), calls=%async_computation.3 | async-start | bytes 32768 | tf_op jit(solution)/shard_map/all_to_all | solution.py:472
  (11 other events, 44.4 us)

commit v12 on v11

--- a/solution.py
+++ b/solution.py
@@ -14,6 +14,7 @@
 
 F32 = jnp.float32
 BF16 = jnp.bfloat16
+TILE = 256
 VMEM_LIMIT = 63 * 1024 * 1024
 
 
@@ -69,34 +70,47 @@
     )(x, *order)
 
 
-def hidden_body(gate_ref, up_ref, hid_ref, by_gate_ref, by_up_ref):
+def hidden_body(gate_ref, up_ref, hid_ref):
     gate = gate_ref[...].astype(F32)
+    hid_ref[...] = (gate * jax.nn.sigmoid(gate) * up_ref[...].astype(F32)).astype(BF16).T
+
+
+def hidden_units(gate, up, first, count, name):
+    toks = gate.shape[0]
+    cols = pl.BlockSpec((toks, TILE), lambda i: (0, first + i))
+    return pl.pallas_call(
+        hidden_body,
+        grid=(count,),
+        in_specs=[cols, cols],
+        out_specs=pl.BlockSpec((TILE, toks), lambda i: (i, 0)),
+        out_shape=jax.ShapeDtypeStruct((count * TILE, toks), BF16),
+        compiler_params=params(),
+        cost_estimate=SMALL,
+        name=name,
+    )(gate, up)
+
+
+def factors_body(gate_ref, up_ref, order_ref, by_gate_ref, by_up_ref):
+    gate = gate_ref[...].astype(F32)
+    sig = jax.nn.sigmoid(gate)
     up = up_ref[...].astype(F32)
-    sig = jax.nn.sigmoid(gate)
-    act = gate * sig
-    hid_ref[...] = (act * up).astype(BF16).T
     by_gate_ref[...] = (up * sig * (1.0 + gate * (1.0 - sig))).astype(BF16)
-    by_up_ref[...] = act.astype(BF16)
-
-
-def hidden_units(gate, up):
+    by_up_ref[...] = (gate * sig).astype(BF16)
+
+
+def factors(gate, up, order):
     toks, units = gate.shape
-    tile = 256
-    cols = pl.BlockSpec((toks, tile), lambda i: (0, i))
-    return pl.pallas_call(
-        hidden_body,
-        grid=(units // tile,),
-        in_specs=[cols, cols],
-        out_specs=[pl.BlockSpec((tile, toks), lambda i: (i, 0)), cols, cols],
-        out_shape=[
-            jax.ShapeDtypeStruct((units, toks), BF16),
-            jax.ShapeDtypeStruct((toks, units), BF16),
-            jax.ShapeDtypeStruct((toks, units), BF16),
-        ],
-        compiler_params=params(),
-        cost_estimate=SMALL,
-        name="hidden",
-    )(gate, up)
+    cols = pl.BlockSpec((toks, TILE), lambda i: (0, i))
+    return pl.pallas_call(
+        factors_body,
+        grid=(units // TILE,),
+        in_specs=[cols, cols, ANY],
+        out_specs=[cols, cols],
+        out_shape=[jax.ShapeDtypeStruct((toks, units), BF16)] * 2,
+        compiler_params=params(),
+        cost_estimate=SMALL,
+        name="factors",
+    )(gate, up, order)
 
 
 def stack_body(n, at_ref, *refs):
@@ -154,62 +168,72 @@
     )(to, *blocks, *order)
 
 
-def grads_body(n, offs_ref, *refs):
-    blocks, (w_ref, by_gate_ref, by_up_ref), (gg_ref, gu_ref, done_ref, piece) = (
-        refs[:n], refs[n : n + 3], refs[-4:]
-    )
+def grads_body(n, last, offs_ref, *refs):
+    blocks, (w_ref, *rest) = refs[:n], refs[n:]
     width = blocks[0].shape[1]
+    piece = refs[-1]
 
     @pl.when(pl.program_id(0) == 0)
     def _():
         for j in range(n):
-            piece[:, pl.ds(pl.multiple_of(offs_ref[j], 128), width)] = blocks[j][...]
+            piece[:, j * width : (j + 1) * width] = blocks[j][...]
+
+    weight = jnp.concatenate(
+        [w_ref[:, pl.ds(pl.multiple_of(offs_ref[j], 128), width)] for j in range(n)], axis=1
+    )
+    total = dot_nt(piece[...], weight)
+    if last:
+        sum_ref, by_gate_ref, by_up_ref = rest[:3]
+        gg_ref, gu_ref, done_ref = refs[-4:-1]
+        total += sum_ref[...]
+        gg_ref[...] = (total * by_gate_ref[...]).astype(BF16)
+        gu_ref[...] = (total * by_up_ref[...]).astype(BF16)
         done_ref[...] = jnp.zeros_like(done_ref)
-
-    total = dot_nt(piece[...], w_ref[...])
-    gg_ref[...] = (total * by_gate_ref[...]).astype(BF16)
-    gu_ref[...] = (total * by_up_ref[...]).astype(BF16)
-
-
-def grads(offs, blocks, weight, by_gate, by_up, order, tiles, made, name):
+    else:
+        refs[-2][...] = total
+
+
+def grads(offs, blocks, weight, more, order, name):
     n = len(blocks)
+    last = len(more) > 0
     toks, width = blocks[0].shape
     units, feats = weight.shape
-    tile = 256
-    first, count = tiles
-    cols = pl.BlockSpec((toks, tile), lambda i, _: (0, first + i))
+    cols = pl.BlockSpec((toks, TILE), lambda i, _: (0, i))
     out = jax.ShapeDtypeStruct((toks, units), BF16)
-    operands = [offs, *blocks, weight, by_gate, by_up, *order, *made]
-    return pl.pallas_call(
-        functools.partial(grads_body, n),
+    if last:
+        out_specs = [cols, cols, whole((8, 128))]
+        out_shape = [out, out, jax.ShapeDtypeStruct((8, 128), F32)]
+    else:
+        out_specs, out_shape = cols, jax.ShapeDtypeStruct((toks, units), F32)
+    return pl.pallas_call(
+        functools.partial(grads_body, n, last),
         grid_spec=pltpu.PrefetchScalarGridSpec(
             num_scalar_prefetch=1,
-            grid=(count,),
+            grid=(units // TILE,),
             in_specs=[whole((toks, width))] * n
-            + [pl.BlockSpec((tile, feats), lambda i, _: (first + i, 0)), cols, cols]
-            + [ANY] * (len(order) + len(made)),
-            out_specs=[cols, cols, whole((8, 128))],
-            scratch_shapes=[pltpu.VMEM((toks, feats), BF16)],
+            + [pl.BlockSpec((TILE, feats), lambda i, _: (i, 0))]
+            + [cols] * len(more)
+            + [ANY] * len(order),
+            out_specs=out_specs,
+            scratch_shapes=[pltpu.VMEM((toks, n * width), BF16)],
         ),
-        out_shape=(out, out, jax.ShapeDtypeStruct((8, 128), F32)),
-        input_output_aliases={len(operands) - len(made) + k: k for k in range(len(made))},
+        out_shape=out_shape,
         compiler_params=params(),
         cost_estimate=pl.CostEstimate(
-            flops=2 * toks * tile * count * feats,
-            bytes_accessed=2 * (tile * count * feats + toks * feats + 4 * toks * tile * count),
+            flops=2 * toks * units * n * width,
+            bytes_accessed=2 * (units * feats + toks * n * width + 4 * toks * units),
             transcendentals=0,
         ),
         name=name,
-    )(*operands)
-
-
-def wgrad_body(n, first, offs_ref, toks_ref, own_ref, *refs):
-    others, hids = refs[:n], refs[n : 2 * n]
+    )(offs, *blocks, weight, *more, *order)
+
+
+def wgrad_body(n, starts, offs_ref, toks_ref, own_ref, *refs):
+    steps = len(starts) - 1
+    others, hids = refs[:n], refs[n : (1 + steps) * n]
     out_ref, done_ref, hid, cols, outs, hid_sems, col_sems, out_sems = refs[-8:]
     done_ref[...] = jnp.zeros_like(done_ref)
     _, toks, width = own_ref.shape
-    steps, tile, _ = outs.shape
-    base = first * tile
     own, other = (pl.ds(pl.multiple_of(offs_ref[half], 128), width) for half in range(2))
     came = []
     for k in range(n):
@@ -219,15 +243,11 @@
     came = [pltpu.make_async_copy(a, b, col_sems.at[j]) for j, (a, b) in enumerate(came)]
     units = []
     for i in range(steps):
-        part = slice(i * tile, (i + 1) * tile)
-        taken = slice(base + i * tile, base + (i + 1) * tile)
+        part = slice(starts[i], starts[i + 1])
         for k in range(n):
             place = pl.ds(pl.multiple_of(toks_ref[k], 128), toks)
-            units.append(
-                pltpu.make_async_copy(
-                    hids[k].at[taken], hid.at[part, place], hid_sems.at[i * n + k]
-                )
-            )
+            copy = (hids[i * n + k], hid.at[part, place], hid_sems.at[i * n + k])
+            units.append(pltpu.make_async_copy(*copy))
     for copy in [*units[:n], *came, *units[n:]]:
         copy.start()
     for copy in came:
@@ -236,49 +256,47 @@
     for i in range(steps):
         for copy in units[i * n : (i + 1) * n]:
             copy.wait()
-        part = slice(i * tile, (i + 1) * tile)
-        outs[i] = lax.dot_general(
+        part = slice(starts[i], starts[i + 1])
+        outs[part] = lax.dot_general(
             hid[part], cols[...], (((1,), (0,)), ((), ())), preferred_element_type=F32
         ).astype(BF16)
-        made = out_ref.at[base + i * tile : base + (i + 1) * tile]
-        gone.append(pltpu.make_async_copy(outs.at[i], made, out_sems.at[i]))
+        gone.append(pltpu.make_async_copy(outs.at[part], out_ref.at[part], out_sems.at[i]))
         gone[-1].start()
     for copy in gone:
         copy.wait()
 
 
-def wgrad(offs, tok_offs, own, others, hids, order, parts, made, name):
+def wgrad(offs, tok_offs, own, others, hids, order):
     n, toks, width = own.shape
-    units = hids[0].shape[0]
     total = n * toks
-    first, steps = parts
-    tile = units // 4
-    smem = pl.BlockSpec(memory_space=pltpu.SMEM)
-    operands = [offs, tok_offs, own, *others, *hids, *order, *made]
-    return pl.pallas_call(
-        functools.partial(wgrad_body, n, first),
-        in_specs=[smem, smem] + [ANY] * (len(operands) - 2),
+    starts = [0]
+    for part in hids:
+        starts.append(starts[-1] + part[0].shape[0])
+    units = starts[-1]
+    operands = [offs, tok_offs, own, *others, *(x for part in hids for x in part), *order]
+    return pl.pallas_call(
+        functools.partial(wgrad_body, n, tuple(starts)),
+        in_specs=[pl.BlockSpec(memory_space=pltpu.SMEM)] * 2 + [ANY] * (len(operands) - 2),
         out_specs=[ANY, pl.BlockSpec(memory_space=pltpu.VMEM)],
         out_shape=[
             jax.ShapeDtypeStruct((units, 2 * width), BF16),
             jax.ShapeDtypeStruct((8, 128), F32),
         ],
         scratch_shapes=[
-            pltpu.VMEM((steps * tile, total), BF16),
+            pltpu.VMEM((units, total), BF16),
             pltpu.VMEM((total, 2 * width), BF16),
-            pltpu.VMEM((steps, tile, 2 * width), BF16),
-            pltpu.SemaphoreType.DMA((steps * n,)),
+            pltpu.VMEM((units, 2 * width), BF16),
+            pltpu.SemaphoreType.DMA((len(hids) * n,)),
             pltpu.SemaphoreType.DMA((2 * n,)),
-            pltpu.SemaphoreType.DMA((steps,)),
+            pltpu.SemaphoreType.DMA((len(hids),)),
         ],
-        input_output_aliases={len(operands) - len(made) + k: k for k in range(len(made))},
         compiler_params=params(),
         cost_estimate=pl.CostEstimate(
-            flops=4 * total * steps * tile * width,
-            bytes_accessed=2 * (total * (steps * tile + 2 * width) + 2 * steps * tile * width),
+            flops=4 * total * units * width,
+            bytes_accessed=2 * (total * (units + 2 * width) + 2 * units * width),
             transcendentals=0,
         ),
-        name=name,
+        name="wgrad",
     )(*operands)
 
 
@@ -308,11 +326,17 @@
 
 def hidden_gram_body(n, cuts, inner_ref, offs_ref, *refs):
     hid, val_ref, (kept_ref, *away_refs, wide) = refs[:n], refs[n], refs[-2 - cuts :]
-    for k, ref in enumerate(hid):
-        toks = ref.shape[1]
-        wide[:, pl.ds(pl.multiple_of(offs_ref[k], 128), toks)] = lax.dot_general(
-            val_ref[...], ref[...], (((1,), (0,)), ((), ())), preferred_element_type=F32
-        )
+    dp_count = offs_ref.shape[0]
+    for k in range(dp_count):
+        start, total = 0, None
+        for ref in hid[k::dp_count]:
+            count, toks = ref.shape
+            term = lax.dot_general(
+                val_ref[:, start : start + count], ref[...], (((1,), (0,)), ((), ())),
+                preferred_element_type=F32,
+            )
+            start, total = start + count, term if total is None else total + term
+        wide[:, pl.ds(pl.multiple_of(offs_ref[k], 128), toks)] = total
     put_slices(inner_ref, wide, kept_ref, away_refs)
 
 
@@ -413,68 +437,61 @@
     inner_at = inner.reshape(1).astype(jnp.int32)
     to = at ^ d
 
-    first = shift(out_grad, "fsdp", 2)
-    others = [swap(out_grad, "fsdp", 1)]
+    def over_dp(x):
+        far = swap(x, "dp", 2)
+        return [x, swap(x, "dp", 1), far, None]
+
+    tiles = units // TILE
+    cuts = [0, tiles // 3, tiles - tiles // 3, tiles]
+    hids = [
+        over_dp(hidden_units(gate_act, up_act, a, b - a, f"hidden_{a}"))
+        for a, b in zip(cuts, cuts[1:])
+    ]
+
+    ring, others = [out_grad], [swap(out_grad, "fsdp", 1)]
+    for step in range(2):
+        came = shift(ring[-1], "fsdp", 2)
+        ring.append(after(came, others[-1], hids[step][2]))
+        others.append(swap(ring[-1], "fsdp", 1))
+    for part in hids:
+        part[3] = swap(part[2], "dp", 1)
+
+    offs = (jnp.stack([inner, 1 - inner]) * width).astype(jnp.int32)
+    places = (offs[None, :] + at[:, None] * (2 * width)).reshape(-1)
+    by_gate, by_up = factors(gate_act, up_act, ring[1])
+    blocks = [x for pair in zip(ring, others) for x in pair]
+    half_sum = grads(places[:4], blocks[:4], down_weight, [], [ring[2], by_up], "grads_first")
+    ring.append(after(shift(ring[2], "fsdp", 2), others[2], hids[2][2], half_sum))
+    others.append(shift(others[2], "fsdp", 2))
+
+    hid_kept, away, hid_came = gram(
+        hidden_gram_body, inner_at, tok_offs, [*(x for part in hids for x in part), val_hidden],
+        [half_sum], n_fs, 1, "hidden_gram",
+    )
     far = swap(out_grad, "dp", 2)
-    near = swap(out_grad, "dp", 1)
-    first = after(first, others[0], far, near)
-    hidden, by_gate, by_up = hidden_units(gate_act, up_act)
-    hidden = after(hidden, first)
-    grad_dp = [out_grad, near, far, swap(far, "dp", 1)]
-    far = swap(hidden, "dp", 2)
-    near = swap(hidden, "dp", 1)
-
+    own = stack(at, ring, [*away, far], "own_features")
+    own_cols = lax.all_to_all(own, "dp", split_axis=0, concat_axis=0, tiled=True)
+
+    grad_dp = [out_grad, swap(out_grad, "dp", 1), far, swap(far, "dp", 1)]
     grad_kept, away, grad_came = gram(
-        grad_gram_body, inner_at, tok_offs, [*grad_dp, val_grad], [first], n_fs, 1, "grad_gram"
-    )
-    ring = [out_grad, first]
-    others.append(swap(ring[1], "fsdp", 1))
-    ring.append(after(shift(ring[1], "fsdp", 2), others[1], *away))
-    others.append(swap(ring[2], "fsdp", 1))
-    ring.append(after(shift(ring[2], "fsdp", 2), others[2], near))
-    others.append(shift(others[2], "fsdp", 2))
-
-    def over_columns(blocks):
-        return [x if k == 0 else swap(x, "dp", k) for k, x in enumerate(blocks)]
-
-    far = after(far, ring[3])
-    hid_dp = [hidden, near, far, swap(far, "dp", 1)]
-    own = stack(at, ring, [far], "own_features")
-    own_cols = lax.all_to_all(own, "dp", split_axis=0, concat_axis=0, tiled=True)
-    hid_kept, away, hid_came = gram(
-        hidden_gram_body, inner_at, tok_offs, [*hid_dp, val_hidden], [own, others[3]], n_fs, 2,
-        "hidden_gram",
-    )
-    offs = (jnp.stack([inner, 1 - inner]) * width).astype(jnp.int32)
-    places = (offs[:, None] + at[None, :] * (2 * width)).reshape(-1)
-    tiles = units // 256
-    *made, done = grads(
-        places, [*ring, *others], down_weight, by_gate, by_up, away, (0, tiles // 2 + 1), [],
-        "grads_first",
-    )
-    grad_pair = pair_sum(grad_kept, grad_came, [done, hid_came[0]], "grad_pair")
+        grad_gram_body, inner_at, tok_offs, [*grad_dp, val_grad], [own], n_fs, 1, "grad_gram"
+    )
+    hid_pair = pair_sum(hid_kept, hid_came, [*away, others[3]], "hidden_pair")
+    hid_sums = spread(hid_pair)
+    other = arrange(to, others, [hid_pair], "other_features")
+    other_cols = [x if k == 0 else swap(x, "dp", k) for k, x in enumerate(other)]
+    grad_gate, grad_up, done = grads(
+        places[4:], [ring[2], others[2], ring[3], others[3]], down_weight,
+        [half_sum, by_gate, by_up], [other[0]], "grads_last",
+    )
+    grad_pair = pair_sum(grad_kept, grad_came, [done, *other_cols[1:3]], "grad_pair")
     grad_sums = spread(grad_pair)
-    other = arrange(to, others, [grad_pair], "other_features")
-    other_cols = over_columns(other)
-    grad_gate, grad_up, done = grads(
-        places, [*ring, *others], down_weight, by_gate, by_up, [other[0]],
-        (tiles // 2 + 1, tiles - tiles // 2 - 1), made, "grads_last",
-    )
-    hid_pair = pair_sum(hid_kept, hid_came, [done, *other_cols[1:3]], "hidden_pair")
-    hid_sums = spread(hid_pair)
-    made, done = wgrad(
-        offs, tok_offs, own_cols, other_cols, hid_dp, [hid_pair], (0, 2), [], "wgrad_first"
-    )
-
-    mine = score_line(
-        assign, hid_sums, grad_sums, [done], n_dp * rows_here, n_dp * n_fs
-    )
+    weight_grad, done = wgrad(offs, tok_offs, own_cols, other_cols, hids, [grad_pair])
+
+    mine = score_line(assign, hid_sums, grad_sums, [done], n_dp * rows_here, n_dp * n_fs)
     every = lax.all_to_all(
         mine, ("dp", "fsdp"), split_axis=0, concat_axis=0, tiled=True
     ).reshape(n_dp, n_fs, 128)
-    weight_grad, _ = wgrad(
-        offs, tok_offs, own_cols, other_cols, hid_dp, [mine], (2, 2), [made], "wgrad_last"
-    )
 
     rows = n_dp * rows_here
     scale = 1.0 / jnp.sqrt(F32(L) * VAL * FFW * D)

time: 173 us -> 183 us (1.058)
  Pallas kernels: 70 us -> 79.3 us
  waiting for transfers between devices: 60.5 us -> 52.1 us
  starting transfers between devices: 33.2 us -> 39.7 us
  local copies, waits for them, and re-layouts: 4.92 us -> 8.22 us
    ppermute x4, waiting for transfers between devices: 22.8 us -> 0.01 us  [shift(): return lax.ppermute(x, axis, [(s, (s + k) % n) for s in range(n)])]
    pallas_call x5 -> x7, Pallas kernels: 46.2 us -> 55.4 us  [the longest x2 26.4 us: grads(): pl.pallas_call(functools.partial(grads_body, n, last), grid_spec=pltpu.Pr...]
    all_to_all x1, waiting for transfers between devices: 0.01 us -> 7.11 us  [per_device(): lax.all_to_all(mine, ('dp', 'fsdp'), split_axis=0, concat_axis=0, tiled=T...]
    ppermute x15 -> x20, waiting for transfers between devices: 37.6 us -> 44.2 us  [swap(): return lax.ppermute(x, axis, [(s, s ^ k) for s in range(n)])]
    ppermute x4, starting transfers between devices: 1.85 us -> 6.31 us  [shift(): return lax.ppermute(x, axis, [(s, (s + k) % n) for s in range(n)])]
    ppermute x15 -> x20, starting transfers between devices: 12.4 us -> 15.3 us  [swap(): return lax.ppermute(x, axis, [(s, s ^ k) for s in range(n)])]
    slice x0 -> x3, local copies, waits for them, and re-layouts: none -> 2.42 us  [the longest x2 1.83 us: per_device(): places[:4]]
    unnamed x25 -> x31, local copies, waits for them, and re-layouts: 4.1 us -> 5.57 us
  transfers between devices with their start and end apart: 23 -> 28, of which waited for: 13 -> 7; matrix products, arithmetic and copies ran while one was open for 1% -> 2% of each run, Pallas kernels for 39% -> 40%
where the time goes in v12:
time: 183 us; the launch traced here: 182 us
  Pallas kernels  79.3 us (43%)
  waiting for transfers between devices  52.1 us (28%)
  starting transfers between devices  39.7 us (22%)
  local copies, waits for them, and re-layouts  8.22 us (4%)
  other arithmetic  2.34 us (1%)
    ppermute x20, waiting for transfers between devices, swap(): return lax.ppermute(x, axis, [(s, s ^ k) for s in range(n)])  44.2 us
    pallas_call x2, Pallas kernels, grads(): pl.pallas_call(functools.partial(grads_body, n, last), grid_spec=pltpu.Pr...  26.4 us
    pallas_call x1, Pallas kernels, wgrad(): pl.pallas_call(functools.partial(wgrad_body, n, tuple(starts)), in_specs=...  15.5 us
    ppermute x20, starting transfers between devices, swap(): return lax.ppermute(x, axis, [(s, s ^ k) for s in range(n)])  15.3 us
    pallas_call x2, Pallas kernels, gram(): pl.pallas_call(functools.partial(body, len(toks), cuts), grid=(1,), in_sp...  10 us
    all_to_all x2, starting transfers between devices, spread(): lax.all_to_all(pair, 'fsdp', split_axis=0, concat_axis=0, axis_index_grou...  8.73 us
    pallas_call x3, Pallas kernels, hidden_units(): pl.pallas_call(hidden_body, grid=(count,), in_specs=[cols, cols], out_spe...  7.28 us
    all_to_all x1, waiting for transfers between devices, per_device(): lax.all_to_all(mine, ('dp', 'fsdp'), split_axis=0, concat_axis=0, tiled=T...  7.11 us
  transfers between devices with their start and end apart: 28, of which 7 were waited for; matrix products, arithmetic and copies ran while one was open for 2% of the time, Pallas kernels for 40%

profile of v12, /device:TPU:0, one launch (start us, length us, event | category | flops | bytes accessed | tf_op | source)
XLA Modules:
  0.0 182.5 jit_solution(2615611979038720553)
XLA Ops:
  0.6 3.0 %collective-permute-start.1 = (bf16[384,640]{1,0:T(8,128)(2,1)}, bf16[384,640]{1,0:T(8,128)(2,1)S(1)}, u32[]{:S(2)}, u32[]{:S(2)}) collective-permute-start(bf16[384,640]{1,0:T(8,128)(2,1)} %refs_0_.5), channel_id=1, source_target_pairs={{0,1},{1,0},{2,3},{3,2},{4,5},{5,4},{6,7},{7,6},{8,9},{9,8},{10,11... | collective-permute-start | bytes 1474568 | tf_op jit(solution)/shard_map/ppermute | solution.py:31
  5.2 2.0 %hidden_0.1.refs_0_.refs_4_ = bf16[512,384]{1,0:T(8,128)(2,1)} custom-call(bf16[384,1792]{1,0:T(8,128)(2,1)} %gate_ref.7, bf16[384,1792]{1,0:T(8,128)(2,1)} %up_ref.7), custom_call_target="tpu_custom_call" | custom-call | flops 1024 | bytes 1024 | tf_op jit(solution)/shard_map/hidden_0/pallas_call | solution.py:81
  8.8 3.2 %hidden_2.1.refs_4_.refs_8_ = bf16[768,384]{1,0:T(8,128)(2,1)} custom-call(bf16[384,1792]{1,0:T(8,128)(2,1)} %gate_ref.7, bf16[384,1792]{1,0:T(8,128)(2,1)} %up_ref.7), custom_call_target="tpu_custom_call" | custom-call | flops 1024 | bytes 1024 | tf_op jit(solution)/shard_map/hidden_2/pallas_call | solution.py:81
  12.5 7.2 %collective-permute-done.2.refs_2_.refs_6_ = bf16[512,384]{1,0:T(8,128)(2,1)} collective-permute-done((bf16[512,384]{1,0:T(8,128)(2,1)}, bf16[512,384]{1,0:T(8,128)(2,1)}, u32[]{:S(2)}, u32[]{:S(2)}) %collective-permute-start.2) | collective-permute-done | bytes 393248 | tf_op jit(solution)/shard_map/ppermute | solution.py:31
  21.8 2.1 %hidden_5.1.refs_8_.refs_12_ = bf16[512,384]{1,0:T(8,128)(2,1)} custom-call(bf16[384,1792]{1,0:T(8,128)(2,1)} %gate_ref.7, bf16[384,1792]{1,0:T(8,128)(2,1)} %up_ref.7), custom_call_target="tpu_custom_call" | custom-call | flops 1024 | bytes 1024 | tf_op jit(solution)/shard_map/hidden_5/pallas_call | solution.py:81
  27.0 11.8 %collective-permute-done.8.refs_2_.refs_10_.refs_14_ = bf16[512,384]{1,0:T(8,128)(2,1)S(1)} collective-permute-done((bf16[512,384]{1,0:T(8,128)(2,1)}, bf16[512,384]{1,0:T(8,128)(2,1)S(1)}, u32[]{:S(2)}, u32[]{:S(2)}) %collective-permute-start.8) | collective-permute-done | bytes 393248 | tf_op jit(solution)/shard_map/ppermute | solution.py:31
  46.8 6.2 %factors.1 = (bf16[384,1792]{1,0:T(8,128)(2,1)}, bf16[384,1792]{1,0:T(8,128)(2,1)}) custom-call(bf16[384,1792]{1,0:T(8,128)(2,1)} %gate_ref.7, bf16[384,1792]{1,0:T(8,128)(2,1)} %up_ref.7, bf16[384,640]{1,0:T(8,128)(2,1)} %after.3.order_ref.refs_2_.refs_1_), custom_call_target="tpu_custom_call" | custom-call | flops 1024 | bytes 1024 | tf_op jit(solution)/shard_map/factors/pallas_call | solution.py:104
  53.0 12.8 %grads_first.1.refs_3_.refs_13_.refs_5_ = f32[384,1792]{1,0:T(8,128)} custom-call(s32[4]{0:T(128)} %slice.21.offs_ref, bf16[384,640]{1,0:T(8,128)(2,1)} %refs_0_.5, bf16[384,640]{1,0:T(8,128)(2,1)} %copy-done.4, bf16[384,640]{1,0:T(8,128)(2,1)} %after.3.order_ref.refs_2_.refs_1_, bf16[384,640]{1,0:T(8,128)(2,1)} %collective-permute-done.4.refs_1_.refs_3_, ...), custom_call_target="tpu_custom_call" | custom-call | flops 3523215360 | bytes 25821184 | tf_op jit(solution)/shard_map/grads_first/pallas_call | solution.py:208
  65.8 6.2 %hidden_gram.1 = (f32[4,32,1536]{2,1,0:T(8,128)}, f32[4,32,1536]{2,1,0:T(8,128)}) custom-call(s32[1]{0:T(128)} %bitcast.inner_ref, s32[4]{0:T(128)} %xor_multiply_fusion.offs_ref.toks_ref, bf16[512,384]{1,0:T(8,128)(2,1)} %hidden_0.1.refs_0_.refs_4_, bf16[512,384]{1,0:T(8,128)(2,1)} %collective-permute-done.10.refs_1_.refs_5_, ...), custom_call_target="tpu_custom_call" | custom-call | flops 1024 | bytes 1024 | tf_op jit(solution)/shard_map/hidden_gram/pallas_call | solution.py:350
  73.6 3.5 %own_features.1.refs_5_ = bf16[4,384,640]{2,1,0:T(8,128)(2,1)} custom-call(s32[4]{0:T(128)} %and_select_fusion.at_ref, bf16[384,640]{1,0:T(8,128)(2,1)} %refs_0_.5, bf16[384,640]{1,0:T(8,128)(2,1)} %after.3.order_ref.refs_2_.refs_1_, bf16[384,640]{1,0:T(8,128)(2,1)} %after.4.refs_5_.refs_2_.refs_0_, bf16[384,640]{1,0:T(8,128)(2,1)} %after.5.refs_3_.refs_2_, ...), custom_call_target="tpu_custom_call" | custom-call | flops 1024 | bytes 1024 | tf_op jit(solution)/shard_map/own_features/pallas_call | solution.py:130
  77.1 4.6 %all-to-all-start = ((bf16[4,384,640]{2,1,0:T(8,128)(2,1)}), bf16[4,384,640]{2,1,0:T(8,128)(2,1)}, u32[]{:S(2)}, u32[]{:S(2)}) async-start(bf16[4,384,640]{2,1,0:T(8,128)(2,1)} %own_features.1.refs_5_), calls=%async_computation | async-start | bytes 3932160 | tf_op jit(solution)/shard_map/all_to_all | solution.py:473
  86.1 3.8 %grad_gram.1 = (f32[4,32,1536]{2,1,0:T(8,128)}, f32[4,32,1536]{2,1,0:T(8,128)}) custom-call(s32[1]{0:T(128)} %bitcast.inner_ref, s32[4]{0:T(128)} %xor_multiply_fusion.offs_ref.toks_ref, bf16[384,640]{1,0:T(8,128)(2,1)} %refs_0_.5, bf16[384,640]{1,0:T(8,128)(2,1)} %copy-done.11, bf16[384,640]{1,0:T(8,128)(2,1)} %collective-permute-done.18.refs_5_.refs_2_, ...), custom_call_target="tpu_custom_call" | custom-call | flops 1024 | bytes 1024 | tf_op jit(solution)/shard_map/grad_gram/pallas_call | solution.py:350
  89.9 12.0 %collective-permute-done.16.refs_0_ = f32[4,32,1536]{2,1,0:T(8,128)} collective-permute-done((f32[4,32,1536]{2,1,0:T(8,128)}, f32[4,32,1536]{2,1,0:T(8,128)}, u32[]{:S(2)}, u32[]{:S(2)}) %collective-permute-start.16) | collective-permute-done | bytes 786464 | tf_op jit(solution)/shard_map/ppermute | solution.py:31
  102.7 2.4 %hidden_pair.1.refs_4_ = f32[4,32,1536]{2,1,0:T(8,128)} custom-call(f32[4,32,1536]{2,1,0:T(8,128)} %get-tuple-element.22.kept_ref, f32[4,32,1536]{2,1,0:T(8,128)} %collective-permute-done.16.refs_0_, f32[4,32,1536]{2,1,0:T(8,128)} %get-tuple-element.24.refs_1_, bf16[384,640]{1,0:T(8,128)(2,1)} %copy-done.3), custom_call_target="tpu_custom_call" | custom-call | flops 1024 | bytes 1024 | tf_op jit(solution)/shard_map/hidden_pair/pallas_call | solution.py:373
  106.0 3.5 %all-to-all-start.1 = ((f32[4,32,1536]{2,1,0:T(8,128)}), f32[4,32,1536]{2,1,0:T(8,128)S(1)}, u32[]{:S(2)}, u32[]{:S(2)}) async-start(f32[4,32,1536]{2,1,0:T(8,128)} %hidden_pair.1.refs_4_), calls=%async_computation.1 | async-start | bytes 1572864 | tf_op jit(solution)/shard_map/all_to_all | solution.py:388
  111.5 3.5 %other_features.1 = (bf16[384,640]{1,0:T(8,128)(2,1)}, bf16[384,640]{1,0:T(8,128)(2,1)}, bf16[384,640]{1,0:T(8,128)(2,1)}, bf16[384,640]{1,0:T(8,128)(2,1)}) custom-call(s32[4]{0:T(128)} %broadcast_xor_fusion.to_ref, bf16[384,640]{1,0:T(8,128)(2,1)} %copy-done.4, bf16[384,640]{1,0:T(8,128)(2,1)} %collective-permute-done.4.refs_1_.refs_3_, ...), custom_call_target="tpu_custom_call" | custom-call | flops 1024 | bytes 1024 | tf_op jit(solution)/shard_map/other_features/pallas_call | solution.py:158
  116.5 13.7 %grads_last.1 = (bf16[384,1792]{1,0:T(8,128)(2,1)}, bf16[384,1792]{1,0:T(8,128)(2,1)}, f32[8,128]{1,0:T(8,128)}) custom-call(s32[4]{0:T(128)} %slice.19.offs_ref, bf16[384,640]{1,0:T(8,128)(2,1)} %after.4.refs_5_.refs_2_.refs_0_, bf16[384,640]{1,0:T(8,128)(2,1)} %copy-done.5, bf16[384,640]{1,0:T(8,128)(2,1)} %after.5.refs_3_.refs_2_, ...), custom_call_target="tpu_custom_call" | custom-call | flops 3523215360 | bytes 25821184 | tf_op jit(solution)/shard_map/grads_last/pallas_call | solution.py:208
  130.2 2.3 %grad_pair.1.refs_16_ = f32[4,32,1536]{2,1,0:T(8,128)} custom-call(f32[4,32,1536]{2,1,0:T(8,128)} %get-tuple-element.31.kept_ref, f32[4,32,1536]{2,1,0:T(8,128)} %collective-permute-done.23.refs_0_, f32[8,128]{1,0:T(8,128)} %get-tuple-element.32.refs_1_, bf16[384,640]{1,0:T(8,128)(2,1)} %collective-permute-done.20.refs_2_.refs_1_, ...), custom_call_target="tpu_custom_call" | custom-call | flops 1024 | bytes 1024 | tf_op jit(solution)/shard_map/grad_pair/pallas_call | solution.py:373
  132.6 5.2 %all-to-all-start.2 = ((f32[4,32,1536]{2,1,0:T(8,128)}), f32[4,32,1536]{2,1,0:T(8,128)}, u32[]{:S(2)}, u32[]{:S(2)}) async-start(f32[4,32,1536]{2,1,0:T(8,128)} %grad_pair.1.refs_16_), calls=%async_computation.2 | async-start | bytes 1572864 | tf_op jit(solution)/shard_map/all_to_all | solution.py:388
  138.6 12.8 %collective-permute-done.22.refs_3_ = bf16[384,640]{1,0:T(8,128)(2,1)} collective-permute-done((bf16[384,640]{1,0:T(8,128)(2,1)S(1)}, bf16[384,640]{1,0:T(8,128)(2,1)}, u32[]{:S(2)}, u32[]{:S(2)}) %collective-permute-start.22) | collective-permute-done | bytes 491552 | tf_op jit(solution)/shard_map/ppermute | solution.py:31
  151.4 15.5 %wgrad.1 = (bf16[1792,1280]{1,0:T(8,128)(2,1)}, f32[8,128]{1,0:T(8,128)}) custom-call(s32[2]{0:T(128)} %copy-done.13, s32[4]{0:T(128)} %xor_multiply_fusion.offs_ref.toks_ref, bf16[4,384,640]{2,1,0:T(8,128)(2,1)} %all-to-all-done.own_ref, bf16[384,640]{1,0:T(8,128)(2,1)} %get-tuple-element.25.refs_8_.refs_0_, ...), custom_call_target="tpu_custom_call" | custom-call | flops 7046430720 | bytes 14024704 | tf_op jit(solution)/shard_map/wgrad/pallas_call | solution.py:277
  166.9 2.1 %score_line.1 = f32[32,128]{1,0:T(8,128)} custom-call(s32[3]{0:T(128)} %assign_ref.1, f32[4,32,1536]{2,1,0:T(8,128)} %copy-done.9, f32[4,32,1536]{2,1,0:T(8,128)} %all-to-all-done.2.grad_ref, f32[8,128]{1,0:T(8,128)} %get-tuple-element.34.refs_0_), custom_call_target="tpu_custom_call" | custom-call | flops 1024 | bytes 1024 | tf_op jit(solution)/shard_map/score_line/pallas_call | solution.py:411
  169.0 4.8 %all-to-all-start.3 = ((f32[32,1,128]{2,1,0:T(1,128)}), f32[32,1,128]{2,1,0:T(1,128)S(1)}, u32[]{:S(2)}, u32[]{:S(2)}) async-start(f32[32,1,128]{2,1,0:T(1,128)} %bitcast.13), calls=%async_computation.3 | async-start | bytes 32768 | tf_op jit(solution)/shard_map/all_to_all | solution.py:492
  173.8 7.1 %all-to-all-done.3 = f32[32,1,128]{2,1,0:T(1,128)S(1)} async-done(((f32[32,1,128]{2,1,0:T(1,128)}), f32[32,1,128]{2,1,0:T(1,128)S(1)}, u32[]{:S(2)}, u32[]{:S(2)}) %all-to-all-start.3) | async-done | bytes 16416 | tf_op jit(solution)/shard_map/all_to_all | solution.py:492
  (94 shorter events, 30.4 us)
Async XLA Ops:
  0.6 19.0 %collective-permute-start.1 = (bf16[384,640]{1,0:T(8,128)(2,1)}, bf16[384,640]{1,0:T(8,128)(2,1)S(1)}, u32[]{:S(2)}, u32[]{:S(2)}) collective-permute-start(bf16[384,640]{1,0:T(8,128)(2,1)} %refs_0_.5), channel_id=1, source_target_pairs={{0,1},{1,0},{2,3},{3,2},{4,5},{5,4},{6,7},{7,6},{8,9},{9,8},{10,11... | collective-permute-start | bytes 1474568 | tf_op jit(solution)/shard_map/ppermute | solution.py:31
  3.6 16.0 %collective-permute-start = (bf16[384,640]{1,0:T(8,128)(2,1)}, bf16[384,640]{1,0:T(8,128)(2,1)S(1)}, u32[]{:S(2)}, u32[]{:S(2)}) collective-permute-start(bf16[384,640]{1,0:T(8,128)(2,1)} %refs_0_.5), channel_id=1, source_target_pairs={{0,2},{1,3},{2,4},{3,5},{4,6},{5,7},{6,0},{7,1},{8,10},{9,11},{10,... | collective-permute-start | bytes 1474568 | tf_op jit(solution)/shard_map/ppermute | solution.py:36
  7.2 12.4 %collective-permute-start.2 = (bf16[512,384]{1,0:T(8,128)(2,1)}, bf16[512,384]{1,0:T(8,128)(2,1)}, u32[]{:S(2)}, u32[]{:S(2)}) collective-permute-start(bf16[512,384]{1,0:T(8,128)(2,1)} %hidden_0.1.refs_0_.refs_4_), channel_id=1, source_target_pairs={{0,16},{8,24},{16,0},{24,8},{1,17},{9,25},{17,1},{25,9},{2,18},{10... | collective-permute-start | bytes 1179656 | tf_op jit(solution)/shard_map/ppermute | solution.py:31
  12.0 26.9 %collective-permute-start.5 = (bf16[768,384]{1,0:T(8,128)(2,1)}, bf16[768,384]{1,0:T(8,128)(2,1)}, u32[]{:S(2)}, u32[]{:S(2)}) collective-permute-start(bf16[768,384]{1,0:T(8,128)(2,1)} %hidden_2.1.refs_4_.refs_8_), channel_id=1, source_target_pairs={{0,16},{8,24},{16,0},{24,8},{1,17},{9,25},{17,1},{25,9},{2,18},{10... | collective-permute-start | bytes 1769480 | tf_op jit(solution)/shard_map/ppermute | solution.py:31
  21.2 18.1 %collective-permute-start.4 = (bf16[384,640]{1,0:T(8,128)(2,1)}, bf16[384,640]{1,0:T(8,128)(2,1)}, u32[]{:S(2)}, u32[]{:S(2)}) collective-permute-start(bf16[384,640]{1,0:T(8,128)(2,1)} %after.3.order_ref.refs_2_.refs_1_), channel_id=1, source_target_pairs={{0,1},{1,0},{2,3},{3,2},{4,5},{5,4},{6,7},{7,6},{8,9},{9,8},{10,11... | collective-permute-start | bytes 1474568 | tf_op jit(solution)/shard_map/ppermute | solution.py:31
  23.8 15.0 %collective-permute-start.8 = (bf16[512,384]{1,0:T(8,128)(2,1)}, bf16[512,384]{1,0:T(8,128)(2,1)S(1)}, u32[]{:S(2)}, u32[]{:S(2)}) collective-permute-start(bf16[512,384]{1,0:T(8,128)(2,1)} %hidden_5.1.refs_8_.refs_12_), channel_id=1, source_target_pairs={{0,16},{8,24},{16,0},{24,8},{1,17},{9,25},{17,1},{25,9},{2,18},{10... | collective-permute-start | bytes 1179656 | tf_op jit(solution)/shard_map/ppermute | solution.py:31
  25.4 14.1 %collective-permute-start.3 = (bf16[384,640]{1,0:T(8,128)(2,1)S(1)}, bf16[384,640]{1,0:T(8,128)(2,1)S(1)}, u32[]{:S(2)}, u32[]{:S(2)}) collective-permute-start(bf16[384,640]{1,0:T(8,128)(2,1)S(1)} %copy-done.1), channel_id=1, source_target_pairs={{0,2},{1,3},{2,4},{3,5},{4,6},{5,7},{6,0},{7,1},{8,10},{9,11},{10,... | collective-permute-start | bytes 1474568 | tf_op jit(solution)/shard_map/ppermute | solution.py:36
  26.9 16.0 %collective-permute-start.12 = (bf16[768,384]{1,0:T(8,128)(2,1)}, bf16[768,384]{1,0:T(8,128)(2,1)}, u32[]{:S(2)}, u32[]{:S(2)}) collective-permute-start(bf16[768,384]{1,0:T(8,128)(2,1)} %hidden_2.1.refs_4_.refs_8_), channel_id=1, source_target_pairs={{0,8},{8,0},{16,24},{24,16},{1,9},{9,1},{17,25},{25,17},{2,10},{10... | collective-permute-start | bytes 1769480 | tf_op jit(solution)/shard_map/ppermute | solution.py:31
  39.3 6.9 %collective-permute-start.11 = (bf16[512,384]{1,0:T(8,128)(2,1)}, bf16[512,384]{1,0:T(8,128)(2,1)}, u32[]{:S(2)}, u32[]{:S(2)}) collective-permute-start(bf16[512,384]{1,0:T(8,128)(2,1)} %collective-permute-done.2.refs_2_.refs_6_), channel_id=1, source_target_pairs={{0,8},{8,0},{16,24},{24,16},{1,9},{9,1},{17,25},{25,17},{2,10},{10... | collective-permute-start | bytes 1179656 | tf_op jit(solution)/shard_map/ppermute | solution.py:31
  39.6 26.2 %collective-permute-start.13 = (bf16[768,384]{1,0:T(8,128)(2,1)}, bf16[768,384]{1,0:T(8,128)(2,1)}, u32[]{:S(2)}, u32[]{:S(2)}) collective-permute-start(bf16[768,384]{1,0:T(8,128)(2,1)} %collective-permute-done.5.refs_2_.refs_6_.refs_10_), channel_id=1, source_target_pairs={{0,8},{8,0},{16,24},{24,16},{1,9},{9,1},{17,25},{25,17},{2,10},{10... | collective-permute-start | bytes 1769480 | tf_op jit(solution)/shard_map/ppermute | solution.py:31
  40.9 32.7 %collective-permute-start.18 = (bf16[384,640]{1,0:T(8,128)(2,1)}, bf16[384,640]{1,0:T(8,128)(2,1)}, u32[]{:S(2)}, u32[]{:S(2)}) collective-permute-start(bf16[384,640]{1,0:T(8,128)(2,1)} %refs_0_.5), channel_id=1, source_target_pairs={{0,16},{8,24},{16,0},{24,8},{1,17},{9,25},{17,1},{25,9},{2,18},{10... | collective-permute-start | bytes 1474568 | tf_op jit(solution)/shard_map/ppermute | solution.py:31
  42.4 29.5 %collective-permute-start.6 = (bf16[384,640]{1,0:T(8,128)(2,1)}, bf16[384,640]{1,0:T(8,128)(2,1)S(1)}, u32[]{:S(2)}, u32[]{:S(2)}) collective-permute-start(bf16[384,640]{1,0:T(8,128)(2,1)} %after.4.refs_5_.refs_2_.refs_0_), channel_id=1, source_target_pairs={{0,1},{1,0},{2,3},{3,2},{4,5},{5,4},{6,7},{7,6},{8,9},{9,8},{10,11... | collective-permute-start | bytes 1474568 | tf_op jit(solution)/shard_map/ppermute | solution.py:31
  43.0 29.0 %collective-permute-start.7 = (bf16[384,640]{1,0:T(8,128)(2,1)}, bf16[384,640]{1,0:T(8,128)(2,1)S(1)}, u32[]{:S(2)}, u32[]{:S(2)}) collective-permute-start(bf16[384,640]{1,0:T(8,128)(2,1)} %after.4.refs_5_.refs_2_.refs_0_), channel_id=1, source_target_pairs={{0,2},{1,3},{2,4},{3,5},{4,6},{5,7},{6,0},{7,1},{8,10},{9,11},{10,... | collective-permute-start | bytes 1474568 | tf_op jit(solution)/shard_map/ppermute | solution.py:36
  46.3 19.5 %collective-permute-start.15 = (bf16[512,384]{1,0:T(8,128)(2,1)}, bf16[512,384]{1,0:T(8,128)(2,1)}, u32[]{:S(2)}, u32[]{:S(2)}) collective-permute-start(bf16[512,384]{1,0:T(8,128)(2,1)} %copy-done.10), channel_id=1, source_target_pairs={{0,8},{8,0},{16,24},{24,16},{1,9},{9,1},{17,25},{25,17},{2,10},{10... | collective-permute-start | bytes 1179656 | tf_op jit(solution)/shard_map/ppermute | solution.py:31
  77.1 28.9 %all-to-all-start = ((bf16[4,384,640]{2,1,0:T(8,128)(2,1)}), bf16[4,384,640]{2,1,0:T(8,128)(2,1)}, u32[]{:S(2)}, u32[]{:S(2)}) async-start(bf16[4,384,640]{2,1,0:T(8,128)(2,1)} %own_features.1.refs_5_), calls=%async_computation | async-start | bytes 3932160 | tf_op jit(solution)/shard_map/all_to_all | solution.py:473
  81.6 20.3 %collective-permute-start.16 = (f32[4,32,1536]{2,1,0:T(8,128)}, f32[4,32,1536]{2,1,0:T(8,128)}, u32[]{:S(2)}, u32[]{:S(2)}) collective-permute-start(f32[4,32,1536]{2,1,0:T(8,128)} %get-tuple-element.23.refs_4_), channel_id=1, source_target_pairs={{0,1},{1,0},{2,3},{3,2},{4,5},{5,4},{6,7},{7,6},{8,9},{9,8},{10,11... | collective-permute-start | bytes 2359304 | tf_op jit(solution)/shard_map/ppermute | solution.py:31
  83.7 18.3 %collective-permute-start.9 = (bf16[384,640]{1,0:T(8,128)(2,1)S(1)}, bf16[384,640]{1,0:T(8,128)(2,1)S(1)}, u32[]{:S(2)}, u32[]{:S(2)}) collective-permute-start(bf16[384,640]{1,0:T(8,128)(2,1)S(1)} %copy-done.6), channel_id=1, source_target_pairs={{0,2},{1,3},{2,4},{3,5},{4,6},{5,7},{6,0},{7,1},{8,10},{9,11},{10,... | collective-permute-start | bytes 1474568 | tf_op jit(solution)/shard_map/ppermute | solution.py:36
  106.0 26.6 %all-to-all-start.1 = ((f32[4,32,1536]{2,1,0:T(8,128)}), f32[4,32,1536]{2,1,0:T(8,128)S(1)}, u32[]{:S(2)}, u32[]{:S(2)}) async-start(f32[4,32,1536]{2,1,0:T(8,128)} %hidden_pair.1.refs_4_), calls=%async_computation.1 | async-start | bytes 1572864 | tf_op jit(solution)/shard_map/all_to_all | solution.py:388
  109.5 20.7 %collective-permute-start.23 = (f32[4,32,1536]{2,1,0:T(8,128)}, f32[4,32,1536]{2,1,0:T(8,128)}, u32[]{:S(2)}, u32[]{:S(2)}) collective-permute-start(f32[4,32,1536]{2,1,0:T(8,128)} %get-tuple-element.24.refs_1_), channel_id=1, source_target_pairs={{0,1},{1,0},{2,3},{3,2},{4,5},{5,4},{6,7},{7,6},{8,9},{9,8},{10,11... | collective-permute-start | bytes 2359304 | tf_op jit(solution)/shard_map/ppermute | solution.py:31
  115.0 15.2 %collective-permute-start.20 = (bf16[384,640]{1,0:T(8,128)(2,1)}, bf16[384,640]{1,0:T(8,128)(2,1)}, u32[]{:S(2)}, u32[]{:S(2)}) collective-permute-start(bf16[384,640]{1,0:T(8,128)(2,1)} %get-tuple-element.28), channel_id=1, source_target_pairs={{0,8},{8,0},{16,24},{24,16},{1,9},{9,1},{17,25},{25,17},{2,10},{10... | collective-permute-start | bytes 1474568 | tf_op jit(solution)/shard_map/ppermute | solution.py:31
  115.1 15.1 %collective-permute-start.21 = (bf16[384,640]{1,0:T(8,128)(2,1)}, bf16[384,640]{1,0:T(8,128)(2,1)}, u32[]{:S(2)}, u32[]{:S(2)}) collective-permute-start(bf16[384,640]{1,0:T(8,128)(2,1)} %get-tuple-element.29), channel_id=1, source_target_pairs={{0,16},{8,24},{16,0},{24,8},{1,17},{9,25},{17,1},{25,9},{2,18},{10... | collective-permute-start | bytes 1474568 | tf_op jit(solution)/shard_map/ppermute | solution.py:31
  132.6 34.3 %all-to-all-start.2 = ((f32[4,32,1536]{2,1,0:T(8,128)}), f32[4,32,1536]{2,1,0:T(8,128)}, u32[]{:S(2)}, u32[]{:S(2)}) async-start(f32[4,32,1536]{2,1,0:T(8,128)} %grad_pair.1.refs_16_), calls=%async_computation.2 | async-start | bytes 1572864 | tf_op jit(solution)/shard_map/all_to_all | solution.py:388
  137.8 13.6 %collective-permute-start.22 = (bf16[384,640]{1,0:T(8,128)(2,1)S(1)}, bf16[384,640]{1,0:T(8,128)(2,1)}, u32[]{:S(2)}, u32[]{:S(2)}) collective-permute-start(bf16[384,640]{1,0:T(8,128)(2,1)S(1)} %copy-done.14), channel_id=1, source_target_pairs={{0,24},{8,16},{16,8},{24,0},{1,25},{9,17},{17,9},{25,1},{2,26},{10... | collective-permute-start | bytes 1474568 | tf_op jit(solution)/shard_map/ppermute | solution.py:31
  169.0 11.9 %all-to-all-start.3 = ((f32[32,1,128]{2,1,0:T(1,128)}), f32[32,1,128]{2,1,0:T(1,128)S(1)}, u32[]{:S(2)}, u32[]{:S(2)}) async-start(f32[32,1,128]{2,1,0:T(1,128)} %bitcast.13), calls=%async_computation.3 | async-start | bytes 32768 | tf_op jit(solution)/shard_map/all_to_all | solution.py:492
  (19 other events, 90.7 us)

commit v13 on v12

--- a/solution.py
+++ b/solution.py
@@ -88,29 +88,6 @@
         cost_estimate=SMALL,
         name=name,
     )(gate, up)
-
-
-def factors_body(gate_ref, up_ref, order_ref, by_gate_ref, by_up_ref):
-    gate = gate_ref[...].astype(F32)
-    sig = jax.nn.sigmoid(gate)
-    up = up_ref[...].astype(F32)
-    by_gate_ref[...] = (up * sig * (1.0 + gate * (1.0 - sig))).astype(BF16)
-    by_up_ref[...] = (gate * sig).astype(BF16)
-
-
-def factors(gate, up, order):
-    toks, units = gate.shape
-    cols = pl.BlockSpec((toks, TILE), lambda i: (0, i))
-    return pl.pallas_call(
-        factors_body,
-        grid=(units // TILE,),
-        in_specs=[cols, cols, ANY],
-        out_specs=[cols, cols],
-        out_shape=[jax.ShapeDtypeStruct((toks, units), BF16)] * 2,
-        compiler_params=params(),
-        cost_estimate=SMALL,
-        name="factors",
-    )(gate, up, order)
 
 
 def stack_body(n, at_ref, *refs):
@@ -168,64 +145,52 @@
     )(to, *blocks, *order)
 
 
-def grads_body(n, last, offs_ref, *refs):
-    blocks, (w_ref, *rest) = refs[:n], refs[n:]
+def grads_body(n, offs_ref, *refs):
+    blocks, (w_ref, gate_ref, up_ref), (gg_ref, gu_ref, done_ref, piece) = (
+        refs[:n], refs[n : n + 3], refs[-4:]
+    )
     width = blocks[0].shape[1]
-    piece = refs[-1]
 
     @pl.when(pl.program_id(0) == 0)
     def _():
         for j in range(n):
-            piece[:, j * width : (j + 1) * width] = blocks[j][...]
-
-    weight = jnp.concatenate(
-        [w_ref[:, pl.ds(pl.multiple_of(offs_ref[j], 128), width)] for j in range(n)], axis=1
-    )
-    total = dot_nt(piece[...], weight)
-    if last:
-        sum_ref, by_gate_ref, by_up_ref = rest[:3]
-        gg_ref, gu_ref, done_ref = refs[-4:-1]
-        total += sum_ref[...]
-        gg_ref[...] = (total * by_gate_ref[...]).astype(BF16)
-        gu_ref[...] = (total * by_up_ref[...]).astype(BF16)
+            piece[:, pl.ds(pl.multiple_of(offs_ref[j], 128), width)] = blocks[j][...]
         done_ref[...] = jnp.zeros_like(done_ref)
-    else:
-        refs[-2][...] = total
-
-
-def grads(offs, blocks, weight, more, order, name):
+
+    total = dot_nt(piece[...], w_ref[...])
+    gate = gate_ref[...].astype(F32)
+    up = up_ref[...].astype(F32)
+    sig = jax.nn.sigmoid(gate)
+    gg_ref[...] = (total * up * sig * (1.0 + gate * (1.0 - sig))).astype(BF16)
+    gu_ref[...] = (total * (gate * sig)).astype(BF16)
+
+
+def grads(offs, blocks, weight, gate, up, order):
     n = len(blocks)
-    last = len(more) > 0
     toks, width = blocks[0].shape
     units, feats = weight.shape
     cols = pl.BlockSpec((toks, TILE), lambda i, _: (0, i))
     out = jax.ShapeDtypeStruct((toks, units), BF16)
-    if last:
-        out_specs = [cols, cols, whole((8, 128))]
-        out_shape = [out, out, jax.ShapeDtypeStruct((8, 128), F32)]
-    else:
-        out_specs, out_shape = cols, jax.ShapeDtypeStruct((toks, units), F32)
-    return pl.pallas_call(
-        functools.partial(grads_body, n, last),
+    return pl.pallas_call(
+        functools.partial(grads_body, n),
         grid_spec=pltpu.PrefetchScalarGridSpec(
             num_scalar_prefetch=1,
             grid=(units // TILE,),
             in_specs=[whole((toks, width))] * n
-            + [pl.BlockSpec((TILE, feats), lambda i, _: (i, 0))]
-            + [cols] * len(more)
+            + [pl.BlockSpec((TILE, feats), lambda i, _: (i, 0)), cols, cols]
             + [ANY] * len(order),
-            out_specs=out_specs,
-            scratch_shapes=[pltpu.VMEM((toks, n * width), BF16)],
+            out_specs=[cols, cols, whole((8, 128))],
+            scratch_shapes=[pltpu.VMEM((toks, feats), BF16)],
         ),
-        out_shape=out_shape,
+        out_shape=(out, out, jax.ShapeDtypeStruct((8, 128), F32)),
         compiler_params=params(),
         cost_estimate=pl.CostEstimate(
-            flops=2 * toks * units * n * width,
-            bytes_accessed=2 * (units * feats + toks * n * width + 4 * toks * units),
-            transcendentals=0,
+            flops=2 * toks * units * feats,
+            bytes_accessed=2 * (units * feats + toks * feats + 4 * toks * units),
+            transcendentals=toks * units,
         ),
-        name=name,
-    )(offs, *blocks, weight, *more, *order)
+        name="grads",
+    )(offs, *blocks, weight, gate, up, *order)
 
 
 def wgrad_body(n, starts, offs_ref, toks_ref, own_ref, *refs):
@@ -455,36 +420,31 @@
         others.append(swap(ring[-1], "fsdp", 1))
     for part in hids:
         part[3] = swap(part[2], "dp", 1)
-
-    offs = (jnp.stack([inner, 1 - inner]) * width).astype(jnp.int32)
-    places = (offs[None, :] + at[:, None] * (2 * width)).reshape(-1)
-    by_gate, by_up = factors(gate_act, up_act, ring[1])
-    blocks = [x for pair in zip(ring, others) for x in pair]
-    half_sum = grads(places[:4], blocks[:4], down_weight, [], [ring[2], by_up], "grads_first")
-    ring.append(after(shift(ring[2], "fsdp", 2), others[2], hids[2][2], half_sum))
-    others.append(shift(others[2], "fsdp", 2))
-
     hid_kept, away, hid_came = gram(
         hidden_gram_body, inner_at, tok_offs, [*(x for part in hids for x in part), val_hidden],
-        [half_sum], n_fs, 1, "hidden_gram",
-    )
+        [ring[2]], n_fs, 1, "hidden_gram",
+    )
+    ring.append(after(shift(ring[2], "fsdp", 2), others[2], *away))
+    others.append(shift(others[2], "fsdp", 2))
+
     far = swap(out_grad, "dp", 2)
-    own = stack(at, ring, [*away, far], "own_features")
+    own = stack(at, ring, [far], "own_features")
     own_cols = lax.all_to_all(own, "dp", split_axis=0, concat_axis=0, tiled=True)
 
     grad_dp = [out_grad, swap(out_grad, "dp", 1), far, swap(far, "dp", 1)]
     grad_kept, away, grad_came = gram(
         grad_gram_body, inner_at, tok_offs, [*grad_dp, val_grad], [own], n_fs, 1, "grad_gram"
     )
-    hid_pair = pair_sum(hid_kept, hid_came, [*away, others[3]], "hidden_pair")
+    other = arrange(to, others, away, "other_features")
+    other_cols = [x if k == 0 else swap(x, "dp", k) for k, x in enumerate(other)]
+    hid_pair = pair_sum(hid_kept, hid_came, [other[0]], "hidden_pair")
     hid_sums = spread(hid_pair)
-    other = arrange(to, others, [hid_pair], "other_features")
-    other_cols = [x if k == 0 else swap(x, "dp", k) for k, x in enumerate(other)]
+    offs = (jnp.stack([inner, 1 - inner]) * width).astype(jnp.int32)
+    places = (offs[:, None] + at[None, :] * (2 * width)).reshape(-1)
     grad_gate, grad_up, done = grads(
-        places[4:], [ring[2], others[2], ring[3], others[3]], down_weight,
-        [half_sum, by_gate, by_up], [other[0]], "grads_last",
-    )
-    grad_pair = pair_sum(grad_kept, grad_came, [done, *other_cols[1:3]], "grad_pair")
+        places, [*ring, *others], down_weight, gate_act, up_act, [hid_pair]
+    )
+    grad_pair = pair_sum(grad_kept, grad_came, [done, *other_cols[1:]], "grad_pair")
     grad_sums = spread(grad_pair)
     weight_grad, done = wgrad(offs, tok_offs, own_cols, other_cols, hids, [grad_pair])
 

time: 183 us -> 161 us (0.88)
  Pallas kernels: 79.3 us -> 62.3 us
  local copies, waits for them, and re-layouts: 8.22 us -> 4.31 us
  starting transfers between devices: 39.7 us -> 36.2 us
  waiting for transfers between devices: 52.1 us -> 54.2 us
    pallas_call x3 -> x1, Pallas kernels: 32.6 us -> 15.9 us  [grads(): pl.pallas_call(functools.partial(grads_body, n), grid_spec=pltpu.Prefetch...]
    ppermute x20, waiting for transfers between devices: 44.2 us -> 28.9 us  [swap(): return lax.ppermute(x, axis, [(s, s ^ k) for s in range(n)])]
    ppermute x4, waiting for transfers between devices: 0.01 us -> 11.4 us  [shift(): return lax.ppermute(x, axis, [(s, (s + k) % n) for s in range(n)])]
    all_to_all x2, waiting for transfers between devices: 0.01 us -> 5.16 us  [spread(): lax.all_to_all(pair, 'fsdp', split_axis=0, concat_axis=0, axis_index_grou...]
    slice x3 -> x0, local copies, waits for them, and re-layouts: 2.42 us -> none  [the longest x2 1.83 us: per_device(): places[:4]]
    all_to_all x1, starting transfers between devices: 4.77 us -> 2.49 us  [per_device(): lax.all_to_all(mine, ('dp', 'fsdp'), split_axis=0, concat_axis=0, tiled=T...]
    unnamed x31 -> x23, local copies, waits for them, and re-layouts: 5.57 us -> 3.49 us
  transfers between devices with their start and end apart: 28 -> 28, of which waited for: 7 -> 12; matrix products, arithmetic and copies ran while one was open for 2% -> 1% of each run, Pallas kernels for 40% -> 35%
where the time goes in v13:
time: 161 us; the launch traced here: 160 us
  Pallas kernels  62.3 us (39%)
  waiting for transfers between devices  54.2 us (34%)
  starting transfers between devices  36.2 us (22%)
  local copies, waits for them, and re-layouts  4.31 us (3%)
  other arithmetic  2.44 us (2%)
    ppermute x20, waiting for transfers between devices, swap(): return lax.ppermute(x, axis, [(s, s ^ k) for s in range(n)])  28.9 us
    pallas_call x1, Pallas kernels, grads(): pl.pallas_call(functools.partial(grads_body, n), grid_spec=pltpu.Prefetch...  15.9 us
    pallas_call x1, Pallas kernels, wgrad(): pl.pallas_call(functools.partial(wgrad_body, n, tuple(starts)), in_specs=...  15.4 us
    ppermute x20, starting transfers between devices, swap(): return lax.ppermute(x, axis, [(s, s ^ k) for s in range(n)])  15 us
    ppermute x4, waiting for transfers between devices, shift(): return lax.ppermute(x, axis, [(s, (s + k) % n) for s in range(n)])  11.4 us
    pallas_call x2, Pallas kernels, gram(): pl.pallas_call(functools.partial(body, len(toks), cuts), grid=(1,), in_sp...  9.97 us
    all_to_all x2, starting transfers between devices, spread(): lax.all_to_all(pair, 'fsdp', split_axis=0, concat_axis=0, axis_index_grou...  8.55 us
    pallas_call x3, Pallas kernels, hidden_units(): pl.pallas_call(hidden_body, grid=(count,), in_specs=[cols, cols], out_spe...  7.26 us
  transfers between devices with their start and end apart: 28, of which 12 were waited for; matrix products, arithmetic and copies ran while one was open for 1% of the time, Pallas kernels for 35%

profile of v13, /device:TPU:0, one launch (start us, length us, event | category | flops | bytes accessed | tf_op | source)
XLA Modules:
  0.0 160.2 jit_solution(3108150551432813730)
XLA Ops:
  0.6 3.0 %collective-permute-start.1 = (bf16[384,640]{1,0:T(8,128)(2,1)}, bf16[384,640]{1,0:T(8,128)(2,1)S(1)}, u32[]{:S(2)}, u32[]{:S(2)}) collective-permute-start(bf16[384,640]{1,0:T(8,128)(2,1)} %refs_0_.5), channel_id=1, source_target_pairs={{0,1},{1,0},{2,3},{3,2},{4,5},{5,4},{6,7},{7,6},{8,9},{9,8},{10,11... | collective-permute-start | bytes 1474568 | tf_op jit(solution)/shard_map/ppermute | solution.py:31
  5.2 2.1 %hidden_0.1.refs_0_.refs_4_ = bf16[512,384]{1,0:T(8,128)(2,1)} custom-call(bf16[384,1792]{1,0:T(8,128)(2,1)} %refs_9_.1, bf16[384,1792]{1,0:T(8,128)(2,1)} %refs_10_.1), custom_call_target="tpu_custom_call" | custom-call | flops 1024 | bytes 1024 | tf_op jit(solution)/shard_map/hidden_0/pallas_call | solution.py:81
  8.8 3.2 %hidden_2.1.refs_4_.refs_8_ = bf16[768,384]{1,0:T(8,128)(2,1)} custom-call(bf16[384,1792]{1,0:T(8,128)(2,1)} %refs_9_.1, bf16[384,1792]{1,0:T(8,128)(2,1)} %refs_10_.1), custom_call_target="tpu_custom_call" | custom-call | flops 1024 | bytes 1024 | tf_op jit(solution)/shard_map/hidden_2/pallas_call | solution.py:81
  12.5 7.2 %collective-permute-done.2.refs_2_.refs_6_ = bf16[512,384]{1,0:T(8,128)(2,1)} collective-permute-done((bf16[512,384]{1,0:T(8,128)(2,1)}, bf16[512,384]{1,0:T(8,128)(2,1)}, u32[]{:S(2)}, u32[]{:S(2)}) %collective-permute-start.2) | collective-permute-done | bytes 393248 | tf_op jit(solution)/shard_map/ppermute | solution.py:31
  21.8 2.0 %hidden_5.1.refs_8_.refs_12_ = bf16[512,384]{1,0:T(8,128)(2,1)} custom-call(bf16[384,1792]{1,0:T(8,128)(2,1)} %refs_9_.1, bf16[384,1792]{1,0:T(8,128)(2,1)} %refs_10_.1), custom_call_target="tpu_custom_call" | custom-call | flops 1024 | bytes 1024 | tf_op jit(solution)/shard_map/hidden_5/pallas_call | solution.py:81
  27.0 12.0 %collective-permute-done.13.refs_10_.refs_14_ = bf16[512,384]{1,0:T(8,128)(2,1)} collective-permute-done((bf16[512,384]{1,0:T(8,128)(2,1)}, bf16[512,384]{1,0:T(8,128)(2,1)}, u32[]{:S(2)}, u32[]{:S(2)}) %collective-permute-start.13) | collective-permute-done | bytes 393248 | tf_op jit(solution)/shard_map/ppermute | solution.py:31
  46.8 6.2 %hidden_gram.1 = (f32[4,32,1536]{2,1,0:T(8,128)}, f32[4,32,1536]{2,1,0:T(8,128)}) custom-call(s32[1]{0:T(128)} %bitcast.inner_ref, s32[4]{0:T(128)} %xor_multiply_fusion.offs_ref.toks_ref, bf16[512,384]{1,0:T(8,128)(2,1)} %hidden_0.1.refs_0_.refs_4_, bf16[512,384]{1,0:T(8,128)(2,1)} %collective-permute-done.8.refs_1_.refs_5_, ...), custom_call_target="tpu_custom_call" | custom-call | flops 1024 | bytes 1024 | tf_op jit(solution)/shard_map/hidden_gram/pallas_call | solution.py:315
  54.5 2.5 %collective-permute-done.6.refs_0_ = bf16[384,640]{1,0:T(8,128)(2,1)} collective-permute-done((bf16[384,640]{1,0:T(8,128)(2,1)}, bf16[384,640]{1,0:T(8,128)(2,1)}, u32[]{:S(2)}, u32[]{:S(2)}) %collective-permute-start.6) | collective-permute-done | bytes 491552 | tf_op jit(solution)/shard_map/ppermute | solution.py:36
  57.0 3.4 %own_features.1.refs_5_ = bf16[4,384,640]{2,1,0:T(8,128)(2,1)} custom-call(s32[4]{0:T(128)} %and_select_fusion.at_ref, bf16[384,640]{1,0:T(8,128)(2,1)} %refs_0_.5, bf16[384,640]{1,0:T(8,128)(2,1)} %after.3.refs_1_, bf16[384,640]{1,0:T(8,128)(2,1)} %after.4.refs_13_.refs_2_, bf16[384,640]{1,0:T(8,128)(2,1)} %after.5.refs_3_, ...), custom_call_target="tpu_custom_call" | custom-call | flops 1024 | bytes 1024 | tf_op jit(solution)/shard_map/own_features/pallas_call | solution.py:107
  60.4 4.5 %all-to-all-start = ((bf16[4,384,640]{2,1,0:T(8,128)(2,1)}), bf16[4,384,640]{2,1,0:T(8,128)(2,1)}, u32[]{:S(2)}, u32[]{:S(2)}) async-start(bf16[4,384,640]{2,1,0:T(8,128)(2,1)} %own_features.1.refs_5_), calls=%async_computation | async-start | bytes 3932160 | tf_op jit(solution)/shard_map/all_to_all | solution.py:432
  69.2 3.8 %grad_gram.1 = (f32[4,32,1536]{2,1,0:T(8,128)}, f32[4,32,1536]{2,1,0:T(8,128)}) custom-call(s32[1]{0:T(128)} %bitcast.inner_ref, s32[4]{0:T(128)} %xor_multiply_fusion.offs_ref.toks_ref, bf16[384,640]{1,0:T(8,128)(2,1)} %refs_0_.5, bf16[384,640]{1,0:T(8,128)(2,1)} %copy-done.9, bf16[384,640]{1,0:T(8,128)(2,1)} %collective-permute-done.18.refs_4_.refs_2_, ...), custom_call_target="tpu_custom_call" | custom-call | flops 1024 | bytes 1024 | tf_op jit(solution)/shard_map/grad_gram/pallas_call | solution.py:315
  73.0 8.9 %collective-permute-done.15.refs_3_.refs_7_ = bf16[384,640]{1,0:T(8,128)(2,1)} collective-permute-done((bf16[384,640]{1,0:T(8,128)(2,1)S(1)}, bf16[384,640]{1,0:T(8,128)(2,1)}, u32[]{:S(2)}, u32[]{:S(2)}) %collective-permute-start.15) | collective-permute-done | bytes 491552 | tf_op jit(solution)/shard_map/ppermute | solution.py:36
  81.9 3.5 %other_features.1 = (bf16[384,640]{1,0:T(8,128)(2,1)}, bf16[384,640]{1,0:T(8,128)(2,1)}, bf16[384,640]{1,0:T(8,128)(2,1)}, bf16[384,640]{1,0:T(8,128)(2,1)}) custom-call(s32[4]{0:T(128)} %broadcast_xor_fusion.to_ref, bf16[384,640]{1,0:T(8,128)(2,1)} %copy-done.2, bf16[384,640]{1,0:T(8,128)(2,1)} %collective-permute-done.4.refs_1_.refs_5_, ...), custom_call_target="tpu_custom_call" | custom-call | flops 1024 | bytes 1024 | tf_op jit(solution)/shard_map/other_features/pallas_call | solution.py:135
  85.4 2.3 %hidden_pair.1.refs_11_ = f32[4,32,1536]{2,1,0:T(8,128)} custom-call(f32[4,32,1536]{2,1,0:T(8,128)} %get-tuple-element.19.kept_ref, f32[4,32,1536]{2,1,0:T(8,128)} %collective-permute-done.16.refs_0_, bf16[384,640]{1,0:T(8,128)(2,1)} %get-tuple-element.21.refs_1_.refs_0_), custom_call_target="tpu_custom_call" | custom-call | flops 1024 | bytes 1024 | tf_op jit(solution)/shard_map/hidden_pair/pallas_call | solution.py:338
  89.3 3.5 %all-to-all-start.1 = ((f32[4,32,1536]{2,1,0:T(8,128)}), f32[4,32,1536]{2,1,0:T(8,128)S(1)}, u32[]{:S(2)}, u32[]{:S(2)}) async-start(f32[4,32,1536]{2,1,0:T(8,128)} %hidden_pair.1.refs_11_), calls=%async_computation.1 | async-start | bytes 1572864 | tf_op jit(solution)/shard_map/all_to_all | solution.py:353
  96.7 15.9 %grads.1 = (bf16[384,1792]{1,0:T(8,128)(2,1)}, bf16[384,1792]{1,0:T(8,128)(2,1)}, f32[8,128]{1,0:T(8,128)}) custom-call(s32[8]{0:T(128)} %add.40.offs_ref, bf16[384,640]{1,0:T(8,128)(2,1)} %refs_0_.5, bf16[384,640]{1,0:T(8,128)(2,1)} %after.3.refs_1_, bf16[384,640]{1,0:T(8,128)(2,1)} %after.4.refs_13_.refs_2_, bf16[384,640]{1,0:T(8,128)(2,1)} %after.5.refs_3_, ...), custom_call_target="tpu_custom_call" | custom-call | flops 7046430720 | bytes 27787264 | tf_op jit(solution)/shard_map/grads/pallas_call | solution.py:174
  112.6 6.3 %collective-permute-done.22.refs_4_.refs_3_ = bf16[384,640]{1,0:T(8,128)(2,1)} collective-permute-done((bf16[384,640]{1,0:T(8,128)(2,1)}, bf16[384,640]{1,0:T(8,128)(2,1)}, u32[]{:S(2)}, u32[]{:S(2)}) %collective-permute-start.22) | collective-permute-done | bytes 491552 | tf_op jit(solution)/shard_map/ppermute | solution.py:31
  118.9 2.4 %grad_pair.1.refs_16_ = f32[4,32,1536]{2,1,0:T(8,128)} custom-call(f32[4,32,1536]{2,1,0:T(8,128)} %get-tuple-element.27.kept_ref, f32[4,32,1536]{2,1,0:T(8,128)} %collective-permute-done.23.refs_0_, f32[8,128]{1,0:T(8,128)} %get-tuple-element.28.refs_1_, bf16[384,640]{1,0:T(8,128)(2,1)} %collective-permute-done.20.refs_2_.refs_1_, ...), custom_call_target="tpu_custom_call" | custom-call | flops 1024 | bytes 1024 | tf_op jit(solution)/shard_map/grad_pair/pallas_call | solution.py:338
  121.3 5.1 %all-to-all-start.2 = ((f32[4,32,1536]{2,1,0:T(8,128)}), f32[4,32,1536]{2,1,0:T(8,128)}, u32[]{:S(2)}, u32[]{:S(2)}) async-start(f32[4,32,1536]{2,1,0:T(8,128)} %grad_pair.1.refs_16_), calls=%async_computation.2 | async-start | bytes 1572864 | tf_op jit(solution)/shard_map/all_to_all | solution.py:353
  126.3 15.4 %wgrad.1 = (bf16[1792,1280]{1,0:T(8,128)(2,1)}, f32[8,128]{1,0:T(8,128)}) custom-call(s32[2]{0:T(128)} %copy-done.10, s32[4]{0:T(128)} %xor_multiply_fusion.offs_ref.toks_ref, bf16[4,384,640]{2,1,0:T(8,128)(2,1)} %all-to-all-done.own_ref, bf16[384,640]{1,0:T(8,128)(2,1)} %get-tuple-element.21.refs_1_.refs_0_, ...), custom_call_target="tpu_custom_call" | custom-call | flops 7046430720 | bytes 14024704 | tf_op jit(solution)/shard_map/wgrad/pallas_call | solution.py:242
  141.8 5.2 %all-to-all-done.2.grad_ref = f32[4,32,1536]{2,1,0:T(8,128)} async-done(((f32[4,32,1536]{2,1,0:T(8,128)}), f32[4,32,1536]{2,1,0:T(8,128)}, u32[]{:S(2)}, u32[]{:S(2)}) %all-to-all-start.2) | async-done | bytes 786464 | tf_op jit(solution)/shard_map/all_to_all | solution.py:353
  146.9 2.1 %score_line.1 = f32[32,128]{1,0:T(8,128)} custom-call(s32[3]{0:T(128)} %assign_ref.1, f32[4,32,1536]{2,1,0:T(8,128)} %copy-done.1, f32[4,32,1536]{2,1,0:T(8,128)} %all-to-all-done.2.grad_ref, f32[8,128]{1,0:T(8,128)} %get-tuple-element.30.refs_0_), custom_call_target="tpu_custom_call" | custom-call | flops 1024 | bytes 1024 | tf_op jit(solution)/shard_map/score_line/pallas_call | solution.py:376
  149.1 2.5 %all-to-all-start.3 = ((f32[32,1,128]{2,1,0:T(1,128)}), f32[32,1,128]{2,1,0:T(1,128)S(1)}, u32[]{:S(2)}, u32[]{:S(2)}) async-start(f32[32,1,128]{2,1,0:T(1,128)} %bitcast.13), calls=%async_computation.3 | async-start | bytes 32768 | tf_op jit(solution)/shard_map/all_to_all | solution.py:452
  151.6 7.1 %all-to-all-done.3 = f32[32,1,128]{2,1,0:T(1,128)S(1)} async-done(((f32[32,1,128]{2,1,0:T(1,128)}), f32[32,1,128]{2,1,0:T(1,128)S(1)}, u32[]{:S(2)}, u32[]{:S(2)}) %all-to-all-start.3) | async-done | bytes 16416 | tf_op jit(solution)/shard_map/all_to_all | solution.py:452
  (82 shorter events, 29.4 us)
Async XLA Ops:
  0.6 19.0 %collective-permute-start.1 = (bf16[384,640]{1,0:T(8,128)(2,1)}, bf16[384,640]{1,0:T(8,128)(2,1)S(1)}, u32[]{:S(2)}, u32[]{:S(2)}) collective-permute-start(bf16[384,640]{1,0:T(8,128)(2,1)} %refs_0_.5), channel_id=1, source_target_pairs={{0,1},{1,0},{2,3},{3,2},{4,5},{5,4},{6,7},{7,6},{8,9},{9,8},{10,11... | collective-permute-start | bytes 1474568 | tf_op jit(solution)/shard_map/ppermute | solution.py:31
  3.6 16.0 %collective-permute-start = (bf16[384,640]{1,0:T(8,128)(2,1)}, bf16[384,640]{1,0:T(8,128)(2,1)S(1)}, u32[]{:S(2)}, u32[]{:S(2)}) collective-permute-start(bf16[384,640]{1,0:T(8,128)(2,1)} %refs_0_.5), channel_id=1, source_target_pairs={{0,2},{1,3},{2,4},{3,5},{4,6},{5,7},{6,0},{7,1},{8,10},{9,11},{10,... | collective-permute-start | bytes 1474568 | tf_op jit(solution)/shard_map/ppermute | solution.py:36
  7.3 12.4 %collective-permute-start.2 = (bf16[512,384]{1,0:T(8,128)(2,1)}, bf16[512,384]{1,0:T(8,128)(2,1)}, u32[]{:S(2)}, u32[]{:S(2)}) collective-permute-start(bf16[512,384]{1,0:T(8,128)(2,1)} %hidden_0.1.refs_0_.refs_4_), channel_id=1, source_target_pairs={{0,16},{8,24},{16,0},{24,8},{1,17},{9,25},{17,1},{25,9},{2,18},{10... | collective-permute-start | bytes 1179656 | tf_op jit(solution)/shard_map/ppermute | solution.py:31
  12.0 27.0 %collective-permute-start.5 = (bf16[768,384]{1,0:T(8,128)(2,1)}, bf16[768,384]{1,0:T(8,128)(2,1)}, u32[]{:S(2)}, u32[]{:S(2)}) collective-permute-start(bf16[768,384]{1,0:T(8,128)(2,1)} %hidden_2.1.refs_4_.refs_8_), channel_id=1, source_target_pairs={{0,16},{8,24},{16,0},{24,8},{1,17},{9,25},{17,1},{25,9},{2,18},{10... | collective-permute-start | bytes 1769480 | tf_op jit(solution)/shard_map/ppermute | solution.py:31
  21.3 18.2 %collective-permute-start.4 = (bf16[384,640]{1,0:T(8,128)(2,1)}, bf16[384,640]{1,0:T(8,128)(2,1)}, u32[]{:S(2)}, u32[]{:S(2)}) collective-permute-start(bf16[384,640]{1,0:T(8,128)(2,1)} %after.3.refs_1_), channel_id=1, source_target_pairs={{0,1},{1,0},{2,3},{3,2},{4,5},{5,4},{6,7},{7,6},{8,9},{9,8},{10,11... | collective-permute-start | bytes 1474568 | tf_op jit(solution)/shard_map/ppermute | solution.py:31
  23.9 15.1 %collective-permute-start.13 = (bf16[512,384]{1,0:T(8,128)(2,1)}, bf16[512,384]{1,0:T(8,128)(2,1)}, u32[]{:S(2)}, u32[]{:S(2)}) collective-permute-start(bf16[512,384]{1,0:T(8,128)(2,1)} %hidden_5.1.refs_8_.refs_12_), channel_id=1, source_target_pairs={{0,16},{8,24},{16,0},{24,8},{1,17},{9,25},{17,1},{25,9},{2,18},{10... | collective-permute-start | bytes 1179656 | tf_op jit(solution)/shard_map/ppermute | solution.py:31
  25.4 14.1 %collective-permute-start.3 = (bf16[384,640]{1,0:T(8,128)(2,1)S(1)}, bf16[384,640]{1,0:T(8,128)(2,1)S(1)}, u32[]{:S(2)}, u32[]{:S(2)}) collective-permute-start(bf16[384,640]{1,0:T(8,128)(2,1)S(1)} %copy-done.4), channel_id=1, source_target_pairs={{0,2},{1,3},{2,4},{3,5},{4,6},{5,7},{6,0},{7,1},{8,10},{9,11},{10,... | collective-permute-start | bytes 1474568 | tf_op jit(solution)/shard_map/ppermute | solution.py:36
  27.0 16.2 %collective-permute-start.10 = (bf16[768,384]{1,0:T(8,128)(2,1)}, bf16[768,384]{1,0:T(8,128)(2,1)}, u32[]{:S(2)}, u32[]{:S(2)}) collective-permute-start(bf16[768,384]{1,0:T(8,128)(2,1)} %hidden_2.1.refs_4_.refs_8_), channel_id=1, source_target_pairs={{0,8},{8,0},{16,24},{24,16},{1,9},{9,1},{17,25},{25,17},{2,10},{10... | collective-permute-start | bytes 1769480 | tf_op jit(solution)/shard_map/ppermute | solution.py:31
  39.5 5.2 %collective-permute-start.14 = (bf16[512,384]{1,0:T(8,128)(2,1)}, bf16[512,384]{1,0:T(8,128)(2,1)}, u32[]{:S(2)}, u32[]{:S(2)}) collective-permute-start(bf16[512,384]{1,0:T(8,128)(2,1)} %collective-permute-done.13.refs_10_.refs_14_), channel_id=1, source_target_pairs={{0,8},{8,0},{16,24},{24,16},{1,9},{9,1},{17,25},{25,17},{2,10},{10... | collective-permute-start | bytes 1179656 | tf_op jit(solution)/shard_map/ppermute | solution.py:31
  39.5 7.2 %collective-permute-start.11 = (bf16[768,384]{1,0:T(8,128)(2,1)}, bf16[768,384]{1,0:T(8,128)(2,1)}, u32[]{:S(2)}, u32[]{:S(2)}) collective-permute-start(bf16[768,384]{1,0:T(8,128)(2,1)} %collective-permute-done.5.refs_2_.refs_6_.refs_10_), channel_id=1, source_target_pairs={{0,8},{8,0},{16,24},{24,16},{1,9},{9,1},{17,25},{25,17},{2,10},{10... | collective-permute-start | bytes 1769480 | tf_op jit(solution)/shard_map/ppermute | solution.py:31
  41.0 13.5 %collective-permute-start.7 = (bf16[384,640]{1,0:T(8,128)(2,1)}, bf16[384,640]{1,0:T(8,128)(2,1)S(1)}, u32[]{:S(2)}, u32[]{:S(2)}) collective-permute-start(bf16[384,640]{1,0:T(8,128)(2,1)} %after.4.refs_13_.refs_2_), channel_id=1, source_target_pairs={{0,1},{1,0},{2,3},{3,2},{4,5},{5,4},{6,7},{7,6},{8,9},{9,8},{10,11... | collective-permute-start | bytes 1474568 | tf_op jit(solution)/shard_map/ppermute | solution.py:31
  41.6 15.4 %collective-permute-start.6 = (bf16[384,640]{1,0:T(8,128)(2,1)}, bf16[384,640]{1,0:T(8,128)(2,1)}, u32[]{:S(2)}, u32[]{:S(2)}) collective-permute-start(bf16[384,640]{1,0:T(8,128)(2,1)} %after.4.refs_13_.refs_2_), channel_id=1, source_target_pairs={{0,2},{1,3},{2,4},{3,5},{4,6},{5,7},{6,0},{7,1},{8,10},{9,11},{10,... | collective-permute-start | bytes 1474568 | tf_op jit(solution)/shard_map/ppermute | solution.py:36
  43.2 13.8 %collective-permute-start.18 = (bf16[384,640]{1,0:T(8,128)(2,1)S(1)}, bf16[384,640]{1,0:T(8,128)(2,1)}, u32[]{:S(2)}, u32[]{:S(2)}) collective-permute-start(bf16[384,640]{1,0:T(8,128)(2,1)S(1)} %copy-done.5), channel_id=1, source_target_pairs={{0,16},{8,24},{16,0},{24,8},{1,17},{9,25},{17,1},{25,9},{2,18},{10... | collective-permute-start | bytes 1474568 | tf_op jit(solution)/shard_map/ppermute | solution.py:31
  60.4 28.9 %all-to-all-start = ((bf16[4,384,640]{2,1,0:T(8,128)(2,1)}), bf16[4,384,640]{2,1,0:T(8,128)(2,1)}, u32[]{:S(2)}, u32[]{:S(2)}) async-start(bf16[4,384,640]{2,1,0:T(8,128)(2,1)} %own_features.1.refs_5_), calls=%async_computation | async-start | bytes 3932160 | tf_op jit(solution)/shard_map/all_to_all | solution.py:432
  65.0 20.4 %collective-permute-start.16 = (f32[4,32,1536]{2,1,0:T(8,128)}, f32[4,32,1536]{2,1,0:T(8,128)}, u32[]{:S(2)}, u32[]{:S(2)}) collective-permute-start(f32[4,32,1536]{2,1,0:T(8,128)} %get-tuple-element.18.refs_2_), channel_id=1, source_target_pairs={{0,1},{1,0},{2,3},{3,2},{4,5},{5,4},{6,7},{7,6},{8,9},{9,8},{10,11... | collective-permute-start | bytes 2359304 | tf_op jit(solution)/shard_map/ppermute | solution.py:31
  66.4 2.8 %collective-permute-start.19 = (bf16[384,640]{1,0:T(8,128)(2,1)}, bf16[384,640]{1,0:T(8,128)(2,1)}, u32[]{:S(2)}, u32[]{:S(2)}) collective-permute-start(bf16[384,640]{1,0:T(8,128)(2,1)} %collective-permute-done.18.refs_4_.refs_2_), channel_id=1, source_target_pairs={{0,8},{8,0},{16,24},{24,16},{1,9},{9,1},{17,25},{25,17},{2,10},{10... | collective-permute-start | bytes 1474568 | tf_op jit(solution)/shard_map/ppermute | solution.py:31
  66.8 15.1 %collective-permute-start.15 = (bf16[384,640]{1,0:T(8,128)(2,1)S(1)}, bf16[384,640]{1,0:T(8,128)(2,1)}, u32[]{:S(2)}, u32[]{:S(2)}) collective-permute-start(bf16[384,640]{1,0:T(8,128)(2,1)S(1)} %copy-done.8), channel_id=1, source_target_pairs={{0,2},{1,3},{2,4},{3,5},{4,6},{5,7},{6,0},{7,1},{8,10},{9,11},{10,... | collective-permute-start | bytes 1474568 | tf_op jit(solution)/shard_map/ppermute | solution.py:36
  89.3 31.9 %all-to-all-start.1 = ((f32[4,32,1536]{2,1,0:T(8,128)}), f32[4,32,1536]{2,1,0:T(8,128)S(1)}, u32[]{:S(2)}, u32[]{:S(2)}) async-start(f32[4,32,1536]{2,1,0:T(8,128)} %hidden_pair.1.refs_11_), calls=%async_computation.1 | async-start | bytes 1572864 | tf_op jit(solution)/shard_map/all_to_all | solution.py:353
  92.9 19.7 %collective-permute-start.23 = (f32[4,32,1536]{2,1,0:T(8,128)}, f32[4,32,1536]{2,1,0:T(8,128)}, u32[]{:S(2)}, u32[]{:S(2)}) collective-permute-start(f32[4,32,1536]{2,1,0:T(8,128)} %get-tuple-element.20.refs_4_), channel_id=1, source_target_pairs={{0,1},{1,0},{2,3},{3,2},{4,5},{5,4},{6,7},{7,6},{8,9},{9,8},{10,11... | collective-permute-start | bytes 2359304 | tf_op jit(solution)/shard_map/ppermute | solution.py:31
  94.8 17.8 %collective-permute-start.20 = (bf16[384,640]{1,0:T(8,128)(2,1)}, bf16[384,640]{1,0:T(8,128)(2,1)}, u32[]{:S(2)}, u32[]{:S(2)}) collective-permute-start(bf16[384,640]{1,0:T(8,128)(2,1)} %get-tuple-element.24), channel_id=1, source_target_pairs={{0,8},{8,0},{16,24},{24,16},{1,9},{9,1},{17,25},{25,17},{2,10},{10... | collective-permute-start | bytes 1474568 | tf_op jit(solution)/shard_map/ppermute | solution.py:31
  94.8 17.8 %collective-permute-start.21 = (bf16[384,640]{1,0:T(8,128)(2,1)}, bf16[384,640]{1,0:T(8,128)(2,1)}, u32[]{:S(2)}, u32[]{:S(2)}) collective-permute-start(bf16[384,640]{1,0:T(8,128)(2,1)} %get-tuple-element.25), channel_id=1, source_target_pairs={{0,16},{8,24},{16,0},{24,8},{1,17},{9,25},{17,1},{25,9},{2,18},{10... | collective-permute-start | bytes 1474568 | tf_op jit(solution)/shard_map/ppermute | solution.py:31
  95.2 23.7 %collective-permute-start.22 = (bf16[384,640]{1,0:T(8,128)(2,1)}, bf16[384,640]{1,0:T(8,128)(2,1)}, u32[]{:S(2)}, u32[]{:S(2)}) collective-permute-start(bf16[384,640]{1,0:T(8,128)(2,1)} %get-tuple-element.26), channel_id=1, source_target_pairs={{0,24},{8,16},{16,8},{24,0},{1,25},{9,17},{17,9},{25,1},{2,26},{10... | collective-permute-start | bytes 1474568 | tf_op jit(solution)/shard_map/ppermute | solution.py:31
  121.3 25.6 %all-to-all-start.2 = ((f32[4,32,1536]{2,1,0:T(8,128)}), f32[4,32,1536]{2,1,0:T(8,128)}, u32[]{:S(2)}, u32[]{:S(2)}) async-start(f32[4,32,1536]{2,1,0:T(8,128)} %grad_pair.1.refs_16_), calls=%async_computation.2 | async-start | bytes 1572864 | tf_op jit(solution)/shard_map/all_to_all | solution.py:353
  149.1 9.6 %all-to-all-start.3 = ((f32[32,1,128]{2,1,0:T(1,128)}), f32[32,1,128]{2,1,0:T(1,128)S(1)}, u32[]{:S(2)}, u32[]{:S(2)}) async-start(f32[32,1,128]{2,1,0:T(1,128)} %bitcast.13), calls=%async_computation.3 | async-start | bytes 32768 | tf_op jit(solution)/shard_map/all_to_all | solution.py:452
  (15 other events, 74.4 us)

commit v14 on v13

--- a/solution.py
+++ b/solution.py
@@ -257,7 +257,7 @@
         ],
         compiler_params=params(),
         cost_estimate=pl.CostEstimate(
-            flops=4 * total * units * width,
+            flops=16 * total * units * width,
             bytes_accessed=2 * (total * (units + 2 * width) + 2 * units * width),
             transcendentals=0,
         ),
@@ -444,7 +444,7 @@
     grad_gate, grad_up, done = grads(
         places, [*ring, *others], down_weight, gate_act, up_act, [hid_pair]
     )
-    grad_pair = pair_sum(grad_kept, grad_came, [done, *other_cols[1:]], "grad_pair")
+    grad_pair = pair_sum(grad_kept, grad_came, [done], "grad_pair")
     grad_sums = spread(grad_pair)
     weight_grad, done = wgrad(offs, tok_offs, own_cols, other_cols, hids, [grad_pair])
 

time: 161 us -> 151 us (0.938)
  waiting for transfers between devices: 54.2 us -> 45.8 us
  starting transfers between devices: 36.2 us -> 34 us
    ppermute x20, waiting for transfers between devices: 28.9 us -> 19.7 us  [swap(): return lax.ppermute(x, axis, [(s, s ^ k) for s in range(n)])]
    ppermute x20, starting transfers between devices: 15 us -> 11.7 us  [swap(): return lax.ppermute(x, axis, [(s, s ^ k) for s in range(n)])]
    unnamed x23 -> x21, local copies, waits for them, and re-layouts: 3.49 us -> 3.91 us
  transfers between devices with their start and end apart: 28 -> 28, of which waited for: 12 -> 15; matrix products, arithmetic and copies ran while one was open for 1% -> 2% of each run, Pallas kernels for 35% -> 38%
where the time goes in v14:
time: 151 us; the launch traced here: 150 us
  Pallas kernels  62.3 us (41%)
  waiting for transfers between devices  45.8 us (30%)
  starting transfers between devices  34 us (23%)
  local copies, waits for them, and re-layouts  4.73 us (3%)
  other arithmetic  2.34 us (2%)
    ppermute x20, waiting for transfers between devices, swap(): return lax.ppermute(x, axis, [(s, s ^ k) for s in range(n)])  19.7 us
    pallas_call x1, Pallas kernels, grads(): pl.pallas_call(functools.partial(grads_body, n), grid_spec=pltpu.Prefetch...  15.9 us
    pallas_call x1, Pallas kernels, wgrad(): pl.pallas_call(functools.partial(wgrad_body, n, tuple(starts)), in_specs=...  15.4 us
    ppermute x4, waiting for transfers between devices, shift(): return lax.ppermute(x, axis, [(s, (s + k) % n) for s in range(n)])  12.2 us
    ppermute x20, starting transfers between devices, swap(): return lax.ppermute(x, axis, [(s, s ^ k) for s in range(n)])  11.7 us
    pallas_call x2, Pallas kernels, gram(): pl.pallas_call(functools.partial(body, len(toks), cuts), grid=(1,), in_sp...  9.96 us
    all_to_all x2, starting transfers between devices, spread(): lax.all_to_all(pair, 'fsdp', split_axis=0, concat_axis=0, axis_index_grou...  8.27 us
    pallas_call x3, Pallas kernels, hidden_units(): pl.pallas_call(hidden_body, grid=(count,), in_specs=[cols, cols], out_spe...  7.26 us
  transfers between devices with their start and end apart: 28, of which 15 were waited for; matrix products, arithmetic and copies ran while one was open for 2% of the time, Pallas kernels for 38%

profile of v14, /device:TPU:0, one launch (start us, length us, event | category | flops | bytes accessed | tf_op | source)
XLA Modules:
  0.0 150.0 jit_solution(15614435174364062500)
XLA Ops:
  0.6 3.1 %collective-permute-start = (bf16[384,640]{1,0:T(8,128)(2,1)}, bf16[384,640]{1,0:T(8,128)(2,1)S(1)}, u32[]{:S(2)}, u32[]{:S(2)}) collective-permute-start(bf16[384,640]{1,0:T(8,128)(2,1)} %refs_0_.5), channel_id=1, source_target_pairs={{0,2},{1,3},{2,4},{3,5},{4,6},{5,7},{6,0},{7,1},{8,10},{9,11},{10,... | collective-permute-start | bytes 1474568 | tf_op jit(solution)/shard_map/ppermute | solution.py:36
  5.2 2.1 %hidden_0.1.refs_0_.refs_4_ = bf16[512,384]{1,0:T(8,128)(2,1)} custom-call(bf16[384,1792]{1,0:T(8,128)(2,1)} %refs_9_.1, bf16[384,1792]{1,0:T(8,128)(2,1)} %refs_10_.1), custom_call_target="tpu_custom_call" | custom-call | flops 1024 | bytes 1024 | tf_op jit(solution)/shard_map/hidden_0/pallas_call | solution.py:81
  8.8 3.2 %hidden_2.1.refs_4_.refs_8_ = bf16[768,384]{1,0:T(8,128)(2,1)} custom-call(bf16[384,1792]{1,0:T(8,128)(2,1)} %refs_9_.1, bf16[384,1792]{1,0:T(8,128)(2,1)} %refs_10_.1), custom_call_target="tpu_custom_call" | custom-call | flops 1024 | bytes 1024 | tf_op jit(solution)/shard_map/hidden_2/pallas_call | solution.py:81
  12.5 7.2 %collective-permute-done.2.refs_2_.refs_6_ = bf16[512,384]{1,0:T(8,128)(2,1)} collective-permute-done((bf16[512,384]{1,0:T(8,128)(2,1)}, bf16[512,384]{1,0:T(8,128)(2,1)}, u32[]{:S(2)}, u32[]{:S(2)}) %collective-permute-start.2) | collective-permute-done | bytes 393248 | tf_op jit(solution)/shard_map/ppermute | solution.py:31
  23.6 2.0 %hidden_5.1.refs_8_.refs_12_ = bf16[512,384]{1,0:T(8,128)(2,1)} custom-call(bf16[384,1792]{1,0:T(8,128)(2,1)} %refs_9_.1, bf16[384,1792]{1,0:T(8,128)(2,1)} %refs_10_.1), custom_call_target="tpu_custom_call" | custom-call | flops 1024 | bytes 1024 | tf_op jit(solution)/shard_map/hidden_5/pallas_call | solution.py:81
  25.9 4.6 %collective-permute-done.5.refs_2_.refs_6_.refs_10_ = bf16[768,384]{1,0:T(8,128)(2,1)} collective-permute-done((bf16[768,384]{1,0:T(8,128)(2,1)}, bf16[768,384]{1,0:T(8,128)(2,1)}, u32[]{:S(2)}, u32[]{:S(2)}) %collective-permute-start.5) | collective-permute-done | bytes 589856 | tf_op jit(solution)/shard_map/ppermute | solution.py:31
  33.2 3.6 %collective-permute-done.4.refs_1_.refs_5_ = bf16[384,640]{1,0:T(8,128)(2,1)} collective-permute-done((bf16[384,640]{1,0:T(8,128)(2,1)}, bf16[384,640]{1,0:T(8,128)(2,1)}, u32[]{:S(2)}, u32[]{:S(2)}) %collective-permute-start.4) | collective-permute-done | bytes 491552 | tf_op jit(solution)/shard_map/ppermute | solution.py:31
  44.3 6.2 %hidden_gram.1 = (f32[4,32,1536]{2,1,0:T(8,128)}, f32[4,32,1536]{2,1,0:T(8,128)}) custom-call(s32[1]{0:T(128)} %bitcast.inner_ref, s32[4]{0:T(128)} %xor_multiply_fusion.offs_ref.toks_ref, bf16[512,384]{1,0:T(8,128)(2,1)} %hidden_0.1.refs_0_.refs_4_, bf16[512,384]{1,0:T(8,128)(2,1)} %collective-permute-done.8.refs_1_.refs_5_, ...), custom_call_target="tpu_custom_call" | custom-call | flops 1024 | bytes 1024 | tf_op jit(solution)/shard_map/hidden_gram/pallas_call | solution.py:315
  50.5 2.1 %collective-permute-done.6.refs_0_ = bf16[384,640]{1,0:T(8,128)(2,1)} collective-permute-done((bf16[384,640]{1,0:T(8,128)(2,1)}, bf16[384,640]{1,0:T(8,128)(2,1)}, u32[]{:S(2)}, u32[]{:S(2)}) %collective-permute-start.6) | collective-permute-done | bytes 491552 | tf_op jit(solution)/shard_map/ppermute | solution.py:36
  53.4 3.4 %own_features.1.refs_5_ = bf16[4,384,640]{2,1,0:T(8,128)(2,1)} custom-call(s32[4]{0:T(128)} %and_select_fusion.at_ref, bf16[384,640]{1,0:T(8,128)(2,1)} %refs_0_.5, bf16[384,640]{1,0:T(8,128)(2,1)} %after.3.refs_1_, bf16[384,640]{1,0:T(8,128)(2,1)} %after.4.refs_13_.refs_2_, bf16[384,640]{1,0:T(8,128)(2,1)} %after.5.refs_3_, ...), custom_call_target="tpu_custom_call" | custom-call | flops 1024 | bytes 1024 | tf_op jit(solution)/shard_map/own_features/pallas_call | solution.py:107
  56.8 4.6 %all-to-all-start = ((bf16[4,384,640]{2,1,0:T(8,128)(2,1)}), bf16[4,384,640]{2,1,0:T(8,128)(2,1)}, u32[]{:S(2)}, u32[]{:S(2)}) async-start(bf16[4,384,640]{2,1,0:T(8,128)(2,1)} %own_features.1.refs_5_), calls=%async_computation | async-start | bytes 3932160 | tf_op jit(solution)/shard_map/all_to_all | solution.py:432
  65.0 3.8 %grad_gram.1 = (f32[4,32,1536]{2,1,0:T(8,128)}, f32[4,32,1536]{2,1,0:T(8,128)}) custom-call(s32[1]{0:T(128)} %bitcast.inner_ref, s32[4]{0:T(128)} %xor_multiply_fusion.offs_ref.toks_ref, bf16[384,640]{1,0:T(8,128)(2,1)} %refs_0_.5, bf16[384,640]{1,0:T(8,128)(2,1)} %copy-done.8, bf16[384,640]{1,0:T(8,128)(2,1)} %collective-permute-done.18.refs_4_.refs_2_, ...), custom_call_target="tpu_custom_call" | custom-call | flops 1024 | bytes 1024 | tf_op jit(solution)/shard_map/grad_gram/pallas_call | solution.py:315
  68.8 8.9 %collective-permute-done.15.refs_3_.refs_7_ = bf16[384,640]{1,0:T(8,128)(2,1)} collective-permute-done((bf16[384,640]{1,0:T(8,128)(2,1)S(1)}, bf16[384,640]{1,0:T(8,128)(2,1)}, u32[]{:S(2)}, u32[]{:S(2)}) %collective-permute-start.15) | collective-permute-done | bytes 491552 | tf_op jit(solution)/shard_map/ppermute | solution.py:36
  77.7 3.5 %other_features.1 = (bf16[384,640]{1,0:T(8,128)(2,1)}, bf16[384,640]{1,0:T(8,128)(2,1)}, bf16[384,640]{1,0:T(8,128)(2,1)}, bf16[384,640]{1,0:T(8,128)(2,1)}) custom-call(s32[4]{0:T(128)} %broadcast_xor_fusion.to_ref, bf16[384,640]{1,0:T(8,128)(2,1)} %copy-done.2, bf16[384,640]{1,0:T(8,128)(2,1)} %collective-permute-done.4.refs_1_.refs_5_, ...), custom_call_target="tpu_custom_call" | custom-call | flops 1024 | bytes 1024 | tf_op jit(solution)/shard_map/other_features/pallas_call | solution.py:135
  81.6 2.3 %hidden_pair.1.refs_11_ = f32[4,32,1536]{2,1,0:T(8,128)} custom-call(f32[4,32,1536]{2,1,0:T(8,128)} %get-tuple-element.19.kept_ref, f32[4,32,1536]{2,1,0:T(8,128)} %collective-permute-done.16.refs_0_, bf16[384,640]{1,0:T(8,128)(2,1)} %get-tuple-element.21.refs_1_.refs_0_), custom_call_target="tpu_custom_call" | custom-call | flops 1024 | bytes 1024 | tf_op jit(solution)/shard_map/hidden_pair/pallas_call | solution.py:338
  85.8 3.5 %all-to-all-start.1 = ((f32[4,32,1536]{2,1,0:T(8,128)}), f32[4,32,1536]{2,1,0:T(8,128)S(1)}, u32[]{:S(2)}, u32[]{:S(2)}) async-start(f32[4,32,1536]{2,1,0:T(8,128)} %hidden_pair.1.refs_11_), calls=%async_computation.1 | async-start | bytes 1572864 | tf_op jit(solution)/shard_map/all_to_all | solution.py:353
  92.4 15.9 %grads.1 = (bf16[384,1792]{1,0:T(8,128)(2,1)}, bf16[384,1792]{1,0:T(8,128)(2,1)}, f32[8,128]{1,0:T(8,128)}) custom-call(s32[8]{0:T(128)} %add.40.offs_ref, bf16[384,640]{1,0:T(8,128)(2,1)} %refs_0_.5, bf16[384,640]{1,0:T(8,128)(2,1)} %after.3.refs_1_, bf16[384,640]{1,0:T(8,128)(2,1)} %after.4.refs_13_.refs_2_, bf16[384,640]{1,0:T(8,128)(2,1)} %after.5.refs_3_, ...), custom_call_target="tpu_custom_call" | custom-call | flops 7046430720 | bytes 27787264 | tf_op jit(solution)/shard_map/grads/pallas_call | solution.py:174
  108.8 2.3 %grad_pair.1.refs_16_ = f32[4,32,1536]{2,1,0:T(8,128)} custom-call(f32[4,32,1536]{2,1,0:T(8,128)} %get-tuple-element.27.kept_ref, f32[4,32,1536]{2,1,0:T(8,128)} %collective-permute-done.23.refs_0_, f32[8,128]{1,0:T(8,128)} %get-tuple-element.28.refs_1_), custom_call_target="tpu_custom_call" | custom-call | flops 1024 | bytes 1024 | tf_op jit(solution)/shard_map/grad_pair/pallas_call | solution.py:338
  111.1 4.8 %all-to-all-start.2 = ((f32[4,32,1536]{2,1,0:T(8,128)}), f32[4,32,1536]{2,1,0:T(8,128)}, u32[]{:S(2)}, u32[]{:S(2)}) async-start(f32[4,32,1536]{2,1,0:T(8,128)} %grad_pair.1.refs_16_), calls=%async_computation.2 | async-start | bytes 1572864 | tf_op jit(solution)/shard_map/all_to_all | solution.py:353
  115.9 15.4 %wgrad.1 = (bf16[1792,1280]{1,0:T(8,128)(2,1)}, f32[8,128]{1,0:T(8,128)}) custom-call(s32[2]{0:T(128)} %copy-done.9, s32[4]{0:T(128)} %xor_multiply_fusion.offs_ref.toks_ref, bf16[4,384,640]{2,1,0:T(8,128)(2,1)} %all-to-all-done.own_ref, bf16[384,640]{1,0:T(8,128)(2,1)} %get-tuple-element.21.refs_1_.refs_0_, ...), custom_call_target="tpu_custom_call" | custom-call | flops 28185722880 | bytes 14024704 | tf_op jit(solution)/shard_map/wgrad/pallas_call | solution.py:242
  131.4 5.0 %all-to-all-done.2.grad_ref = f32[4,32,1536]{2,1,0:T(8,128)} async-done(((f32[4,32,1536]{2,1,0:T(8,128)}), f32[4,32,1536]{2,1,0:T(8,128)}, u32[]{:S(2)}, u32[]{:S(2)}) %all-to-all-start.2) | async-done | bytes 786464 | tf_op jit(solution)/shard_map/all_to_all | solution.py:353
  136.4 2.2 %score_line.1 = f32[32,128]{1,0:T(8,128)} custom-call(s32[3]{0:T(128)} %assign_ref.1, f32[4,32,1536]{2,1,0:T(8,128)} %copy-done.1, f32[4,32,1536]{2,1,0:T(8,128)} %all-to-all-done.2.grad_ref, f32[8,128]{1,0:T(8,128)} %get-tuple-element.30.refs_0_), custom_call_target="tpu_custom_call" | custom-call | flops 1024 | bytes 1024 | tf_op jit(solution)/shard_map/score_line/pallas_call | solution.py:376
  138.6 2.8 %all-to-all-start.3 = ((f32[32,1,128]{2,1,0:T(1,128)}), f32[32,1,128]{2,1,0:T(1,128)S(1)}, u32[]{:S(2)}, u32[]{:S(2)}) async-start(f32[32,1,128]{2,1,0:T(1,128)} %bitcast.13), calls=%async_computation.3 | async-start | bytes 32768 | tf_op jit(solution)/shard_map/all_to_all | solution.py:452
  141.3 7.1 %all-to-all-done.3 = f32[32,1,128]{2,1,0:T(1,128)S(1)} async-done(((f32[32,1,128]{2,1,0:T(1,128)}), f32[32,1,128]{2,1,0:T(1,128)S(1)}, u32[]{:S(2)}, u32[]{:S(2)}) %all-to-all-start.3) | async-done | bytes 16416 | tf_op jit(solution)/shard_map/all_to_all | solution.py:452
  (80 shorter events, 29.8 us)
Async XLA Ops:
  0.6 19.0 %collective-permute-start = (bf16[384,640]{1,0:T(8,128)(2,1)}, bf16[384,640]{1,0:T(8,128)(2,1)S(1)}, u32[]{:S(2)}, u32[]{:S(2)}) collective-permute-start(bf16[384,640]{1,0:T(8,128)(2,1)} %refs_0_.5), channel_id=1, source_target_pairs={{0,2},{1,3},{2,4},{3,5},{4,6},{5,7},{6,0},{7,1},{8,10},{9,11},{10,... | collective-permute-start | bytes 1474568 | tf_op jit(solution)/shard_map/ppermute | solution.py:36
  3.7 15.9 %collective-permute-start.1 = (bf16[384,640]{1,0:T(8,128)(2,1)}, bf16[384,640]{1,0:T(8,128)(2,1)S(1)}, u32[]{:S(2)}, u32[]{:S(2)}) collective-permute-start(bf16[384,640]{1,0:T(8,128)(2,1)} %refs_0_.5), channel_id=1, source_target_pairs={{0,1},{1,0},{2,3},{3,2},{4,5},{5,4},{6,7},{7,6},{8,9},{9,8},{10,11... | collective-permute-start | bytes 1474568 | tf_op jit(solution)/shard_map/ppermute | solution.py:31
  7.3 12.4 %collective-permute-start.2 = (bf16[512,384]{1,0:T(8,128)(2,1)}, bf16[512,384]{1,0:T(8,128)(2,1)}, u32[]{:S(2)}, u32[]{:S(2)}) collective-permute-start(bf16[512,384]{1,0:T(8,128)(2,1)} %hidden_0.1.refs_0_.refs_4_), channel_id=1, source_target_pairs={{0,16},{8,24},{16,0},{24,8},{1,17},{9,25},{17,1},{25,9},{2,18},{10... | collective-permute-start | bytes 1179656 | tf_op jit(solution)/shard_map/ppermute | solution.py:31
  11.9 18.6 %collective-permute-start.5 = (bf16[768,384]{1,0:T(8,128)(2,1)}, bf16[768,384]{1,0:T(8,128)(2,1)}, u32[]{:S(2)}, u32[]{:S(2)}) collective-permute-start(bf16[768,384]{1,0:T(8,128)(2,1)} %hidden_2.1.refs_4_.refs_8_), channel_id=1, source_target_pairs={{0,16},{8,24},{16,0},{24,8},{1,17},{9,25},{17,1},{25,9},{2,18},{10... | collective-permute-start | bytes 1769480 | tf_op jit(solution)/shard_map/ppermute | solution.py:31
  21.3 11.9 %collective-permute-start.3 = (bf16[384,640]{1,0:T(8,128)(2,1)}, bf16[384,640]{1,0:T(8,128)(2,1)S(1)}, u32[]{:S(2)}, u32[]{:S(2)}) collective-permute-start(bf16[384,640]{1,0:T(8,128)(2,1)} %after.3.refs_1_), channel_id=1, source_target_pairs={{0,2},{1,3},{2,4},{3,5},{4,6},{5,7},{6,0},{7,1},{8,10},{9,11},{10,... | collective-permute-start | bytes 1474568 | tf_op jit(solution)/shard_map/ppermute | solution.py:36
  22.9 13.9 %collective-permute-start.4 = (bf16[384,640]{1,0:T(8,128)(2,1)}, bf16[384,640]{1,0:T(8,128)(2,1)}, u32[]{:S(2)}, u32[]{:S(2)}) collective-permute-start(bf16[384,640]{1,0:T(8,128)(2,1)} %after.3.refs_1_), channel_id=1, source_target_pairs={{0,1},{1,0},{2,3},{3,2},{4,5},{5,4},{6,7},{7,6},{8,9},{9,8},{10,11... | collective-permute-start | bytes 1474568 | tf_op jit(solution)/shard_map/ppermute | solution.py:31
  23.4 17.3 %collective-permute-start.10 = (bf16[768,384]{1,0:T(8,128)(2,1)}, bf16[768,384]{1,0:T(8,128)(2,1)}, u32[]{:S(2)}, u32[]{:S(2)}) collective-permute-start(bf16[768,384]{1,0:T(8,128)(2,1)} %hidden_2.1.refs_4_.refs_8_), channel_id=1, source_target_pairs={{0,8},{8,0},{16,24},{24,16},{1,9},{9,1},{17,25},{25,17},{2,10},{10... | collective-permute-start | bytes 1769480 | tf_op jit(solution)/shard_map/ppermute | solution.py:31
  25.7 11.2 %collective-permute-start.12 = (bf16[512,384]{1,0:T(8,128)(2,1)}, bf16[512,384]{1,0:T(8,128)(2,1)}, u32[]{:S(2)}, u32[]{:S(2)}) collective-permute-start(bf16[512,384]{1,0:T(8,128)(2,1)} %hidden_5.1.refs_8_.refs_12_), channel_id=1, source_target_pairs={{0,8},{8,0},{16,24},{24,16},{1,9},{9,1},{17,25},{25,17},{2,10},{10... | collective-permute-start | bytes 1179656 | tf_op jit(solution)/shard_map/ppermute | solution.py:31
  30.5 9.7 %collective-permute-start.13 = (bf16[512,384]{1,0:T(8,128)(2,1)}, bf16[512,384]{1,0:T(8,128)(2,1)}, u32[]{:S(2)}, u32[]{:S(2)}) collective-permute-start(bf16[512,384]{1,0:T(8,128)(2,1)} %hidden_5.1.refs_8_.refs_12_), channel_id=1, source_target_pairs={{0,16},{8,24},{16,0},{24,8},{1,17},{9,25},{17,1},{25,9},{2,18},{10... | collective-permute-start | bytes 1179656 | tf_op jit(solution)/shard_map/ppermute | solution.py:31
  33.2 9.0 %collective-permute-start.9 = (bf16[512,384]{1,0:T(8,128)(2,1)}, bf16[512,384]{1,0:T(8,128)(2,1)}, u32[]{:S(2)}, u32[]{:S(2)}) collective-permute-start(bf16[512,384]{1,0:T(8,128)(2,1)} %collective-permute-done.2.refs_2_.refs_6_), channel_id=1, source_target_pairs={{0,8},{8,0},{16,24},{24,16},{1,9},{9,1},{17,25},{25,17},{2,10},{10... | collective-permute-start | bytes 1179656 | tf_op jit(solution)/shard_map/ppermute | solution.py:31
  36.8 7.5 %collective-permute-start.11 = (bf16[768,384]{1,0:T(8,128)(2,1)}, bf16[768,384]{1,0:T(8,128)(2,1)}, u32[]{:S(2)}, u32[]{:S(2)}) collective-permute-start(bf16[768,384]{1,0:T(8,128)(2,1)} %collective-permute-done.5.refs_2_.refs_6_.refs_10_), channel_id=1, source_target_pairs={{0,8},{8,0},{16,24},{24,16},{1,9},{9,1},{17,25},{25,17},{2,10},{10... | collective-permute-start | bytes 1769480 | tf_op jit(solution)/shard_map/ppermute | solution.py:31
  36.8 15.7 %collective-permute-start.6 = (bf16[384,640]{1,0:T(8,128)(2,1)}, bf16[384,640]{1,0:T(8,128)(2,1)}, u32[]{:S(2)}, u32[]{:S(2)}) collective-permute-start(bf16[384,640]{1,0:T(8,128)(2,1)} %after.4.refs_13_.refs_2_), channel_id=1, source_target_pairs={{0,2},{1,3},{2,4},{3,5},{4,6},{5,7},{6,0},{7,1},{8,10},{9,11},{10,... | collective-permute-start | bytes 1474568 | tf_op jit(solution)/shard_map/ppermute | solution.py:36
  40.2 12.4 %collective-permute-start.7 = (bf16[384,640]{1,0:T(8,128)(2,1)}, bf16[384,640]{1,0:T(8,128)(2,1)S(1)}, u32[]{:S(2)}, u32[]{:S(2)}) collective-permute-start(bf16[384,640]{1,0:T(8,128)(2,1)} %after.4.refs_13_.refs_2_), channel_id=1, source_target_pairs={{0,1},{1,0},{2,3},{3,2},{4,5},{5,4},{6,7},{7,6},{8,9},{9,8},{10,11... | collective-permute-start | bytes 1474568 | tf_op jit(solution)/shard_map/ppermute | solution.py:31
  40.7 12.6 %collective-permute-start.18 = (bf16[384,640]{1,0:T(8,128)(2,1)S(1)}, bf16[384,640]{1,0:T(8,128)(2,1)}, u32[]{:S(2)}, u32[]{:S(2)}) collective-permute-start(bf16[384,640]{1,0:T(8,128)(2,1)S(1)} %copy-done.4), channel_id=1, source_target_pairs={{0,16},{8,24},{16,0},{24,8},{1,17},{9,25},{17,1},{25,9},{2,18},{10... | collective-permute-start | bytes 1474568 | tf_op jit(solution)/shard_map/ppermute | solution.py:31
  56.8 28.9 %all-to-all-start = ((bf16[4,384,640]{2,1,0:T(8,128)(2,1)}), bf16[4,384,640]{2,1,0:T(8,128)(2,1)}, u32[]{:S(2)}, u32[]{:S(2)}) async-start(bf16[4,384,640]{2,1,0:T(8,128)(2,1)} %own_features.1.refs_5_), calls=%async_computation | async-start | bytes 3932160 | tf_op jit(solution)/shard_map/all_to_all | solution.py:432
  61.4 20.2 %collective-permute-start.16 = (f32[4,32,1536]{2,1,0:T(8,128)}, f32[4,32,1536]{2,1,0:T(8,128)}, u32[]{:S(2)}, u32[]{:S(2)}) collective-permute-start(f32[4,32,1536]{2,1,0:T(8,128)} %get-tuple-element.18.refs_2_), channel_id=1, source_target_pairs={{0,1},{1,0},{2,3},{3,2},{4,5},{5,4},{6,7},{7,6},{8,9},{9,8},{10,11... | collective-permute-start | bytes 2359304 | tf_op jit(solution)/shard_map/ppermute | solution.py:31
  62.6 15.1 %collective-permute-start.15 = (bf16[384,640]{1,0:T(8,128)(2,1)S(1)}, bf16[384,640]{1,0:T(8,128)(2,1)}, u32[]{:S(2)}, u32[]{:S(2)}) collective-permute-start(bf16[384,640]{1,0:T(8,128)(2,1)S(1)} %copy-done.7), channel_id=1, source_target_pairs={{0,2},{1,3},{2,4},{3,5},{4,6},{5,7},{6,0},{7,1},{8,10},{9,11},{10,... | collective-permute-start | bytes 1474568 | tf_op jit(solution)/shard_map/ppermute | solution.py:36
  85.8 25.3 %all-to-all-start.1 = ((f32[4,32,1536]{2,1,0:T(8,128)}), f32[4,32,1536]{2,1,0:T(8,128)S(1)}, u32[]{:S(2)}, u32[]{:S(2)}) async-start(f32[4,32,1536]{2,1,0:T(8,128)} %hidden_pair.1.refs_11_), calls=%async_computation.1 | async-start | bytes 1572864 | tf_op jit(solution)/shard_map/all_to_all | solution.py:353
  89.4 19.4 %collective-permute-start.23 = (f32[4,32,1536]{2,1,0:T(8,128)}, f32[4,32,1536]{2,1,0:T(8,128)}, u32[]{:S(2)}, u32[]{:S(2)}) collective-permute-start(f32[4,32,1536]{2,1,0:T(8,128)} %get-tuple-element.20.refs_4_), channel_id=1, source_target_pairs={{0,1},{1,0},{2,3},{3,2},{4,5},{5,4},{6,7},{7,6},{8,9},{9,8},{10,11... | collective-permute-start | bytes 2359304 | tf_op jit(solution)/shard_map/ppermute | solution.py:31
  90.6 25.3 %collective-permute-start.20 = (bf16[384,640]{1,0:T(8,128)(2,1)}, bf16[384,640]{1,0:T(8,128)(2,1)}, u32[]{:S(2)}, u32[]{:S(2)}) collective-permute-start(bf16[384,640]{1,0:T(8,128)(2,1)} %get-tuple-element.24), channel_id=1, source_target_pairs={{0,8},{8,0},{16,24},{24,16},{1,9},{9,1},{17,25},{25,17},{2,10},{10... | collective-permute-start | bytes 1474568 | tf_op jit(solution)/shard_map/ppermute | solution.py:31
  90.6 25.3 %collective-permute-start.21 = (bf16[384,640]{1,0:T(8,128)(2,1)}, bf16[384,640]{1,0:T(8,128)(2,1)}, u32[]{:S(2)}, u32[]{:S(2)}) collective-permute-start(bf16[384,640]{1,0:T(8,128)(2,1)} %get-tuple-element.25), channel_id=1, source_target_pairs={{0,16},{8,24},{16,0},{24,8},{1,17},{9,25},{17,1},{25,9},{2,18},{10... | collective-permute-start | bytes 1474568 | tf_op jit(solution)/shard_map/ppermute | solution.py:31
  91.1 24.8 %collective-permute-start.22 = (bf16[384,640]{1,0:T(8,128)(2,1)}, bf16[384,640]{1,0:T(8,128)(2,1)}, u32[]{:S(2)}, u32[]{:S(2)}) collective-permute-start(bf16[384,640]{1,0:T(8,128)(2,1)} %get-tuple-element.26), channel_id=1, source_target_pairs={{0,24},{8,16},{16,8},{24,0},{1,25},{9,17},{17,9},{25,1},{2,26},{10... | collective-permute-start | bytes 1474568 | tf_op jit(solution)/shard_map/ppermute | solution.py:31
  111.1 25.3 %all-to-all-start.2 = ((f32[4,32,1536]{2,1,0:T(8,128)}), f32[4,32,1536]{2,1,0:T(8,128)}, u32[]{:S(2)}, u32[]{:S(2)}) async-start(f32[4,32,1536]{2,1,0:T(8,128)} %grad_pair.1.refs_16_), calls=%async_computation.2 | async-start | bytes 1572864 | tf_op jit(solution)/shard_map/all_to_all | solution.py:353
  138.6 9.9 %all-to-all-start.3 = ((f32[32,1,128]{2,1,0:T(1,128)}), f32[32,1,128]{2,1,0:T(1,128)S(1)}, u32[]{:S(2)}, u32[]{:S(2)}) async-start(f32[32,1,128]{2,1,0:T(1,128)} %bitcast.13), calls=%async_computation.3 | async-start | bytes 32768 | tf_op jit(solution)/shard_map/all_to_all | solution.py:452
  (14 other events, 86.0 us)

commit v15 on v14

--- a/solution.py
+++ b/solution.py
@@ -145,42 +145,66 @@
     )(to, *blocks, *order)
 
 
-def grads_body(n, offs_ref, *refs):
-    blocks, (w_ref, gate_ref, up_ref), (gg_ref, gu_ref, done_ref, piece) = (
-        refs[:n], refs[n : n + 3], refs[-4:]
+def grads_body(n, tiles, offs_ref, *refs):
+    blocks, (w_ref, gate_ref, up_ref), (gg_ref, gu_ref, done_ref, piece, sums, sems) = (
+        refs[:n], refs[n : n + 3], refs[-6:]
     )
     width = blocks[0].shape[1]
-
-    @pl.when(pl.program_id(0) == 0)
+    step = pl.program_id(0)
+
+    def work_off(total):
+        gate = gate_ref[...].astype(F32)
+        up = up_ref[...].astype(F32)
+        sig = jax.nn.sigmoid(gate)
+        gg_ref[...] = (total * up * sig * (1.0 + gate * (1.0 - sig))).astype(BF16)
+        gu_ref[...] = (total * (gate * sig)).astype(BF16)
+
+    @pl.when(step == 0)
     def _():
+        copies = []
         for j in range(n):
-            piece[:, pl.ds(pl.multiple_of(offs_ref[j], 128), width)] = blocks[j][...]
+            place = pl.ds(pl.multiple_of(offs_ref[j], 128), width)
+            copies.append(pltpu.make_async_copy(blocks[j], piece.at[:, place], sems.at[j]))
+        for copy in copies:
+            copy.start()
         done_ref[...] = jnp.zeros_like(done_ref)
-
-    total = dot_nt(piece[...], w_ref[...])
-    gate = gate_ref[...].astype(F32)
-    up = up_ref[...].astype(F32)
-    sig = jax.nn.sigmoid(gate)
-    gg_ref[...] = (total * up * sig * (1.0 + gate * (1.0 - sig))).astype(BF16)
-    gu_ref[...] = (total * (gate * sig)).astype(BF16)
+        sums[1] = jnp.zeros(sums.shape[1:], F32)
+        for copy in copies:
+            copy.wait()
+
+    for odd in range(2):
+
+        @pl.when((step < tiles) & (step % 2 == odd))
+        def _():
+            work_off(sums[1 - odd])
+            sums[odd] = dot_nt(piece[...], w_ref[...])
+
+    @pl.when(step == tiles)
+    def _():
+        work_off(sums[(tiles - 1) % 2])
 
 
 def grads(offs, blocks, weight, gate, up, order):
     n = len(blocks)
     toks, width = blocks[0].shape
     units, feats = weight.shape
-    cols = pl.BlockSpec((toks, TILE), lambda i, _: (0, i))
+    tiles = units // TILE
+    cols = pl.BlockSpec((toks, TILE), lambda i, _: (0, jnp.maximum(i - 1, 0)))
     out = jax.ShapeDtypeStruct((toks, units), BF16)
     return pl.pallas_call(
-        functools.partial(grads_body, n),
+        functools.partial(grads_body, n, tiles),
         grid_spec=pltpu.PrefetchScalarGridSpec(
             num_scalar_prefetch=1,
-            grid=(units // TILE,),
-            in_specs=[whole((toks, width))] * n
-            + [pl.BlockSpec((TILE, feats), lambda i, _: (i, 0)), cols, cols]
+            grid=(tiles + 1,),
+            in_specs=[ANY] * n
+            + [pl.BlockSpec((TILE, feats), lambda i, _: (jnp.minimum(i, tiles - 1), 0)), cols, cols]
             + [ANY] * len(order),
             out_specs=[cols, cols, whole((8, 128))],
-            scratch_shapes=[pltpu.VMEM((toks, feats), BF16)],
+            scratch_shapes=[
+                pltpu.VMEM((toks, feats), BF16),
+                pltpu.VMEM((2, toks, TILE), F32),
+                pltpu.SemaphoreType.DMA((n,)),
+            ],
         ),
         out_shape=(out, out, jax.ShapeDtypeStruct((8, 128), F32)),
         compiler_params=params(),

time: 151 us -> 153 us (1.013)
  Pallas kernels: 62.3 us -> 64.3 us
    pallas_call x1, Pallas kernels: 15.9 us -> 17.9 us  [grads(): pl.pallas_call(functools.partial(grads_body, n, tiles), grid_spec=pltpu.P...]
  transfers between devices with their start and end apart: 28 -> 28, of which waited for: 15 -> 14; matrix products, arithmetic and copies ran while one was open for 2% -> 2% of each run, Pallas kernels for 38% -> 39%
where the time goes in v15:
time: 153 us; the launch traced here: 152 us
  Pallas kernels  64.3 us (42%)
  waiting for transfers between devices  45.5 us (30%)
  starting transfers between devices  34.3 us (22%)
  local copies, waits for them, and re-layouts  4.73 us (3%)
  other arithmetic  2.34 us (2%)
    ppermute x20, waiting for transfers between devices, swap(): return lax.ppermute(x, axis, [(s, s ^ k) for s in range(n)])  19.3 us
    pallas_call x1, Pallas kernels, grads(): pl.pallas_call(functools.partial(grads_body, n, tiles), grid_spec=pltpu.P...  17.9 us
    pallas_call x1, Pallas kernels, wgrad(): pl.pallas_call(functools.partial(wgrad_body, n, tuple(starts)), in_specs=...  15.4 us
    ppermute x4, waiting for transfers between devices, shift(): return lax.ppermute(x, axis, [(s, (s + k) % n) for s in range(n)])  12.2 us
    ppermute x20, starting transfers between devices, swap(): return lax.ppermute(x, axis, [(s, s ^ k) for s in range(n)])  11.7 us
    pallas_call x2, Pallas kernels, gram(): pl.pallas_call(functools.partial(body, len(toks), cuts), grid=(1,), in_sp...  9.96 us
    all_to_all x2, starting transfers between devices, spread(): lax.all_to_all(pair, 'fsdp', split_axis=0, concat_axis=0, axis_index_grou...  8.57 us
    pallas_call x3, Pallas kernels, hidden_units(): pl.pallas_call(hidden_body, grid=(count,), in_specs=[cols, cols], out_spe...  7.26 us
  transfers between devices with their start and end apart: 28, of which 14 were waited for; matrix products, arithmetic and copies ran while one was open for 2% of the time, Pallas kernels for 39%

profile of v15, /device:TPU:0, one launch (start us, length us, event | category | flops | bytes accessed | tf_op | source)
XLA Modules:
  0.0 152.0 jit_solution(11426070699542001436)
XLA Ops:
  0.6 3.1 %collective-permute-start = (bf16[384,640]{1,0:T(8,128)(2,1)}, bf16[384,640]{1,0:T(8,128)(2,1)S(1)}, u32[]{:S(2)}, u32[]{:S(2)}) collective-permute-start(bf16[384,640]{1,0:T(8,128)(2,1)} %refs_0_.5), channel_id=1, source_target_pairs={{0,2},{1,3},{2,4},{3,5},{4,6},{5,7},{6,0},{7,1},{8,10},{9,11},{10,... | collective-permute-start | bytes 1474568 | tf_op jit(solution)/shard_map/ppermute | solution.py:36
  5.2 2.1 %hidden_0.1.refs_0_.refs_4_ = bf16[512,384]{1,0:T(8,128)(2,1)} custom-call(bf16[384,1792]{1,0:T(8,128)(2,1)} %refs_9_.1, bf16[384,1792]{1,0:T(8,128)(2,1)} %refs_10_.1), custom_call_target="tpu_custom_call" | custom-call | flops 1024 | bytes 1024 | tf_op jit(solution)/shard_map/hidden_0/pallas_call | solution.py:81
  8.8 3.2 %hidden_2.1.refs_4_.refs_8_ = bf16[768,384]{1,0:T(8,128)(2,1)} custom-call(bf16[384,1792]{1,0:T(8,128)(2,1)} %refs_9_.1, bf16[384,1792]{1,0:T(8,128)(2,1)} %refs_10_.1), custom_call_target="tpu_custom_call" | custom-call | flops 1024 | bytes 1024 | tf_op jit(solution)/shard_map/hidden_2/pallas_call | solution.py:81
  12.5 7.2 %collective-permute-done.2.refs_2_.refs_6_ = bf16[512,384]{1,0:T(8,128)(2,1)} collective-permute-done((bf16[512,384]{1,0:T(8,128)(2,1)}, bf16[512,384]{1,0:T(8,128)(2,1)}, u32[]{:S(2)}, u32[]{:S(2)}) %collective-permute-start.2) | collective-permute-done | bytes 393248 | tf_op jit(solution)/shard_map/ppermute | solution.py:31
  23.6 2.0 %hidden_5.1.refs_8_.refs_12_ = bf16[512,384]{1,0:T(8,128)(2,1)} custom-call(bf16[384,1792]{1,0:T(8,128)(2,1)} %refs_9_.1, bf16[384,1792]{1,0:T(8,128)(2,1)} %refs_10_.1), custom_call_target="tpu_custom_call" | custom-call | flops 1024 | bytes 1024 | tf_op jit(solution)/shard_map/hidden_5/pallas_call | solution.py:81
  25.9 4.6 %collective-permute-done.5.refs_2_.refs_6_.refs_10_ = bf16[768,384]{1,0:T(8,128)(2,1)} collective-permute-done((bf16[768,384]{1,0:T(8,128)(2,1)}, bf16[768,384]{1,0:T(8,128)(2,1)}, u32[]{:S(2)}, u32[]{:S(2)}) %collective-permute-start.5) | collective-permute-done | bytes 589856 | tf_op jit(solution)/shard_map/ppermute | solution.py:31
  33.2 3.6 %collective-permute-done.4.refs_1_.refs_5_ = bf16[384,640]{1,0:T(8,128)(2,1)} collective-permute-done((bf16[384,640]{1,0:T(8,128)(2,1)}, bf16[384,640]{1,0:T(8,128)(2,1)}, u32[]{:S(2)}, u32[]{:S(2)}) %collective-permute-start.4) | collective-permute-done | bytes 491552 | tf_op jit(solution)/shard_map/ppermute | solution.py:31
  44.3 6.2 %hidden_gram.1 = (f32[4,32,1536]{2,1,0:T(8,128)}, f32[4,32,1536]{2,1,0:T(8,128)}) custom-call(s32[1]{0:T(128)} %bitcast.inner_ref, s32[4]{0:T(128)} %xor_multiply_fusion.offs_ref.toks_ref, bf16[512,384]{1,0:T(8,128)(2,1)} %hidden_0.1.refs_0_.refs_4_, bf16[512,384]{1,0:T(8,128)(2,1)} %collective-permute-done.8.refs_1_.refs_5_, ...), custom_call_target="tpu_custom_call" | custom-call | flops 1024 | bytes 1024 | tf_op jit(solution)/shard_map/hidden_gram/pallas_call | solution.py:339
  50.5 2.1 %collective-permute-done.6.refs_0_ = bf16[384,640]{1,0:T(8,128)(2,1)} collective-permute-done((bf16[384,640]{1,0:T(8,128)(2,1)}, bf16[384,640]{1,0:T(8,128)(2,1)}, u32[]{:S(2)}, u32[]{:S(2)}) %collective-permute-start.6) | collective-permute-done | bytes 491552 | tf_op jit(solution)/shard_map/ppermute | solution.py:36
  53.4 3.4 %own_features.1.refs_5_ = bf16[4,384,640]{2,1,0:T(8,128)(2,1)} custom-call(s32[4]{0:T(128)} %and_select_fusion.at_ref, bf16[384,640]{1,0:T(8,128)(2,1)} %refs_0_.5, bf16[384,640]{1,0:T(8,128)(2,1)} %after.3.refs_1_, bf16[384,640]{1,0:T(8,128)(2,1)} %after.4.refs_13_.refs_2_, bf16[384,640]{1,0:T(8,128)(2,1)} %after.5.refs_3_, ...), custom_call_target="tpu_custom_call" | custom-call | flops 1024 | bytes 1024 | tf_op jit(solution)/shard_map/own_features/pallas_call | solution.py:107
  56.8 4.6 %all-to-all-start = ((bf16[4,384,640]{2,1,0:T(8,128)(2,1)}), bf16[4,384,640]{2,1,0:T(8,128)(2,1)}, u32[]{:S(2)}, u32[]{:S(2)}) async-start(bf16[4,384,640]{2,1,0:T(8,128)(2,1)} %own_features.1.refs_5_), calls=%async_computation | async-start | bytes 3932160 | tf_op jit(solution)/shard_map/all_to_all | solution.py:456
  65.0 3.8 %grad_gram.1 = (f32[4,32,1536]{2,1,0:T(8,128)}, f32[4,32,1536]{2,1,0:T(8,128)}) custom-call(s32[1]{0:T(128)} %bitcast.inner_ref, s32[4]{0:T(128)} %xor_multiply_fusion.offs_ref.toks_ref, bf16[384,640]{1,0:T(8,128)(2,1)} %refs_0_.5, bf16[384,640]{1,0:T(8,128)(2,1)} %copy-done.8, bf16[384,640]{1,0:T(8,128)(2,1)} %collective-permute-done.18.refs_4_.refs_2_, ...), custom_call_target="tpu_custom_call" | custom-call | flops 1024 | bytes 1024 | tf_op jit(solution)/shard_map/grad_gram/pallas_call | solution.py:339
  68.8 8.9 %collective-permute-done.15.refs_3_.refs_7_ = bf16[384,640]{1,0:T(8,128)(2,1)} collective-permute-done((bf16[384,640]{1,0:T(8,128)(2,1)S(1)}, bf16[384,640]{1,0:T(8,128)(2,1)}, u32[]{:S(2)}, u32[]{:S(2)}) %collective-permute-start.15) | collective-permute-done | bytes 491552 | tf_op jit(solution)/shard_map/ppermute | solution.py:36
  77.7 3.5 %other_features.1 = (bf16[384,640]{1,0:T(8,128)(2,1)}, bf16[384,640]{1,0:T(8,128)(2,1)}, bf16[384,640]{1,0:T(8,128)(2,1)}, bf16[384,640]{1,0:T(8,128)(2,1)}) custom-call(s32[4]{0:T(128)} %broadcast_xor_fusion.to_ref, bf16[384,640]{1,0:T(8,128)(2,1)} %copy-done.2, bf16[384,640]{1,0:T(8,128)(2,1)} %collective-permute-done.4.refs_1_.refs_5_, ...), custom_call_target="tpu_custom_call" | custom-call | flops 1024 | bytes 1024 | tf_op jit(solution)/shard_map/other_features/pallas_call | solution.py:135
  81.6 2.3 %hidden_pair.1.refs_11_ = f32[4,32,1536]{2,1,0:T(8,128)} custom-call(f32[4,32,1536]{2,1,0:T(8,128)} %get-tuple-element.19.kept_ref, f32[4,32,1536]{2,1,0:T(8,128)} %collective-permute-done.16.refs_0_, bf16[384,640]{1,0:T(8,128)(2,1)} %get-tuple-element.21.refs_1_.refs_0_), custom_call_target="tpu_custom_call" | custom-call | flops 1024 | bytes 1024 | tf_op jit(solution)/shard_map/hidden_pair/pallas_call | solution.py:362
  85.8 3.5 %all-to-all-start.1 = ((f32[4,32,1536]{2,1,0:T(8,128)}), f32[4,32,1536]{2,1,0:T(8,128)S(1)}, u32[]{:S(2)}, u32[]{:S(2)}) async-start(f32[4,32,1536]{2,1,0:T(8,128)} %hidden_pair.1.refs_11_), calls=%async_computation.1 | async-start | bytes 1572864 | tf_op jit(solution)/shard_map/all_to_all | solution.py:377
  92.4 17.9 %grads.1 = (bf16[384,1792]{1,0:T(8,128)(2,1)}, bf16[384,1792]{1,0:T(8,128)(2,1)}, f32[8,128]{1,0:T(8,128)}) custom-call(s32[8]{0:T(128)} %add.40.offs_ref, bf16[384,640]{1,0:T(8,128)(2,1)} %refs_0_.5, bf16[384,640]{1,0:T(8,128)(2,1)} %after.3.refs_1_, bf16[384,640]{1,0:T(8,128)(2,1)} %after.4.refs_13_.refs_2_, bf16[384,640]{1,0:T(8,128)(2,1)} %after.5.refs_3_, ...), custom_call_target="tpu_custom_call" | custom-call | flops 7046430720 | bytes 27787264 | tf_op jit(solution)/shard_map/grads/pallas_call | solution.py:194
  110.4 2.3 %grad_pair.1.refs_16_ = f32[4,32,1536]{2,1,0:T(8,128)} custom-call(f32[4,32,1536]{2,1,0:T(8,128)} %get-tuple-element.27.kept_ref, f32[4,32,1536]{2,1,0:T(8,128)} %collective-permute-done.23.refs_0_, f32[8,128]{1,0:T(8,128)} %get-tuple-element.28.refs_1_), custom_call_target="tpu_custom_call" | custom-call | flops 1024 | bytes 1024 | tf_op jit(solution)/shard_map/grad_pair/pallas_call | solution.py:362
  112.7 5.1 %all-to-all-start.2 = ((f32[4,32,1536]{2,1,0:T(8,128)}), f32[4,32,1536]{2,1,0:T(8,128)}, u32[]{:S(2)}, u32[]{:S(2)}) async-start(f32[4,32,1536]{2,1,0:T(8,128)} %grad_pair.1.refs_16_), calls=%async_computation.2 | async-start | bytes 1572864 | tf_op jit(solution)/shard_map/all_to_all | solution.py:377
  117.8 15.4 %wgrad.1 = (bf16[1792,1280]{1,0:T(8,128)(2,1)}, f32[8,128]{1,0:T(8,128)}) custom-call(s32[2]{0:T(128)} %copy-done.9, s32[4]{0:T(128)} %xor_multiply_fusion.offs_ref.toks_ref, bf16[4,384,640]{2,1,0:T(8,128)(2,1)} %all-to-all-done.own_ref, bf16[384,640]{1,0:T(8,128)(2,1)} %get-tuple-element.21.refs_1_.refs_0_, ...), custom_call_target="tpu_custom_call" | custom-call | flops 28185722880 | bytes 14024704 | tf_op jit(solution)/shard_map/wgrad/pallas_call | solution.py:266
  133.2 5.2 %all-to-all-done.2.grad_ref = f32[4,32,1536]{2,1,0:T(8,128)} async-done(((f32[4,32,1536]{2,1,0:T(8,128)}), f32[4,32,1536]{2,1,0:T(8,128)}, u32[]{:S(2)}, u32[]{:S(2)}) %all-to-all-start.2) | async-done | bytes 786464 | tf_op jit(solution)/shard_map/all_to_all | solution.py:377
  138.4 2.2 %score_line.1 = f32[32,128]{1,0:T(8,128)} custom-call(s32[3]{0:T(128)} %assign_ref.1, f32[4,32,1536]{2,1,0:T(8,128)} %copy-done.1, f32[4,32,1536]{2,1,0:T(8,128)} %all-to-all-done.2.grad_ref, f32[8,128]{1,0:T(8,128)} %get-tuple-element.30.refs_0_), custom_call_target="tpu_custom_call" | custom-call | flops 1024 | bytes 1024 | tf_op jit(solution)/shard_map/score_line/pallas_call | solution.py:400
  140.6 2.8 %all-to-all-start.3 = ((f32[32,1,128]{2,1,0:T(1,128)}), f32[32,1,128]{2,1,0:T(1,128)S(1)}, u32[]{:S(2)}, u32[]{:S(2)}) async-start(f32[32,1,128]{2,1,0:T(1,128)} %bitcast.13), calls=%async_computation.3 | async-start | bytes 32768 | tf_op jit(solution)/shard_map/all_to_all | solution.py:476
  143.4 7.1 %all-to-all-done.3 = f32[32,1,128]{2,1,0:T(1,128)S(1)} async-done(((f32[32,1,128]{2,1,0:T(1,128)}), f32[32,1,128]{2,1,0:T(1,128)S(1)}, u32[]{:S(2)}, u32[]{:S(2)}) %all-to-all-start.3) | async-done | bytes 16416 | tf_op jit(solution)/shard_map/all_to_all | solution.py:476
  (80 shorter events, 29.4 us)
Async XLA Ops:
  0.6 19.0 %collective-permute-start = (bf16[384,640]{1,0:T(8,128)(2,1)}, bf16[384,640]{1,0:T(8,128)(2,1)S(1)}, u32[]{:S(2)}, u32[]{:S(2)}) collective-permute-start(bf16[384,640]{1,0:T(8,128)(2,1)} %refs_0_.5), channel_id=1, source_target_pairs={{0,2},{1,3},{2,4},{3,5},{4,6},{5,7},{6,0},{7,1},{8,10},{9,11},{10,... | collective-permute-start | bytes 1474568 | tf_op jit(solution)/shard_map/ppermute | solution.py:36
  3.7 15.9 %collective-permute-start.1 = (bf16[384,640]{1,0:T(8,128)(2,1)}, bf16[384,640]{1,0:T(8,128)(2,1)S(1)}, u32[]{:S(2)}, u32[]{:S(2)}) collective-permute-start(bf16[384,640]{1,0:T(8,128)(2,1)} %refs_0_.5), channel_id=1, source_target_pairs={{0,1},{1,0},{2,3},{3,2},{4,5},{5,4},{6,7},{7,6},{8,9},{9,8},{10,11... | collective-permute-start | bytes 1474568 | tf_op jit(solution)/shard_map/ppermute | solution.py:31
  7.3 12.4 %collective-permute-start.2 = (bf16[512,384]{1,0:T(8,128)(2,1)}, bf16[512,384]{1,0:T(8,128)(2,1)}, u32[]{:S(2)}, u32[]{:S(2)}) collective-permute-start(bf16[512,384]{1,0:T(8,128)(2,1)} %hidden_0.1.refs_0_.refs_4_), channel_id=1, source_target_pairs={{0,16},{8,24},{16,0},{24,8},{1,17},{9,25},{17,1},{25,9},{2,18},{10... | collective-permute-start | bytes 1179656 | tf_op jit(solution)/shard_map/ppermute | solution.py:31
  11.9 18.6 %collective-permute-start.5 = (bf16[768,384]{1,0:T(8,128)(2,1)}, bf16[768,384]{1,0:T(8,128)(2,1)}, u32[]{:S(2)}, u32[]{:S(2)}) collective-permute-start(bf16[768,384]{1,0:T(8,128)(2,1)} %hidden_2.1.refs_4_.refs_8_), channel_id=1, source_target_pairs={{0,16},{8,24},{16,0},{24,8},{1,17},{9,25},{17,1},{25,9},{2,18},{10... | collective-permute-start | bytes 1769480 | tf_op jit(solution)/shard_map/ppermute | solution.py:31
  21.3 11.9 %collective-permute-start.3 = (bf16[384,640]{1,0:T(8,128)(2,1)}, bf16[384,640]{1,0:T(8,128)(2,1)S(1)}, u32[]{:S(2)}, u32[]{:S(2)}) collective-permute-start(bf16[384,640]{1,0:T(8,128)(2,1)} %after.3.refs_1_), channel_id=1, source_target_pairs={{0,2},{1,3},{2,4},{3,5},{4,6},{5,7},{6,0},{7,1},{8,10},{9,11},{10,... | collective-permute-start | bytes 1474568 | tf_op jit(solution)/shard_map/ppermute | solution.py:36
  22.9 13.9 %collective-permute-start.4 = (bf16[384,640]{1,0:T(8,128)(2,1)}, bf16[384,640]{1,0:T(8,128)(2,1)}, u32[]{:S(2)}, u32[]{:S(2)}) collective-permute-start(bf16[384,640]{1,0:T(8,128)(2,1)} %after.3.refs_1_), channel_id=1, source_target_pairs={{0,1},{1,0},{2,3},{3,2},{4,5},{5,4},{6,7},{7,6},{8,9},{9,8},{10,11... | collective-permute-start | bytes 1474568 | tf_op jit(solution)/shard_map/ppermute | solution.py:31
  23.4 17.3 %collective-permute-start.10 = (bf16[768,384]{1,0:T(8,128)(2,1)}, bf16[768,384]{1,0:T(8,128)(2,1)}, u32[]{:S(2)}, u32[]{:S(2)}) collective-permute-start(bf16[768,384]{1,0:T(8,128)(2,1)} %hidden_2.1.refs_4_.refs_8_), channel_id=1, source_target_pairs={{0,8},{8,0},{16,24},{24,16},{1,9},{9,1},{17,25},{25,17},{2,10},{10... | collective-permute-start | bytes 1769480 | tf_op jit(solution)/shard_map/ppermute | solution.py:31
  25.7 11.2 %collective-permute-start.12 = (bf16[512,384]{1,0:T(8,128)(2,1)}, bf16[512,384]{1,0:T(8,128)(2,1)}, u32[]{:S(2)}, u32[]{:S(2)}) collective-permute-start(bf16[512,384]{1,0:T(8,128)(2,1)} %hidden_5.1.refs_8_.refs_12_), channel_id=1, source_target_pairs={{0,8},{8,0},{16,24},{24,16},{1,9},{9,1},{17,25},{25,17},{2,10},{10... | collective-permute-start | bytes 1179656 | tf_op jit(solution)/shard_map/ppermute | solution.py:31
  30.5 9.7 %collective-permute-start.13 = (bf16[512,384]{1,0:T(8,128)(2,1)}, bf16[512,384]{1,0:T(8,128)(2,1)}, u32[]{:S(2)}, u32[]{:S(2)}) collective-permute-start(bf16[512,384]{1,0:T(8,128)(2,1)} %hidden_5.1.refs_8_.refs_12_), channel_id=1, source_target_pairs={{0,16},{8,24},{16,0},{24,8},{1,17},{9,25},{17,1},{25,9},{2,18},{10... | collective-permute-start | bytes 1179656 | tf_op jit(solution)/shard_map/ppermute | solution.py:31
  33.2 9.0 %collective-permute-start.9 = (bf16[512,384]{1,0:T(8,128)(2,1)}, bf16[512,384]{1,0:T(8,128)(2,1)}, u32[]{:S(2)}, u32[]{:S(2)}) collective-permute-start(bf16[512,384]{1,0:T(8,128)(2,1)} %collective-permute-done.2.refs_2_.refs_6_), channel_id=1, source_target_pairs={{0,8},{8,0},{16,24},{24,16},{1,9},{9,1},{17,25},{25,17},{2,10},{10... | collective-permute-start | bytes 1179656 | tf_op jit(solution)/shard_map/ppermute | solution.py:31
  36.8 7.5 %collective-permute-start.11 = (bf16[768,384]{1,0:T(8,128)(2,1)}, bf16[768,384]{1,0:T(8,128)(2,1)}, u32[]{:S(2)}, u32[]{:S(2)}) collective-permute-start(bf16[768,384]{1,0:T(8,128)(2,1)} %collective-permute-done.5.refs_2_.refs_6_.refs_10_), channel_id=1, source_target_pairs={{0,8},{8,0},{16,24},{24,16},{1,9},{9,1},{17,25},{25,17},{2,10},{10... | collective-permute-start | bytes 1769480 | tf_op jit(solution)/shard_map/ppermute | solution.py:31
  36.8 15.7 %collective-permute-start.6 = (bf16[384,640]{1,0:T(8,128)(2,1)}, bf16[384,640]{1,0:T(8,128)(2,1)}, u32[]{:S(2)}, u32[]{:S(2)}) collective-permute-start(bf16[384,640]{1,0:T(8,128)(2,1)} %after.4.refs_13_.refs_2_), channel_id=1, source_target_pairs={{0,2},{1,3},{2,4},{3,5},{4,6},{5,7},{6,0},{7,1},{8,10},{9,11},{10,... | collective-permute-start | bytes 1474568 | tf_op jit(solution)/shard_map/ppermute | solution.py:36
  40.2 12.4 %collective-permute-start.7 = (bf16[384,640]{1,0:T(8,128)(2,1)}, bf16[384,640]{1,0:T(8,128)(2,1)S(1)}, u32[]{:S(2)}, u32[]{:S(2)}) collective-permute-start(bf16[384,640]{1,0:T(8,128)(2,1)} %after.4.refs_13_.refs_2_), channel_id=1, source_target_pairs={{0,1},{1,0},{2,3},{3,2},{4,5},{5,4},{6,7},{7,6},{8,9},{9,8},{10,11... | collective-permute-start | bytes 1474568 | tf_op jit(solution)/shard_map/ppermute | solution.py:31
  40.7 12.6 %collective-permute-start.18 = (bf16[384,640]{1,0:T(8,128)(2,1)S(1)}, bf16[384,640]{1,0:T(8,128)(2,1)}, u32[]{:S(2)}, u32[]{:S(2)}) collective-permute-start(bf16[384,640]{1,0:T(8,128)(2,1)S(1)} %copy-done.4), channel_id=1, source_target_pairs={{0,16},{8,24},{16,0},{24,8},{1,17},{9,25},{17,1},{25,9},{2,18},{10... | collective-permute-start | bytes 1474568 | tf_op jit(solution)/shard_map/ppermute | solution.py:31
  56.8 28.9 %all-to-all-start = ((bf16[4,384,640]{2,1,0:T(8,128)(2,1)}), bf16[4,384,640]{2,1,0:T(8,128)(2,1)}, u32[]{:S(2)}, u32[]{:S(2)}) async-start(bf16[4,384,640]{2,1,0:T(8,128)(2,1)} %own_features.1.refs_5_), calls=%async_computation | async-start | bytes 3932160 | tf_op jit(solution)/shard_map/all_to_all | solution.py:456
  61.4 20.2 %collective-permute-start.16 = (f32[4,32,1536]{2,1,0:T(8,128)}, f32[4,32,1536]{2,1,0:T(8,128)}, u32[]{:S(2)}, u32[]{:S(2)}) collective-permute-start(f32[4,32,1536]{2,1,0:T(8,128)} %get-tuple-element.18.refs_2_), channel_id=1, source_target_pairs={{0,1},{1,0},{2,3},{3,2},{4,5},{5,4},{6,7},{7,6},{8,9},{9,8},{10,11... | collective-permute-start | bytes 2359304 | tf_op jit(solution)/shard_map/ppermute | solution.py:31
  62.6 15.1 %collective-permute-start.15 = (bf16[384,640]{1,0:T(8,128)(2,1)S(1)}, bf16[384,640]{1,0:T(8,128)(2,1)}, u32[]{:S(2)}, u32[]{:S(2)}) collective-permute-start(bf16[384,640]{1,0:T(8,128)(2,1)S(1)} %copy-done.7), channel_id=1, source_target_pairs={{0,2},{1,3},{2,4},{3,5},{4,6},{5,7},{6,0},{7,1},{8,10},{9,11},{10,... | collective-permute-start | bytes 1474568 | tf_op jit(solution)/shard_map/ppermute | solution.py:36
  85.8 26.9 %all-to-all-start.1 = ((f32[4,32,1536]{2,1,0:T(8,128)}), f32[4,32,1536]{2,1,0:T(8,128)S(1)}, u32[]{:S(2)}, u32[]{:S(2)}) async-start(f32[4,32,1536]{2,1,0:T(8,128)} %hidden_pair.1.refs_11_), calls=%async_computation.1 | async-start | bytes 1572864 | tf_op jit(solution)/shard_map/all_to_all | solution.py:377
  89.4 21.0 %collective-permute-start.23 = (f32[4,32,1536]{2,1,0:T(8,128)}, f32[4,32,1536]{2,1,0:T(8,128)}, u32[]{:S(2)}, u32[]{:S(2)}) collective-permute-start(f32[4,32,1536]{2,1,0:T(8,128)} %get-tuple-element.20.refs_4_), channel_id=1, source_target_pairs={{0,1},{1,0},{2,3},{3,2},{4,5},{5,4},{6,7},{7,6},{8,9},{9,8},{10,11... | collective-permute-start | bytes 2359304 | tf_op jit(solution)/shard_map/ppermute | solution.py:31
  90.6 27.2 %collective-permute-start.20 = (bf16[384,640]{1,0:T(8,128)(2,1)}, bf16[384,640]{1,0:T(8,128)(2,1)}, u32[]{:S(2)}, u32[]{:S(2)}) collective-permute-start(bf16[384,640]{1,0:T(8,128)(2,1)} %get-tuple-element.24), channel_id=1, source_target_pairs={{0,8},{8,0},{16,24},{24,16},{1,9},{9,1},{17,25},{25,17},{2,10},{10... | collective-permute-start | bytes 1474568 | tf_op jit(solution)/shard_map/ppermute | solution.py:31
  90.6 27.2 %collective-permute-start.21 = (bf16[384,640]{1,0:T(8,128)(2,1)}, bf16[384,640]{1,0:T(8,128)(2,1)}, u32[]{:S(2)}, u32[]{:S(2)}) collective-permute-start(bf16[384,640]{1,0:T(8,128)(2,1)} %get-tuple-element.25), channel_id=1, source_target_pairs={{0,16},{8,24},{16,0},{24,8},{1,17},{9,25},{17,1},{25,9},{2,18},{10... | collective-permute-start | bytes 1474568 | tf_op jit(solution)/shard_map/ppermute | solution.py:31
  91.1 26.7 %collective-permute-start.22 = (bf16[384,640]{1,0:T(8,128)(2,1)}, bf16[384,640]{1,0:T(8,128)(2,1)}, u32[]{:S(2)}, u32[]{:S(2)}) collective-permute-start(bf16[384,640]{1,0:T(8,128)(2,1)} %get-tuple-element.26), channel_id=1, source_target_pairs={{0,24},{8,16},{16,8},{24,0},{1,25},{9,17},{17,9},{25,1},{2,26},{10... | collective-permute-start | bytes 1474568 | tf_op jit(solution)/shard_map/ppermute | solution.py:31
  112.7 25.7 %all-to-all-start.2 = ((f32[4,32,1536]{2,1,0:T(8,128)}), f32[4,32,1536]{2,1,0:T(8,128)}, u32[]{:S(2)}, u32[]{:S(2)}) async-start(f32[4,32,1536]{2,1,0:T(8,128)} %grad_pair.1.refs_16_), calls=%async_computation.2 | async-start | bytes 1572864 | tf_op jit(solution)/shard_map/all_to_all | solution.py:377
  140.6 9.9 %all-to-all-start.3 = ((f32[32,1,128]{2,1,0:T(1,128)}), f32[32,1,128]{2,1,0:T(1,128)S(1)}, u32[]{:S(2)}, u32[]{:S(2)}) async-start(f32[32,1,128]{2,1,0:T(1,128)} %bitcast.13), calls=%async_computation.3 | async-start | bytes 32768 | tf_op jit(solution)/shard_map/all_to_all | solution.py:476
  (14 other events, 88.3 us)

commit v16 on v14

--- a/solution.py
+++ b/solution.py
@@ -347,6 +347,33 @@
     )(kept, *came, *order)
 
 
+def slices_body(n, cuts, outer_ref, kept_ref, *refs):
+    came_refs, outs = refs[:cuts], refs[-n:]
+    cut = kept_ref.shape[2] // cuts
+    for step, out_ref in enumerate(outs):
+        at = lax.rem(outer_ref[0] + step, n)
+        for h in range(cuts):
+            cols = slice(h * cut, (h + 1) * cut)
+            out_ref[:, cols] = kept_ref[at, :, cols] + came_refs[h][at]
+
+
+def pair_slices(outer, kept, came, order, name):
+    n, *size = kept.shape
+    outs = [jax.ShapeDtypeStruct(size, F32)] * n
+    return pl.pallas_call(
+        functools.partial(slices_body, n, len(came)),
+        grid=(1,),
+        in_specs=[pl.BlockSpec(memory_space=pltpu.SMEM)]
+        + each([kept, *came])
+        + [ANY] * len(order),
+        out_specs=each(outs),
+        out_shape=outs,
+        compiler_params=params(),
+        cost_estimate=SMALL,
+        name=name,
+    )(outer, kept, *came, *order)
+
+
 def spread(pair):
     n_fs = lax.axis_size("fsdp")
     groups = [list(range(x, n_fs, 2)) for x in range(2)]
@@ -355,11 +382,10 @@
     )
 
 
-def line_body(rows, assign_ref, hid_ref, grad_ref, *refs):
-    out_ref = refs[-1]
-    n = hid_ref.shape[0]
+def line_body(rows, n, assign_ref, hid_ref, *refs):
+    grad, out_ref = refs[:n], refs[-1]
     hid_sum = sum(hid_ref[j] for j in range(n))
-    grad_sum = sum(grad_ref[j] for j in range(n))
+    grad_sum = sum(ref[...] for ref in grad)
     by_tok = jnp.sum(hid_sum * grad_sum, axis=0, keepdims=True)
     size = by_tok.shape[1] // rows
     lane = lax.broadcasted_iota(jnp.int32, (1, 128), 1)
@@ -374,15 +400,15 @@
 
 def score_line(assign, hid, grad, order, rows, copies):
     return pl.pallas_call(
-        functools.partial(line_body, rows),
+        functools.partial(line_body, rows, len(grad)),
         grid=(1,),
-        in_specs=[pl.BlockSpec(memory_space=pltpu.SMEM)] + each([hid, grad]) + [ANY] * len(order),
+        in_specs=[pl.BlockSpec(memory_space=pltpu.SMEM)] + each([hid, *grad]) + [ANY] * len(order),
         out_specs=whole((copies, 128)),
         out_shape=jax.ShapeDtypeStruct((copies, 128), F32),
         compiler_params=params(),
         cost_estimate=SMALL,
         name="score_line",
-    )(assign, hid, grad, *order)
+    )(assign, hid, *grad, *order)
 
 
 def per_device(gate_act, up_act, out_grad, down_weight, val_hidden, val_grad, assign):
@@ -401,6 +427,7 @@
     tok_offs = (d ^ jnp.arange(n_dp, dtype=jnp.int32)) * toks
     inner_at = inner.reshape(1).astype(jnp.int32)
     to = at ^ d
+    outer_at = outer.reshape(1).astype(jnp.int32)
 
     def over_dp(x):
         far = swap(x, "dp", 2)
@@ -437,16 +464,16 @@
     )
     other = arrange(to, others, away, "other_features")
     other_cols = [x if k == 0 else swap(x, "dp", k) for k, x in enumerate(other)]
-    hid_pair = pair_sum(hid_kept, hid_came, [other[0]], "hidden_pair")
+    hid_pair = pair_sum(hid_kept, hid_came, [other[0], own_cols], "hidden_pair")
     hid_sums = spread(hid_pair)
     offs = (jnp.stack([inner, 1 - inner]) * width).astype(jnp.int32)
     places = (offs[:, None] + at[None, :] * (2 * width)).reshape(-1)
     grad_gate, grad_up, done = grads(
         places, [*ring, *others], down_weight, gate_act, up_act, [hid_pair]
     )
-    grad_pair = pair_sum(grad_kept, grad_came, [done], "grad_pair")
-    grad_sums = spread(grad_pair)
-    weight_grad, done = wgrad(offs, tok_offs, own_cols, other_cols, hids, [grad_pair])
+    grad_pair = pair_slices(outer_at, grad_kept, grad_came, [done, hid_sums], "grad_pair")
+    grad_sums = [x if j == 0 else shift(x, "fsdp", 2 * j) for j, x in enumerate(grad_pair)]
+    weight_grad, done = wgrad(offs, tok_offs, own_cols, other_cols, hids, [grad_pair[0]])
 
     mine = score_line(assign, hid_sums, grad_sums, [done], n_dp * rows_here, n_dp * n_fs)
     every = lax.all_to_all(

time: 151 us -> 155 us (1.026)
  starting transfers between devices: 34 us -> 37.2 us
    all_to_all x2 -> x1, starting transfers between devices: 8.27 us -> 3.49 us  [spread(): lax.all_to_all(pair, 'fsdp', split_axis=0, concat_axis=0, axis_index_grou...]
    all_to_all x2 -> x1, waiting for transfers between devices: 5.05 us -> 0.41 us  [spread(): lax.all_to_all(pair, 'fsdp', split_axis=0, concat_axis=0, axis_index_grou...]
    ppermute x4 -> x7, starting transfers between devices: 6.74 us -> 11 us  [shift(): return lax.ppermute(x, axis, [(s, (s + k) % n) for s in range(n)])]
    ppermute x20, starting transfers between devices: 11.7 us -> 15 us  [swap(): return lax.ppermute(x, axis, [(s, s ^ k) for s in range(n)])]
    ppermute x20, waiting for transfers between devices: 19.7 us -> 22.7 us  [swap(): return lax.ppermute(x, axis, [(s, s ^ k) for s in range(n)])]
    pallas_call x1 -> x2, Pallas kernels: 2.15 us -> 4.61 us  [the longest x1 2.42 us: pair_slices(): pl.pallas_call(functools.partial(slices_body, n, len(came)), grid=(1,), i...]
    pallas_call x2 -> x1, Pallas kernels: 4.66 us -> 2.33 us  [pair_sum(): pl.pallas_call(functools.partial(pair_body, len(came)), grid=(1,), in_spe...]
    all_to_all x1, waiting for transfers between devices: 1.8 us -> 4 us  [per_device(): lax.all_to_all(own, 'dp', split_axis=0, concat_axis=0, tiled=True)]
  transfers between devices with their start and end apart: 28 -> 30, of which waited for: 15 -> 11; matrix products, arithmetic and copies ran while one was open for 2% -> 2% of each run, Pallas kernels for 38% -> 35%
where the time goes in v16:
time: 155 us; the launch traced here: 154 us
  Pallas kernels  62.4 us (40%)
  waiting for transfers between devices  45.6 us (29%)
  starting transfers between devices  37.2 us (24%)
  local copies, waits for them, and re-layouts  5.88 us (4%)
  other arithmetic  2.41 us (2%)
    ppermute x20, waiting for transfers between devices, swap(): return lax.ppermute(x, axis, [(s, s ^ k) for s in range(n)])  22.7 us
    pallas_call x1, Pallas kernels, grads(): pl.pallas_call(functools.partial(grads_body, n), grid_spec=pltpu.Prefetch...  15.9 us
    pallas_call x1, Pallas kernels, wgrad(): pl.pallas_call(functools.partial(wgrad_body, n, tuple(starts)), in_specs=...  15.4 us
    ppermute x20, starting transfers between devices, swap(): return lax.ppermute(x, axis, [(s, s ^ k) for s in range(n)])  15 us
    ppermute x7, waiting for transfers between devices, shift(): return lax.ppermute(x, axis, [(s, (s + k) % n) for s in range(n)])  11.4 us
    ppermute x7, starting transfers between devices, shift(): return lax.ppermute(x, axis, [(s, (s + k) % n) for s in range(n)])  11 us
    pallas_call x2, Pallas kernels, gram(): pl.pallas_call(functools.partial(body, len(toks), cuts), grid=(1,), in_sp...  9.96 us
    pallas_call x3, Pallas kernels, hidden_units(): pl.pallas_call(hidden_body, grid=(count,), in_specs=[cols, cols], out_spe...  7.29 us
  transfers between devices with their start and end apart: 30, of which 11 were waited for; matrix products, arithmetic and copies ran while one was open for 2% of the time, Pallas kernels for 35%

profile of v16, /device:TPU:0, one launch (start us, length us, event | category | flops | bytes accessed | tf_op | source)
XLA Modules:
  0.0 154.2 jit_solution(17158455093385086752)
XLA Ops:
  0.6 3.0 %collective-permute-start.1 = (bf16[384,640]{1,0:T(8,128)(2,1)}, bf16[384,640]{1,0:T(8,128)(2,1)S(1)}, u32[]{:S(2)}, u32[]{:S(2)}) collective-permute-start(bf16[384,640]{1,0:T(8,128)(2,1)} %refs_0_.5), channel_id=1, source_target_pairs={{0,1},{1,0},{2,3},{3,2},{4,5},{5,4},{6,7},{7,6},{8,9},{9,8},{10,11... | collective-permute-start | bytes 1474568 | tf_op jit(solution)/shard_map/ppermute | solution.py:31
  5.2 2.0 %hidden_0.1.refs_0_.refs_4_ = bf16[512,384]{1,0:T(8,128)(2,1)} custom-call(bf16[384,1792]{1,0:T(8,128)(2,1)} %refs_9_.1, bf16[384,1792]{1,0:T(8,128)(2,1)} %refs_10_.1), custom_call_target="tpu_custom_call" | custom-call | flops 1024 | bytes 1024 | tf_op jit(solution)/shard_map/hidden_0/pallas_call | solution.py:81
  8.8 3.2 %hidden_2.1.refs_4_.refs_8_ = bf16[768,384]{1,0:T(8,128)(2,1)} custom-call(bf16[384,1792]{1,0:T(8,128)(2,1)} %refs_9_.1, bf16[384,1792]{1,0:T(8,128)(2,1)} %refs_10_.1), custom_call_target="tpu_custom_call" | custom-call | flops 1024 | bytes 1024 | tf_op jit(solution)/shard_map/hidden_2/pallas_call | solution.py:81
  12.5 7.2 %collective-permute-done.2.refs_2_.refs_6_ = bf16[512,384]{1,0:T(8,128)(2,1)} collective-permute-done((bf16[512,384]{1,0:T(8,128)(2,1)}, bf16[512,384]{1,0:T(8,128)(2,1)}, u32[]{:S(2)}, u32[]{:S(2)}) %collective-permute-start.2) | collective-permute-done | bytes 393248 | tf_op jit(solution)/shard_map/ppermute | solution.py:31
  21.7 2.1 %hidden_5.1.refs_8_.refs_12_ = bf16[512,384]{1,0:T(8,128)(2,1)} custom-call(bf16[384,1792]{1,0:T(8,128)(2,1)} %refs_9_.1, bf16[384,1792]{1,0:T(8,128)(2,1)} %refs_10_.1), custom_call_target="tpu_custom_call" | custom-call | flops 1024 | bytes 1024 | tf_op jit(solution)/shard_map/hidden_5/pallas_call | solution.py:81
  26.9 12.0 %collective-permute-done.13.refs_10_.refs_14_ = bf16[512,384]{1,0:T(8,128)(2,1)} collective-permute-done((bf16[512,384]{1,0:T(8,128)(2,1)}, bf16[512,384]{1,0:T(8,128)(2,1)}, u32[]{:S(2)}, u32[]{:S(2)}) %collective-permute-start.13) | collective-permute-done | bytes 393248 | tf_op jit(solution)/shard_map/ppermute | solution.py:31
  46.7 6.2 %hidden_gram.1 = (f32[4,32,1536]{2,1,0:T(8,128)}, f32[4,32,1536]{2,1,0:T(8,128)}) custom-call(s32[1]{0:T(128)} %bitcast.inner_ref, s32[4]{0:T(128)} %xor_multiply_fusion.offs_ref.toks_ref, bf16[512,384]{1,0:T(8,128)(2,1)} %hidden_0.1.refs_0_.refs_4_, bf16[512,384]{1,0:T(8,128)(2,1)} %collective-permute-done.8.refs_1_.refs_5_, ...), custom_call_target="tpu_custom_call" | custom-call | flops 1024 | bytes 1024 | tf_op jit(solution)/shard_map/hidden_gram/pallas_call | solution.py:315
  54.5 2.5 %collective-permute-done.6.refs_0_ = bf16[384,640]{1,0:T(8,128)(2,1)} collective-permute-done((bf16[384,640]{1,0:T(8,128)(2,1)}, bf16[384,640]{1,0:T(8,128)(2,1)}, u32[]{:S(2)}, u32[]{:S(2)}) %collective-permute-start.6) | collective-permute-done | bytes 491552 | tf_op jit(solution)/shard_map/ppermute | solution.py:36
  56.9 3.4 %own_features.1.refs_5_ = bf16[4,384,640]{2,1,0:T(8,128)(2,1)} custom-call(s32[4]{0:T(128)} %and_select_fusion.at_ref, bf16[384,640]{1,0:T(8,128)(2,1)} %refs_0_.5, bf16[384,640]{1,0:T(8,128)(2,1)} %after.3.refs_1_, bf16[384,640]{1,0:T(8,128)(2,1)} %after.4.refs_13_.refs_2_, bf16[384,640]{1,0:T(8,128)(2,1)} %after.5.refs_3_, ...), custom_call_target="tpu_custom_call" | custom-call | flops 1024 | bytes 1024 | tf_op jit(solution)/shard_map/own_features/pallas_call | solution.py:107
  60.4 4.6 %all-to-all-start = ((bf16[4,384,640]{2,1,0:T(8,128)(2,1)}), bf16[4,384,640]{2,1,0:T(8,128)(2,1)}, u32[]{:S(2)}, u32[]{:S(2)}) async-start(bf16[4,384,640]{2,1,0:T(8,128)(2,1)} %own_features.1.refs_5_), calls=%async_computation | async-start | bytes 3932160 | tf_op jit(solution)/shard_map/all_to_all | solution.py:459
  69.2 3.8 %grad_gram.1 = (f32[4,32,1536]{2,1,0:T(8,128)}, f32[4,32,1536]{2,1,0:T(8,128)}) custom-call(s32[1]{0:T(128)} %bitcast.inner_ref, s32[4]{0:T(128)} %xor_multiply_fusion.offs_ref.toks_ref, bf16[384,640]{1,0:T(8,128)(2,1)} %refs_0_.5, bf16[384,640]{1,0:T(8,128)(2,1)} %copy-done.9, bf16[384,640]{1,0:T(8,128)(2,1)} %collective-permute-done.18.refs_4_.refs_2_, ...), custom_call_target="tpu_custom_call" | custom-call | flops 1024 | bytes 1024 | tf_op jit(solution)/shard_map/grad_gram/pallas_call | solution.py:315
  73.0 8.9 %collective-permute-done.15.refs_3_.refs_7_ = bf16[384,640]{1,0:T(8,128)(2,1)} collective-permute-done((bf16[384,640]{1,0:T(8,128)(2,1)S(1)}, bf16[384,640]{1,0:T(8,128)(2,1)}, u32[]{:S(2)}, u32[]{:S(2)}) %collective-permute-start.15) | collective-permute-done | bytes 491552 | tf_op jit(solution)/shard_map/ppermute | solution.py:36
  81.9 3.4 %other_features.1 = (bf16[384,640]{1,0:T(8,128)(2,1)}, bf16[384,640]{1,0:T(8,128)(2,1)}, bf16[384,640]{1,0:T(8,128)(2,1)}, bf16[384,640]{1,0:T(8,128)(2,1)}) custom-call(s32[4]{0:T(128)} %broadcast_xor_fusion.to_ref, bf16[384,640]{1,0:T(8,128)(2,1)} %copy-done.2, bf16[384,640]{1,0:T(8,128)(2,1)} %collective-permute-done.4.refs_1_.refs_5_, ...), custom_call_target="tpu_custom_call" | custom-call | flops 1024 | bytes 1024 | tf_op jit(solution)/shard_map/other_features/pallas_call | solution.py:135
  85.3 4.0 %all-to-all-done.refs_2_.own_ref = bf16[4,384,640]{2,1,0:T(8,128)(2,1)} async-done(((bf16[4,384,640]{2,1,0:T(8,128)(2,1)}), bf16[4,384,640]{2,1,0:T(8,128)(2,1)}, u32[]{:S(2)}, u32[]{:S(2)}) %all-to-all-start) | async-done | bytes 1966112 | tf_op jit(solution)/shard_map/all_to_all | solution.py:459
  89.3 2.3 %hidden_pair.1.refs_11_ = f32[4,32,1536]{2,1,0:T(8,128)} custom-call(f32[4,32,1536]{2,1,0:T(8,128)} %get-tuple-element.23.kept_ref, f32[4,32,1536]{2,1,0:T(8,128)} %collective-permute-done.16.refs_0_, bf16[384,640]{1,0:T(8,128)(2,1)} %get-tuple-element.25.refs_1_.refs_0_, bf16[4,384,640]{2,1,0:T(8,128)(2,1)} %all-to-all-done.refs_2_.own_ref), custom_call_target="tpu_custom_call" | custom-call | flops 1024 | bytes 1024 | tf_op jit(solution)/shard_map/hidden_pair/pallas_call | solution.py:338
  91.7 3.5 %all-to-all-start.1 = ((f32[4,32,1536]{2,1,0:T(8,128)}), f32[4,32,1536]{2,1,0:T(8,128)S(1)}, u32[]{:S(2)}, u32[]{:S(2)}) async-start(f32[4,32,1536]{2,1,0:T(8,128)} %hidden_pair.1.refs_11_), calls=%async_computation.1 | async-start | bytes 1572864 | tf_op jit(solution)/shard_map/all_to_all | solution.py:380
  99.0 15.9 %grads.1 = (bf16[384,1792]{1,0:T(8,128)(2,1)}, bf16[384,1792]{1,0:T(8,128)(2,1)}, f32[8,128]{1,0:T(8,128)}) custom-call(s32[8]{0:T(128)} %add.40.offs_ref, bf16[384,640]{1,0:T(8,128)(2,1)} %refs_0_.5, bf16[384,640]{1,0:T(8,128)(2,1)} %after.3.refs_1_, bf16[384,640]{1,0:T(8,128)(2,1)} %after.4.refs_13_.refs_2_, bf16[384,640]{1,0:T(8,128)(2,1)} %after.5.refs_3_, ...), custom_call_target="tpu_custom_call" | custom-call | flops 7046430720 | bytes 27787264 | tf_op jit(solution)/shard_map/grads/pallas_call | solution.py:174
  116.2 2.4 %grad_pair.1 = (f32[32,1536]{1,0:T(8,128)}, f32[32,1536]{1,0:T(8,128)}, f32[32,1536]{1,0:T(8,128)}, f32[32,1536]{1,0:T(8,128)}) custom-call(s32[1]{0:T(128)} %bitcast.2.outer_ref, f32[4,32,1536]{2,1,0:T(8,128)} %get-tuple-element.31.kept_ref, f32[4,32,1536]{2,1,0:T(8,128)} %collective-permute-done.23.refs_0_, f32[8,128]{1,0:T(8,128)} %get-tuple-element.32.refs_1_, ...), custom_call_target="tpu_custom_call" | custom-call | flops 1024 | bytes 1024 | tf_op jit(solution)/shard_map/grad_pair/pallas_call | solution.py:363
  118.7 1.6 %collective-permute-start.24 = (f32[32,1536]{1,0:T(8,128)}, f32[32,1536]{1,0:T(8,128)S(1)}, u32[]{:S(2)}, u32[]{:S(2)}) collective-permute-start(f32[32,1536]{1,0:T(8,128)} %get-tuple-element.35), channel_id=1, source_target_pairs={{0,2},{1,3},{2,4},{3,5},{4,6},{5,7},{6,0},{7,1},{8,10},{9,11},{10,... | collective-permute-start | bytes 589832 | tf_op jit(solution)/shard_map/ppermute | solution.py:36
  120.2 2.4 %collective-permute-start.25 = (f32[32,1536]{1,0:T(8,128)}, f32[32,1536]{1,0:T(8,128)S(1)}, u32[]{:S(2)}, u32[]{:S(2)}) collective-permute-start(f32[32,1536]{1,0:T(8,128)} %get-tuple-element.36), channel_id=1, source_target_pairs={{0,4},{1,5},{2,6},{3,7},{4,0},{5,1},{6,2},{7,3},{8,12},{9,13},{10,... | collective-permute-start | bytes 589832 | tf_op jit(solution)/shard_map/ppermute | solution.py:36
  124.1 15.4 %wgrad.1 = (bf16[1792,1280]{1,0:T(8,128)(2,1)}, f32[8,128]{1,0:T(8,128)}) custom-call(s32[2]{0:T(128)} %copy-done.13, s32[4]{0:T(128)} %xor_multiply_fusion.offs_ref.toks_ref, bf16[4,384,640]{2,1,0:T(8,128)(2,1)} %all-to-all-done.refs_2_.own_ref, bf16[384,640]{1,0:T(8,128)(2,1)} %get-tuple-element.25.refs_1_.refs_0_, ...), custom_call_target="tpu_custom_call" | custom-call | flops 28185722880 | bytes 14024704 | tf_op jit(solution)/shard_map/wgrad/pallas_call | solution.py:242
  140.3 2.2 %score_line.1 = f32[32,128]{1,0:T(8,128)} custom-call(s32[3]{0:T(128)} %assign_ref.1, f32[4,32,1536]{2,1,0:T(8,128)} %copy-done, f32[32,1536]{1,0:T(8,128)} %get-tuple-element.33.refs_16_.refs_0_, f32[32,1536]{1,0:T(8,128)} %copy-done.10, f32[32,1536]{1,0:T(8,128)} %copy-done.11, f32[32,1536]{1,0:T(8,128)} %copy-done.12, f32[8,128]{1,0:T(8,128)} %get-tuple-element.38.refs_4_), custom_call_target="tpu_custom_call" | custom-call | flops 1024 | bytes 1024 | tf_op jit(solution)/shard_map/score_line/pallas_call | solution.py:402
  142.5 3.1 %all-to-all-start.2 = ((f32[32,1,128]{2,1,0:T(1,128)}), f32[32,1,128]{2,1,0:T(1,128)S(1)}, u32[]{:S(2)}, u32[]{:S(2)}) async-start(f32[32,1,128]{2,1,0:T(1,128)} %bitcast.14), calls=%async_computation.2 | async-start | bytes 32768 | tf_op jit(solution)/shard_map/all_to_all | solution.py:479
  145.6 7.1 %all-to-all-done.2 = f32[32,1,128]{2,1,0:T(1,128)S(1)} async-done(((f32[32,1,128]{2,1,0:T(1,128)}), f32[32,1,128]{2,1,0:T(1,128)S(1)}, u32[]{:S(2)}, u32[]{:S(2)}) %all-to-all-start.2) | async-done | bytes 16416 | tf_op jit(solution)/shard_map/all_to_all | solution.py:479
  (92 shorter events, 31.3 us)
Async XLA Ops:
  0.6 19.0 %collective-permute-start.1 = (bf16[384,640]{1,0:T(8,128)(2,1)}, bf16[384,640]{1,0:T(8,128)(2,1)S(1)}, u32[]{:S(2)}, u32[]{:S(2)}) collective-permute-start(bf16[384,640]{1,0:T(8,128)(2,1)} %refs_0_.5), channel_id=1, source_target_pairs={{0,1},{1,0},{2,3},{3,2},{4,5},{5,4},{6,7},{7,6},{8,9},{9,8},{10,11... | collective-permute-start | bytes 1474568 | tf_op jit(solution)/shard_map/ppermute | solution.py:31
  3.6 16.0 %collective-permute-start = (bf16[384,640]{1,0:T(8,128)(2,1)}, bf16[384,640]{1,0:T(8,128)(2,1)S(1)}, u32[]{:S(2)}, u32[]{:S(2)}) collective-permute-start(bf16[384,640]{1,0:T(8,128)(2,1)} %refs_0_.5), channel_id=1, source_target_pairs={{0,2},{1,3},{2,4},{3,5},{4,6},{5,7},{6,0},{7,1},{8,10},{9,11},{10,... | collective-permute-start | bytes 1474568 | tf_op jit(solution)/shard_map/ppermute | solution.py:36
  7.2 12.4 %collective-permute-start.2 = (bf16[512,384]{1,0:T(8,128)(2,1)}, bf16[512,384]{1,0:T(8,128)(2,1)}, u32[]{:S(2)}, u32[]{:S(2)}) collective-permute-start(bf16[512,384]{1,0:T(8,128)(2,1)} %hidden_0.1.refs_0_.refs_4_), channel_id=1, source_target_pairs={{0,16},{8,24},{16,0},{24,8},{1,17},{9,25},{17,1},{25,9},{2,18},{10... | collective-permute-start | bytes 1179656 | tf_op jit(solution)/shard_map/ppermute | solution.py:31
  12.0 27.0 %collective-permute-start.5 = (bf16[768,384]{1,0:T(8,128)(2,1)}, bf16[768,384]{1,0:T(8,128)(2,1)}, u32[]{:S(2)}, u32[]{:S(2)}) collective-permute-start(bf16[768,384]{1,0:T(8,128)(2,1)} %hidden_2.1.refs_4_.refs_8_), channel_id=1, source_target_pairs={{0,16},{8,24},{16,0},{24,8},{1,17},{9,25},{17,1},{25,9},{2,18},{10... | collective-permute-start | bytes 1769480 | tf_op jit(solution)/shard_map/ppermute | solution.py:31
  21.2 18.2 %collective-permute-start.4 = (bf16[384,640]{1,0:T(8,128)(2,1)}, bf16[384,640]{1,0:T(8,128)(2,1)}, u32[]{:S(2)}, u32[]{:S(2)}) collective-permute-start(bf16[384,640]{1,0:T(8,128)(2,1)} %after.3.refs_1_), channel_id=1, source_target_pairs={{0,1},{1,0},{2,3},{3,2},{4,5},{5,4},{6,7},{7,6},{8,9},{9,8},{10,11... | collective-permute-start | bytes 1474568 | tf_op jit(solution)/shard_map/ppermute | solution.py:31
  23.8 15.1 %collective-permute-start.13 = (bf16[512,384]{1,0:T(8,128)(2,1)}, bf16[512,384]{1,0:T(8,128)(2,1)}, u32[]{:S(2)}, u32[]{:S(2)}) collective-permute-start(bf16[512,384]{1,0:T(8,128)(2,1)} %hidden_5.1.refs_8_.refs_12_), channel_id=1, source_target_pairs={{0,16},{8,24},{16,0},{24,8},{1,17},{9,25},{17,1},{25,9},{2,18},{10... | collective-permute-start | bytes 1179656 | tf_op jit(solution)/shard_map/ppermute | solution.py:31
  25.3 14.2 %collective-permute-start.3 = (bf16[384,640]{1,0:T(8,128)(2,1)S(1)}, bf16[384,640]{1,0:T(8,128)(2,1)S(1)}, u32[]{:S(2)}, u32[]{:S(2)}) collective-permute-start(bf16[384,640]{1,0:T(8,128)(2,1)S(1)} %copy-done.4), channel_id=1, source_target_pairs={{0,2},{1,3},{2,4},{3,5},{4,6},{5,7},{6,0},{7,1},{8,10},{9,11},{10,... | collective-permute-start | bytes 1474568 | tf_op jit(solution)/shard_map/ppermute | solution.py:36
  26.9 16.2 %collective-permute-start.10 = (bf16[768,384]{1,0:T(8,128)(2,1)}, bf16[768,384]{1,0:T(8,128)(2,1)}, u32[]{:S(2)}, u32[]{:S(2)}) collective-permute-start(bf16[768,384]{1,0:T(8,128)(2,1)} %hidden_2.1.refs_4_.refs_8_), channel_id=1, source_target_pairs={{0,8},{8,0},{16,24},{24,16},{1,9},{9,1},{17,25},{25,17},{2,10},{10... | collective-permute-start | bytes 1769480 | tf_op jit(solution)/shard_map/ppermute | solution.py:31
  39.5 7.2 %collective-permute-start.11 = (bf16[768,384]{1,0:T(8,128)(2,1)}, bf16[768,384]{1,0:T(8,128)(2,1)}, u32[]{:S(2)}, u32[]{:S(2)}) collective-permute-start(bf16[768,384]{1,0:T(8,128)(2,1)} %collective-permute-done.5.refs_2_.refs_6_.refs_10_), channel_id=1, source_target_pairs={{0,8},{8,0},{16,24},{24,16},{1,9},{9,1},{17,25},{25,17},{2,10},{10... | collective-permute-start | bytes 1769480 | tf_op jit(solution)/shard_map/ppermute | solution.py:31
  41.0 13.5 %collective-permute-start.7 = (bf16[384,640]{1,0:T(8,128)(2,1)}, bf16[384,640]{1,0:T(8,128)(2,1)S(1)}, u32[]{:S(2)}, u32[]{:S(2)}) collective-permute-start(bf16[384,640]{1,0:T(8,128)(2,1)} %after.4.refs_13_.refs_2_), channel_id=1, source_target_pairs={{0,1},{1,0},{2,3},{3,2},{4,5},{5,4},{6,7},{7,6},{8,9},{9,8},{10,11... | collective-permute-start | bytes 1474568 | tf_op jit(solution)/shard_map/ppermute | solution.py:31
  41.5 15.4 %collective-permute-start.6 = (bf16[384,640]{1,0:T(8,128)(2,1)}, bf16[384,640]{1,0:T(8,128)(2,1)}, u32[]{:S(2)}, u32[]{:S(2)}) collective-permute-start(bf16[384,640]{1,0:T(8,128)(2,1)} %after.4.refs_13_.refs_2_), channel_id=1, source_target_pairs={{0,2},{1,3},{2,4},{3,5},{4,6},{5,7},{6,0},{7,1},{8,10},{9,11},{10,... | collective-permute-start | bytes 1474568 | tf_op jit(solution)/shard_map/ppermute | solution.py:36
  43.1 13.8 %collective-permute-start.18 = (bf16[384,640]{1,0:T(8,128)(2,1)S(1)}, bf16[384,640]{1,0:T(8,128)(2,1)}, u32[]{:S(2)}, u32[]{:S(2)}) collective-permute-start(bf16[384,640]{1,0:T(8,128)(2,1)S(1)} %copy-done.5), channel_id=1, source_target_pairs={{0,16},{8,24},{16,0},{24,8},{1,17},{9,25},{17,1},{25,9},{2,18},{10... | collective-permute-start | bytes 1474568 | tf_op jit(solution)/shard_map/ppermute | solution.py:31
  60.4 28.9 %all-to-all-start = ((bf16[4,384,640]{2,1,0:T(8,128)(2,1)}), bf16[4,384,640]{2,1,0:T(8,128)(2,1)}, u32[]{:S(2)}, u32[]{:S(2)}) async-start(bf16[4,384,640]{2,1,0:T(8,128)(2,1)} %own_features.1.refs_5_), calls=%async_computation | async-start | bytes 3932160 | tf_op jit(solution)/shard_map/all_to_all | solution.py:459
  65.0 20.3 %collective-permute-start.16 = (f32[4,32,1536]{2,1,0:T(8,128)}, f32[4,32,1536]{2,1,0:T(8,128)}, u32[]{:S(2)}, u32[]{:S(2)}) collective-permute-start(f32[4,32,1536]{2,1,0:T(8,128)} %get-tuple-element.22.refs_2_), channel_id=1, source_target_pairs={{0,1},{1,0},{2,3},{3,2},{4,5},{5,4},{6,7},{7,6},{8,9},{9,8},{10,11... | collective-permute-start | bytes 2359304 | tf_op jit(solution)/shard_map/ppermute | solution.py:31
  66.8 15.1 %collective-permute-start.15 = (bf16[384,640]{1,0:T(8,128)(2,1)S(1)}, bf16[384,640]{1,0:T(8,128)(2,1)}, u32[]{:S(2)}, u32[]{:S(2)}) collective-permute-start(bf16[384,640]{1,0:T(8,128)(2,1)S(1)} %copy-done.8), channel_id=1, source_target_pairs={{0,2},{1,3},{2,4},{3,5},{4,6},{5,7},{6,0},{7,1},{8,10},{9,11},{10,... | collective-permute-start | bytes 1474568 | tf_op jit(solution)/shard_map/ppermute | solution.py:36
  91.7 23.7 %all-to-all-start.1 = ((f32[4,32,1536]{2,1,0:T(8,128)}), f32[4,32,1536]{2,1,0:T(8,128)S(1)}, u32[]{:S(2)}, u32[]{:S(2)}) async-start(f32[4,32,1536]{2,1,0:T(8,128)} %hidden_pair.1.refs_11_), calls=%async_computation.1 | async-start | bytes 1572864 | tf_op jit(solution)/shard_map/all_to_all | solution.py:380
  95.3 19.6 %collective-permute-start.23 = (f32[4,32,1536]{2,1,0:T(8,128)}, f32[4,32,1536]{2,1,0:T(8,128)}, u32[]{:S(2)}, u32[]{:S(2)}) collective-permute-start(f32[4,32,1536]{2,1,0:T(8,128)} %get-tuple-element.24.refs_4_), channel_id=1, source_target_pairs={{0,1},{1,0},{2,3},{3,2},{4,5},{5,4},{6,7},{7,6},{8,9},{9,8},{10,11... | collective-permute-start | bytes 2359304 | tf_op jit(solution)/shard_map/ppermute | solution.py:31
  97.1 25.5 %collective-permute-start.20 = (bf16[384,640]{1,0:T(8,128)(2,1)}, bf16[384,640]{1,0:T(8,128)(2,1)}, u32[]{:S(2)}, u32[]{:S(2)}) collective-permute-start(bf16[384,640]{1,0:T(8,128)(2,1)} %get-tuple-element.28), channel_id=1, source_target_pairs={{0,8},{8,0},{16,24},{24,16},{1,9},{9,1},{17,25},{25,17},{2,10},{10... | collective-permute-start | bytes 1474568 | tf_op jit(solution)/shard_map/ppermute | solution.py:31
  97.1 26.9 %collective-permute-start.21 = (bf16[384,640]{1,0:T(8,128)(2,1)}, bf16[384,640]{1,0:T(8,128)(2,1)}, u32[]{:S(2)}, u32[]{:S(2)}) collective-permute-start(bf16[384,640]{1,0:T(8,128)(2,1)} %get-tuple-element.29), channel_id=1, source_target_pairs={{0,16},{8,24},{16,0},{24,8},{1,17},{9,25},{17,1},{25,9},{2,18},{10... | collective-permute-start | bytes 1474568 | tf_op jit(solution)/shard_map/ppermute | solution.py:31
  97.5 26.6 %collective-permute-start.22 = (bf16[384,640]{1,0:T(8,128)(2,1)}, bf16[384,640]{1,0:T(8,128)(2,1)}, u32[]{:S(2)}, u32[]{:S(2)}) collective-permute-start(bf16[384,640]{1,0:T(8,128)(2,1)} %get-tuple-element.30), channel_id=1, source_target_pairs={{0,24},{8,16},{16,8},{24,0},{1,25},{9,17},{17,9},{25,1},{2,26},{10... | collective-permute-start | bytes 1474568 | tf_op jit(solution)/shard_map/ppermute | solution.py:31
  118.7 20.8 %collective-permute-start.24 = (f32[32,1536]{1,0:T(8,128)}, f32[32,1536]{1,0:T(8,128)S(1)}, u32[]{:S(2)}, u32[]{:S(2)}) collective-permute-start(f32[32,1536]{1,0:T(8,128)} %get-tuple-element.35), channel_id=1, source_target_pairs={{0,2},{1,3},{2,4},{3,5},{4,6},{5,7},{6,0},{7,1},{8,10},{9,11},{10,... | collective-permute-start | bytes 589832 | tf_op jit(solution)/shard_map/ppermute | solution.py:36
  120.2 19.3 %collective-permute-start.25 = (f32[32,1536]{1,0:T(8,128)}, f32[32,1536]{1,0:T(8,128)S(1)}, u32[]{:S(2)}, u32[]{:S(2)}) collective-permute-start(f32[32,1536]{1,0:T(8,128)} %get-tuple-element.36), channel_id=1, source_target_pairs={{0,4},{1,5},{2,6},{3,7},{4,0},{5,1},{6,2},{7,3},{8,12},{9,13},{10,... | collective-permute-start | bytes 589832 | tf_op jit(solution)/shard_map/ppermute | solution.py:36
  122.6 16.9 %collective-permute-start.26 = (f32[32,1536]{1,0:T(8,128)}, f32[32,1536]{1,0:T(8,128)S(1)}, u32[]{:S(2)}, u32[]{:S(2)}) collective-permute-start(f32[32,1536]{1,0:T(8,128)} %get-tuple-element.37), channel_id=1, source_target_pairs={{0,6},{1,7},{2,0},{3,1},{4,2},{5,3},{6,4},{7,5},{8,14},{9,15},{10,... | collective-permute-start | bytes 589832 | tf_op jit(solution)/shard_map/ppermute | solution.py:36
  142.5 10.2 %all-to-all-start.2 = ((f32[32,1,128]{2,1,0:T(1,128)}), f32[32,1,128]{2,1,0:T(1,128)S(1)}, u32[]{:S(2)}, u32[]{:S(2)}) async-start(f32[32,1,128]{2,1,0:T(1,128)} %bitcast.14), calls=%async_computation.2 | async-start | bytes 32768 | tf_op jit(solution)/shard_map/all_to_all | solution.py:479
  (20 other events, 65.1 us)

commit v17 on v16

--- a/solution.py
+++ b/solution.py
@@ -443,7 +443,7 @@
     ring, others = [out_grad], [swap(out_grad, "fsdp", 1)]
     for step in range(2):
         came = shift(ring[-1], "fsdp", 2)
-        ring.append(after(came, others[-1], hids[step][2]))
+        ring.append(after(came, others[-1], hids[step][2], hids[step][1]))
         others.append(swap(ring[-1], "fsdp", 1))
     for part in hids:
         part[3] = swap(part[2], "dp", 1)

time: 155 us -> 153 us (0.987)
  starting transfers between devices: 37.2 us -> 35.6 us
    ppermute x7, waiting for transfers between devices: 11.4 us -> 14.2 us  [shift(): return lax.ppermute(x, axis, [(s, (s + k) % n) for s in range(n)])]
    unnamed x29 -> x27, local copies, waits for them, and re-layouts: 5.06 us -> 4.71 us
  transfers between devices with their start and end apart: 30 -> 30, of which waited for: 11 -> 13; matrix products, arithmetic and copies ran while one was open for 2% -> 2% of each run, Pallas kernels for 35% -> 34%
where the time goes in v17:
time: 153 us
  Pallas kernels  62.4 us (41%)
  waiting for transfers between devices  45.8 us (30%)
  starting transfers between devices  35.6 us (23%)
  local copies, waits for them, and re-layouts  5.53 us (4%)
  other arithmetic  2.42 us (2%)
    ppermute x20, waiting for transfers between devices, swap(): return lax.ppermute(x, axis, [(s, s ^ k) for s in range(n)])  21.5 us
    pallas_call x1, Pallas kernels, grads(): pl.pallas_call(functools.partial(grads_body, n), grid_spec=pltpu.Prefetch...  15.9 us
    pallas_call x1, Pallas kernels, wgrad(): pl.pallas_call(functools.partial(wgrad_body, n, tuple(starts)), in_specs=...  15.4 us
    ppermute x20, starting transfers between devices, swap(): return lax.ppermute(x, axis, [(s, s ^ k) for s in range(n)])  14.8 us
    ppermute x7, waiting for transfers between devices, shift(): return lax.ppermute(x, axis, [(s, (s + k) % n) for s in range(n)])  14.2 us
    pallas_call x2, Pallas kernels, gram(): pl.pallas_call(functools.partial(body, len(toks), cuts), grid=(1,), in_sp...  9.96 us
    ppermute x7, starting transfers between devices, shift(): return lax.ppermute(x, axis, [(s, (s + k) % n) for s in range(n)])  9.9 us
    pallas_call x3, Pallas kernels, hidden_units(): pl.pallas_call(hidden_body, grid=(count,), in_specs=[cols, cols], out_spe...  7.33 us
  transfers between devices with their start and end apart: 30, of which 13 were waited for; matrix products, arithmetic and copies ran while one was open for 2% of the time, Pallas kernels for 34%

profile of v17, /device:TPU:0, one launch (start us, length us, event | category | flops | bytes accessed | tf_op | source)
XLA Modules:
  0.0 152.6 jit_solution(4660949530692807298)
XLA Ops:
  0.6 2.1 %hidden_0.1.refs_0_.refs_4_ = bf16[512,384]{1,0:T(8,128)(2,1)} custom-call(bf16[384,1792]{1,0:T(8,128)(2,1)} %refs_9_.1, bf16[384,1792]{1,0:T(8,128)(2,1)} %refs_10_.1), custom_call_target="tpu_custom_call" | custom-call | flops 1024 | bytes 1024 | tf_op jit(solution)/shard_map/hidden_0/pallas_call | solution.py:81
  3.2 2.5 %collective-permute-start.2 = (bf16[512,384]{1,0:T(8,128)(2,1)}, bf16[512,384]{1,0:T(8,128)(2,1)}, u32[]{:S(2)}, u32[]{:S(2)}) collective-permute-start(bf16[512,384]{1,0:T(8,128)(2,1)} %hidden_0.1.refs_0_.refs_4_), channel_id=1, source_target_pairs={{0,16},{8,24},{16,0},{24,8},{1,17},{9,25},{17,1},{25,9},{2,18},{10... | collective-permute-start | bytes 1179656 | tf_op jit(solution)/shard_map/ppermute | solution.py:31
  8.8 3.2 %hidden_2.1.refs_4_.refs_8_ = bf16[768,384]{1,0:T(8,128)(2,1)} custom-call(bf16[384,1792]{1,0:T(8,128)(2,1)} %refs_9_.1, bf16[384,1792]{1,0:T(8,128)(2,1)} %refs_10_.1), custom_call_target="tpu_custom_call" | custom-call | flops 1024 | bytes 1024 | tf_op jit(solution)/shard_map/hidden_2/pallas_call | solution.py:81
  19.1 3.2 %collective-permute-done.refs_0_ = bf16[384,640]{1,0:T(8,128)(2,1)} collective-permute-done((bf16[384,640]{1,0:T(8,128)(2,1)S(1)}, bf16[384,640]{1,0:T(8,128)(2,1)}, u32[]{:S(2)}, u32[]{:S(2)}) %collective-permute-start) | collective-permute-done | bytes 491552 | tf_op jit(solution)/shard_map/ppermute | solution.py:36
  23.0 3.3 %collective-permute-done.13.refs_10_.refs_14_ = bf16[512,384]{1,0:T(8,128)(2,1)} collective-permute-done((bf16[512,384]{1,0:T(8,128)(2,1)}, bf16[512,384]{1,0:T(8,128)(2,1)}, u32[]{:S(2)}, u32[]{:S(2)}) %collective-permute-start.13) | collective-permute-done | bytes 393248 | tf_op jit(solution)/shard_map/ppermute | solution.py:31
  26.8 11.7 %collective-permute-done.6.refs_2_.refs_6_.refs_10_ = bf16[768,384]{1,0:T(8,128)(2,1)} collective-permute-done((bf16[768,384]{1,0:T(8,128)(2,1)}, bf16[768,384]{1,0:T(8,128)(2,1)}, u32[]{:S(2)}, u32[]{:S(2)}) %collective-permute-start.6) | collective-permute-done | bytes 589856 | tf_op jit(solution)/shard_map/ppermute | solution.py:31
  44.6 6.2 %hidden_gram.1 = (f32[4,32,1536]{2,1,0:T(8,128)}, f32[4,32,1536]{2,1,0:T(8,128)}) custom-call(s32[1]{0:T(128)} %bitcast.inner_ref, s32[4]{0:T(128)} %xor_multiply_fusion.offs_ref.toks_ref, bf16[512,384]{1,0:T(8,128)(2,1)} %hidden_0.1.refs_0_.refs_4_, bf16[512,384]{1,0:T(8,128)(2,1)} %collective-permute-done.3.refs_3_.refs_1_.refs_5_, ...), custom_call_target="tpu_custom_call" | custom-call | flops 1024 | bytes 1024 | tf_op jit(solution)/shard_map/hidden_gram/pallas_call | solution.py:315
  50.7 2.4 %collective-permute-done.9.refs_1_.refs_2_.refs_6_ = bf16[384,640]{1,0:T(8,128)(2,1)S(1)} collective-permute-done((bf16[384,640]{1,0:T(8,128)(2,1)}, bf16[384,640]{1,0:T(8,128)(2,1)S(1)}, u32[]{:S(2)}, u32[]{:S(2)}) %collective-permute-start.9) | collective-permute-done | bytes 491552 | tf_op jit(solution)/shard_map/ppermute | solution.py:31
  53.2 2.2 %collective-permute-done.8.refs_0_ = bf16[384,640]{1,0:T(8,128)(2,1)} collective-permute-done((bf16[384,640]{1,0:T(8,128)(2,1)}, bf16[384,640]{1,0:T(8,128)(2,1)}, u32[]{:S(2)}, u32[]{:S(2)}) %collective-permute-start.8) | collective-permute-done | bytes 491552 | tf_op jit(solution)/shard_map/ppermute | solution.py:36
  55.3 3.4 %own_features.1.refs_5_ = bf16[4,384,640]{2,1,0:T(8,128)(2,1)} custom-call(s32[4]{0:T(128)} %and_select_fusion.at_ref, bf16[384,640]{1,0:T(8,128)(2,1)} %refs_0_.5, bf16[384,640]{1,0:T(8,128)(2,1)} %after.3.refs_1_, bf16[384,640]{1,0:T(8,128)(2,1)} %after.4.refs_13_.refs_2_, bf16[384,640]{1,0:T(8,128)(2,1)} %after.5.refs_3_, ...), custom_call_target="tpu_custom_call" | custom-call | flops 1024 | bytes 1024 | tf_op jit(solution)/shard_map/own_features/pallas_call | solution.py:107
  58.8 4.6 %all-to-all-start = ((bf16[4,384,640]{2,1,0:T(8,128)(2,1)}), bf16[4,384,640]{2,1,0:T(8,128)(2,1)}, u32[]{:S(2)}, u32[]{:S(2)}) async-start(bf16[4,384,640]{2,1,0:T(8,128)(2,1)} %own_features.1.refs_5_), calls=%async_computation | async-start | bytes 3932160 | tf_op jit(solution)/shard_map/all_to_all | solution.py:459
  67.9 3.8 %grad_gram.1 = (f32[4,32,1536]{2,1,0:T(8,128)}, f32[4,32,1536]{2,1,0:T(8,128)}) custom-call(s32[1]{0:T(128)} %bitcast.inner_ref, s32[4]{0:T(128)} %xor_multiply_fusion.offs_ref.toks_ref, bf16[384,640]{1,0:T(8,128)(2,1)} %refs_0_.5, bf16[384,640]{1,0:T(8,128)(2,1)} %copy-done.8, bf16[384,640]{1,0:T(8,128)(2,1)} %collective-permute-done.18.refs_4_.refs_2_, ...), custom_call_target="tpu_custom_call" | custom-call | flops 1024 | bytes 1024 | tf_op jit(solution)/shard_map/grad_gram/pallas_call | solution.py:315
  71.7 8.8 %collective-permute-done.15.refs_3_.refs_7_ = bf16[384,640]{1,0:T(8,128)(2,1)S(1)} collective-permute-done((bf16[384,640]{1,0:T(8,128)(2,1)S(1)}, bf16[384,640]{1,0:T(8,128)(2,1)S(1)}, u32[]{:S(2)}, u32[]{:S(2)}) %collective-permute-start.15) | collective-permute-done | bytes 491552 | tf_op jit(solution)/shard_map/ppermute | solution.py:36
  81.3 3.5 %other_features.1 = (bf16[384,640]{1,0:T(8,128)(2,1)}, bf16[384,640]{1,0:T(8,128)(2,1)}, bf16[384,640]{1,0:T(8,128)(2,1)}, bf16[384,640]{1,0:T(8,128)(2,1)}) custom-call(s32[4]{0:T(128)} %broadcast_xor_fusion.to_ref, bf16[384,640]{1,0:T(8,128)(2,1)} %copy-done.4, bf16[384,640]{1,0:T(8,128)(2,1)} %collective-permute-done.5.refs_1_.refs_5_, ...), custom_call_target="tpu_custom_call" | custom-call | flops 1024 | bytes 1024 | tf_op jit(solution)/shard_map/other_features/pallas_call | solution.py:135
  84.7 3.0 %all-to-all-done.refs_2_.own_ref = bf16[4,384,640]{2,1,0:T(8,128)(2,1)} async-done(((bf16[4,384,640]{2,1,0:T(8,128)(2,1)}), bf16[4,384,640]{2,1,0:T(8,128)(2,1)}, u32[]{:S(2)}, u32[]{:S(2)}) %all-to-all-start) | async-done | bytes 1966112 | tf_op jit(solution)/shard_map/all_to_all | solution.py:459
  87.7 2.3 %hidden_pair.1.refs_11_ = f32[4,32,1536]{2,1,0:T(8,128)} custom-call(f32[4,32,1536]{2,1,0:T(8,128)} %get-tuple-element.23.kept_ref, f32[4,32,1536]{2,1,0:T(8,128)} %collective-permute-done.16.refs_0_, bf16[384,640]{1,0:T(8,128)(2,1)} %get-tuple-element.25.refs_1_.refs_0_, bf16[4,384,640]{2,1,0:T(8,128)(2,1)} %all-to-all-done.refs_2_.own_ref), custom_call_target="tpu_custom_call" | custom-call | flops 1024 | bytes 1024 | tf_op jit(solution)/shard_map/hidden_pair/pallas_call | solution.py:338
  90.0 3.5 %all-to-all-start.1 = ((f32[4,32,1536]{2,1,0:T(8,128)}), f32[4,32,1536]{2,1,0:T(8,128)S(1)}, u32[]{:S(2)}, u32[]{:S(2)}) async-start(f32[4,32,1536]{2,1,0:T(8,128)} %hidden_pair.1.refs_11_), calls=%async_computation.1 | async-start | bytes 1572864 | tf_op jit(solution)/shard_map/all_to_all | solution.py:380
  97.7 15.9 %grads.1 = (bf16[384,1792]{1,0:T(8,128)(2,1)}, bf16[384,1792]{1,0:T(8,128)(2,1)}, f32[8,128]{1,0:T(8,128)}) custom-call(s32[8]{0:T(128)} %add.40.offs_ref, bf16[384,640]{1,0:T(8,128)(2,1)} %refs_0_.5, bf16[384,640]{1,0:T(8,128)(2,1)} %after.3.refs_1_, bf16[384,640]{1,0:T(8,128)(2,1)} %after.4.refs_13_.refs_2_, bf16[384,640]{1,0:T(8,128)(2,1)} %after.5.refs_3_, ...), custom_call_target="tpu_custom_call" | custom-call | flops 7046430720 | bytes 27787264 | tf_op jit(solution)/shard_map/grads/pallas_call | solution.py:174
  114.6 2.3 %grad_pair.1 = (f32[32,1536]{1,0:T(8,128)}, f32[32,1536]{1,0:T(8,128)}, f32[32,1536]{1,0:T(8,128)}, f32[32,1536]{1,0:T(8,128)}) custom-call(s32[1]{0:T(128)} %bitcast.2.outer_ref, f32[4,32,1536]{2,1,0:T(8,128)} %get-tuple-element.31.kept_ref, f32[4,32,1536]{2,1,0:T(8,128)} %collective-permute-done.23.refs_0_, f32[8,128]{1,0:T(8,128)} %get-tuple-element.32.refs_1_, ...), custom_call_target="tpu_custom_call" | custom-call | flops 1024 | bytes 1024 | tf_op jit(solution)/shard_map/grad_pair/pallas_call | solution.py:363
  118.8 2.4 %collective-permute-start.25 = (f32[32,1536]{1,0:T(8,128)}, f32[32,1536]{1,0:T(8,128)S(1)}, u32[]{:S(2)}, u32[]{:S(2)}) collective-permute-start(f32[32,1536]{1,0:T(8,128)} %get-tuple-element.36), channel_id=1, source_target_pairs={{0,4},{1,5},{2,6},{3,7},{4,0},{5,1},{6,2},{7,3},{8,12},{9,13},{10,... | collective-permute-start | bytes 589832 | tf_op jit(solution)/shard_map/ppermute | solution.py:36
  122.7 15.4 %wgrad.1 = (bf16[1792,1280]{1,0:T(8,128)(2,1)}, f32[8,128]{1,0:T(8,128)}) custom-call(s32[2]{0:T(128)} %copy-done.12, s32[4]{0:T(128)} %xor_multiply_fusion.offs_ref.toks_ref, bf16[4,384,640]{2,1,0:T(8,128)(2,1)} %all-to-all-done.refs_2_.own_ref, bf16[384,640]{1,0:T(8,128)(2,1)} %get-tuple-element.25.refs_1_.refs_0_, ...), custom_call_target="tpu_custom_call" | custom-call | flops 28185722880 | bytes 14024704 | tf_op jit(solution)/shard_map/wgrad/pallas_call | solution.py:242
  138.9 2.2 %score_line.1 = f32[32,128]{1,0:T(8,128)} custom-call(s32[3]{0:T(128)} %assign_ref.1, f32[4,32,1536]{2,1,0:T(8,128)} %copy-done, f32[32,1536]{1,0:T(8,128)} %get-tuple-element.33.refs_16_.refs_0_, f32[32,1536]{1,0:T(8,128)} %copy-done.9, f32[32,1536]{1,0:T(8,128)} %copy-done.10, f32[32,1536]{1,0:T(8,128)} %copy-done.11, f32[8,128]{1,0:T(8,128)} %get-tuple-element.38.refs_4_), custom_call_target="tpu_custom_call" | custom-call | flops 1024 | bytes 1024 | tf_op jit(solution)/shard_map/score_line/pallas_call | solution.py:402
  141.1 2.8 %all-to-all-start.2 = ((f32[32,1,128]{2,1,0:T(1,128)}), f32[32,1,128]{2,1,0:T(1,128)S(1)}, u32[]{:S(2)}, u32[]{:S(2)}) async-start(f32[32,1,128]{2,1,0:T(1,128)} %bitcast.14), calls=%async_computation.2 | async-start | bytes 32768 | tf_op jit(solution)/shard_map/all_to_all | solution.py:479
  143.9 7.1 %all-to-all-done.2 = f32[32,1,128]{2,1,0:T(1,128)S(1)} async-done(((f32[32,1,128]{2,1,0:T(1,128)}), f32[32,1,128]{2,1,0:T(1,128)S(1)}, u32[]{:S(2)}, u32[]{:S(2)}) %all-to-all-start.2) | async-done | bytes 16416 | tf_op jit(solution)/shard_map/all_to_all | solution.py:479
  (90 shorter events, 34.0 us)
Async XLA Ops:
  3.2 12.6 %collective-permute-start.2 = (bf16[512,384]{1,0:T(8,128)(2,1)}, bf16[512,384]{1,0:T(8,128)(2,1)}, u32[]{:S(2)}, u32[]{:S(2)}) collective-permute-start(bf16[512,384]{1,0:T(8,128)(2,1)} %hidden_0.1.refs_0_.refs_4_), channel_id=1, source_target_pairs={{0,16},{8,24},{16,0},{24,8},{1,17},{9,25},{17,1},{25,9},{2,18},{10... | collective-permute-start | bytes 1179656 | tf_op jit(solution)/shard_map/ppermute | solution.py:31
  5.7 13.4 %collective-permute-start.1 = (bf16[384,640]{1,0:T(8,128)(2,1)S(1)}, bf16[384,640]{1,0:T(8,128)(2,1)S(1)}, u32[]{:S(2)}, u32[]{:S(2)}) collective-permute-start(bf16[384,640]{1,0:T(8,128)(2,1)S(1)} %copy-done.2), channel_id=1, source_target_pairs={{0,1},{1,0},{2,3},{3,2},{4,5},{5,4},{6,7},{7,6},{8,9},{9,8},{10,11... | collective-permute-start | bytes 1474568 | tf_op jit(solution)/shard_map/ppermute | solution.py:31
  7.2 15.0 %collective-permute-start = (bf16[384,640]{1,0:T(8,128)(2,1)S(1)}, bf16[384,640]{1,0:T(8,128)(2,1)}, u32[]{:S(2)}, u32[]{:S(2)}) collective-permute-start(bf16[384,640]{1,0:T(8,128)(2,1)S(1)} %copy-done.2), channel_id=1, source_target_pairs={{0,2},{1,3},{2,4},{3,5},{4,6},{5,7},{6,0},{7,1},{8,10},{9,11},{10,... | collective-permute-start | bytes 1474568 | tf_op jit(solution)/shard_map/ppermute | solution.py:36
  12.0 14.3 %collective-permute-start.7 = (bf16[768,384]{1,0:T(8,128)(2,1)}, bf16[768,384]{1,0:T(8,128)(2,1)}, u32[]{:S(2)}, u32[]{:S(2)}) collective-permute-start(bf16[768,384]{1,0:T(8,128)(2,1)} %hidden_2.1.refs_4_.refs_8_), channel_id=1, source_target_pairs={{0,8},{8,0},{16,24},{24,16},{1,9},{9,1},{17,25},{25,17},{2,10},{10... | collective-permute-start | bytes 1769480 | tf_op jit(solution)/shard_map/ppermute | solution.py:31
  14.0 12.2 %collective-permute-start.13 = (bf16[512,384]{1,0:T(8,128)(2,1)}, bf16[512,384]{1,0:T(8,128)(2,1)}, u32[]{:S(2)}, u32[]{:S(2)}) collective-permute-start(bf16[512,384]{1,0:T(8,128)(2,1)} %hidden_5.1.refs_8_.refs_12_), channel_id=1, source_target_pairs={{0,16},{8,24},{16,0},{24,8},{1,17},{9,25},{17,1},{25,9},{2,18},{10... | collective-permute-start | bytes 1179656 | tf_op jit(solution)/shard_map/ppermute | solution.py:31
  15.8 22.7 %collective-permute-start.6 = (bf16[768,384]{1,0:T(8,128)(2,1)}, bf16[768,384]{1,0:T(8,128)(2,1)}, u32[]{:S(2)}, u32[]{:S(2)}) collective-permute-start(bf16[768,384]{1,0:T(8,128)(2,1)} %hidden_2.1.refs_4_.refs_8_), channel_id=1, source_target_pairs={{0,16},{8,24},{16,0},{24,8},{1,17},{9,25},{17,1},{25,9},{2,18},{10... | collective-permute-start | bytes 1769480 | tf_op jit(solution)/shard_map/ppermute | solution.py:31
  22.2 16.3 %collective-permute-start.5 = (bf16[384,640]{1,0:T(8,128)(2,1)}, bf16[384,640]{1,0:T(8,128)(2,1)}, u32[]{:S(2)}, u32[]{:S(2)}) collective-permute-start(bf16[384,640]{1,0:T(8,128)(2,1)} %after.3.refs_1_), channel_id=1, source_target_pairs={{0,1},{1,0},{2,3},{3,2},{4,5},{5,4},{6,7},{7,6},{8,9},{9,8},{10,11... | collective-permute-start | bytes 1474568 | tf_op jit(solution)/shard_map/ppermute | solution.py:31
  22.8 15.7 %collective-permute-start.4 = (bf16[384,640]{1,0:T(8,128)(2,1)}, bf16[384,640]{1,0:T(8,128)(2,1)S(1)}, u32[]{:S(2)}, u32[]{:S(2)}) collective-permute-start(bf16[384,640]{1,0:T(8,128)(2,1)} %after.3.refs_1_), channel_id=1, source_target_pairs={{0,2},{1,3},{2,4},{3,5},{4,6},{5,7},{6,0},{7,1},{8,10},{9,11},{10,... | collective-permute-start | bytes 1474568 | tf_op jit(solution)/shard_map/ppermute | solution.py:36
  26.3 15.2 %collective-permute-start.12 = (bf16[512,384]{1,0:T(8,128)(2,1)}, bf16[512,384]{1,0:T(8,128)(2,1)}, u32[]{:S(2)}, u32[]{:S(2)}) collective-permute-start(bf16[512,384]{1,0:T(8,128)(2,1)} %hidden_5.1.refs_8_.refs_12_), channel_id=1, source_target_pairs={{0,8},{8,0},{16,24},{24,16},{1,9},{9,1},{17,25},{25,17},{2,10},{10... | collective-permute-start | bytes 1179656 | tf_op jit(solution)/shard_map/ppermute | solution.py:31
  26.3 16.2 %collective-permute-start.14 = (bf16[512,384]{1,0:T(8,128)(2,1)}, bf16[512,384]{1,0:T(8,128)(2,1)}, u32[]{:S(2)}, u32[]{:S(2)}) collective-permute-start(bf16[512,384]{1,0:T(8,128)(2,1)} %collective-permute-done.13.refs_10_.refs_14_), channel_id=1, source_target_pairs={{0,8},{8,0},{16,24},{24,16},{1,9},{9,1},{17,25},{25,17},{2,10},{10... | collective-permute-start | bytes 1179656 | tf_op jit(solution)/shard_map/ppermute | solution.py:31
  39.3 13.8 %collective-permute-start.9 = (bf16[384,640]{1,0:T(8,128)(2,1)}, bf16[384,640]{1,0:T(8,128)(2,1)S(1)}, u32[]{:S(2)}, u32[]{:S(2)}) collective-permute-start(bf16[384,640]{1,0:T(8,128)(2,1)} %after.4.refs_13_.refs_2_), channel_id=1, source_target_pairs={{0,1},{1,0},{2,3},{3,2},{4,5},{5,4},{6,7},{7,6},{8,9},{9,8},{10,11... | collective-permute-start | bytes 1474568 | tf_op jit(solution)/shard_map/ppermute | solution.py:31
  39.8 15.5 %collective-permute-start.8 = (bf16[384,640]{1,0:T(8,128)(2,1)}, bf16[384,640]{1,0:T(8,128)(2,1)}, u32[]{:S(2)}, u32[]{:S(2)}) collective-permute-start(bf16[384,640]{1,0:T(8,128)(2,1)} %after.4.refs_13_.refs_2_), channel_id=1, source_target_pairs={{0,2},{1,3},{2,4},{3,5},{4,6},{5,7},{6,0},{7,1},{8,10},{9,11},{10,... | collective-permute-start | bytes 1474568 | tf_op jit(solution)/shard_map/ppermute | solution.py:36
  41.4 13.9 %collective-permute-start.18 = (bf16[384,640]{1,0:T(8,128)(2,1)S(1)}, bf16[384,640]{1,0:T(8,128)(2,1)}, u32[]{:S(2)}, u32[]{:S(2)}) collective-permute-start(bf16[384,640]{1,0:T(8,128)(2,1)S(1)} %copy-done.2), channel_id=1, source_target_pairs={{0,16},{8,24},{16,0},{24,8},{1,17},{9,25},{17,1},{25,9},{2,18},{10... | collective-permute-start | bytes 1474568 | tf_op jit(solution)/shard_map/ppermute | solution.py:31
  58.8 28.9 %all-to-all-start = ((bf16[4,384,640]{2,1,0:T(8,128)(2,1)}), bf16[4,384,640]{2,1,0:T(8,128)(2,1)}, u32[]{:S(2)}, u32[]{:S(2)}) async-start(bf16[4,384,640]{2,1,0:T(8,128)(2,1)} %own_features.1.refs_5_), calls=%async_computation | async-start | bytes 3932160 | tf_op jit(solution)/shard_map/all_to_all | solution.py:459
  63.4 21.4 %collective-permute-start.16 = (f32[4,32,1536]{2,1,0:T(8,128)}, f32[4,32,1536]{2,1,0:T(8,128)}, u32[]{:S(2)}, u32[]{:S(2)}) collective-permute-start(f32[4,32,1536]{2,1,0:T(8,128)} %get-tuple-element.22.refs_2_), channel_id=1, source_target_pairs={{0,1},{1,0},{2,3},{3,2},{4,5},{5,4},{6,7},{7,6},{8,9},{9,8},{10,11... | collective-permute-start | bytes 2359304 | tf_op jit(solution)/shard_map/ppermute | solution.py:31
  65.5 15.0 %collective-permute-start.15 = (bf16[384,640]{1,0:T(8,128)(2,1)S(1)}, bf16[384,640]{1,0:T(8,128)(2,1)S(1)}, u32[]{:S(2)}, u32[]{:S(2)}) collective-permute-start(bf16[384,640]{1,0:T(8,128)(2,1)S(1)} %copy-done.6), channel_id=1, source_target_pairs={{0,2},{1,3},{2,4},{3,5},{4,6},{5,7},{6,0},{7,1},{8,10},{9,11},{10,... | collective-permute-start | bytes 1474568 | tf_op jit(solution)/shard_map/ppermute | solution.py:36
  90.0 23.7 %all-to-all-start.1 = ((f32[4,32,1536]{2,1,0:T(8,128)}), f32[4,32,1536]{2,1,0:T(8,128)S(1)}, u32[]{:S(2)}, u32[]{:S(2)}) async-start(f32[4,32,1536]{2,1,0:T(8,128)} %hidden_pair.1.refs_11_), calls=%async_computation.1 | async-start | bytes 1572864 | tf_op jit(solution)/shard_map/all_to_all | solution.py:380
  93.6 20.0 %collective-permute-start.23 = (f32[4,32,1536]{2,1,0:T(8,128)}, f32[4,32,1536]{2,1,0:T(8,128)}, u32[]{:S(2)}, u32[]{:S(2)}) collective-permute-start(f32[4,32,1536]{2,1,0:T(8,128)} %get-tuple-element.24.refs_4_), channel_id=1, source_target_pairs={{0,1},{1,0},{2,3},{3,2},{4,5},{5,4},{6,7},{7,6},{8,9},{9,8},{10,11... | collective-permute-start | bytes 2359304 | tf_op jit(solution)/shard_map/ppermute | solution.py:31
  95.8 25.4 %collective-permute-start.20 = (bf16[384,640]{1,0:T(8,128)(2,1)}, bf16[384,640]{1,0:T(8,128)(2,1)}, u32[]{:S(2)}, u32[]{:S(2)}) collective-permute-start(bf16[384,640]{1,0:T(8,128)(2,1)} %get-tuple-element.28), channel_id=1, source_target_pairs={{0,8},{8,0},{16,24},{24,16},{1,9},{9,1},{17,25},{25,17},{2,10},{10... | collective-permute-start | bytes 1474568 | tf_op jit(solution)/shard_map/ppermute | solution.py:31
  95.8 26.8 %collective-permute-start.21 = (bf16[384,640]{1,0:T(8,128)(2,1)}, bf16[384,640]{1,0:T(8,128)(2,1)}, u32[]{:S(2)}, u32[]{:S(2)}) collective-permute-start(bf16[384,640]{1,0:T(8,128)(2,1)} %get-tuple-element.29), channel_id=1, source_target_pairs={{0,16},{8,24},{16,0},{24,8},{1,17},{9,25},{17,1},{25,9},{2,18},{10... | collective-permute-start | bytes 1474568 | tf_op jit(solution)/shard_map/ppermute | solution.py:31
  96.2 26.5 %collective-permute-start.22 = (bf16[384,640]{1,0:T(8,128)(2,1)}, bf16[384,640]{1,0:T(8,128)(2,1)}, u32[]{:S(2)}, u32[]{:S(2)}) collective-permute-start(bf16[384,640]{1,0:T(8,128)(2,1)} %get-tuple-element.30), channel_id=1, source_target_pairs={{0,24},{8,16},{16,8},{24,0},{1,25},{9,17},{17,9},{25,1},{2,26},{10... | collective-permute-start | bytes 1474568 | tf_op jit(solution)/shard_map/ppermute | solution.py:31
  116.9 21.1 %collective-permute-start.24 = (f32[32,1536]{1,0:T(8,128)}, f32[32,1536]{1,0:T(8,128)S(1)}, u32[]{:S(2)}, u32[]{:S(2)}) collective-permute-start(f32[32,1536]{1,0:T(8,128)} %get-tuple-element.35), channel_id=1, source_target_pairs={{0,2},{1,3},{2,4},{3,5},{4,6},{5,7},{6,0},{7,1},{8,10},{9,11},{10,... | collective-permute-start | bytes 589832 | tf_op jit(solution)/shard_map/ppermute | solution.py:36
  118.8 19.3 %collective-permute-start.25 = (f32[32,1536]{1,0:T(8,128)}, f32[32,1536]{1,0:T(8,128)S(1)}, u32[]{:S(2)}, u32[]{:S(2)}) collective-permute-start(f32[32,1536]{1,0:T(8,128)} %get-tuple-element.36), channel_id=1, source_target_pairs={{0,4},{1,5},{2,6},{3,7},{4,0},{5,1},{6,2},{7,3},{8,12},{9,13},{10,... | collective-permute-start | bytes 589832 | tf_op jit(solution)/shard_map/ppermute | solution.py:36
  121.2 16.9 %collective-permute-start.26 = (f32[32,1536]{1,0:T(8,128)}, f32[32,1536]{1,0:T(8,128)S(1)}, u32[]{:S(2)}, u32[]{:S(2)}) collective-permute-start(f32[32,1536]{1,0:T(8,128)} %get-tuple-element.37), channel_id=1, source_target_pairs={{0,6},{1,7},{2,0},{3,1},{4,2},{5,3},{6,4},{7,5},{8,14},{9,15},{10,... | collective-permute-start | bytes 589832 | tf_op jit(solution)/shard_map/ppermute | solution.py:36
  (19 other events, 82.7 us)

commit v18 on v14

--- a/solution.py
+++ b/solution.py
@@ -407,7 +407,7 @@
         return [x, swap(x, "dp", 1), far, None]
 
     tiles = units // TILE
-    cuts = [0, tiles // 3, tiles - tiles // 3, tiles]
+    cuts = [0, tiles // 7, tiles // 7 * 4, tiles]
     hids = [
         over_dp(hidden_units(gate_act, up_act, a, b - a, f"hidden_{a}"))
         for a, b in zip(cuts, cuts[1:])

time: 151 us -> 157 us (1.040)
  starting transfers between devices: 34 us -> 37.4 us
  waiting for transfers between devices: 45.8 us -> 48.2 us
    ppermute x4, waiting for transfers between devices: 12.2 us -> 18.6 us  [shift(): return lax.ppermute(x, axis, [(s, (s + k) % n) for s in range(n)])]
    ppermute x20, starting transfers between devices: 11.7 us -> 17.3 us  [swap(): return lax.ppermute(x, axis, [(s, s ^ k) for s in range(n)])]
    ppermute x20, waiting for transfers between devices: 19.7 us -> 16.2 us  [swap(): return lax.ppermute(x, axis, [(s, s ^ k) for s in range(n)])]
    ppermute x4, starting transfers between devices: 6.74 us -> 4.51 us  [shift(): return lax.ppermute(x, axis, [(s, (s + k) % n) for s in range(n)])]
    unnamed x21 -> x19, local copies, waits for them, and re-layouts: 3.91 us -> 3.31 us
  transfers between devices with their start and end apart: 28 -> 28, of which waited for: 15 -> 10; matrix products, arithmetic and copies ran while one was open for 2% -> 2% of each run, Pallas kernels for 38% -> 35%
where the time goes in v18:
time: 157 us
  Pallas kernels  63.6 us (41%)
  waiting for transfers between devices  48.2 us (31%)
  starting transfers between devices  37.4 us (24%)
  local copies, waits for them, and re-layouts  4.13 us (3%)
  other arithmetic  2.43 us (2%)
    ppermute x4, waiting for transfers between devices, shift(): return lax.ppermute(x, axis, [(s, (s + k) % n) for s in range(n)])  18.6 us
    ppermute x20, starting transfers between devices, swap(): return lax.ppermute(x, axis, [(s, s ^ k) for s in range(n)])  17.3 us
    ppermute x20, waiting for transfers between devices, swap(): return lax.ppermute(x, axis, [(s, s ^ k) for s in range(n)])  16.2 us
    pallas_call x1, Pallas kernels, grads(): pl.pallas_call(functools.partial(grads_body, n), grid_spec=pltpu.Prefetch...  15.9 us
    pallas_call x1, Pallas kernels, wgrad(): pl.pallas_call(functools.partial(wgrad_body, n, tuple(starts)), in_specs=...  15.8 us
    pallas_call x2, Pallas kernels, gram(): pl.pallas_call(functools.partial(body, len(toks), cuts), grid=(1,), in_sp...  10 us
    all_to_all x2, starting transfers between devices, spread(): lax.all_to_all(pair, 'fsdp', split_axis=0, concat_axis=0, axis_index_grou...  8.55 us
    pallas_call x3, Pallas kernels, hidden_units(): pl.pallas_call(hidden_body, grid=(count,), in_specs=[cols, cols], out_spe...  8.25 us
  transfers between devices with their start and end apart: 28, of which 10 were waited for; matrix products, arithmetic and copies ran while one was open for 2% of the time, Pallas kernels for 35%

profile of v18, /device:TPU:0, one launch (start us, length us, event | category | flops | bytes accessed | tf_op | source)
XLA Modules:
  0.0 156.6 jit_solution(2502960642909414754)
XLA Ops:
  0.6 3.2 %hidden_1.1.refs_4_.refs_8_ = bf16[768,384]{1,0:T(8,128)(2,1)} custom-call(bf16[384,1792]{1,0:T(8,128)(2,1)} %refs_9_.1, bf16[384,1792]{1,0:T(8,128)(2,1)} %refs_10_.1), custom_call_target="tpu_custom_call" | custom-call | flops 1024 | bytes 1024 | tf_op jit(solution)/shard_map/hidden_1/pallas_call | solution.py:81
  3.9 3.0 %collective-permute-start.5 = (bf16[768,384]{1,0:T(8,128)(2,1)}, bf16[768,384]{1,0:T(8,128)(2,1)}, u32[]{:S(2)}, u32[]{:S(2)}) collective-permute-start(bf16[768,384]{1,0:T(8,128)(2,1)} %hidden_1.1.refs_4_.refs_8_), channel_id=1, source_target_pairs={{0,16},{8,24},{16,0},{24,8},{1,17},{9,25},{17,1},{25,9},{2,18},{10... | collective-permute-start | bytes 1769480 | tf_op jit(solution)/shard_map/ppermute | solution.py:31
  12.3 3.2 %hidden_4.1.refs_8_.refs_12_ = bf16[768,384]{1,0:T(8,128)(2,1)} custom-call(bf16[384,1792]{1,0:T(8,128)(2,1)} %refs_9_.1, bf16[384,1792]{1,0:T(8,128)(2,1)} %refs_10_.1), custom_call_target="tpu_custom_call" | custom-call | flops 1024 | bytes 1024 | tf_op jit(solution)/shard_map/hidden_4/pallas_call | solution.py:81
  17.0 8.6 %collective-permute-done.2.refs_2_.refs_6_ = bf16[256,384]{1,0:T(8,128)(2,1)} collective-permute-done((bf16[256,384]{1,0:T(8,128)(2,1)}, bf16[256,384]{1,0:T(8,128)(2,1)}, u32[]{:S(2)}, u32[]{:S(2)}) %collective-permute-start.2) | collective-permute-done | bytes 196640 | tf_op jit(solution)/shard_map/ppermute | solution.py:31
  26.3 2.1 %collective-permute-start.3 = (bf16[384,640]{1,0:T(8,128)(2,1)}, bf16[384,640]{1,0:T(8,128)(2,1)S(1)}, u32[]{:S(2)}, u32[]{:S(2)}) collective-permute-start(bf16[384,640]{1,0:T(8,128)(2,1)} %after.3.refs_1_), channel_id=1, source_target_pairs={{0,2},{1,3},{2,4},{3,5},{4,6},{5,7},{6,0},{7,1},{8,10},{9,11},{10,... | collective-permute-start | bytes 1474568 | tf_op jit(solution)/shard_map/ppermute | solution.py:36
  30.5 6.9 %collective-permute-done.13.refs_10_.refs_14_ = bf16[768,384]{1,0:T(8,128)(2,1)} collective-permute-done((bf16[768,384]{1,0:T(8,128)(2,1)}, bf16[768,384]{1,0:T(8,128)(2,1)}, u32[]{:S(2)}, u32[]{:S(2)}) %collective-permute-start.13) | collective-permute-done | bytes 589856 | tf_op jit(solution)/shard_map/ppermute | solution.py:31
  37.3 5.2 %collective-permute-done.3.refs_0_ = bf16[384,640]{1,0:T(8,128)(2,1)S(1)} collective-permute-done((bf16[384,640]{1,0:T(8,128)(2,1)}, bf16[384,640]{1,0:T(8,128)(2,1)S(1)}, u32[]{:S(2)}, u32[]{:S(2)}) %collective-permute-start.3) | collective-permute-done | bytes 491552 | tf_op jit(solution)/shard_map/ppermute | solution.py:36
  47.9 6.3 %hidden_gram.1 = (f32[4,32,1536]{2,1,0:T(8,128)}, f32[4,32,1536]{2,1,0:T(8,128)}) custom-call(s32[1]{0:T(128)} %bitcast.inner_ref, s32[4]{0:T(128)} %xor_multiply_fusion.offs_ref.toks_ref, bf16[256,384]{1,0:T(8,128)(2,1)} %hidden_0.1.refs_0_.refs_4_, bf16[256,384]{1,0:T(8,128)(2,1)} %collective-permute-done.8.refs_1_.refs_5_, ...), custom_call_target="tpu_custom_call" | custom-call | flops 1024 | bytes 1024 | tf_op jit(solution)/shard_map/hidden_gram/pallas_call | solution.py:315
  54.1 4.4 %collective-permute-done.6.refs_0_ = bf16[384,640]{1,0:T(8,128)(2,1)} collective-permute-done((bf16[384,640]{1,0:T(8,128)(2,1)}, bf16[384,640]{1,0:T(8,128)(2,1)}, u32[]{:S(2)}, u32[]{:S(2)}) %collective-permute-start.6) | collective-permute-done | bytes 491552 | tf_op jit(solution)/shard_map/ppermute | solution.py:36
  59.3 3.4 %own_features.1.refs_5_ = bf16[4,384,640]{2,1,0:T(8,128)(2,1)} custom-call(s32[4]{0:T(128)} %and_select_fusion.at_ref, bf16[384,640]{1,0:T(8,128)(2,1)} %refs_0_.5, bf16[384,640]{1,0:T(8,128)(2,1)} %after.3.refs_1_, bf16[384,640]{1,0:T(8,128)(2,1)} %after.4.refs_13_.refs_2_, bf16[384,640]{1,0:T(8,128)(2,1)} %after.5.refs_3_, ...), custom_call_target="tpu_custom_call" | custom-call | flops 1024 | bytes 1024 | tf_op jit(solution)/shard_map/own_features/pallas_call | solution.py:107
  62.8 4.6 %all-to-all-start = ((bf16[4,384,640]{2,1,0:T(8,128)(2,1)}), bf16[4,384,640]{2,1,0:T(8,128)(2,1)}, u32[]{:S(2)}, u32[]{:S(2)}) async-start(bf16[4,384,640]{2,1,0:T(8,128)(2,1)} %own_features.1.refs_5_), calls=%async_computation | async-start | bytes 3932160 | tf_op jit(solution)/shard_map/all_to_all | solution.py:432
  71.8 3.8 %grad_gram.1 = (f32[4,32,1536]{2,1,0:T(8,128)}, f32[4,32,1536]{2,1,0:T(8,128)}) custom-call(s32[1]{0:T(128)} %bitcast.inner_ref, s32[4]{0:T(128)} %xor_multiply_fusion.offs_ref.toks_ref, bf16[384,640]{1,0:T(8,128)(2,1)} %refs_0_.5, bf16[384,640]{1,0:T(8,128)(2,1)} %copy-done.7, bf16[384,640]{1,0:T(8,128)(2,1)} %collective-permute-done.18.refs_4_.refs_2_, ...), custom_call_target="tpu_custom_call" | custom-call | flops 1024 | bytes 1024 | tf_op jit(solution)/shard_map/grad_gram/pallas_call | solution.py:315
  75.6 8.9 %collective-permute-done.15.refs_3_.refs_7_ = bf16[384,640]{1,0:T(8,128)(2,1)} collective-permute-done((bf16[384,640]{1,0:T(8,128)(2,1)S(1)}, bf16[384,640]{1,0:T(8,128)(2,1)}, u32[]{:S(2)}, u32[]{:S(2)}) %collective-permute-start.15) | collective-permute-done | bytes 491552 | tf_op jit(solution)/shard_map/ppermute | solution.py:36
  84.5 3.4 %other_features.1 = (bf16[384,640]{1,0:T(8,128)(2,1)}, bf16[384,640]{1,0:T(8,128)(2,1)}, bf16[384,640]{1,0:T(8,128)(2,1)}, bf16[384,640]{1,0:T(8,128)(2,1)}) custom-call(s32[4]{0:T(128)} %broadcast_xor_fusion.to_ref, bf16[384,640]{1,0:T(8,128)(2,1)} %copy-done.4, bf16[384,640]{1,0:T(8,128)(2,1)} %collective-permute-done.4.refs_1_.refs_5_, ...), custom_call_target="tpu_custom_call" | custom-call | flops 1024 | bytes 1024 | tf_op jit(solution)/shard_map/other_features/pallas_call | solution.py:135
  87.9 2.3 %hidden_pair.1.refs_11_ = f32[4,32,1536]{2,1,0:T(8,128)} custom-call(f32[4,32,1536]{2,1,0:T(8,128)} %get-tuple-element.19.kept_ref, f32[4,32,1536]{2,1,0:T(8,128)} %collective-permute-done.16.refs_0_, bf16[384,640]{1,0:T(8,128)(2,1)} %get-tuple-element.21.refs_1_.refs_0_), custom_call_target="tpu_custom_call" | custom-call | flops 1024 | bytes 1024 | tf_op jit(solution)/shard_map/hidden_pair/pallas_call | solution.py:338
  91.7 3.5 %all-to-all-start.1 = ((f32[4,32,1536]{2,1,0:T(8,128)}), f32[4,32,1536]{2,1,0:T(8,128)S(1)}, u32[]{:S(2)}, u32[]{:S(2)}) async-start(f32[4,32,1536]{2,1,0:T(8,128)} %hidden_pair.1.refs_11_), calls=%async_computation.1 | async-start | bytes 1572864 | tf_op jit(solution)/shard_map/all_to_all | solution.py:353
  99.3 15.9 %grads.1 = (bf16[384,1792]{1,0:T(8,128)(2,1)}, bf16[384,1792]{1,0:T(8,128)(2,1)}, f32[8,128]{1,0:T(8,128)}) custom-call(s32[8]{0:T(128)} %add.40.offs_ref, bf16[384,640]{1,0:T(8,128)(2,1)} %refs_0_.5, bf16[384,640]{1,0:T(8,128)(2,1)} %after.3.refs_1_, bf16[384,640]{1,0:T(8,128)(2,1)} %after.4.refs_13_.refs_2_, bf16[384,640]{1,0:T(8,128)(2,1)} %after.5.refs_3_, ...), custom_call_target="tpu_custom_call" | custom-call | flops 7046430720 | bytes 27787264 | tf_op jit(solution)/shard_map/grads/pallas_call | solution.py:174
  115.2 2.3 %grad_pair.1.refs_16_ = f32[4,32,1536]{2,1,0:T(8,128)} custom-call(f32[4,32,1536]{2,1,0:T(8,128)} %get-tuple-element.27.kept_ref, f32[4,32,1536]{2,1,0:T(8,128)} %collective-permute-done.23.refs_0_, f32[8,128]{1,0:T(8,128)} %get-tuple-element.28.refs_1_), custom_call_target="tpu_custom_call" | custom-call | flops 1024 | bytes 1024 | tf_op jit(solution)/shard_map/grad_pair/pallas_call | solution.py:338
  117.5 5.1 %all-to-all-start.2 = ((f32[4,32,1536]{2,1,0:T(8,128)}), f32[4,32,1536]{2,1,0:T(8,128)}, u32[]{:S(2)}, u32[]{:S(2)}) async-start(f32[4,32,1536]{2,1,0:T(8,128)} %grad_pair.1.refs_16_), calls=%async_computation.2 | async-start | bytes 1572864 | tf_op jit(solution)/shard_map/all_to_all | solution.py:353
  122.6 15.8 %wgrad.1 = (bf16[1792,1280]{1,0:T(8,128)(2,1)}, f32[8,128]{1,0:T(8,128)}) custom-call(s32[2]{0:T(128)} %copy-done.8, s32[4]{0:T(128)} %xor_multiply_fusion.offs_ref.toks_ref, bf16[4,384,640]{2,1,0:T(8,128)(2,1)} %all-to-all-done.own_ref, bf16[384,640]{1,0:T(8,128)(2,1)} %get-tuple-element.21.refs_1_.refs_0_, ...), custom_call_target="tpu_custom_call" | custom-call | flops 28185722880 | bytes 14024704 | tf_op jit(solution)/shard_map/wgrad/pallas_call | solution.py:242
  138.4 4.9 %all-to-all-done.2.grad_ref = f32[4,32,1536]{2,1,0:T(8,128)} async-done(((f32[4,32,1536]{2,1,0:T(8,128)}), f32[4,32,1536]{2,1,0:T(8,128)}, u32[]{:S(2)}, u32[]{:S(2)}) %all-to-all-start.2) | async-done | bytes 786464 | tf_op jit(solution)/shard_map/all_to_all | solution.py:353
  143.3 2.1 %score_line.1 = f32[32,128]{1,0:T(8,128)} custom-call(s32[3]{0:T(128)} %assign_ref.1, f32[4,32,1536]{2,1,0:T(8,128)} %copy-done.1, f32[4,32,1536]{2,1,0:T(8,128)} %all-to-all-done.2.grad_ref, f32[8,128]{1,0:T(8,128)} %get-tuple-element.30.refs_0_), custom_call_target="tpu_custom_call" | custom-call | flops 1024 | bytes 1024 | tf_op jit(solution)/shard_map/score_line/pallas_call | solution.py:376
  145.4 2.5 %all-to-all-start.3 = ((f32[32,1,128]{2,1,0:T(1,128)}), f32[32,1,128]{2,1,0:T(1,128)S(1)}, u32[]{:S(2)}, u32[]{:S(2)}) async-start(f32[32,1,128]{2,1,0:T(1,128)} %bitcast.13), calls=%async_computation.3 | async-start | bytes 32768 | tf_op jit(solution)/shard_map/all_to_all | solution.py:452
  147.9 7.1 %all-to-all-done.3 = f32[32,1,128]{2,1,0:T(1,128)S(1)} async-done(((f32[32,1,128]{2,1,0:T(1,128)}), f32[32,1,128]{2,1,0:T(1,128)S(1)}, u32[]{:S(2)}, u32[]{:S(2)}) %all-to-all-start.3) | async-done | bytes 16416 | tf_op jit(solution)/shard_map/all_to_all | solution.py:452
  (78 shorter events, 27.3 us)
Async XLA Ops:
  3.9 26.1 %collective-permute-start.5 = (bf16[768,384]{1,0:T(8,128)(2,1)}, bf16[768,384]{1,0:T(8,128)(2,1)}, u32[]{:S(2)}, u32[]{:S(2)}) collective-permute-start(bf16[768,384]{1,0:T(8,128)(2,1)} %hidden_1.1.refs_4_.refs_8_), channel_id=1, source_target_pairs={{0,16},{8,24},{16,0},{24,8},{1,17},{9,25},{17,1},{25,9},{2,18},{10... | collective-permute-start | bytes 1769480 | tf_op jit(solution)/shard_map/ppermute | solution.py:31
  6.8 18.7 %collective-permute-start = (bf16[384,640]{1,0:T(8,128)(2,1)S(1)}, bf16[384,640]{1,0:T(8,128)(2,1)}, u32[]{:S(2)}, u32[]{:S(2)}) collective-permute-start(bf16[384,640]{1,0:T(8,128)(2,1)S(1)} %copy-done.2), channel_id=1, source_target_pairs={{0,2},{1,3},{2,4},{3,5},{4,6},{5,7},{6,0},{7,1},{8,10},{9,11},{10,... | collective-permute-start | bytes 1474568 | tf_op jit(solution)/shard_map/ppermute | solution.py:36
  8.4 17.1 %collective-permute-start.1 = (bf16[384,640]{1,0:T(8,128)(2,1)S(1)}, bf16[384,640]{1,0:T(8,128)(2,1)S(1)}, u32[]{:S(2)}, u32[]{:S(2)}) collective-permute-start(bf16[384,640]{1,0:T(8,128)(2,1)S(1)} %copy-done.2), channel_id=1, source_target_pairs={{0,1},{1,0},{2,3},{3,2},{4,5},{5,4},{6,7},{7,6},{8,9},{9,8},{10,11... | collective-permute-start | bytes 1474568 | tf_op jit(solution)/shard_map/ppermute | solution.py:31
  11.8 13.8 %collective-permute-start.2 = (bf16[256,384]{1,0:T(8,128)(2,1)}, bf16[256,384]{1,0:T(8,128)(2,1)}, u32[]{:S(2)}, u32[]{:S(2)}) collective-permute-start(bf16[256,384]{1,0:T(8,128)(2,1)} %hidden_0.1.refs_0_.refs_4_), channel_id=1, source_target_pairs={{0,16},{8,24},{16,0},{24,8},{1,17},{9,25},{17,1},{25,9},{2,18},{10... | collective-permute-start | bytes 589832 | tf_op jit(solution)/shard_map/ppermute | solution.py:31
  15.4 21.9 %collective-permute-start.13 = (bf16[768,384]{1,0:T(8,128)(2,1)}, bf16[768,384]{1,0:T(8,128)(2,1)}, u32[]{:S(2)}, u32[]{:S(2)}) collective-permute-start(bf16[768,384]{1,0:T(8,128)(2,1)} %hidden_4.1.refs_8_.refs_12_), channel_id=1, source_target_pairs={{0,16},{8,24},{16,0},{24,8},{1,17},{9,25},{17,1},{25,9},{2,18},{10... | collective-permute-start | bytes 1769480 | tf_op jit(solution)/shard_map/ppermute | solution.py:31
  26.3 16.2 %collective-permute-start.3 = (bf16[384,640]{1,0:T(8,128)(2,1)}, bf16[384,640]{1,0:T(8,128)(2,1)S(1)}, u32[]{:S(2)}, u32[]{:S(2)}) collective-permute-start(bf16[384,640]{1,0:T(8,128)(2,1)} %after.3.refs_1_), channel_id=1, source_target_pairs={{0,2},{1,3},{2,4},{3,5},{4,6},{5,7},{6,0},{7,1},{8,10},{9,11},{10,... | collective-permute-start | bytes 1474568 | tf_op jit(solution)/shard_map/ppermute | solution.py:36
  28.5 14.1 %collective-permute-start.4 = (bf16[384,640]{1,0:T(8,128)(2,1)}, bf16[384,640]{1,0:T(8,128)(2,1)}, u32[]{:S(2)}, u32[]{:S(2)}) collective-permute-start(bf16[384,640]{1,0:T(8,128)(2,1)} %after.3.refs_1_), channel_id=1, source_target_pairs={{0,1},{1,0},{2,3},{3,2},{4,5},{5,4},{6,7},{7,6},{8,9},{9,8},{10,11... | collective-permute-start | bytes 1474568 | tf_op jit(solution)/shard_map/ppermute | solution.py:31
  30.0 13.8 %collective-permute-start.10 = (bf16[768,384]{1,0:T(8,128)(2,1)}, bf16[768,384]{1,0:T(8,128)(2,1)}, u32[]{:S(2)}, u32[]{:S(2)}) collective-permute-start(bf16[768,384]{1,0:T(8,128)(2,1)} %hidden_1.1.refs_4_.refs_8_), channel_id=1, source_target_pairs={{0,8},{8,0},{16,24},{24,16},{1,9},{9,1},{17,25},{25,17},{2,10},{10... | collective-permute-start | bytes 1769480 | tf_op jit(solution)/shard_map/ppermute | solution.py:31
  30.0 15.3 %collective-permute-start.12 = (bf16[768,384]{1,0:T(8,128)(2,1)}, bf16[768,384]{1,0:T(8,128)(2,1)}, u32[]{:S(2)}, u32[]{:S(2)}) collective-permute-start(bf16[768,384]{1,0:T(8,128)(2,1)} %hidden_4.1.refs_8_.refs_12_), channel_id=1, source_target_pairs={{0,8},{8,0},{16,24},{24,16},{1,9},{9,1},{17,25},{25,17},{2,10},{10... | collective-permute-start | bytes 1769480 | tf_op jit(solution)/shard_map/ppermute | solution.py:31
  37.3 6.0 %collective-permute-start.9 = (bf16[256,384]{1,0:T(8,128)(2,1)}, bf16[256,384]{1,0:T(8,128)(2,1)}, u32[]{:S(2)}, u32[]{:S(2)}) collective-permute-start(bf16[256,384]{1,0:T(8,128)(2,1)} %collective-permute-done.2.refs_2_.refs_6_), channel_id=1, source_target_pairs={{0,8},{8,0},{16,24},{24,16},{1,9},{9,1},{17,25},{25,17},{2,10},{10... | collective-permute-start | bytes 589832 | tf_op jit(solution)/shard_map/ppermute | solution.py:31
  42.6 5.3 %collective-permute-start.11 = (bf16[768,384]{1,0:T(8,128)(2,1)}, bf16[768,384]{1,0:T(8,128)(2,1)}, u32[]{:S(2)}, u32[]{:S(2)}) collective-permute-start(bf16[768,384]{1,0:T(8,128)(2,1)} %collective-permute-done.5.refs_2_.refs_6_.refs_10_), channel_id=1, source_target_pairs={{0,8},{8,0},{16,24},{24,16},{1,9},{9,1},{17,25},{25,17},{2,10},{10... | collective-permute-start | bytes 1769480 | tf_op jit(solution)/shard_map/ppermute | solution.py:31
  43.4 15.2 %collective-permute-start.6 = (bf16[384,640]{1,0:T(8,128)(2,1)}, bf16[384,640]{1,0:T(8,128)(2,1)}, u32[]{:S(2)}, u32[]{:S(2)}) collective-permute-start(bf16[384,640]{1,0:T(8,128)(2,1)} %after.4.refs_13_.refs_2_), channel_id=1, source_target_pairs={{0,2},{1,3},{2,4},{3,5},{4,6},{5,7},{6,0},{7,1},{8,10},{9,11},{10,... | collective-permute-start | bytes 1474568 | tf_op jit(solution)/shard_map/ppermute | solution.py:36
  43.8 14.8 %collective-permute-start.7 = (bf16[384,640]{1,0:T(8,128)(2,1)}, bf16[384,640]{1,0:T(8,128)(2,1)S(1)}, u32[]{:S(2)}, u32[]{:S(2)}) collective-permute-start(bf16[384,640]{1,0:T(8,128)(2,1)} %after.4.refs_13_.refs_2_), channel_id=1, source_target_pairs={{0,1},{1,0},{2,3},{3,2},{4,5},{5,4},{6,7},{7,6},{8,9},{9,8},{10,11... | collective-permute-start | bytes 1474568 | tf_op jit(solution)/shard_map/ppermute | solution.py:31
  45.3 14.1 %collective-permute-start.18 = (bf16[384,640]{1,0:T(8,128)(2,1)S(1)}, bf16[384,640]{1,0:T(8,128)(2,1)}, u32[]{:S(2)}, u32[]{:S(2)}) collective-permute-start(bf16[384,640]{1,0:T(8,128)(2,1)S(1)} %copy-done.2), channel_id=1, source_target_pairs={{0,16},{8,24},{16,0},{24,8},{1,17},{9,25},{17,1},{25,9},{2,18},{10... | collective-permute-start | bytes 1474568 | tf_op jit(solution)/shard_map/ppermute | solution.py:31
  62.8 28.9 %all-to-all-start = ((bf16[4,384,640]{2,1,0:T(8,128)(2,1)}), bf16[4,384,640]{2,1,0:T(8,128)(2,1)}, u32[]{:S(2)}, u32[]{:S(2)}) async-start(bf16[4,384,640]{2,1,0:T(8,128)(2,1)} %own_features.1.refs_5_), calls=%async_computation | async-start | bytes 3932160 | tf_op jit(solution)/shard_map/all_to_all | solution.py:432
  67.4 20.5 %collective-permute-start.16 = (f32[4,32,1536]{2,1,0:T(8,128)}, f32[4,32,1536]{2,1,0:T(8,128)}, u32[]{:S(2)}, u32[]{:S(2)}) collective-permute-start(f32[4,32,1536]{2,1,0:T(8,128)} %get-tuple-element.18.refs_2_), channel_id=1, source_target_pairs={{0,1},{1,0},{2,3},{3,2},{4,5},{5,4},{6,7},{7,6},{8,9},{9,8},{10,11... | collective-permute-start | bytes 2359304 | tf_op jit(solution)/shard_map/ppermute | solution.py:31
  69.4 15.1 %collective-permute-start.15 = (bf16[384,640]{1,0:T(8,128)(2,1)S(1)}, bf16[384,640]{1,0:T(8,128)(2,1)}, u32[]{:S(2)}, u32[]{:S(2)}) collective-permute-start(bf16[384,640]{1,0:T(8,128)(2,1)S(1)} %copy-done.6), channel_id=1, source_target_pairs={{0,2},{1,3},{2,4},{3,5},{4,6},{5,7},{6,0},{7,1},{8,10},{9,11},{10,... | collective-permute-start | bytes 1474568 | tf_op jit(solution)/shard_map/ppermute | solution.py:36
  91.7 25.8 %all-to-all-start.1 = ((f32[4,32,1536]{2,1,0:T(8,128)}), f32[4,32,1536]{2,1,0:T(8,128)S(1)}, u32[]{:S(2)}, u32[]{:S(2)}) async-start(f32[4,32,1536]{2,1,0:T(8,128)} %hidden_pair.1.refs_11_), calls=%async_computation.1 | async-start | bytes 1572864 | tf_op jit(solution)/shard_map/all_to_all | solution.py:353
  95.3 19.8 %collective-permute-start.23 = (f32[4,32,1536]{2,1,0:T(8,128)}, f32[4,32,1536]{2,1,0:T(8,128)}, u32[]{:S(2)}, u32[]{:S(2)}) collective-permute-start(f32[4,32,1536]{2,1,0:T(8,128)} %get-tuple-element.20.refs_4_), channel_id=1, source_target_pairs={{0,1},{1,0},{2,3},{3,2},{4,5},{5,4},{6,7},{7,6},{8,9},{9,8},{10,11... | collective-permute-start | bytes 2359304 | tf_op jit(solution)/shard_map/ppermute | solution.py:31
  97.4 25.2 %collective-permute-start.20 = (bf16[384,640]{1,0:T(8,128)(2,1)}, bf16[384,640]{1,0:T(8,128)(2,1)}, u32[]{:S(2)}, u32[]{:S(2)}) collective-permute-start(bf16[384,640]{1,0:T(8,128)(2,1)} %get-tuple-element.24), channel_id=1, source_target_pairs={{0,8},{8,0},{16,24},{24,16},{1,9},{9,1},{17,25},{25,17},{2,10},{10... | collective-permute-start | bytes 1474568 | tf_op jit(solution)/shard_map/ppermute | solution.py:31
  97.4 25.2 %collective-permute-start.21 = (bf16[384,640]{1,0:T(8,128)(2,1)}, bf16[384,640]{1,0:T(8,128)(2,1)}, u32[]{:S(2)}, u32[]{:S(2)}) collective-permute-start(bf16[384,640]{1,0:T(8,128)(2,1)} %get-tuple-element.25), channel_id=1, source_target_pairs={{0,16},{8,24},{16,0},{24,8},{1,17},{9,25},{17,1},{25,9},{2,18},{10... | collective-permute-start | bytes 1474568 | tf_op jit(solution)/shard_map/ppermute | solution.py:31
  97.8 24.8 %collective-permute-start.22 = (bf16[384,640]{1,0:T(8,128)(2,1)}, bf16[384,640]{1,0:T(8,128)(2,1)}, u32[]{:S(2)}, u32[]{:S(2)}) collective-permute-start(bf16[384,640]{1,0:T(8,128)(2,1)} %get-tuple-element.26), channel_id=1, source_target_pairs={{0,24},{8,16},{16,8},{24,0},{1,25},{9,17},{17,9},{25,1},{2,26},{10... | collective-permute-start | bytes 1474568 | tf_op jit(solution)/shard_map/ppermute | solution.py:31
  117.5 25.7 %all-to-all-start.2 = ((f32[4,32,1536]{2,1,0:T(8,128)}), f32[4,32,1536]{2,1,0:T(8,128)}, u32[]{:S(2)}, u32[]{:S(2)}) async-start(f32[4,32,1536]{2,1,0:T(8,128)} %grad_pair.1.refs_16_), calls=%async_computation.2 | async-start | bytes 1572864 | tf_op jit(solution)/shard_map/all_to_all | solution.py:353
  145.4 9.6 %all-to-all-start.3 = ((f32[32,1,128]{2,1,0:T(1,128)}), f32[32,1,128]{2,1,0:T(1,128)S(1)}, u32[]{:S(2)}, u32[]{:S(2)}) async-start(f32[32,1,128]{2,1,0:T(1,128)} %bitcast.13), calls=%async_computation.3 | async-start | bytes 32768 | tf_op jit(solution)/shard_map/all_to_all | solution.py:452
  (13 other events, 77.2 us)

commit v19 on v14

--- a/solution.py
+++ b/solution.py
@@ -444,7 +444,7 @@
     grad_gate, grad_up, done = grads(
         places, [*ring, *others], down_weight, gate_act, up_act, [hid_pair]
     )
-    grad_pair = pair_sum(grad_kept, grad_came, [done], "grad_pair")
+    grad_pair = grad_kept + after(grad_came[0], done)
     grad_sums = spread(grad_pair)
     weight_grad, done = wgrad(offs, tok_offs, own_cols, other_cols, hids, [grad_pair])
 

time: 151 us -> 151 us (level)
  other arithmetic: 2.34 us -> 4.68 us
  Pallas kernels: 62.3 us -> 60 us
    add x0 -> x1, other arithmetic: none -> 2.34 us  [per_device(): grad_pair = grad_kept + after(grad_came[0], done)]
    pallas_call x2 -> x1, Pallas kernels: 4.66 us -> 2.33 us  [pair_sum(): pl.pallas_call(functools.partial(pair_body, len(came)), grid=(1,), in_spe...]
  transfers between devices with their start and end apart: 28 -> 28, of which waited for: 15 -> 15; matrix products, arithmetic and copies ran while one was open for 2% -> 3% of each run, Pallas kernels for 38% -> 36%
where the time goes in v19:
time: 151 us; the launch traced here: 150 us
  Pallas kernels  60 us (40%)
  waiting for transfers between devices  45.8 us (30%)
  starting transfers between devices  34 us (23%)
  local copies, waits for them, and re-layouts  4.72 us (3%)
  other arithmetic  4.68 us (3%)
    ppermute x20, waiting for transfers between devices, swap(): return lax.ppermute(x, axis, [(s, s ^ k) for s in range(n)])  19.7 us
    pallas_call x1, Pallas kernels, grads(): pl.pallas_call(functools.partial(grads_body, n), grid_spec=pltpu.Prefetch...  15.9 us
    pallas_call x1, Pallas kernels, wgrad(): pl.pallas_call(functools.partial(wgrad_body, n, tuple(starts)), in_specs=...  15.4 us
    ppermute x4, waiting for transfers between devices, shift(): return lax.ppermute(x, axis, [(s, (s + k) % n) for s in range(n)])  12.2 us
    ppermute x20, starting transfers between devices, swap(): return lax.ppermute(x, axis, [(s, s ^ k) for s in range(n)])  11.7 us
    pallas_call x2, Pallas kernels, gram(): pl.pallas_call(functools.partial(body, len(toks), cuts), grid=(1,), in_sp...  9.96 us
    all_to_all x2, starting transfers between devices, spread(): lax.all_to_all(pair, 'fsdp', split_axis=0, concat_axis=0, axis_index_grou...  8.27 us
    pallas_call x3, Pallas kernels, hidden_units(): pl.pallas_call(hidden_body, grid=(count,), in_specs=[cols, cols], out_spe...  7.26 us
  transfers between devices with their start and end apart: 28, of which 15 were waited for; matrix products, arithmetic and copies ran while one was open for 3% of the time, Pallas kernels for 36%

profile of v19, /device:TPU:0, one launch (start us, length us, event | category | flops | bytes accessed | tf_op | source)
XLA Modules:
  0.0 150.0 jit_solution(13398130371547948604)
XLA Ops:
  0.6 3.1 %collective-permute-start = (bf16[384,640]{1,0:T(8,128)(2,1)}, bf16[384,640]{1,0:T(8,128)(2,1)S(1)}, u32[]{:S(2)}, u32[]{:S(2)}) collective-permute-start(bf16[384,640]{1,0:T(8,128)(2,1)} %refs_0_.5), channel_id=1, source_target_pairs={{0,2},{1,3},{2,4},{3,5},{4,6},{5,7},{6,0},{7,1},{8,10},{9,11},{10,... | collective-permute-start | bytes 1474568 | tf_op jit(solution)/shard_map/ppermute | solution.py:36
  5.2 2.1 %hidden_0.1.refs_0_.refs_4_ = bf16[512,384]{1,0:T(8,128)(2,1)} custom-call(bf16[384,1792]{1,0:T(8,128)(2,1)} %refs_9_.1, bf16[384,1792]{1,0:T(8,128)(2,1)} %refs_10_.1), custom_call_target="tpu_custom_call" | custom-call | flops 1024 | bytes 1024 | tf_op jit(solution)/shard_map/hidden_0/pallas_call | solution.py:81
  8.8 3.2 %hidden_2.1.refs_4_.refs_8_ = bf16[768,384]{1,0:T(8,128)(2,1)} custom-call(bf16[384,1792]{1,0:T(8,128)(2,1)} %refs_9_.1, bf16[384,1792]{1,0:T(8,128)(2,1)} %refs_10_.1), custom_call_target="tpu_custom_call" | custom-call | flops 1024 | bytes 1024 | tf_op jit(solution)/shard_map/hidden_2/pallas_call | solution.py:81
  12.5 7.2 %collective-permute-done.2.refs_2_.refs_6_ = bf16[512,384]{1,0:T(8,128)(2,1)} collective-permute-done((bf16[512,384]{1,0:T(8,128)(2,1)}, bf16[512,384]{1,0:T(8,128)(2,1)}, u32[]{:S(2)}, u32[]{:S(2)}) %collective-permute-start.2) | collective-permute-done | bytes 393248 | tf_op jit(solution)/shard_map/ppermute | solution.py:31
  23.6 2.0 %hidden_5.1.refs_8_.refs_12_ = bf16[512,384]{1,0:T(8,128)(2,1)} custom-call(bf16[384,1792]{1,0:T(8,128)(2,1)} %refs_9_.1, bf16[384,1792]{1,0:T(8,128)(2,1)} %refs_10_.1), custom_call_target="tpu_custom_call" | custom-call | flops 1024 | bytes 1024 | tf_op jit(solution)/shard_map/hidden_5/pallas_call | solution.py:81
  25.9 4.6 %collective-permute-done.5.refs_2_.refs_6_.refs_10_ = bf16[768,384]{1,0:T(8,128)(2,1)} collective-permute-done((bf16[768,384]{1,0:T(8,128)(2,1)}, bf16[768,384]{1,0:T(8,128)(2,1)}, u32[]{:S(2)}, u32[]{:S(2)}) %collective-permute-start.5) | collective-permute-done | bytes 589856 | tf_op jit(solution)/shard_map/ppermute | solution.py:31
  33.2 3.6 %collective-permute-done.4.refs_1_.refs_5_ = bf16[384,640]{1,0:T(8,128)(2,1)} collective-permute-done((bf16[384,640]{1,0:T(8,128)(2,1)}, bf16[384,640]{1,0:T(8,128)(2,1)}, u32[]{:S(2)}, u32[]{:S(2)}) %collective-permute-start.4) | collective-permute-done | bytes 491552 | tf_op jit(solution)/shard_map/ppermute | solution.py:31
  44.3 6.2 %hidden_gram.1 = (f32[4,32,1536]{2,1,0:T(8,128)}, f32[4,32,1536]{2,1,0:T(8,128)}) custom-call(s32[1]{0:T(128)} %bitcast.inner_ref, s32[4]{0:T(128)} %xor_multiply_fusion.offs_ref.toks_ref, bf16[512,384]{1,0:T(8,128)(2,1)} %hidden_0.1.refs_0_.refs_4_, bf16[512,384]{1,0:T(8,128)(2,1)} %collective-permute-done.8.refs_1_.refs_5_, ...), custom_call_target="tpu_custom_call" | custom-call | flops 1024 | bytes 1024 | tf_op jit(solution)/shard_map/hidden_gram/pallas_call | solution.py:315
  50.5 2.1 %collective-permute-done.6.refs_0_ = bf16[384,640]{1,0:T(8,128)(2,1)} collective-permute-done((bf16[384,640]{1,0:T(8,128)(2,1)}, bf16[384,640]{1,0:T(8,128)(2,1)}, u32[]{:S(2)}, u32[]{:S(2)}) %collective-permute-start.6) | collective-permute-done | bytes 491552 | tf_op jit(solution)/shard_map/ppermute | solution.py:36
  53.4 3.4 %own_features.1.refs_5_ = bf16[4,384,640]{2,1,0:T(8,128)(2,1)} custom-call(s32[4]{0:T(128)} %and_select_fusion.at_ref, bf16[384,640]{1,0:T(8,128)(2,1)} %refs_0_.5, bf16[384,640]{1,0:T(8,128)(2,1)} %after.4.refs_1_, bf16[384,640]{1,0:T(8,128)(2,1)} %after.5.refs_13_.refs_2_, bf16[384,640]{1,0:T(8,128)(2,1)} %after.6.refs_3_, ...), custom_call_target="tpu_custom_call" | custom-call | flops 1024 | bytes 1024 | tf_op jit(solution)/shard_map/own_features/pallas_call | solution.py:107
  56.8 4.6 %all-to-all-start = ((bf16[4,384,640]{2,1,0:T(8,128)(2,1)}), bf16[4,384,640]{2,1,0:T(8,128)(2,1)}, u32[]{:S(2)}, u32[]{:S(2)}) async-start(bf16[4,384,640]{2,1,0:T(8,128)(2,1)} %own_features.1.refs_5_), calls=%async_computation | async-start | bytes 3932160 | tf_op jit(solution)/shard_map/all_to_all | solution.py:432
  65.0 3.8 %grad_gram.1 = (f32[4,32,1536]{2,1,0:T(8,128)}, f32[4,32,1536]{2,1,0:T(8,128)}) custom-call(s32[1]{0:T(128)} %bitcast.inner_ref, s32[4]{0:T(128)} %xor_multiply_fusion.offs_ref.toks_ref, bf16[384,640]{1,0:T(8,128)(2,1)} %refs_0_.5, bf16[384,640]{1,0:T(8,128)(2,1)} %copy-done.8, bf16[384,640]{1,0:T(8,128)(2,1)} %collective-permute-done.18.refs_4_.refs_2_, ...), custom_call_target="tpu_custom_call" | custom-call | flops 1024 | bytes 1024 | tf_op jit(solution)/shard_map/grad_gram/pallas_call | solution.py:315
  68.8 8.9 %collective-permute-done.15.refs_3_.refs_7_ = bf16[384,640]{1,0:T(8,128)(2,1)} collective-permute-done((bf16[384,640]{1,0:T(8,128)(2,1)S(1)}, bf16[384,640]{1,0:T(8,128)(2,1)}, u32[]{:S(2)}, u32[]{:S(2)}) %collective-permute-start.15) | collective-permute-done | bytes 491552 | tf_op jit(solution)/shard_map/ppermute | solution.py:36
  77.7 3.4 %other_features.1 = (bf16[384,640]{1,0:T(8,128)(2,1)}, bf16[384,640]{1,0:T(8,128)(2,1)}, bf16[384,640]{1,0:T(8,128)(2,1)}, bf16[384,640]{1,0:T(8,128)(2,1)}) custom-call(s32[4]{0:T(128)} %broadcast_xor_fusion.to_ref, bf16[384,640]{1,0:T(8,128)(2,1)} %copy-done.2, bf16[384,640]{1,0:T(8,128)(2,1)} %collective-permute-done.4.refs_1_.refs_5_, ...), custom_call_target="tpu_custom_call" | custom-call | flops 1024 | bytes 1024 | tf_op jit(solution)/shard_map/other_features/pallas_call | solution.py:135
  81.6 2.3 %hidden_pair.1.refs_11_ = f32[4,32,1536]{2,1,0:T(8,128)} custom-call(f32[4,32,1536]{2,1,0:T(8,128)} %get-tuple-element.19.kept_ref, f32[4,32,1536]{2,1,0:T(8,128)} %collective-permute-done.16.refs_0_, bf16[384,640]{1,0:T(8,128)(2,1)} %get-tuple-element.21.refs_1_.refs_0_), custom_call_target="tpu_custom_call" | custom-call | flops 1024 | bytes 1024 | tf_op jit(solution)/shard_map/hidden_pair/pallas_call | solution.py:338
  85.8 3.5 %all-to-all-start.1 = ((f32[4,32,1536]{2,1,0:T(8,128)}), f32[4,32,1536]{2,1,0:T(8,128)S(1)}, u32[]{:S(2)}, u32[]{:S(2)}) async-start(f32[4,32,1536]{2,1,0:T(8,128)} %hidden_pair.1.refs_11_), calls=%async_computation.1 | async-start | bytes 1572864 | tf_op jit(solution)/shard_map/all_to_all | solution.py:353
  92.4 15.9 %grads.1 = (bf16[384,1792]{1,0:T(8,128)(2,1)}, bf16[384,1792]{1,0:T(8,128)(2,1)}, f32[8,128]{1,0:T(8,128)}) custom-call(s32[8]{0:T(128)} %add.43.offs_ref, bf16[384,640]{1,0:T(8,128)(2,1)} %refs_0_.5, bf16[384,640]{1,0:T(8,128)(2,1)} %after.4.refs_1_, bf16[384,640]{1,0:T(8,128)(2,1)} %after.5.refs_13_.refs_2_, bf16[384,640]{1,0:T(8,128)(2,1)} %after.6.refs_3_, ...), custom_call_target="tpu_custom_call" | custom-call | flops 7046430720 | bytes 27787264 | tf_op jit(solution)/shard_map/grads/pallas_call | solution.py:174
  108.8 2.3 %add.44.refs_16_ = f32[4,32,1536]{2,1,0:T(8,128)} add(f32[4,32,1536]{2,1,0:T(8,128)} %get-tuple-element.27, f32[4,32,1536]{2,1,0:T(8,128)} %after.7) | non-fusion elementwise | flops 196608 | bytes 2359296 | tf_op jit(solution)/shard_map/add | solution.py:447
  111.1 4.8 %all-to-all-start.2 = ((f32[4,32,1536]{2,1,0:T(8,128)}), f32[4,32,1536]{2,1,0:T(8,128)}, u32[]{:S(2)}, u32[]{:S(2)}) async-start(f32[4,32,1536]{2,1,0:T(8,128)} %add.44.refs_16_), calls=%async_computation.2 | async-start | bytes 1572864 | tf_op jit(solution)/shard_map/all_to_all | solution.py:353
  115.9 15.4 %wgrad.1 = (bf16[1792,1280]{1,0:T(8,128)(2,1)}, f32[8,128]{1,0:T(8,128)}) custom-call(s32[2]{0:T(128)} %copy-done.9, s32[4]{0:T(128)} %xor_multiply_fusion.offs_ref.toks_ref, bf16[4,384,640]{2,1,0:T(8,128)(2,1)} %all-to-all-done.own_ref, bf16[384,640]{1,0:T(8,128)(2,1)} %get-tuple-element.21.refs_1_.refs_0_, ...), custom_call_target="tpu_custom_call" | custom-call | flops 28185722880 | bytes 14024704 | tf_op jit(solution)/shard_map/wgrad/pallas_call | solution.py:242
  131.4 5.1 %all-to-all-done.2.grad_ref = f32[4,32,1536]{2,1,0:T(8,128)} async-done(((f32[4,32,1536]{2,1,0:T(8,128)}), f32[4,32,1536]{2,1,0:T(8,128)}, u32[]{:S(2)}, u32[]{:S(2)}) %all-to-all-start.2) | async-done | bytes 786464 | tf_op jit(solution)/shard_map/all_to_all | solution.py:353
  136.4 2.2 %score_line.1 = f32[32,128]{1,0:T(8,128)} custom-call(s32[3]{0:T(128)} %assign_ref.1, f32[4,32,1536]{2,1,0:T(8,128)} %copy-done.1, f32[4,32,1536]{2,1,0:T(8,128)} %all-to-all-done.2.grad_ref, f32[8,128]{1,0:T(8,128)} %get-tuple-element.30.refs_0_), custom_call_target="tpu_custom_call" | custom-call | flops 1024 | bytes 1024 | tf_op jit(solution)/shard_map/score_line/pallas_call | solution.py:376
  138.6 2.8 %all-to-all-start.3 = ((f32[32,1,128]{2,1,0:T(1,128)}), f32[32,1,128]{2,1,0:T(1,128)S(1)}, u32[]{:S(2)}, u32[]{:S(2)}) async-start(f32[32,1,128]{2,1,0:T(1,128)} %bitcast.13), calls=%async_computation.3 | async-start | bytes 32768 | tf_op jit(solution)/shard_map/all_to_all | solution.py:452
  141.3 7.1 %all-to-all-done.3 = f32[32,1,128]{2,1,0:T(1,128)S(1)} async-done(((f32[32,1,128]{2,1,0:T(1,128)}), f32[32,1,128]{2,1,0:T(1,128)S(1)}, u32[]{:S(2)}, u32[]{:S(2)}) %all-to-all-start.3) | async-done | bytes 16416 | tf_op jit(solution)/shard_map/all_to_all | solution.py:452
  (81 shorter events, 29.8 us)
Async XLA Ops:
  0.6 19.0 %collective-permute-start = (bf16[384,640]{1,0:T(8,128)(2,1)}, bf16[384,640]{1,0:T(8,128)(2,1)S(1)}, u32[]{:S(2)}, u32[]{:S(2)}) collective-permute-start(bf16[384,640]{1,0:T(8,128)(2,1)} %refs_0_.5), channel_id=1, source_target_pairs={{0,2},{1,3},{2,4},{3,5},{4,6},{5,7},{6,0},{7,1},{8,10},{9,11},{10,... | collective-permute-start | bytes 1474568 | tf_op jit(solution)/shard_map/ppermute | solution.py:36
  3.7 15.9 %collective-permute-start.1 = (bf16[384,640]{1,0:T(8,128)(2,1)}, bf16[384,640]{1,0:T(8,128)(2,1)S(1)}, u32[]{:S(2)}, u32[]{:S(2)}) collective-permute-start(bf16[384,640]{1,0:T(8,128)(2,1)} %refs_0_.5), channel_id=1, source_target_pairs={{0,1},{1,0},{2,3},{3,2},{4,5},{5,4},{6,7},{7,6},{8,9},{9,8},{10,11... | collective-permute-start | bytes 1474568 | tf_op jit(solution)/shard_map/ppermute | solution.py:31
  7.3 12.4 %collective-permute-start.2 = (bf16[512,384]{1,0:T(8,128)(2,1)}, bf16[512,384]{1,0:T(8,128)(2,1)}, u32[]{:S(2)}, u32[]{:S(2)}) collective-permute-start(bf16[512,384]{1,0:T(8,128)(2,1)} %hidden_0.1.refs_0_.refs_4_), channel_id=1, source_target_pairs={{0,16},{8,24},{16,0},{24,8},{1,17},{9,25},{17,1},{25,9},{2,18},{10... | collective-permute-start | bytes 1179656 | tf_op jit(solution)/shard_map/ppermute | solution.py:31
  11.9 18.6 %collective-permute-start.5 = (bf16[768,384]{1,0:T(8,128)(2,1)}, bf16[768,384]{1,0:T(8,128)(2,1)}, u32[]{:S(2)}, u32[]{:S(2)}) collective-permute-start(bf16[768,384]{1,0:T(8,128)(2,1)} %hidden_2.1.refs_4_.refs_8_), channel_id=1, source_target_pairs={{0,16},{8,24},{16,0},{24,8},{1,17},{9,25},{17,1},{25,9},{2,18},{10... | collective-permute-start | bytes 1769480 | tf_op jit(solution)/shard_map/ppermute | solution.py:31
  21.3 11.9 %collective-permute-start.3 = (bf16[384,640]{1,0:T(8,128)(2,1)}, bf16[384,640]{1,0:T(8,128)(2,1)S(1)}, u32[]{:S(2)}, u32[]{:S(2)}) collective-permute-start(bf16[384,640]{1,0:T(8,128)(2,1)} %after.4.refs_1_), channel_id=1, source_target_pairs={{0,2},{1,3},{2,4},{3,5},{4,6},{5,7},{6,0},{7,1},{8,10},{9,11},{10,... | collective-permute-start | bytes 1474568 | tf_op jit(solution)/shard_map/ppermute | solution.py:36
  22.9 13.9 %collective-permute-start.4 = (bf16[384,640]{1,0:T(8,128)(2,1)}, bf16[384,640]{1,0:T(8,128)(2,1)}, u32[]{:S(2)}, u32[]{:S(2)}) collective-permute-start(bf16[384,640]{1,0:T(8,128)(2,1)} %after.4.refs_1_), channel_id=1, source_target_pairs={{0,1},{1,0},{2,3},{3,2},{4,5},{5,4},{6,7},{7,6},{8,9},{9,8},{10,11... | collective-permute-start | bytes 1474568 | tf_op jit(solution)/shard_map/ppermute | solution.py:31
  23.4 17.3 %collective-permute-start.10 = (bf16[768,384]{1,0:T(8,128)(2,1)}, bf16[768,384]{1,0:T(8,128)(2,1)}, u32[]{:S(2)}, u32[]{:S(2)}) collective-permute-start(bf16[768,384]{1,0:T(8,128)(2,1)} %hidden_2.1.refs_4_.refs_8_), channel_id=1, source_target_pairs={{0,8},{8,0},{16,24},{24,16},{1,9},{9,1},{17,25},{25,17},{2,10},{10... | collective-permute-start | bytes 1769480 | tf_op jit(solution)/shard_map/ppermute | solution.py:31
  25.7 11.2 %collective-permute-start.12 = (bf16[512,384]{1,0:T(8,128)(2,1)}, bf16[512,384]{1,0:T(8,128)(2,1)}, u32[]{:S(2)}, u32[]{:S(2)}) collective-permute-start(bf16[512,384]{1,0:T(8,128)(2,1)} %hidden_5.1.refs_8_.refs_12_), channel_id=1, source_target_pairs={{0,8},{8,0},{16,24},{24,16},{1,9},{9,1},{17,25},{25,17},{2,10},{10... | collective-permute-start | bytes 1179656 | tf_op jit(solution)/shard_map/ppermute | solution.py:31
  30.5 9.7 %collective-permute-start.13 = (bf16[512,384]{1,0:T(8,128)(2,1)}, bf16[512,384]{1,0:T(8,128)(2,1)}, u32[]{:S(2)}, u32[]{:S(2)}) collective-permute-start(bf16[512,384]{1,0:T(8,128)(2,1)} %hidden_5.1.refs_8_.refs_12_), channel_id=1, source_target_pairs={{0,16},{8,24},{16,0},{24,8},{1,17},{9,25},{17,1},{25,9},{2,18},{10... | collective-permute-start | bytes 1179656 | tf_op jit(solution)/shard_map/ppermute | solution.py:31
  33.2 9.0 %collective-permute-start.9 = (bf16[512,384]{1,0:T(8,128)(2,1)}, bf16[512,384]{1,0:T(8,128)(2,1)}, u32[]{:S(2)}, u32[]{:S(2)}) collective-permute-start(bf16[512,384]{1,0:T(8,128)(2,1)} %collective-permute-done.2.refs_2_.refs_6_), channel_id=1, source_target_pairs={{0,8},{8,0},{16,24},{24,16},{1,9},{9,1},{17,25},{25,17},{2,10},{10... | collective-permute-start | bytes 1179656 | tf_op jit(solution)/shard_map/ppermute | solution.py:31
  36.8 7.5 %collective-permute-start.11 = (bf16[768,384]{1,0:T(8,128)(2,1)}, bf16[768,384]{1,0:T(8,128)(2,1)}, u32[]{:S(2)}, u32[]{:S(2)}) collective-permute-start(bf16[768,384]{1,0:T(8,128)(2,1)} %collective-permute-done.5.refs_2_.refs_6_.refs_10_), channel_id=1, source_target_pairs={{0,8},{8,0},{16,24},{24,16},{1,9},{9,1},{17,25},{25,17},{2,10},{10... | collective-permute-start | bytes 1769480 | tf_op jit(solution)/shard_map/ppermute | solution.py:31
  36.8 15.7 %collective-permute-start.6 = (bf16[384,640]{1,0:T(8,128)(2,1)}, bf16[384,640]{1,0:T(8,128)(2,1)}, u32[]{:S(2)}, u32[]{:S(2)}) collective-permute-start(bf16[384,640]{1,0:T(8,128)(2,1)} %after.5.refs_13_.refs_2_), channel_id=1, source_target_pairs={{0,2},{1,3},{2,4},{3,5},{4,6},{5,7},{6,0},{7,1},{8,10},{9,11},{10,... | collective-permute-start | bytes 1474568 | tf_op jit(solution)/shard_map/ppermute | solution.py:36
  40.2 12.4 %collective-permute-start.7 = (bf16[384,640]{1,0:T(8,128)(2,1)}, bf16[384,640]{1,0:T(8,128)(2,1)S(1)}, u32[]{:S(2)}, u32[]{:S(2)}) collective-permute-start(bf16[384,640]{1,0:T(8,128)(2,1)} %after.5.refs_13_.refs_2_), channel_id=1, source_target_pairs={{0,1},{1,0},{2,3},{3,2},{4,5},{5,4},{6,7},{7,6},{8,9},{9,8},{10,11... | collective-permute-start | bytes 1474568 | tf_op jit(solution)/shard_map/ppermute | solution.py:31
  40.7 12.6 %collective-permute-start.18 = (bf16[384,640]{1,0:T(8,128)(2,1)S(1)}, bf16[384,640]{1,0:T(8,128)(2,1)}, u32[]{:S(2)}, u32[]{:S(2)}) collective-permute-start(bf16[384,640]{1,0:T(8,128)(2,1)S(1)} %copy-done.4), channel_id=1, source_target_pairs={{0,16},{8,24},{16,0},{24,8},{1,17},{9,25},{17,1},{25,9},{2,18},{10... | collective-permute-start | bytes 1474568 | tf_op jit(solution)/shard_map/ppermute | solution.py:31
  56.8 28.9 %all-to-all-start = ((bf16[4,384,640]{2,1,0:T(8,128)(2,1)}), bf16[4,384,640]{2,1,0:T(8,128)(2,1)}, u32[]{:S(2)}, u32[]{:S(2)}) async-start(bf16[4,384,640]{2,1,0:T(8,128)(2,1)} %own_features.1.refs_5_), calls=%async_computation | async-start | bytes 3932160 | tf_op jit(solution)/shard_map/all_to_all | solution.py:432
  61.4 20.2 %collective-permute-start.16 = (f32[4,32,1536]{2,1,0:T(8,128)}, f32[4,32,1536]{2,1,0:T(8,128)}, u32[]{:S(2)}, u32[]{:S(2)}) collective-permute-start(f32[4,32,1536]{2,1,0:T(8,128)} %get-tuple-element.18.refs_2_), channel_id=1, source_target_pairs={{0,1},{1,0},{2,3},{3,2},{4,5},{5,4},{6,7},{7,6},{8,9},{9,8},{10,11... | collective-permute-start | bytes 2359304 | tf_op jit(solution)/shard_map/ppermute | solution.py:31
  62.6 15.1 %collective-permute-start.15 = (bf16[384,640]{1,0:T(8,128)(2,1)S(1)}, bf16[384,640]{1,0:T(8,128)(2,1)}, u32[]{:S(2)}, u32[]{:S(2)}) collective-permute-start(bf16[384,640]{1,0:T(8,128)(2,1)S(1)} %copy-done.7), channel_id=1, source_target_pairs={{0,2},{1,3},{2,4},{3,5},{4,6},{5,7},{6,0},{7,1},{8,10},{9,11},{10,... | collective-permute-start | bytes 1474568 | tf_op jit(solution)/shard_map/ppermute | solution.py:36
  85.8 25.4 %all-to-all-start.1 = ((f32[4,32,1536]{2,1,0:T(8,128)}), f32[4,32,1536]{2,1,0:T(8,128)S(1)}, u32[]{:S(2)}, u32[]{:S(2)}) async-start(f32[4,32,1536]{2,1,0:T(8,128)} %hidden_pair.1.refs_11_), calls=%async_computation.1 | async-start | bytes 1572864 | tf_op jit(solution)/shard_map/all_to_all | solution.py:353
  89.4 19.4 %collective-permute-start.23 = (f32[4,32,1536]{2,1,0:T(8,128)}, f32[4,32,1536]{2,1,0:T(8,128)}, u32[]{:S(2)}, u32[]{:S(2)}) collective-permute-start(f32[4,32,1536]{2,1,0:T(8,128)} %get-tuple-element.20.refs_4_), channel_id=1, source_target_pairs={{0,1},{1,0},{2,3},{3,2},{4,5},{5,4},{6,7},{7,6},{8,9},{9,8},{10,11... | collective-permute-start | bytes 2359304 | tf_op jit(solution)/shard_map/ppermute | solution.py:31
  90.6 25.3 %collective-permute-start.20 = (bf16[384,640]{1,0:T(8,128)(2,1)}, bf16[384,640]{1,0:T(8,128)(2,1)}, u32[]{:S(2)}, u32[]{:S(2)}) collective-permute-start(bf16[384,640]{1,0:T(8,128)(2,1)} %get-tuple-element.24), channel_id=1, source_target_pairs={{0,8},{8,0},{16,24},{24,16},{1,9},{9,1},{17,25},{25,17},{2,10},{10... | collective-permute-start | bytes 1474568 | tf_op jit(solution)/shard_map/ppermute | solution.py:31
  90.6 25.3 %collective-permute-start.21 = (bf16[384,640]{1,0:T(8,128)(2,1)}, bf16[384,640]{1,0:T(8,128)(2,1)}, u32[]{:S(2)}, u32[]{:S(2)}) collective-permute-start(bf16[384,640]{1,0:T(8,128)(2,1)} %get-tuple-element.25), channel_id=1, source_target_pairs={{0,16},{8,24},{16,0},{24,8},{1,17},{9,25},{17,1},{25,9},{2,18},{10... | collective-permute-start | bytes 1474568 | tf_op jit(solution)/shard_map/ppermute | solution.py:31
  91.1 24.9 %collective-permute-start.22 = (bf16[384,640]{1,0:T(8,128)(2,1)}, bf16[384,640]{1,0:T(8,128)(2,1)}, u32[]{:S(2)}, u32[]{:S(2)}) collective-permute-start(bf16[384,640]{1,0:T(8,128)(2,1)} %get-tuple-element.26), channel_id=1, source_target_pairs={{0,24},{8,16},{16,8},{24,0},{1,25},{9,17},{17,9},{25,1},{2,26},{10... | collective-permute-start | bytes 1474568 | tf_op jit(solution)/shard_map/ppermute | solution.py:31
  111.1 25.3 %all-to-all-start.2 = ((f32[4,32,1536]{2,1,0:T(8,128)}), f32[4,32,1536]{2,1,0:T(8,128)}, u32[]{:S(2)}, u32[]{:S(2)}) async-start(f32[4,32,1536]{2,1,0:T(8,128)} %add.44.refs_16_), calls=%async_computation.2 | async-start | bytes 1572864 | tf_op jit(solution)/shard_map/all_to_all | solution.py:353
  138.6 9.9 %all-to-all-start.3 = ((f32[32,1,128]{2,1,0:T(1,128)}), f32[32,1,128]{2,1,0:T(1,128)S(1)}, u32[]{:S(2)}, u32[]{:S(2)}) async-start(f32[32,1,128]{2,1,0:T(1,128)} %bitcast.13), calls=%async_computation.3 | async-start | bytes 32768 | tf_op jit(solution)/shard_map/all_to_all | solution.py:452
  (14 other events, 86.0 us)
